TPU v7x, 32 devices: a whole 2x2x4 slice. The times are simulated.
32 devices in a mesh: var: 16 (over z, y, x), samp: 2 (over core).
Axes of the slice: x: 2, y: 2, z: 4, core: 2. Of those that a mesh axis runs over, the one named last changes fastest.
Arguments:
- data: float32 [512, 8192], P('samp', 'var'), may hold values from -6 to 6
- tiles: float32 [16, 3, 512, 512], P('var'), as said below
- offsets: int32 [16, 3], P('var'), may hold values from 0 to 5, as said below
- step: float32 [1], replicated, may hold values from 0.3 to 0.7
Outputs:
- new_tiles: float32 [16, 3, 512, 512], P('var', None, 'samp')
Inputs may be any that keep to these rules, and one draw needn't show every extreme that they name: Slot 0 of every block row has offset 0. Every other slot holds 0 (empty) or an offset of 1 to 5; live slots come first in a row and their offsets differ. Some block row has all 3 slots live, one of them at offset 5. `tiles`: tiles of empty slots are zero. Slot 0 is symmetric with its diagonal between 1 and 2.
All inputs are finite; a program needn't handle non-finite values.
Results may differ from a plain program's by a relative error of at most 0.0003.
Values sent between devices are 32-bit elements; how exact they have to be, the bound alone decides.
No kernel may reach another device: no remote copies, remote signals or barrier semaphores. Data moves between devices by JAX's collectives and lax.ppermute only.
A program may use at most 64 MiB of HBM per device.

v0:
```python
import functools

import jax
import jax.numpy as jnp
from jax import lax
from jax.experimental import pallas as pl
from jax.experimental.pallas import tpu as pltpu
from jax.sharding import PartitionSpec as P

penalty_weight = 0.05
BAND = 6
VMEM_LIMIT = 48 * 1024 * 1024
NN = (((1,), (0,)), ((), ()))
NT = (((1,), (1,)), ((), ()))
f32, bf16 = jnp.float32, jnp.bfloat16


def params(**kw):
    return pltpu.CompilerParams(vmem_limit_bytes=VMEM_LIMIT, **kw)


def cost(flops, nbytes):
    return pl.CostEstimate(flops=0, bytes_accessed=0, transcendentals=0)


def any_spec():
    return pl.BlockSpec(memory_space=pl.ANY)


def vmem_spec():
    return pl.BlockSpec(memory_space=pltpu.VMEM)


def smem_spec():
    return pl.BlockSpec(memory_space=pltpu.SMEM)


def split(value):
    high = value.astype(bf16)
    return high, (value - high.astype(f32)).astype(bf16)


def dot3(left, right, dims):
    dot = functools.partial(lax.dot_general, dimension_numbers=dims, preferred_element_type=f32)
    return dot(left[0], right[0]) + (dot(left[0], right[1]) + dot(left[1], right[0]))


def route(p, k, flip):
    xbit = k & 1
    ybit = (((p + k) >> 1) ^ (p >> 1)) & 1
    first = jnp.where(flip == 0, xbit, ybit)
    last = jnp.where(flip == 0, ybit, xbit)
    return last, first + 2 * ((p + k) >> 2)


def place():
    return lax.axis_index("var") & 3, lax.axis_index("samp") & 1


def last_partner(p, flip):
    return jnp.where(flip == 0, p ^ 2, p ^ 1)


def wanted(first, last, groups):
    found = set()
    for p in range(4):
        for k in range(1, BAND):
            bits = p ^ ((p + k) & 3)
            if bits & first and (p + k) >> 2 == groups:
                found.add(p ^ (bits & last))
    return found


def hop(var_count, samp_count, kind, reverse=False):
    pairs = []
    for var in range(var_count):
        for samp in range(samp_count):
            first, last = (2, 1) if samp & 1 else (1, 2)
            back = (var - 4) % var_count
            use = True
            if kind == "first":
                target = var ^ first
            elif kind == "last":
                target = var ^ last
            elif kind == "group":
                target = back
            elif kind == "two":
                target = back ^ first
                use = (var & 3) == 0
            elif kind == "column":
                target = back
                use = (var & 3) in wanted(first, last, 2)
            else:
                target = back ^ last
                use = (var & 3) in wanted(first, last, 2)
            if kind == "column" and not use:
                target, use = var, True
            pair = (var * samp_count + samp, target * samp_count + samp)
            if use:
                pairs.append(pair[::-1] if reverse else pair)
    return pairs


def send(value, kind, reverse=False):
    pairs = hop(lax.axis_size("var"), lax.axis_size("samp"), kind, reverse)
    return lax.ppermute(value, ("var", "samp"), pairs)


def forward_kernel(gate_ref, data_ref, tile_ref, own_ref, far_ref):
    del gate_ref
    slot = pl.program_id(0)
    value = dot3(split(data_ref[...]), split(tile_ref[...]), NN)

    @pl.when(slot == 0)
    def _():
        own_ref[...] = value

    @pl.when(slot > 0)
    def _():
        far_ref[...] = value


def forward(gate, data, tiles):
    slots, block = tiles.shape[:2]
    rows = data.shape[0]
    return pl.pallas_call(
        forward_kernel,
        grid=(slots,),
        in_specs=[
            smem_spec(),
            pl.BlockSpec((rows, block), lambda j: (0, 0)),
            pl.BlockSpec((None, block, block), lambda j: (j, 0, 0)),
        ],
        out_specs=[
            pl.BlockSpec((rows, block), lambda j: (0, 0)),
            pl.BlockSpec((None, rows, block), lambda j: (jnp.maximum(j - 1, 0), 0, 0)),
        ],
        out_shape=[
            jax.ShapeDtypeStruct((rows, block), f32),
            jax.ShapeDtypeStruct((slots - 1, rows, block), f32),
        ],
        compiler_params=params(),
        cost_estimate=cost(6 * slots * rows * block * block, 4 * slots * block * (block + 2 * rows)),
        name="forward",
    )(gate, data, tiles)


CODES = (0, 1, 2, 3, 5)


def choose_kernel(slots, count, offs_ref, *refs):
    sources, outs, sems = refs[:count], refs[count:-1], refs[-1]
    p, flip = place()
    target = last_partner(p, flip)
    copies = []
    for slot in range(slots):
        last, code = route(target, offs_ref[0, slot + 1], flip)
        for value, source in zip(CODES, sources):
            copy = pltpu.make_async_copy(source, outs[slot], sems.at[slot])
            pl.when((last == 1) & (code == value))(copy.start)
        known = (last == 1) & (code <= CODES[count - 1])
        copies.append((known, pltpu.make_async_copy(sources[0], outs[slot], sems.at[slot])))
    for known, copy in copies:
        pl.when(known)(copy.wait)


def choose(offsets_next, *sources):
    slots = offsets_next.shape[1] - 1
    own = sources[0]
    return pl.pallas_call(
        functools.partial(choose_kernel, slots, len(sources)),
        in_specs=[smem_spec()] + [any_spec()] * len(sources),
        out_specs=[any_spec()] * slots,
        out_shape=[jax.ShapeDtypeStruct(own.shape, f32)] * slots,
        scratch_shapes=[pltpu.SemaphoreType.DMA((slots,))],
        compiler_params=params(),
        cost_estimate=cost(0, 8 * slots * own.size),
        name="choose",
    )(offsets_next, *sources)


def start_pick(offset, sources, target, sem):
    p, flip = place()
    last, code = route(p, offset, flip)
    for value, source in zip(CODES, sources[:4]):
        pl.when((last == 0) & (code == value))(pltpu.make_async_copy(source, target, sem).start)
    over_last = last == 1
    if len(sources) > 5:
        over_last = over_last & (code != CODES[4])
        pl.when(code == CODES[4])(pltpu.make_async_copy(sources[5], target, sem).start)
    pl.when(over_last)(pltpu.make_async_copy(sources[4], target, sem).start)


def backward_kernel(slots, offs_ref, tile_ref, own, first, group, both, *refs):
    lasts = refs[:slots]
    out_ref, picked, sems = refs[slots:]
    slot = pl.program_id(0)

    @pl.when(slot == 0)
    def _():
        out_ref[...] = jnp.zeros_like(out_ref)
        for each in range(slots):
            sources = (own, first, group, both, lasts[each])
            start_pick(offs_ref[0, each + 1], sources, picked.at[each], sems.at[each])

    pltpu.make_async_copy(own, picked.at[slot], sems.at[slot]).wait()
    mirror = jnp.where(offs_ref[0, slot + 1] > 0, 1.0, 0.0).astype(f32)
    out_ref[...] += mirror * dot3(split(picked[slot]), split(tile_ref[...]), NT)


def backward(offsets, tiles, sources):
    slots, block = tiles.shape[0] - 1, tiles.shape[1]
    own = sources[0]
    rows = own.shape[0]
    return pl.pallas_call(
        functools.partial(backward_kernel, slots),
        grid=(slots,),
        in_specs=[smem_spec(), pl.BlockSpec((None, block, block), lambda j: (j + 1, 0, 0))]
        + [any_spec()] * len(sources),
        out_specs=pl.BlockSpec((rows, block), lambda j: (0, 0)),
        out_shape=jax.ShapeDtypeStruct((rows, block), f32),
        scratch_shapes=[pltpu.VMEM((slots, rows, block), f32), pltpu.SemaphoreType.DMA((slots,))],
        compiler_params=params(),
        cost_estimate=cost(6 * slots * rows * block * block, 4 * slots * block * (block + rows)),
        name="backward",
    )(offsets, tiles, *sources)


def bins_kernel(slots, offs_ref, next_ref, own_in, mine_ref, theirs_ref, own_out, first, group, both, two):
    p, flip = place()
    target = last_partner(p, flip)
    totals = [own_in[...], None, None, None, None]
    for which, value in enumerate((0, 1, 2, 3, 5)):
        total = totals[which]
        for slot in range(slots):
            for there, offs, source in ((0, offs_ref, mine_ref), (1, next_ref, theirs_ref)):
                offset = offs[0, slot + 1]
                last, code = route(jnp.where(there == 1, target, p), offset, flip)
                use = (last == there) & (code == value) & (offset > 0)
                term = jnp.where(use, source[slot], 0.0)
                total = term if total is None else total + term
        totals[which] = total
    for ref, total in zip((own_out, first, group, both, two), totals):
        ref[...] = total


def make_bins(offsets, offsets_next, own, mine, theirs):
    slots, rows, block = mine.shape
    step = rows // 4
    flat = pl.BlockSpec((step, block), lambda i: (i, 0))
    deep = pl.BlockSpec((slots, step, block), lambda i: (0, i, 0))
    return pl.pallas_call(
        functools.partial(bins_kernel, slots),
        grid=(rows // step,),
        in_specs=[smem_spec(), smem_spec(), flat, deep, deep],
        out_specs=[flat] * 5,
        out_shape=[jax.ShapeDtypeStruct((rows, block), f32)] * 5,
        compiler_params=params(),
        cost_estimate=cost(20 * rows * block, 40 * rows * block),
        name="bins",
    )(offsets, offsets_next, own, mine, theirs)


def halves(pair):
    return lax.axis_index("samp") if pair else 0


def right_kernel(slots, pair, offs_ref, data_ref, image_ref, own, first, group, both, *refs):
    lasts = refs[:slots]
    keep_ref, send_ref, high_ref, low_ref, picked, sems = refs[-6:]
    for slot in range(slots):
        sources = (own, first, group, both, lasts[slot])
        start_pick(offs_ref[0, slot + 1], sources, picked.at[slot], sems.at[slot])
    half = image_ref.shape[1] // 2
    samp = halves(pair)
    data = data_ref[...]
    image = image_ref[...]
    data_turned = split(data.T)
    high_ref[...], low_ref[...] = data_turned
    turned = split(image.T)
    image_pair, data_pair = split(image), split(data)

    def store(which, total):
        lower, upper = total[:half], total[half:]

        @pl.when(samp == 0)
        def _():
            keep_ref[which] = lower
            send_ref[which] = upper

        @pl.when(samp != 0)
        def _():
            keep_ref[which] = upper
            send_ref[which] = lower

    store(0, dot3(turned, data_pair, NN) + dot3(data_turned, image_pair, NN))
    for slot in range(slots):
        pltpu.make_async_copy(own, picked.at[slot], sems.at[slot]).wait()
        store(slot + 1, dot3(turned, split(picked[slot]), NN))


def right(offsets, data, image, gate, sources, pair):
    slots = offsets.shape[1] - 1
    rows, block = data.shape
    part = jax.ShapeDtypeStruct((slots + 1, block // 2, block), f32)
    turned = jax.ShapeDtypeStruct((block, rows), bf16)
    return pl.pallas_call(
        functools.partial(right_kernel, slots, pair),
        in_specs=[smem_spec(), vmem_spec(), vmem_spec()] + [any_spec()] * (len(gate) + len(sources)),
        out_specs=[vmem_spec()] * 4,
        out_shape=[part, part, turned, turned],
        scratch_shapes=[pltpu.VMEM((slots, rows, block), f32), pltpu.SemaphoreType.DMA((slots,))],
        compiler_params=params(),
        cost_estimate=cost(6 * (slots + 2) * rows * block * block, 4 * (slots + 1) * block * (block + rows)),
        name="right",
    )(offsets, data, image, *sources, *gate)


def left_kernel(start, begin, pair, offs_ref, keep_in, send_in, high_ref, low_ref, own, first, group, both, two, *refs):
    lasts = refs[:-4]
    keep_ref, send_ref, picked, sems = refs[-4:]
    slots = range(start, start + len(lasts))
    for slot, last_ref in zip(slots, lasts):
        sources = (own, first, group, both, last_ref, two)
        start_pick(offs_ref[0, slot], sources, picked.at[slot - start], sems.at[slot - start])
    half = send_ref.shape[1]
    samp = halves(pair)
    mine = samp * half
    yours = half - mine
    for slot in range(begin, start):
        keep_ref[slot - begin] = keep_in[slot]
        send_ref[slot - begin] = send_in[slot]
    for slot in slots:
        pltpu.make_async_copy(own, picked.at[slot - start], sems.at[slot - start]).wait()
        chosen = split(picked[slot - start])
        for out_ref, in_ref, row in ((send_ref, send_in, yours), (keep_ref, keep_in, mine)):
            rows = pl.ds(pl.multiple_of(row, half), half)
            out_ref[slot - begin] = in_ref[slot] + dot3((high_ref[rows], low_ref[rows]), chosen, NN)


def left(offsets, start, begin, parts, turned, sources, lasts, pair):
    keep = parts[0]
    block, rows = turned[0].shape
    count = start + len(lasts) - begin
    part = jax.ShapeDtypeStruct((count,) + keep.shape[1:], f32)
    return pl.pallas_call(
        functools.partial(left_kernel, start, begin, pair),
        in_specs=[smem_spec()] + [vmem_spec()] * 4 + [any_spec()] * (len(sources) + len(lasts)),
        out_specs=[vmem_spec()] * 2,
        out_shape=[part, part],
        scratch_shapes=[pltpu.VMEM((len(lasts), rows, block), f32), pltpu.SemaphoreType.DMA((len(lasts),))],
        compiler_params=params(),
        cost_estimate=cost(6 * len(lasts) * rows * block * block, 4 * count * block * (2 * block + rows)),
        name="left",
    )(offsets, *parts, *turned, *sources, *lasts)


def finish_kernel(begin, factor, offs_ref, step_ref, tile_ref, keep_ref, other_ref, *refs):
    out_ref = refs[-1]
    slot = pl.program_id(0) + begin
    half, block = out_ref.shape
    step_size = step_ref[0]
    old = tile_ref[...]
    bound = step_size * penalty_weight
    stepped = old - (step_size * factor) * (keep_ref[...] + other_ref[...])

    def shrunk(value):
        return value - jnp.clip(value, -bound, bound)

    @pl.when(slot == 0)
    def _():
        rows = lax.axis_index("samp") * half + lax.broadcasted_iota(jnp.int32, (half, block), 0)
        on_diag = rows == lax.broadcasted_iota(jnp.int32, (half, block), 1)
        out_ref[...] = jnp.where(on_diag, stepped + step_size / jnp.where(on_diag, old, 1.0), shrunk(stepped))

    @pl.when(slot > 0)
    def _():
        out_ref[...] = jnp.where(offs_ref[0, slot] > 0, shrunk(stepped), 0.0)


def finish(offsets, step, tiles, keep, other, factor, begin, earlier=()):
    slots, block = tiles.shape[:2]
    count, half = keep.shape[:2]
    spec = pl.BlockSpec((None, half, block), lambda j: (j, 0, 0))
    tile_spec = pl.BlockSpec((None, half, block), lambda j: (j + begin, lax.axis_index("samp"), 0))
    return pl.pallas_call(
        functools.partial(finish_kernel, begin, factor),
        grid=(count,),
        in_specs=[smem_spec(), smem_spec(), tile_spec, spec, spec] + [any_spec()] * len(earlier),
        out_specs=pl.BlockSpec((None, half, block), lambda j: (j + begin, 0, 0)),
        out_shape=jax.ShapeDtypeStruct((slots, half, block), f32),
        input_output_aliases={5: 0} if earlier else {},
        compiler_params=params(),
        cost_estimate=cost(6 * keep.size, 16 * keep.size),
        name="finish",
    )(offsets, step, tiles, keep, other, *earlier)


def after(value, other):
    return lax.optimization_barrier((value, other))[0]


def swap(value):
    return lax.ppermute(value, "samp", [(0, 1), (1, 0)])


def shards(data, tiles, offsets, step):
    local_tiles = tiles[0]
    slot_count, block = local_tiles.shape[:2]
    samp_count = lax.axis_size("samp")
    pair = samp_count == 2
    factor = 1.0 / (2.0 * data.shape[0] * samp_count)

    offsets_next = send(offsets, "last")
    data_first = send(data, "first")
    data_group = send(data, "group")
    own, far = forward(offsets_next, data, local_tiles)
    theirs = send(far, "last")
    data_both = send(after(data_first, data_group), "group")
    own, bin_first, bin_group, bin_both, bin_two = make_bins(offsets, offsets_next, own, far, theirs)
    bin_group = bin_group + send(bin_both, "first") + send(bin_two, "two", reverse=True)
    data_two = send(after(data_both, own), "column")
    chosen = choose(offsets_next, data, data_first, data_group, data_both, data_two)
    data_sources = (data, data_first, data_group, data_both) + tuple(send(each, "last") for each in chosen)
    got_first = send(after(bin_first, bin_group), "first")
    got_group = send(bin_group, "group", reverse=True)
    image = own + backward(offsets, local_tiles, data_sources) + got_first + got_group

    image_group = send(image, "group")
    image_first = send(image, "first")
    image_group, image_first = lax.optimization_barrier((image_group, image_first))
    image_both = send(image_group, "first")
    chosen = choose(offsets_next, image, image_first, image_group, image_both)
    image_lasts = [send(each, "last") for each in chosen]
    keep, other, high, low = right(offsets, data, image, (chosen[0],), data_sources, pair)
    image_two = send(after(image_both, image_lasts[0]), "direct")
    image_sources = (image, image_first, image_group, image_both, image_two)
    if pair:
        begin, result = 0, ()
        for slot in range(1, slot_count):
            keep_now, other_now = left(
                offsets, slot, begin, (keep, other), (high, low), image_sources, image_lasts[slot - 1 : slot], pair)
            result = (finish(offsets, step, local_tiles, keep_now, swap(other_now), factor, begin, result),)
            begin = slot + 1
        return result[0][None]
    keep, other = left(offsets, 1, 0, (keep, other), (high, low), image_sources, image_lasts, pair)
    summed = lax.psum_scatter(jnp.concatenate([keep, other], axis=1), "samp", scatter_dimension=1, tiled=True)
    none = jnp.zeros_like(summed)
    return finish(offsets, step, local_tiles, summed, none, factor, 0)[None]


def solution(mesh):
    return jax.shard_map(
        shards,
        mesh=mesh,
        in_specs=(P("samp", "var"), P("var", None, None, None), P("var", None), P()),
        out_specs=P("var", None, "samp", None),
        check_vma=False,
    )
```

profile of v0, /device:TPU:7, one launch (start us, length us, event | category | flops | bytes accessed | tf_op | source)
XLA Modules:
  0.0 135.4 jit_solution(2871930838793277473)
XLA Ops:
  0.3 2.3 %collective-permute-done.gate_ref.next_ref.offs_ref = s32[1,3]{1,0:T(1,128)S(1)} collective-permute-done((s32[1,3]{1,0:T(1,128)}, s32[1,3]{1,0:T(1,128)S(1)}, u32[]{:S(2)}, u32[]{:S(2)}) %collective-permute-start) | collective-permute-done | bytes 44 | tf_op jit(solution)/shard_map/ppermute | solution.py:106
  2.5 1.9 %copy-done = f32[1,3,512,512]{3,2,1,0:T(8,128)S(1)} copy-done((f32[1,3,512,512]{3,2,1,0:T(8,128)S(1)}, f32[1,3,512,512]{3,2,1,0:T(8,128)}, u32[]{:S(2)}) %copy-start) | copy-done | bytes 3145752
  5.5 2.5 %forward.1 = (f32[256,512]{1,0:T(8,128)S(1)}, f32[2,256,512]{2,1,0:T(8,128)S(1)}) custom-call(s32[1,3]{1,0:T(1,128)S(1)} %collective-permute-done.gate_ref.next_ref.offs_ref, f32[256,512]{1,0:T(8,128)S(1)} %copy-done.2, f32[3,512,512]{2,1,0:T(8,128)S(1)} %bitcast.3), custom_call_target="tpu_custom_call" | custom-call | tf_op jit(solution)/shard_map/forward/pallas_call | solution.py:126
  8.3 3.5 %collective-permute-start.3 = (f32[256,512]{1,0:T(8,128)S(1)}, f32[256,512]{1,0:T(8,128)S(1)}, u32[]{:S(2)}, u32[]{:S(2)}) collective-permute-start(f32[256,512]{1,0:T(8,128)S(1)} %copy-done.2), channel_id=1, source_target_pairs={{0,24},{1,25},{2,26},{3,27},{4,28},{5,29},{6,30},{7,31},{8,0},{9,1... | collective-permute-start | bytes 1572872 | tf_op jit(solution)/shard_map/ppermute | solution.py:106
  11.8 8.3 %collective-permute-done.2.refs_1_.first = f32[256,512]{1,0:T(8,128)S(1)} collective-permute-done((f32[256,512]{1,0:T(8,128)S(1)}, f32[256,512]{1,0:T(8,128)S(1)}, u32[]{:S(2)}, u32[]{:S(2)}) %collective-permute-start.2) | collective-permute-done | bytes 524320 | tf_op jit(solution)/shard_map/ppermute | solution.py:106
  20.7 4.0 %collective-permute-start.4 = (f32[256,512]{1,0:T(8,128)S(1)}, f32[256,512]{1,0:T(8,128)S(1)}, u32[]{:S(2)}, u32[]{:S(2)}) collective-permute-start(f32[256,512]{1,0:T(8,128)S(1)} %collective-permute-done.2.refs_1_.first), channel_id=1, source_target_pairs={{0,24},{1,25},{2,26},{3,27},{4,28},{5,29},{6,30},{7,31},{8,0},{9,1... | collective-permute-start | bytes 1572872 | tf_op jit(solution)/shard_map/ppermute | solution.py:106
  24.7 2.9 %collective-permute-done.1.theirs_ref = f32[2,256,512]{2,1,0:T(8,128)S(1)} collective-permute-done((f32[2,256,512]{2,1,0:T(8,128)S(1)}, f32[2,256,512]{2,1,0:T(8,128)S(1)}, u32[]{:S(2)}, u32[]{:S(2)}) %collective-permute-start.1) | collective-permute-done | bytes 1048608 | tf_op jit(solution)/shard_map/ppermute | solution.py:106
  30.3 1.7 %collective-permute-done.4.refs_3_.both = f32[256,512]{1,0:T(8,128)S(1)} collective-permute-done((f32[256,512]{1,0:T(8,128)S(1)}, f32[256,512]{1,0:T(8,128)S(1)}, u32[]{:S(2)}, u32[]{:S(2)}) %collective-permute-start.4) | collective-permute-done | bytes 524320 | tf_op jit(solution)/shard_map/ppermute | solution.py:106
  32.7 5.7 %collective-permute-done.8 = f32[256,512]{1,0:T(8,128)S(1)} collective-permute-done((f32[256,512]{1,0:T(8,128)S(1)}, f32[256,512]{1,0:T(8,128)S(1)}, u32[]{:S(2)}, u32[]{:S(2)}) %collective-permute-start.8) | collective-permute-done | bytes 524320 | tf_op jit(solution)/shard_map/ppermute | solution.py:106
  40.5 14.4 %collective-permute-start.6 = (f32[256,512]{1,0:T(8,128)S(1)}, f32[256,512]{1,0:T(8,128)S(1)}, u32[]{:S(2)}, u32[]{:S(2)}) collective-permute-start(f32[256,512]{1,0:T(8,128)S(1)} %get-tuple-element.35), channel_id=1, source_target_pairs={{0,4},{1,3},{2,6},{3,1},{4,0},{5,7},{6,2},{7,5},{8,12},{9,11},{10,... | collective-permute-start | bytes 1572872 | tf_op jit(solution)/shard_map/ppermute | solution.py:106
  55.1 9.0 %collective-permute-done.6.refs_0_ = f32[256,512]{1,0:T(8,128)S(1)} collective-permute-done((f32[256,512]{1,0:T(8,128)S(1)}, f32[256,512]{1,0:T(8,128)S(1)}, u32[]{:S(2)}, u32[]{:S(2)}) %collective-permute-start.6) | collective-permute-done | bytes 524320 | tf_op jit(solution)/shard_map/ppermute | solution.py:106
  64.0 9.0 %collective-permute-done.7.refs_1_ = f32[256,512]{1,0:T(8,128)S(1)} collective-permute-done((f32[256,512]{1,0:T(8,128)S(1)}, f32[256,512]{1,0:T(8,128)S(1)}, u32[]{:S(2)}, u32[]{:S(2)}) %collective-permute-start.7) | collective-permute-done | bytes 524320 | tf_op jit(solution)/shard_map/ppermute | solution.py:106
  73.1 2.7 %backward.1 = f32[256,512]{1,0:T(8,128)S(1)} custom-call(s32[1,3]{1,0:T(1,128)S(1)} %copy-done.4, f32[3,512,512]{2,1,0:T(8,128)} %bitcast.2, f32[256,512]{1,0:T(8,128)S(1)} %copy-done.3, f32[256,512]{1,0:T(8,128)S(1)} %collective-permute-done.2.refs_1_.first, f32[256,512]{1,0:T(8,128)S(1)} %collective-permute-done.3.refs_2_.group, ...), custom_call_target="tpu_custom_call" | custom-call | tf_op jit(solution)/shard_map/backward/pallas_call | solution.py:215
  76.0 3.8 %collective-permute-start.12 = (f32[256,512]{1,0:T(8,128)S(1)}, f32[256,512]{1,0:T(8,128)S(1)}, u32[]{:S(2)}, u32[]{:S(2)}) collective-permute-start(f32[256,512]{1,0:T(8,128)S(1)} %add_add_fusion.refs_0_.image_ref.own), channel_id=1, source_target_pairs={{0,24},{1,25},{2,26},{3,27},{4,28},{5,29},{6,30},{7,31},{8,0},{9,1... | collective-permute-start | bytes 1572872 | tf_op jit(solution)/shard_map/ppermute | solution.py:106
  79.8 9.4 %collective-permute-done.12.refs_2_.group = f32[256,512]{1,0:T(8,128)S(1)} collective-permute-done((f32[256,512]{1,0:T(8,128)S(1)}, f32[256,512]{1,0:T(8,128)S(1)}, u32[]{:S(2)}, u32[]{:S(2)}) %collective-permute-start.12) | collective-permute-done | bytes 524320 | tf_op jit(solution)/shard_map/ppermute | solution.py:106
  89.2 8.3 %collective-permute-done.14.refs_3_.both = f32[256,512]{1,0:T(8,128)S(1)} collective-permute-done((f32[256,512]{1,0:T(8,128)S(1)}, f32[256,512]{1,0:T(8,128)S(1)}, u32[]{:S(2)}, u32[]{:S(2)}) %collective-permute-start.14) | collective-permute-done | bytes 524320 | tf_op jit(solution)/shard_map/ppermute | solution.py:106
  98.3 8.2 %collective-permute-done.15.refs_0_ = f32[256,512]{1,0:T(8,128)S(1)} collective-permute-done((f32[256,512]{1,0:T(8,128)S(1)}, f32[256,512]{1,0:T(8,128)S(1)}, u32[]{:S(2)}, u32[]{:S(2)}) %collective-permute-start.15) | collective-permute-done | bytes 524320 | tf_op jit(solution)/shard_map/ppermute | solution.py:106
  107.8 5.9 %collective-permute-start.17 = (f32[256,512]{1,0:T(8,128)S(1)}, f32[256,512]{1,0:T(8,128)S(1)}, u32[]{:S(2)}, u32[]{:S(2)}) collective-permute-start(f32[256,512]{1,0:T(8,128)S(1)} %get-tuple-element.50), channel_id=1, source_target_pairs={{0,4},{1,3},{2,6},{3,1},{4,0},{5,7},{6,2},{7,5},{8,12},{9,11},{10,... | collective-permute-start | bytes 1572872 | tf_op jit(solution)/shard_map/ppermute | solution.py:106
  113.8 4.8 %right.1 = (f32[3,256,512]{2,1,0:T(8,128)}, f32[3,256,512]{2,1,0:T(8,128)}, bf16[512,256]{1,0:T(8,128)(2,1)S(1)}, bf16[512,256]{1,0:T(8,128)(2,1)S(1)}) custom-call(s32[1,3]{1,0:T(1,128)S(1)} %copy-done.4, f32[256,512]{1,0:T(8,128)S(1)} %copy-done.3, f32[256,512]{1,0:T(8,128)S(1)} %add_add_fusion.refs_0_.image_ref.own, f32[256,512]{1,0:T(8,128)S(1)} %copy-done.3, ...), custom_call_target="tpu_custom_call" | custom-call | tf_op jit(solution)/shard_map/right/pallas_call | solution.py:307
  118.6 2.6 %left.3 = (f32[2,256,512]{2,1,0:T(8,128)S(1)}, f32[2,256,512]{2,1,0:T(8,128)S(1)}) custom-call(s32[1,3]{1,0:T(1,128)S(1)} %copy-done.4, f32[3,256,512]{2,1,0:T(8,128)} %get-tuple-element.45.keep_in, f32[3,256,512]{2,1,0:T(8,128)} %get-tuple-element.46.send_in, bf16[512,256]{1,0:T(8,128)(2,1)S(1)} %get-tuple-element.47.high_ref, ...), custom_call_target="tpu_custom_call" | custom-call | tf_op jit(solution)/shard_map/left/pallas_call | solution.py:346
  121.2 5.0 %collective-permute-start.19 = (f32[2,256,512]{2,1,0:T(8,128)S(1)}, f32[2,256,512]{2,1,0:T(8,128)S(1)}, u32[]{:S(2)}, u32[]{:S(2)}) collective-permute-start(f32[2,256,512]{2,1,0:T(8,128)S(1)} %get-tuple-element.54), channel_id=1, source_target_pairs={{0,1},{1,0},{2,3},{3,2},{4,5},{5,4},{6,7},{7,6},{8,9},{9,8},{10,11... | collective-permute-start | bytes 3145736 | tf_op jit(solution)/shard_map/ppermute | solution.py:404
  126.2 2.7 %left.2 = (f32[1,256,512]{2,1,0:T(8,128)S(1)}, f32[1,256,512]{2,1,0:T(8,128)S(1)}) custom-call(s32[1,3]{1,0:T(1,128)S(1)} %copy-done.4, f32[3,256,512]{2,1,0:T(8,128)} %get-tuple-element.45.keep_in, f32[3,256,512]{2,1,0:T(8,128)} %get-tuple-element.46.send_in, bf16[512,256]{1,0:T(8,128)(2,1)S(1)} %get-tuple-element.47.high_ref, ...), custom_call_target="tpu_custom_call" | custom-call | tf_op jit(solution)/shard_map/left/pallas_call | solution.py:346
  129.0 2.4 %collective-permute-start.18 = (f32[1,256,512]{2,1,0:T(8,128)S(1)}, f32[1,256,512]{2,1,0:T(8,128)S(1)}, u32[]{:S(2)}, u32[]{:S(2)}) collective-permute-start(f32[1,256,512]{2,1,0:T(8,128)S(1)} %get-tuple-element.52), channel_id=1, source_target_pairs={{0,1},{1,0},{2,3},{3,2},{4,5},{5,4},{6,7},{7,6},{8,9},{9,8},{10,11... | collective-permute-start | bytes 1572872 | tf_op jit(solution)/shard_map/ppermute | solution.py:404
  132.0 1.9 %finish.2.refs_0_ = f32[3,256,512]{2,1,0:T(8,128)} custom-call(s32[1,3]{1,0:T(1,128)S(1)} %copy-done.4, f32[1]{0:T(128)S(6)} %copy.7.step_ref, f32[3,512,512]{2,1,0:T(8,128)S(1)} %bitcast.4, f32[2,256,512]{2,1,0:T(8,128)S(1)} %get-tuple-element.53.keep_ref, f32[2,256,512]{2,1,0:T(8,128)S(1)} %collective-permute-done.19.other_ref), custom_call_target="tpu_custom_call" | custom-call | tf_op jit(solution)/shard_map/finish/pallas_call | solution.py:386
  (38 shorter events, 11.6 us)
Async XLA Ops:
  0.0 2.5 %collective-permute-start = (s32[1,3]{1,0:T(1,128)}, s32[1,3]{1,0:T(1,128)S(1)}, u32[]{:S(2)}, u32[]{:S(2)}) collective-permute-start(s32[1,3]{1,0:T(1,128)} %offs_ref.13), channel_id=1, source_target_pairs={{0,4},{1,3},{2,6},{3,1},{4,0},{5,7},{6,2},{7,5},{8,12},{9,11},{10,... | collective-permute-start | bytes 44 | tf_op jit(solution)/shard_map/ppermute | solution.py:106
  2.5 1.9 %copy-start = (f32[1,3,512,512]{3,2,1,0:T(8,128)S(1)}, f32[1,3,512,512]{3,2,1,0:T(8,128)}, u32[]{:S(2)}) copy-start(f32[1,3,512,512]{3,2,1,0:T(8,128)} %param.5) | copy-start | bytes 9437188
  5.5 22.1 %copy-start.4 = (s32[1,3]{1,0:T(1,128)S(1)}, s32[1,3]{1,0:T(1,128)}, u32[]{:S(2)}) copy-start(s32[1,3]{1,0:T(1,128)} %offs_ref.13) | copy-start | bytes 40
  8.0 19.6 %collective-permute-start.1 = (f32[2,256,512]{2,1,0:T(8,128)S(1)}, f32[2,256,512]{2,1,0:T(8,128)S(1)}, u32[]{:S(2)}, u32[]{:S(2)}) collective-permute-start(f32[2,256,512]{2,1,0:T(8,128)S(1)} %get-tuple-element.31.mine_ref), channel_id=1, source_target_pairs={{0,4},{1,3},{2,6},{3,1},{4,0},{5,7},{6,2},{7,5},{8,12},{9,11},{10,... | collective-permute-start | bytes 3145736 | tf_op jit(solution)/shard_map/ppermute | solution.py:106
  8.3 11.8 %collective-permute-start.2 = (f32[256,512]{1,0:T(8,128)S(1)}, f32[256,512]{1,0:T(8,128)S(1)}, u32[]{:S(2)}, u32[]{:S(2)}) collective-permute-start(f32[256,512]{1,0:T(8,128)S(1)} %copy-done.2), channel_id=1, source_target_pairs={{0,2},{1,5},{2,0},{3,7},{4,6},{5,1},{6,4},{7,3},{8,10},{9,13},{10,... | collective-permute-start | bytes 1572872 | tf_op jit(solution)/shard_map/ppermute | solution.py:106
  8.3 12.3 %collective-permute-start.3 = (f32[256,512]{1,0:T(8,128)S(1)}, f32[256,512]{1,0:T(8,128)S(1)}, u32[]{:S(2)}, u32[]{:S(2)}) collective-permute-start(f32[256,512]{1,0:T(8,128)S(1)} %copy-done.2), channel_id=1, source_target_pairs={{0,24},{1,25},{2,26},{3,27},{4,28},{5,29},{6,30},{7,31},{8,0},{9,1... | collective-permute-start | bytes 1572872 | tf_op jit(solution)/shard_map/ppermute | solution.py:106
  20.7 11.3 %collective-permute-start.4 = (f32[256,512]{1,0:T(8,128)S(1)}, f32[256,512]{1,0:T(8,128)S(1)}, u32[]{:S(2)}, u32[]{:S(2)}) collective-permute-start(f32[256,512]{1,0:T(8,128)S(1)} %collective-permute-done.2.refs_1_.first), channel_id=1, source_target_pairs={{0,24},{1,25},{2,26},{3,27},{4,28},{5,29},{6,30},{7,31},{8,0},{9,1... | collective-permute-start | bytes 1572872 | tf_op jit(solution)/shard_map/ppermute | solution.py:106
  29.1 10.7 %copy-start.3 = (f32[256,512]{1,0:T(8,128)S(1)}, f32[256,512]{1,0:T(8,128)}, u32[]{:S(2)}) copy-start(f32[256,512]{1,0:T(8,128)} %own.3) | copy-start | bytes 1572868
  29.1 3.5 %collective-permute-start.9 = (f32[256,512]{1,0:T(8,128)S(1)}, f32[256,512]{1,0:T(8,128)S(1)}, u32[]{:S(2)}, u32[]{:S(2)}) collective-permute-start(f32[256,512]{1,0:T(8,128)S(1)} %get-tuple-element.40), channel_id=1, source_target_pairs={{26,0},{29,1},{2,8},{5,9},{10,16},{13,17},{18,24},{21,25}} | collective-permute-start | bytes 1572872 | tf_op jit(solution)/shard_map/ppermute | solution.py:106
  30.0 8.4 %collective-permute-start.8 = (f32[256,512]{1,0:T(8,128)S(1)}, f32[256,512]{1,0:T(8,128)S(1)}, u32[]{:S(2)}, u32[]{:S(2)}) collective-permute-start(f32[256,512]{1,0:T(8,128)S(1)} %get-tuple-element.39), channel_id=1, source_target_pairs={{0,2},{1,5},{2,0},{3,7},{4,6},{5,1},{6,4},{7,3},{8,10},{9,13},{10,... | collective-permute-start | bytes 1572872 | tf_op jit(solution)/shard_map/ppermute | solution.py:106
  32.0 7.9 %collective-permute-start.5 = (f32[256,512]{1,0:T(8,128)S(1)}, f32[256,512]{1,0:T(8,128)S(1)}, u32[]{:S(2)}, u32[]{:S(2)}) collective-permute-start(f32[256,512]{1,0:T(8,128)S(1)} %collective-permute-done.4.refs_3_.both), channel_id=1, source_target_pairs={{0,0},{1,1},{2,26},{3,3},{4,4},{5,29},{6,6},{7,7},{8,8},{9,9},{10,... | collective-permute-start | bytes 1572872 | tf_op jit(solution)/shard_map/ppermute | solution.py:106
  38.5 37.3 %collective-permute-start.11 = (f32[256,512]{1,0:T(8,128)S(1)}, f32[256,512]{1,0:T(8,128)S(1)}, u32[]{:S(2)}, u32[]{:S(2)}) collective-permute-start(f32[256,512]{1,0:T(8,128)S(1)} %add_add_fusion.1), channel_id=1, source_target_pairs={{24,0},{25,1},{26,2},{27,3},{28,4},{29,5},{30,6},{31,7},{0,8},{1,9... | collective-permute-start | bytes 1572872 | tf_op jit(solution)/shard_map/ppermute | solution.py:106
  40.5 23.5 %collective-permute-start.6 = (f32[256,512]{1,0:T(8,128)S(1)}, f32[256,512]{1,0:T(8,128)S(1)}, u32[]{:S(2)}, u32[]{:S(2)}) collective-permute-start(f32[256,512]{1,0:T(8,128)S(1)} %get-tuple-element.35), channel_id=1, source_target_pairs={{0,4},{1,3},{2,6},{3,1},{4,0},{5,7},{6,2},{7,5},{8,12},{9,11},{10,... | collective-permute-start | bytes 1572872 | tf_op jit(solution)/shard_map/ppermute | solution.py:106
  55.0 18.1 %collective-permute-start.7 = (f32[256,512]{1,0:T(8,128)S(1)}, f32[256,512]{1,0:T(8,128)S(1)}, u32[]{:S(2)}, u32[]{:S(2)}) collective-permute-start(f32[256,512]{1,0:T(8,128)S(1)} %get-tuple-element.36), channel_id=1, source_target_pairs={{0,4},{1,3},{2,6},{3,1},{4,0},{5,7},{6,2},{7,5},{8,12},{9,11},{10,... | collective-permute-start | bytes 1572872 | tf_op jit(solution)/shard_map/ppermute | solution.py:106
  55.1 20.7 %collective-permute-start.10 = (f32[256,512]{1,0:T(8,128)S(1)}, f32[256,512]{1,0:T(8,128)S(1)}, u32[]{:S(2)}, u32[]{:S(2)}) collective-permute-start(f32[256,512]{1,0:T(8,128)S(1)} %get-tuple-element.41), channel_id=1, source_target_pairs={{0,2},{1,5},{2,0},{3,7},{4,6},{5,1},{6,4},{7,3},{8,10},{9,13},{10,... | collective-permute-start | bytes 1572872 | tf_op jit(solution)/shard_map/ppermute | solution.py:106
  76.0 13.2 %collective-permute-start.12 = (f32[256,512]{1,0:T(8,128)S(1)}, f32[256,512]{1,0:T(8,128)S(1)}, u32[]{:S(2)}, u32[]{:S(2)}) collective-permute-start(f32[256,512]{1,0:T(8,128)S(1)} %add_add_fusion.refs_0_.image_ref.own), channel_id=1, source_target_pairs={{0,24},{1,25},{2,26},{3,27},{4,28},{5,29},{6,30},{7,31},{8,0},{9,1... | collective-permute-start | bytes 1572872 | tf_op jit(solution)/shard_map/ppermute | solution.py:106
  79.8 9.4 %collective-permute-start.13 = (f32[256,512]{1,0:T(8,128)S(1)}, f32[256,512]{1,0:T(8,128)S(1)}, u32[]{:S(2)}, u32[]{:S(2)}) collective-permute-start(f32[256,512]{1,0:T(8,128)S(1)} %add_add_fusion.refs_0_.image_ref.own), channel_id=1, source_target_pairs={{0,2},{1,5},{2,0},{3,7},{4,6},{5,1},{6,4},{7,3},{8,10},{9,13},{10,... | collective-permute-start | bytes 1572872 | tf_op jit(solution)/shard_map/ppermute | solution.py:106
  89.2 8.3 %collective-permute-start.14 = (f32[256,512]{1,0:T(8,128)S(1)}, f32[256,512]{1,0:T(8,128)S(1)}, u32[]{:S(2)}, u32[]{:S(2)}) collective-permute-start(f32[256,512]{1,0:T(8,128)S(1)} %collective-permute-done.12.refs_2_.group), channel_id=1, source_target_pairs={{0,2},{1,5},{2,0},{3,7},{4,6},{5,1},{6,4},{7,3},{8,10},{9,13},{10,... | collective-permute-start | bytes 1572872 | tf_op jit(solution)/shard_map/ppermute | solution.py:106
  98.2 8.4 %collective-permute-start.15 = (f32[256,512]{1,0:T(8,128)S(1)}, f32[256,512]{1,0:T(8,128)S(1)}, u32[]{:S(2)}, u32[]{:S(2)}) collective-permute-start(f32[256,512]{1,0:T(8,128)S(1)} %get-tuple-element.44.refs_2_), channel_id=1, source_target_pairs={{0,4},{1,3},{2,6},{3,1},{4,0},{5,7},{6,2},{7,5},{8,12},{9,11},{10,... | collective-permute-start | bytes 1572872 | tf_op jit(solution)/shard_map/ppermute | solution.py:106
  106.5 12.0 %collective-permute-start.16 = (f32[256,512]{1,0:T(8,128)S(1)}, f32[256,512]{1,0:T(8,128)S(1)}, u32[]{:S(2)}, u32[]{:S(2)}) collective-permute-start(f32[256,512]{1,0:T(8,128)S(1)} %collective-permute-done.14.refs_3_.both), channel_id=1, source_target_pairs={{2,30},{5,31},{10,6},{13,7},{18,14},{21,15},{26,22},{29,23}} | collective-permute-start | bytes 1572872 | tf_op jit(solution)/shard_map/ppermute | solution.py:106
  107.8 18.4 %collective-permute-start.17 = (f32[256,512]{1,0:T(8,128)S(1)}, f32[256,512]{1,0:T(8,128)S(1)}, u32[]{:S(2)}, u32[]{:S(2)}) collective-permute-start(f32[256,512]{1,0:T(8,128)S(1)} %get-tuple-element.50), channel_id=1, source_target_pairs={{0,4},{1,3},{2,6},{3,1},{4,0},{5,7},{6,2},{7,5},{8,12},{9,11},{10,... | collective-permute-start | bytes 1572872 | tf_op jit(solution)/shard_map/ppermute | solution.py:106
  121.2 10.8 %collective-permute-start.19 = (f32[2,256,512]{2,1,0:T(8,128)S(1)}, f32[2,256,512]{2,1,0:T(8,128)S(1)}, u32[]{:S(2)}, u32[]{:S(2)}) collective-permute-start(f32[2,256,512]{2,1,0:T(8,128)S(1)} %get-tuple-element.54), channel_id=1, source_target_pairs={{0,1},{1,0},{2,3},{3,2},{4,5},{5,4},{6,7},{7,6},{8,9},{9,8},{10,11... | collective-permute-start | bytes 3145736 | tf_op jit(solution)/shard_map/ppermute | solution.py:404
  126.2 5.8 %copy-start.1 = (f32[1,3,512,512]{3,2,1,0:T(8,128)S(1)}, f32[1,3,512,512]{3,2,1,0:T(8,128)}, u32[]{:S(2)}) copy-start(f32[1,3,512,512]{3,2,1,0:T(8,128)} %param.5) | copy-start | bytes 9437188
  129.0 5.0 %collective-permute-start.18 = (f32[1,256,512]{2,1,0:T(8,128)S(1)}, f32[1,256,512]{2,1,0:T(8,128)S(1)}, u32[]{:S(2)}, u32[]{:S(2)}) collective-permute-start(f32[1,256,512]{2,1,0:T(8,128)S(1)} %get-tuple-element.52), channel_id=1, source_target_pairs={{0,1},{1,0},{2,3},{3,2},{4,5},{5,4},{6,7},{7,6},{8,9},{9,8},{10,11... | collective-permute-start | bytes 1572872 | tf_op jit(solution)/shard_map/ppermute | solution.py:404
  (1 other events, 1.0 us)
where the time goes:
time: 136 us; the launch traced here: 135 us
  waiting for transfers between devices  65.4 us (48%)
  starting transfers between devices  44.4 us (33%)
  Pallas kernels  21.5 us (16%)
  local copies, waits for them, and re-layouts  2.94 us (2%)
    ppermute x18, waiting for transfers between devices, send(): return lax.ppermute(value, ('var', 'samp'), pairs)  65.4 us
    ppermute x18, starting transfers between devices, send(): return lax.ppermute(value, ('var', 'samp'), pairs)  37 us
    ppermute x2, starting transfers between devices, swap(): return lax.ppermute(value, 'samp', [(0, 1), (1, 0)])  7.41 us
    pallas_call x2, Pallas kernels, left(): pl.pallas_call(functools.partial(left_kernel, start, begin, pair), in_spe...  5.35 us
    pallas_call x1, Pallas kernels, right(): pl.pallas_call(functools.partial(right_kernel, slots, pair), in_specs=[sm...  4.82 us
    pallas_call x2, Pallas kernels, finish(): pl.pallas_call(functools.partial(finish_kernel, begin, factor), grid=(cou...  3.39 us
    unnamed x10, local copies, waits for them, and re-layouts  2.94 us
  transfers between devices with their start and end apart: 20, of which 11 were waited for; matrix products, arithmetic and copies ran while one was open for 0% of the time, Pallas kernels for 13%

commit v1 on v0

--- a/solution.py
+++ b/solution.py
@@ -106,8 +106,7 @@
     return lax.ppermute(value, ("var", "samp"), pairs)
 
 
-def forward_kernel(gate_ref, data_ref, tile_ref, own_ref, far_ref):
-    del gate_ref
+def forward_kernel(data_ref, tile_ref, own_ref, far_ref):
     slot = pl.program_id(0)
     value = dot3(split(data_ref[...]), split(tile_ref[...]), NN)
 
@@ -120,14 +119,13 @@
         far_ref[...] = value
 
 
-def forward(gate, data, tiles):
+def forward(data, tiles):
     slots, block = tiles.shape[:2]
     rows = data.shape[0]
     return pl.pallas_call(
         forward_kernel,
         grid=(slots,),
         in_specs=[
-            smem_spec(),
             pl.BlockSpec((rows, block), lambda j: (0, 0)),
             pl.BlockSpec((None, block, block), lambda j: (j, 0, 0)),
         ],
@@ -142,24 +140,24 @@
         compiler_params=params(),
         cost_estimate=cost(6 * slots * rows * block * block, 4 * slots * block * (block + 2 * rows)),
         name="forward",
-    )(gate, data, tiles)
+    )(data, tiles)
 
 
 CODES = (0, 1, 2, 3, 5)
 
 
 def choose_kernel(slots, count, offs_ref, *refs):
-    sources, outs, sems = refs[:count], refs[count:-1], refs[-1]
+    sources, (out, sems) = refs[:count], refs[count:]
     p, flip = place()
     target = last_partner(p, flip)
     copies = []
     for slot in range(slots):
         last, code = route(target, offs_ref[0, slot + 1], flip)
         for value, source in zip(CODES, sources):
-            copy = pltpu.make_async_copy(source, outs[slot], sems.at[slot])
+            copy = pltpu.make_async_copy(source, out.at[slot], sems.at[slot])
             pl.when((last == 1) & (code == value))(copy.start)
         known = (last == 1) & (code <= CODES[count - 1])
-        copies.append((known, pltpu.make_async_copy(sources[0], outs[slot], sems.at[slot])))
+        copies.append((known, pltpu.make_async_copy(sources[0], out.at[slot], sems.at[slot])))
     for known, copy in copies:
         pl.when(known)(copy.wait)
 
@@ -170,8 +168,8 @@
     return pl.pallas_call(
         functools.partial(choose_kernel, slots, len(sources)),
         in_specs=[smem_spec()] + [any_spec()] * len(sources),
-        out_specs=[any_spec()] * slots,
-        out_shape=[jax.ShapeDtypeStruct(own.shape, f32)] * slots,
+        out_specs=any_spec(),
+        out_shape=jax.ShapeDtypeStruct((slots,) + own.shape, f32),
         scratch_shapes=[pltpu.SemaphoreType.DMA((slots,))],
         compiler_params=params(),
         cost_estimate=cost(0, 8 * slots * own.size),
@@ -192,15 +190,14 @@
 
 
 def backward_kernel(slots, offs_ref, tile_ref, own, first, group, both, *refs):
-    lasts = refs[:slots]
-    out_ref, picked, sems = refs[slots:]
+    lasts_ref, out_ref, picked, sems = refs
     slot = pl.program_id(0)
 
     @pl.when(slot == 0)
     def _():
         out_ref[...] = jnp.zeros_like(out_ref)
         for each in range(slots):
-            sources = (own, first, group, both, lasts[each])
+            sources = (own, first, group, both, lasts_ref.at[each])
             start_pick(offs_ref[0, each + 1], sources, picked.at[each], sems.at[each])
 
     pltpu.make_async_copy(own, picked.at[slot], sems.at[slot]).wait()
@@ -266,10 +263,10 @@
 
 
 def right_kernel(slots, pair, offs_ref, data_ref, image_ref, own, first, group, both, *refs):
-    lasts = refs[:slots]
+    lasts_ref = refs[0]
     keep_ref, send_ref, high_ref, low_ref, picked, sems = refs[-6:]
     for slot in range(slots):
-        sources = (own, first, group, both, lasts[slot])
+        sources = (own, first, group, both, lasts_ref.at[slot])
         start_pick(offs_ref[0, slot + 1], sources, picked.at[slot], sems.at[slot])
     half = image_ref.shape[1] // 2
     samp = halves(pair)
@@ -311,17 +308,16 @@
         out_shape=[part, part, turned, turned],
         scratch_shapes=[pltpu.VMEM((slots, rows, block), f32), pltpu.SemaphoreType.DMA((slots,))],
         compiler_params=params(),
-        cost_estimate=cost(6 * (slots + 2) * rows * block * block, 4 * (slots + 1) * block * (block + rows)),
+        cost_estimate=pl.CostEstimate(flops=400 * rows * block * block, bytes_accessed=0, transcendentals=0),
         name="right",
     )(offsets, data, image, *sources, *gate)
 
 
-def left_kernel(start, begin, pair, offs_ref, keep_in, send_in, high_ref, low_ref, own, first, group, both, two, *refs):
-    lasts = refs[:-4]
-    keep_ref, send_ref, picked, sems = refs[-4:]
-    slots = range(start, start + len(lasts))
-    for slot, last_ref in zip(slots, lasts):
-        sources = (own, first, group, both, last_ref, two)
+def left_kernel(slots, begin, pair, offs_ref, keep_in, send_in, high_ref, low_ref, own, first, group, both, two,
+                lasts_ref, keep_ref, send_ref, picked, sems):
+    start = slots[0]
+    for slot in slots:
+        sources = (own, first, group, both, lasts_ref.at[slot - 1], two)
         start_pick(offs_ref[0, slot], sources, picked.at[slot - start], sems.at[slot - start])
     half = send_ref.shape[1]
     samp = halves(pair)
@@ -338,21 +334,21 @@
             out_ref[slot - begin] = in_ref[slot] + dot3((high_ref[rows], low_ref[rows]), chosen, NN)
 
 
-def left(offsets, start, begin, parts, turned, sources, lasts, pair):
+def left(offsets, slots, begin, parts, turned, sources, pair):
     keep = parts[0]
     block, rows = turned[0].shape
-    count = start + len(lasts) - begin
+    count = slots[-1] + 1 - begin
     part = jax.ShapeDtypeStruct((count,) + keep.shape[1:], f32)
     return pl.pallas_call(
-        functools.partial(left_kernel, start, begin, pair),
-        in_specs=[smem_spec()] + [vmem_spec()] * 4 + [any_spec()] * (len(sources) + len(lasts)),
+        functools.partial(left_kernel, slots, begin, pair),
+        in_specs=[smem_spec()] + [vmem_spec()] * 4 + [any_spec()] * len(sources),
         out_specs=[vmem_spec()] * 2,
         out_shape=[part, part],
-        scratch_shapes=[pltpu.VMEM((len(lasts), rows, block), f32), pltpu.SemaphoreType.DMA((len(lasts),))],
-        compiler_params=params(),
-        cost_estimate=cost(6 * len(lasts) * rows * block * block, 4 * count * block * (2 * block + rows)),
+        scratch_shapes=[pltpu.VMEM((len(slots), rows, block), f32), pltpu.SemaphoreType.DMA((len(slots),))],
+        compiler_params=params(),
+        cost_estimate=cost(6 * len(slots) * rows * block * block, 4 * count * block * (2 * block + rows)),
         name="left",
-    )(offsets, *parts, *turned, *sources, *lasts)
+    )(offsets, *parts, *turned, *sources)
 
 
 def finish_kernel(begin, factor, offs_ref, step_ref, tile_ref, keep_ref, other_ref, *refs):
@@ -414,36 +410,36 @@
     offsets_next = send(offsets, "last")
     data_first = send(data, "first")
     data_group = send(data, "group")
-    own, far = forward(offsets_next, data, local_tiles)
-    theirs = send(far, "last")
+    own, far = forward(data, local_tiles)
+    theirs = send(after(far, offsets_next), "last")
     data_both = send(after(data_first, data_group), "group")
     own, bin_first, bin_group, bin_both, bin_two = make_bins(offsets, offsets_next, own, far, theirs)
     bin_group = bin_group + send(bin_both, "first") + send(bin_two, "two", reverse=True)
     data_two = send(after(data_both, own), "column")
     chosen = choose(offsets_next, data, data_first, data_group, data_both, data_two)
-    data_sources = (data, data_first, data_group, data_both) + tuple(send(each, "last") for each in chosen)
+    data_sources = (data, data_first, data_group, data_both, send(chosen, "last"))
     got_first = send(after(bin_first, bin_group), "first")
     got_group = send(bin_group, "group", reverse=True)
     image = own + backward(offsets, local_tiles, data_sources) + got_first + got_group
 
     image_group = send(image, "group")
     image_first = send(image, "first")
-    image_group, image_first = lax.optimization_barrier((image_group, image_first))
     image_both = send(image_group, "first")
     chosen = choose(offsets_next, image, image_first, image_group, image_both)
-    image_lasts = [send(each, "last") for each in chosen]
-    keep, other, high, low = right(offsets, data, image, (chosen[0],), data_sources, pair)
-    image_two = send(after(image_both, image_lasts[0]), "direct")
-    image_sources = (image, image_first, image_group, image_both, image_two)
+    image_last = send(chosen, "last")
+    keep, other, high, low = right(offsets, data, image, (chosen,), data_sources, pair)
+    image_two = send(after(image_both, chosen), "direct")
+    image_sources = (image, image_first, image_group, image_both, image_two, image_last)
     if pair:
         begin, result = 0, ()
         for slot in range(1, slot_count):
             keep_now, other_now = left(
-                offsets, slot, begin, (keep, other), (high, low), image_sources, image_lasts[slot - 1 : slot], pair)
+                offsets, (slot,), begin, (keep, other), (high, low), image_sources, pair)
             result = (finish(offsets, step, local_tiles, keep_now, swap(other_now), factor, begin, result),)
             begin = slot + 1
         return result[0][None]
-    keep, other = left(offsets, 1, 0, (keep, other), (high, low), image_sources, image_lasts, pair)
+    slots = tuple(range(1, slot_count))
+    keep, other = left(offsets, slots, 0, (keep, other), (high, low), image_sources, pair)
     summed = lax.psum_scatter(jnp.concatenate([keep, other], axis=1), "samp", scatter_dimension=1, tiled=True)
     none = jnp.zeros_like(summed)
     return finish(offsets, step, local_tiles, summed, none, factor, 0)[None]

time: 136 us -> 129 us (0.949); the launches traced: 135 us -> 126 us
  waiting for transfers between devices: 65.4 us -> 46.1 us
  starting transfers between devices: 44.4 us -> 52.9 us
  local copies, waits for them, and re-layouts: 2.94 us -> 5.16 us
    ppermute x18 -> x16, waiting for transfers between devices: 65.4 us -> 46.1 us  [send(): return lax.ppermute(value, ('var', 'samp'), pairs)]
    ppermute x2, starting transfers between devices: 7.41 us -> 12.2 us  [swap(): return lax.ppermute(value, 'samp', [(0, 1), (1, 0)])]
    ppermute x18 -> x16, starting transfers between devices: 37 us -> 40.7 us  [send(): return lax.ppermute(value, ('var', 'samp'), pairs)]
    unnamed x10 -> x14, local copies, waits for them, and re-layouts: 2.94 us -> 5.16 us
  transfers between devices with their start and end apart: 20 -> 18, of which waited for: 11 -> 9; matrix products, arithmetic and copies ran while one was open for 0% -> 0% of each run, Pallas kernels for 13% -> 13%
where the time goes in v1:
time: 129 us; the launch traced here: 126 us
  starting transfers between devices  52.9 us (41%)
  waiting for transfers between devices  46.1 us (36%)
  Pallas kernels  20.9 us (16%)
  local copies, waits for them, and re-layouts  5.16 us (4%)
    ppermute x16, waiting for transfers between devices, send(): return lax.ppermute(value, ('var', 'samp'), pairs)  46.1 us
    ppermute x16, starting transfers between devices, send(): return lax.ppermute(value, ('var', 'samp'), pairs)  40.7 us
    ppermute x2, starting transfers between devices, swap(): return lax.ppermute(value, 'samp', [(0, 1), (1, 0)])  12.2 us
    pallas_call x2, Pallas kernels, left(): pl.pallas_call(functools.partial(left_kernel, slots, begin, pair), in_spe...  5.34 us
    unnamed x14, local copies, waits for them, and re-layouts  5.16 us
    pallas_call x1, Pallas kernels, right(): pl.pallas_call(functools.partial(right_kernel, slots, pair), in_specs=[sm...  4.84 us
    pallas_call x2, Pallas kernels, finish(): pl.pallas_call(functools.partial(finish_kernel, begin, factor), grid=(cou...  3.4 us
    pallas_call x1, Pallas kernels, backward(): pl.pallas_call(functools.partial(backward_kernel, slots), grid=(slots,),...  2.68 us
  transfers between devices with their start and end apart: 18, of which 9 were waited for; matrix products, arithmetic and copies ran while one was open for 0% of the time, Pallas kernels for 13%

profile of v1, /device:TPU:7, one launch (start us, length us, event | category | flops | bytes accessed | tf_op | source)
XLA Modules:
  0.0 126.4 jit_solution(4933894269732071111)
XLA Ops:
  0.2 3.3 %collective-permute-start.3 = (f32[256,512]{1,0:T(8,128)}, f32[256,512]{1,0:T(8,128)S(1)}, u32[]{:S(2)}, u32[]{:S(2)}) collective-permute-start(f32[256,512]{1,0:T(8,128)} %own.3), channel_id=1, source_target_pairs={{0,24},{1,25},{2,26},{3,27},{4,28},{5,29},{6,30},{7,31},{8,0},{9,1... | collective-permute-start | bytes 1572872 | tf_op jit(solution)/shard_map/ppermute | solution.py:106
  3.8 1.9 %copy-done = f32[1,3,512,512]{3,2,1,0:T(8,128)S(1)} copy-done((f32[1,3,512,512]{3,2,1,0:T(8,128)S(1)}, f32[1,3,512,512]{3,2,1,0:T(8,128)}, u32[]{:S(2)}) %copy-start) | copy-done | bytes 3145752
  6.7 1.9 %forward.1 = (f32[256,512]{1,0:T(8,128)S(1)}, f32[2,256,512]{2,1,0:T(8,128)S(1)}) custom-call(f32[256,512]{1,0:T(8,128)S(1)} %copy-done.2, f32[3,512,512]{2,1,0:T(8,128)S(1)} %bitcast.3), custom_call_target="tpu_custom_call" | custom-call | tf_op jit(solution)/shard_map/forward/pallas_call | solution.py:125
  9.9 4.2 %collective-permute-done.3.refs_2_.group = f32[256,512]{1,0:T(8,128)S(1)} collective-permute-done((f32[256,512]{1,0:T(8,128)}, f32[256,512]{1,0:T(8,128)S(1)}, u32[]{:S(2)}, u32[]{:S(2)}) %collective-permute-start.3) | collective-permute-done | bytes 524320 | tf_op jit(solution)/shard_map/ppermute | solution.py:106
  14.1 3.9 %collective-permute-start.4 = (f32[256,512]{1,0:T(8,128)S(1)}, f32[256,512]{1,0:T(8,128)S(1)}, u32[]{:S(2)}, u32[]{:S(2)}) collective-permute-start(f32[256,512]{1,0:T(8,128)S(1)} %collective-permute-done.2.refs_1_.first), channel_id=1, source_target_pairs={{0,24},{1,25},{2,26},{3,27},{4,28},{5,29},{6,30},{7,31},{8,0},{9,1... | collective-permute-start | bytes 1572872 | tf_op jit(solution)/shard_map/ppermute | solution.py:106
  18.0 4.7 %collective-permute-done.1.theirs_ref = f32[2,256,512]{2,1,0:T(8,128)S(1)} collective-permute-done((f32[2,256,512]{2,1,0:T(8,128)S(1)}, f32[2,256,512]{2,1,0:T(8,128)S(1)}, u32[]{:S(2)}, u32[]{:S(2)}) %collective-permute-start.1) | collective-permute-done | bytes 1048608 | tf_op jit(solution)/shard_map/ppermute | solution.py:106
  24.2 3.1 %collective-permute-done.4.refs_3_.both = f32[256,512]{1,0:T(8,128)S(1)} collective-permute-done((f32[256,512]{1,0:T(8,128)S(1)}, f32[256,512]{1,0:T(8,128)S(1)}, u32[]{:S(2)}, u32[]{:S(2)}) %collective-permute-start.4) | collective-permute-done | bytes 524320 | tf_op jit(solution)/shard_map/ppermute | solution.py:106
  28.7 3.7 %collective-permute-start.7 = (f32[256,512]{1,0:T(8,128)S(1)}, f32[256,512]{1,0:T(8,128)S(1)}, u32[]{:S(2)}, u32[]{:S(2)}) collective-permute-start(f32[256,512]{1,0:T(8,128)S(1)} %get-tuple-element.33), channel_id=1, source_target_pairs={{0,2},{1,5},{2,0},{3,7},{4,6},{5,1},{6,4},{7,3},{8,10},{9,13},{10,... | collective-permute-start | bytes 1572872 | tf_op jit(solution)/shard_map/ppermute | solution.py:106
  33.0 5.4 %collective-permute-start.6 = (f32[2,256,512]{2,1,0:T(8,128)S(1)}, f32[2,256,512]{2,1,0:T(8,128)S(1)}, u32[]{:S(2)}, u32[]{:S(2)}) collective-permute-start(f32[2,256,512]{2,1,0:T(8,128)S(1)} %choose.2), channel_id=1, source_target_pairs={{0,4},{1,3},{2,6},{3,1},{4,0},{5,7},{6,2},{7,5},{8,12},{9,11},{10,... | collective-permute-start | bytes 3145736 | tf_op jit(solution)/shard_map/ppermute | solution.py:106
  41.0 10.6 %collective-permute-done.6.refs_0_ = f32[2,256,512]{2,1,0:T(8,128)S(1)} collective-permute-done((f32[2,256,512]{2,1,0:T(8,128)S(1)}, f32[2,256,512]{2,1,0:T(8,128)S(1)}, u32[]{:S(2)}, u32[]{:S(2)}) %collective-permute-start.6) | collective-permute-done | bytes 1048608 | tf_op jit(solution)/shard_map/ppermute | solution.py:106
  51.6 2.7 %backward.1 = f32[256,512]{1,0:T(8,128)S(1)} custom-call(s32[1,3]{1,0:T(1,128)S(1)} %copy-done.6, f32[3,512,512]{2,1,0:T(8,128)} %bitcast.2, f32[256,512]{1,0:T(8,128)S(1)} %copy-done.3, f32[256,512]{1,0:T(8,128)S(1)} %collective-permute-done.2.refs_1_.first, f32[256,512]{1,0:T(8,128)S(1)} %collective-permute-done.3.refs_2_.group, ...), custom_call_target="tpu_custom_call" | custom-call | tf_op jit(solution)/shard_map/backward/pallas_call | solution.py:212
  54.5 4.1 %collective-permute-start.12 = (f32[256,512]{1,0:T(8,128)S(1)}, f32[256,512]{1,0:T(8,128)S(1)}, u32[]{:S(2)}, u32[]{:S(2)}) collective-permute-start(f32[256,512]{1,0:T(8,128)S(1)} %add_add_fusion.refs_0_.image_ref.own), channel_id=1, source_target_pairs={{0,24},{1,25},{2,26},{3,27},{4,28},{5,29},{6,30},{7,31},{8,0},{9,1... | collective-permute-start | bytes 1572872 | tf_op jit(solution)/shard_map/ppermute | solution.py:106
  58.6 4.5 %collective-permute-start.11 = (f32[256,512]{1,0:T(8,128)S(1)}, f32[256,512]{1,0:T(8,128)S(1)}, u32[]{:S(2)}, u32[]{:S(2)}) collective-permute-start(f32[256,512]{1,0:T(8,128)S(1)} %add_add_fusion.refs_0_.image_ref.own), channel_id=1, source_target_pairs={{0,2},{1,5},{2,0},{3,7},{4,6},{5,1},{6,4},{7,3},{8,10},{9,13},{10,... | collective-permute-start | bytes 1572872 | tf_op jit(solution)/shard_map/ppermute | solution.py:106
  63.1 3.5 %collective-permute-done.12.refs_2_.group = f32[256,512]{1,0:T(8,128)S(1)} collective-permute-done((f32[256,512]{1,0:T(8,128)S(1)}, f32[256,512]{1,0:T(8,128)S(1)}, u32[]{:S(2)}, u32[]{:S(2)}) %collective-permute-start.12) | collective-permute-done | bytes 524320 | tf_op jit(solution)/shard_map/ppermute | solution.py:106
  66.6 7.6 %collective-permute-start.13 = (f32[256,512]{1,0:T(8,128)S(1)}, f32[256,512]{1,0:T(8,128)S(1)}, u32[]{:S(2)}, u32[]{:S(2)}) collective-permute-start(f32[256,512]{1,0:T(8,128)S(1)} %collective-permute-done.12.refs_2_.group), channel_id=1, source_target_pairs={{0,2},{1,5},{2,0},{3,7},{4,6},{5,1},{6,4},{7,3},{8,10},{9,13},{10,... | collective-permute-start | bytes 1572872 | tf_op jit(solution)/shard_map/ppermute | solution.py:106
  74.2 6.9 %collective-permute-done.13.refs_3_.both = f32[256,512]{1,0:T(8,128)S(1)} collective-permute-done((f32[256,512]{1,0:T(8,128)S(1)}, f32[256,512]{1,0:T(8,128)S(1)}, u32[]{:S(2)}, u32[]{:S(2)}) %collective-permute-start.13) | collective-permute-done | bytes 524320 | tf_op jit(solution)/shard_map/ppermute | solution.py:106
  81.7 2.3 %collective-permute-start.15 = (f32[2,256,512]{2,1,0:T(8,128)S(1)}, f32[2,256,512]{2,1,0:T(8,128)S(1)}, u32[]{:S(2)}, u32[]{:S(2)}) collective-permute-start(f32[2,256,512]{2,1,0:T(8,128)S(1)} %choose.3.refs_1_), channel_id=1, source_target_pairs={{0,4},{1,3},{2,6},{3,1},{4,0},{5,7},{6,2},{7,5},{8,12},{9,11},{10,... | collective-permute-start | bytes 3145736 | tf_op jit(solution)/shard_map/ppermute | solution.py:106
  85.3 4.8 %right.1 = (f32[3,256,512]{2,1,0:T(8,128)}, f32[3,256,512]{2,1,0:T(8,128)}, bf16[512,256]{1,0:T(8,128)(2,1)S(1)}, bf16[512,256]{1,0:T(8,128)(2,1)S(1)}) custom-call(s32[1,3]{1,0:T(1,128)S(1)} %copy-done.6, f32[256,512]{1,0:T(8,128)S(1)} %copy-done.3, f32[256,512]{1,0:T(8,128)S(1)} %add_add_fusion.refs_0_.image_ref.own, f32[256,512]{1,0:T(8,128)S(1)} %copy-done.3, ...), custom_call_target="tpu_custom_call" | custom-call | flops 26843545600 | tf_op jit(solution)/shard_map/right/pallas_call | solution.py:304
  90.1 4.9 %collective-permute-done.14.two = f32[256,512]{1,0:T(8,128)S(1)} collective-permute-done((f32[256,512]{1,0:T(8,128)S(1)}, f32[256,512]{1,0:T(8,128)S(1)}, u32[]{:S(2)}, u32[]{:S(2)}) %collective-permute-start.14) | collective-permute-done | bytes 524320 | tf_op jit(solution)/shard_map/ppermute | solution.py:106
  95.1 7.4 %collective-permute-done.15.lasts_ref = f32[2,256,512]{2,1,0:T(8,128)S(1)} collective-permute-done((f32[2,256,512]{2,1,0:T(8,128)S(1)}, f32[2,256,512]{2,1,0:T(8,128)S(1)}, u32[]{:S(2)}, u32[]{:S(2)}) %collective-permute-start.15) | collective-permute-done | bytes 1048608 | tf_op jit(solution)/shard_map/ppermute | solution.py:106
  103.5 2.6 %left.3 = (f32[2,256,512]{2,1,0:T(8,128)S(1)}, f32[2,256,512]{2,1,0:T(8,128)S(1)}) custom-call(s32[1,3]{1,0:T(1,128)S(1)} %copy-done.6, f32[3,256,512]{2,1,0:T(8,128)} %get-tuple-element.36.keep_in, f32[3,256,512]{2,1,0:T(8,128)} %get-tuple-element.37.send_in, bf16[512,256]{1,0:T(8,128)(2,1)S(1)} %get-tuple-element.38.high_ref, ...), custom_call_target="tpu_custom_call" | custom-call | tf_op jit(solution)/shard_map/left/pallas_call | solution.py:342
  106.1 12.1 %collective-permute-start.17 = (f32[2,256,512]{2,1,0:T(8,128)S(1)}, f32[2,256,512]{2,1,0:T(8,128)S(1)}, u32[]{:S(2)}, u32[]{:S(2)}) collective-permute-start(f32[2,256,512]{2,1,0:T(8,128)S(1)} %get-tuple-element.44), channel_id=1, source_target_pairs={{0,1},{1,0},{2,3},{3,2},{4,5},{5,4},{6,7},{7,6},{8,9},{9,8},{10,11... | collective-permute-start | bytes 3145736 | tf_op jit(solution)/shard_map/ppermute | solution.py:400
  119.5 2.7 %left.2 = (f32[1,256,512]{2,1,0:T(8,128)S(1)}, f32[1,256,512]{2,1,0:T(8,128)S(1)}) custom-call(s32[1,3]{1,0:T(1,128)S(1)} %copy-done.6, f32[3,256,512]{2,1,0:T(8,128)} %get-tuple-element.36.keep_in, f32[3,256,512]{2,1,0:T(8,128)} %get-tuple-element.37.send_in, bf16[512,256]{1,0:T(8,128)(2,1)S(1)} %get-tuple-element.38.high_ref, ...), custom_call_target="tpu_custom_call" | custom-call | tf_op jit(solution)/shard_map/left/pallas_call | solution.py:342
  123.0 1.9 %finish.2.refs_0_ = f32[3,256,512]{2,1,0:T(8,128)} custom-call(s32[1,3]{1,0:T(1,128)S(1)} %copy-done.6, f32[1]{0:T(128)S(6)} %copy.7.step_ref, f32[3,512,512]{2,1,0:T(8,128)S(1)} %bitcast.4, f32[2,256,512]{2,1,0:T(8,128)S(1)} %get-tuple-element.43.keep_ref, f32[2,256,512]{2,1,0:T(8,128)S(1)} %collective-permute-done.17.other_ref), custom_call_target="tpu_custom_call" | custom-call | tf_op jit(solution)/shard_map/finish/pallas_call | solution.py:382
  (38 shorter events, 14.8 us)
Async XLA Ops:
  0.0 9.9 %collective-permute-start.2 = (f32[256,512]{1,0:T(8,128)}, f32[256,512]{1,0:T(8,128)S(1)}, u32[]{:S(2)}, u32[]{:S(2)}) collective-permute-start(f32[256,512]{1,0:T(8,128)} %own.3), channel_id=1, source_target_pairs={{0,2},{1,5},{2,0},{3,7},{4,6},{5,1},{6,4},{7,3},{8,10},{9,13},{10,... | collective-permute-start | bytes 1572872 | tf_op jit(solution)/shard_map/ppermute | solution.py:106
  0.2 13.9 %collective-permute-start.3 = (f32[256,512]{1,0:T(8,128)}, f32[256,512]{1,0:T(8,128)S(1)}, u32[]{:S(2)}, u32[]{:S(2)}) collective-permute-start(f32[256,512]{1,0:T(8,128)} %own.3), channel_id=1, source_target_pairs={{0,24},{1,25},{2,26},{3,27},{4,28},{5,29},{6,30},{7,31},{8,0},{9,1... | collective-permute-start | bytes 1572872 | tf_op jit(solution)/shard_map/ppermute | solution.py:106
  3.5 5.1 %collective-permute-start = (s32[1,3]{1,0:T(1,128)}, s32[1,3]{1,0:T(1,128)S(1)}, u32[]{:S(2)}, u32[]{:S(2)}) collective-permute-start(s32[1,3]{1,0:T(1,128)} %offs_ref.13), channel_id=1, source_target_pairs={{0,4},{1,3},{2,6},{3,1},{4,0},{5,7},{6,2},{7,5},{8,12},{9,11},{10,... | collective-permute-start | bytes 44 | tf_op jit(solution)/shard_map/ppermute | solution.py:106
  3.8 1.9 %copy-start = (f32[1,3,512,512]{3,2,1,0:T(8,128)S(1)}, f32[1,3,512,512]{3,2,1,0:T(8,128)}, u32[]{:S(2)}) copy-start(f32[1,3,512,512]{3,2,1,0:T(8,128)} %param.5) | copy-start | bytes 9437188
  5.7 1.0 copy-start.2
  6.7 15.9 %copy-start.6 = (s32[1,3]{1,0:T(1,128)S(1)}, s32[1,3]{1,0:T(1,128)}, u32[]{:S(2)}) copy-start(s32[1,3]{1,0:T(1,128)} %offs_ref.13) | copy-start | bytes 40
  8.6 23.7 %copy-start.3 = (f32[256,512]{1,0:T(8,128)S(1)}, f32[256,512]{1,0:T(8,128)}, u32[]{:S(2)}) copy-start(f32[256,512]{1,0:T(8,128)} %own.3) | copy-start | bytes 1572868
  8.6 14.0 %collective-permute-start.1 = (f32[2,256,512]{2,1,0:T(8,128)S(1)}, f32[2,256,512]{2,1,0:T(8,128)S(1)}, u32[]{:S(2)}, u32[]{:S(2)}) collective-permute-start(f32[2,256,512]{2,1,0:T(8,128)S(1)} %get-tuple-element.27.mine_ref), channel_id=1, source_target_pairs={{0,4},{1,3},{2,6},{3,1},{4,0},{5,7},{6,2},{7,5},{8,12},{9,11},{10,... | collective-permute-start | bytes 3145736 | tf_op jit(solution)/shard_map/ppermute | solution.py:106
  14.1 13.2 %collective-permute-start.4 = (f32[256,512]{1,0:T(8,128)S(1)}, f32[256,512]{1,0:T(8,128)S(1)}, u32[]{:S(2)}, u32[]{:S(2)}) collective-permute-start(f32[256,512]{1,0:T(8,128)S(1)} %collective-permute-done.2.refs_1_.first), channel_id=1, source_target_pairs={{0,24},{1,25},{2,26},{3,27},{4,28},{5,29},{6,30},{7,31},{8,0},{9,1... | collective-permute-start | bytes 1572872 | tf_op jit(solution)/shard_map/ppermute | solution.py:106
  27.3 5.1 %collective-permute-start.5 = (f32[256,512]{1,0:T(8,128)S(1)}, f32[256,512]{1,0:T(8,128)S(1)}, u32[]{:S(2)}, u32[]{:S(2)}) collective-permute-start(f32[256,512]{1,0:T(8,128)S(1)} %collective-permute-done.4.refs_3_.both), channel_id=1, source_target_pairs={{0,0},{1,1},{2,26},{3,3},{4,4},{5,29},{6,6},{7,7},{8,8},{9,9},{10,... | collective-permute-start | bytes 1572872 | tf_op jit(solution)/shard_map/ppermute | solution.py:106
  28.0 10.5 %collective-permute-start.8 = (f32[256,512]{1,0:T(8,128)S(1)}, f32[256,512]{1,0:T(8,128)S(1)}, u32[]{:S(2)}, u32[]{:S(2)}) collective-permute-start(f32[256,512]{1,0:T(8,128)S(1)} %get-tuple-element.34), channel_id=1, source_target_pairs={{26,0},{29,1},{2,8},{5,9},{10,16},{13,17},{18,24},{21,25}} | collective-permute-start | bytes 1572872 | tf_op jit(solution)/shard_map/ppermute | solution.py:106
  28.7 10.5 %collective-permute-start.7 = (f32[256,512]{1,0:T(8,128)S(1)}, f32[256,512]{1,0:T(8,128)S(1)}, u32[]{:S(2)}, u32[]{:S(2)}) collective-permute-start(f32[256,512]{1,0:T(8,128)S(1)} %get-tuple-element.33), channel_id=1, source_target_pairs={{0,2},{1,5},{2,0},{3,7},{4,6},{5,1},{6,4},{7,3},{8,10},{9,13},{10,... | collective-permute-start | bytes 1572872 | tf_op jit(solution)/shard_map/ppermute | solution.py:106
  33.0 18.6 %collective-permute-start.6 = (f32[2,256,512]{2,1,0:T(8,128)S(1)}, f32[2,256,512]{2,1,0:T(8,128)S(1)}, u32[]{:S(2)}, u32[]{:S(2)}) collective-permute-start(f32[2,256,512]{2,1,0:T(8,128)S(1)} %choose.2), channel_id=1, source_target_pairs={{0,4},{1,3},{2,6},{3,1},{4,0},{5,7},{6,2},{7,5},{8,12},{9,11},{10,... | collective-permute-start | bytes 3145736 | tf_op jit(solution)/shard_map/ppermute | solution.py:106
  39.4 14.9 %collective-permute-start.10 = (f32[256,512]{1,0:T(8,128)S(1)}, f32[256,512]{1,0:T(8,128)S(1)}, u32[]{:S(2)}, u32[]{:S(2)}) collective-permute-start(f32[256,512]{1,0:T(8,128)S(1)} %add_add_fusion.1), channel_id=1, source_target_pairs={{24,0},{25,1},{26,2},{27,3},{28,4},{29,5},{30,6},{31,7},{0,8},{1,9... | collective-permute-start | bytes 1572872 | tf_op jit(solution)/shard_map/ppermute | solution.py:106
  39.4 14.9 %collective-permute-start.9 = (f32[256,512]{1,0:T(8,128)S(1)}, f32[256,512]{1,0:T(8,128)S(1)}, u32[]{:S(2)}, u32[]{:S(2)}) collective-permute-start(f32[256,512]{1,0:T(8,128)S(1)} %get-tuple-element.35), channel_id=1, source_target_pairs={{0,2},{1,5},{2,0},{3,7},{4,6},{5,1},{6,4},{7,3},{8,10},{9,13},{10,... | collective-permute-start | bytes 1572872 | tf_op jit(solution)/shard_map/ppermute | solution.py:106
  54.5 12.1 %collective-permute-start.12 = (f32[256,512]{1,0:T(8,128)S(1)}, f32[256,512]{1,0:T(8,128)S(1)}, u32[]{:S(2)}, u32[]{:S(2)}) collective-permute-start(f32[256,512]{1,0:T(8,128)S(1)} %add_add_fusion.refs_0_.image_ref.own), channel_id=1, source_target_pairs={{0,24},{1,25},{2,26},{3,27},{4,28},{5,29},{6,30},{7,31},{8,0},{9,1... | collective-permute-start | bytes 1572872 | tf_op jit(solution)/shard_map/ppermute | solution.py:106
  58.6 15.6 %collective-permute-start.11 = (f32[256,512]{1,0:T(8,128)S(1)}, f32[256,512]{1,0:T(8,128)S(1)}, u32[]{:S(2)}, u32[]{:S(2)}) collective-permute-start(f32[256,512]{1,0:T(8,128)S(1)} %add_add_fusion.refs_0_.image_ref.own), channel_id=1, source_target_pairs={{0,2},{1,5},{2,0},{3,7},{4,6},{5,1},{6,4},{7,3},{8,10},{9,13},{10,... | collective-permute-start | bytes 1572872 | tf_op jit(solution)/shard_map/ppermute | solution.py:106
  66.6 14.5 %collective-permute-start.13 = (f32[256,512]{1,0:T(8,128)S(1)}, f32[256,512]{1,0:T(8,128)S(1)}, u32[]{:S(2)}, u32[]{:S(2)}) collective-permute-start(f32[256,512]{1,0:T(8,128)S(1)} %collective-permute-done.12.refs_2_.group), channel_id=1, source_target_pairs={{0,2},{1,5},{2,0},{3,7},{4,6},{5,1},{6,4},{7,3},{8,10},{9,13},{10,... | collective-permute-start | bytes 1572872 | tf_op jit(solution)/shard_map/ppermute | solution.py:106
  81.7 20.8 %collective-permute-start.15 = (f32[2,256,512]{2,1,0:T(8,128)S(1)}, f32[2,256,512]{2,1,0:T(8,128)S(1)}, u32[]{:S(2)}, u32[]{:S(2)}) collective-permute-start(f32[2,256,512]{2,1,0:T(8,128)S(1)} %choose.3.refs_1_), channel_id=1, source_target_pairs={{0,4},{1,3},{2,6},{3,1},{4,0},{5,7},{6,2},{7,5},{8,12},{9,11},{10,... | collective-permute-start | bytes 3145736 | tf_op jit(solution)/shard_map/ppermute | solution.py:106
  84.0 11.1 %collective-permute-start.14 = (f32[256,512]{1,0:T(8,128)S(1)}, f32[256,512]{1,0:T(8,128)S(1)}, u32[]{:S(2)}, u32[]{:S(2)}) collective-permute-start(f32[256,512]{1,0:T(8,128)S(1)} %collective-permute-done.13.refs_3_.both), channel_id=1, source_target_pairs={{2,30},{5,31},{10,6},{13,7},{18,14},{21,15},{26,22},{29,23}} | collective-permute-start | bytes 1572872 | tf_op jit(solution)/shard_map/ppermute | solution.py:106
  106.1 16.8 %collective-permute-start.17 = (f32[2,256,512]{2,1,0:T(8,128)S(1)}, f32[2,256,512]{2,1,0:T(8,128)S(1)}, u32[]{:S(2)}, u32[]{:S(2)}) collective-permute-start(f32[2,256,512]{2,1,0:T(8,128)S(1)} %get-tuple-element.44), channel_id=1, source_target_pairs={{0,1},{1,0},{2,3},{3,2},{4,5},{5,4},{6,7},{7,6},{8,9},{9,8},{10,11... | collective-permute-start | bytes 3145736 | tf_op jit(solution)/shard_map/ppermute | solution.py:400
  118.2 1.2 copy-start.5
  119.5 3.5 %copy-start.1 = (f32[1,3,512,512]{3,2,1,0:T(8,128)S(1)}, f32[1,3,512,512]{3,2,1,0:T(8,128)}, u32[]{:S(2)}) copy-start(f32[1,3,512,512]{3,2,1,0:T(8,128)} %param.5) | copy-start | bytes 9437188
  122.2 2.7 %collective-permute-start.16 = (f32[1,256,512]{2,1,0:T(8,128)S(1)}, f32[1,256,512]{2,1,0:T(8,128)S(1)}, u32[]{:S(2)}, u32[]{:S(2)}) collective-permute-start(f32[1,256,512]{2,1,0:T(8,128)S(1)} %get-tuple-element.42), channel_id=1, source_target_pairs={{0,1},{1,0},{2,3},{3,2},{4,5},{5,4},{6,7},{7,6},{8,9},{9,8},{10,11... | collective-permute-start | bytes 1572872 | tf_op jit(solution)/shard_map/ppermute | solution.py:400
  (1 other events, 1.0 us)

commit v2 on v1

--- a/solution.py
+++ b/solution.py
@@ -84,9 +84,6 @@
                 target = var ^ last
             elif kind == "group":
                 target = back
-            elif kind == "two":
-                target = back ^ first
-                use = (var & 3) == 0
             elif kind == "column":
                 target = back
                 use = (var & 3) in wanted(first, last, 2)
@@ -264,7 +261,7 @@
 
 def right_kernel(slots, pair, offs_ref, data_ref, image_ref, own, first, group, both, *refs):
     lasts_ref = refs[0]
-    keep_ref, send_ref, high_ref, low_ref, picked, sems = refs[-6:]
+    keep0_ref, send0_ref, keep_ref, send_ref, high_ref, low_ref, picked, sems = refs[-8:]
     for slot in range(slots):
         sources = (own, first, group, both, lasts_ref.at[slot])
         start_pick(offs_ref[0, slot + 1], sources, picked.at[slot], sems.at[slot])
@@ -277,35 +274,36 @@
     turned = split(image.T)
     image_pair, data_pair = split(image), split(data)
 
-    def store(which, total):
+    def store(keep, send_out, which, total):
         lower, upper = total[:half], total[half:]
 
         @pl.when(samp == 0)
         def _():
-            keep_ref[which] = lower
-            send_ref[which] = upper
+            keep[which] = lower
+            send_out[which] = upper
 
         @pl.when(samp != 0)
         def _():
-            keep_ref[which] = upper
-            send_ref[which] = lower
-
-    store(0, dot3(turned, data_pair, NN) + dot3(data_turned, image_pair, NN))
+            keep[which] = upper
+            send_out[which] = lower
+
+    store(keep0_ref, send0_ref, 0, dot3(turned, data_pair, NN) + dot3(data_turned, image_pair, NN))
     for slot in range(slots):
         pltpu.make_async_copy(own, picked.at[slot], sems.at[slot]).wait()
-        store(slot + 1, dot3(turned, split(picked[slot]), NN))
+        store(keep_ref, send_ref, slot, dot3(turned, split(picked[slot]), NN))
 
 
 def right(offsets, data, image, gate, sources, pair):
     slots = offsets.shape[1] - 1
     rows, block = data.shape
-    part = jax.ShapeDtypeStruct((slots + 1, block // 2, block), f32)
+    part0 = jax.ShapeDtypeStruct((1, block // 2, block), f32)
+    part = jax.ShapeDtypeStruct((slots, block // 2, block), f32)
     turned = jax.ShapeDtypeStruct((block, rows), bf16)
     return pl.pallas_call(
         functools.partial(right_kernel, slots, pair),
         in_specs=[smem_spec(), vmem_spec(), vmem_spec()] + [any_spec()] * (len(gate) + len(sources)),
-        out_specs=[vmem_spec()] * 4,
-        out_shape=[part, part, turned, turned],
+        out_specs=[vmem_spec()] * 6,
+        out_shape=[part0, part0, part, part, turned, turned],
         scratch_shapes=[pltpu.VMEM((slots, rows, block), f32), pltpu.SemaphoreType.DMA((slots,))],
         compiler_params=params(),
         cost_estimate=pl.CostEstimate(flops=400 * rows * block * block, bytes_accessed=0, transcendentals=0),
@@ -313,40 +311,41 @@
     )(offsets, data, image, *sources, *gate)
 
 
-def left_kernel(slots, begin, pair, offs_ref, keep_in, send_in, high_ref, low_ref, own, first, group, both, two,
-                lasts_ref, keep_ref, send_ref, picked, sems):
-    start = slots[0]
-    for slot in slots:
-        sources = (own, first, group, both, lasts_ref.at[slot - 1], two)
-        start_pick(offs_ref[0, slot], sources, picked.at[slot - start], sems.at[slot - start])
-    half = send_ref.shape[1]
-    samp = halves(pair)
-    mine = samp * half
-    yours = half - mine
-    for slot in range(begin, start):
-        keep_ref[slot - begin] = keep_in[slot]
-        send_ref[slot - begin] = send_in[slot]
-    for slot in slots:
-        pltpu.make_async_copy(own, picked.at[slot - start], sems.at[slot - start]).wait()
-        chosen = split(picked[slot - start])
-        for out_ref, in_ref, row in ((send_ref, send_in, yours), (keep_ref, keep_in, mine)):
-            rows = pl.ds(pl.multiple_of(row, half), half)
-            out_ref[slot - begin] = in_ref[slot] + dot3((high_ref[rows], low_ref[rows]), chosen, NN)
-
-
-def left(offsets, slots, begin, parts, turned, sources, pair):
+def left_kernel(slots, pair, offs_ref, keep_in, send_in, high_ref, low_ref, own, first, group, both, two, lasts_ref,
+                keep_ref, send_ref, picked, sems):
+    slot = pl.program_id(0)
+
+    @pl.when(slot == 0)
+    def _():
+        for each in range(slots):
+            sources = (own, first, group, both, lasts_ref.at[each], two)
+            start_pick(offs_ref[0, each + 1], sources, picked.at[each], sems.at[each])
+
+    pltpu.make_async_copy(own, picked.at[slot], sems.at[slot]).wait()
+    half = send_ref.shape[0]
+    mine = halves(pair) * half
+    chosen = split(picked[slot])
+    for out_ref, in_ref, row in ((send_ref, send_in, half - mine), (keep_ref, keep_in, mine)):
+        rows = pl.ds(pl.multiple_of(row, half), half)
+        out_ref[...] = in_ref[...] + dot3((high_ref[rows], low_ref[rows]), chosen, NN)
+
+
+def left(offsets, parts, turned, sources, pair):
     keep = parts[0]
+    slots, half = keep.shape[:2]
     block, rows = turned[0].shape
-    count = slots[-1] + 1 - begin
-    part = jax.ShapeDtypeStruct((count,) + keep.shape[1:], f32)
-    return pl.pallas_call(
-        functools.partial(left_kernel, slots, begin, pair),
-        in_specs=[smem_spec()] + [vmem_spec()] * 4 + [any_spec()] * len(sources),
-        out_specs=[vmem_spec()] * 2,
+    spec = pl.BlockSpec((None, half, block), lambda j: (j, 0, 0))
+    whole = pl.BlockSpec((block, rows), lambda j: (0, 0))
+    part = jax.ShapeDtypeStruct(keep.shape, f32)
+    return pl.pallas_call(
+        functools.partial(left_kernel, slots, pair),
+        grid=(slots,),
+        in_specs=[smem_spec(), spec, spec, whole, whole] + [any_spec()] * len(sources),
+        out_specs=[spec, spec],
         out_shape=[part, part],
-        scratch_shapes=[pltpu.VMEM((len(slots), rows, block), f32), pltpu.SemaphoreType.DMA((len(slots),))],
-        compiler_params=params(),
-        cost_estimate=cost(6 * len(slots) * rows * block * block, 4 * count * block * (2 * block + rows)),
+        scratch_shapes=[pltpu.VMEM((slots, rows, block), f32), pltpu.SemaphoreType.DMA((slots,))],
+        compiler_params=params(),
+        cost_estimate=cost(6 * slots * rows * block * block, 4 * slots * block * (2 * block + rows)),
         name="left",
     )(offsets, *parts, *turned, *sources)
 
@@ -411,35 +410,34 @@
     data_first = send(data, "first")
     data_group = send(data, "group")
     own, far = forward(data, local_tiles)
-    theirs = send(after(far, offsets_next), "last")
+    theirs = send(after(far, (offsets_next, data_first)), "last")
     data_both = send(after(data_first, data_group), "group")
     own, bin_first, bin_group, bin_both, bin_two = make_bins(offsets, offsets_next, own, far, theirs)
-    bin_group = bin_group + send(bin_both, "first") + send(bin_two, "two", reverse=True)
+    got_two = send(bin_two, "column", reverse=True)
+    got_both = send(bin_both, "first")
+    got_first = send(bin_first + got_two, "first")
+    onward = (lax.axis_index("var") & 3) == 0
+    bin_group = bin_group + got_both + jnp.where(onward, got_first, 0.0)
     data_two = send(after(data_both, own), "column")
     chosen = choose(offsets_next, data, data_first, data_group, data_both, data_two)
     data_sources = (data, data_first, data_group, data_both, send(chosen, "last"))
-    got_first = send(after(bin_first, bin_group), "first")
     got_group = send(bin_group, "group", reverse=True)
-    image = own + backward(offsets, local_tiles, data_sources) + got_first + got_group
+    image = own + backward(offsets, local_tiles, data_sources) + jnp.where(onward, 0.0, got_first) + got_group
 
     image_group = send(image, "group")
     image_first = send(image, "first")
     image_both = send(image_group, "first")
     chosen = choose(offsets_next, image, image_first, image_group, image_both)
     image_last = send(chosen, "last")
-    keep, other, high, low = right(offsets, data, image, (chosen,), data_sources, pair)
+    keep0, other0, keep, other, high, low = right(offsets, data, image, (chosen,), data_sources, pair)
     image_two = send(after(image_both, chosen), "direct")
     image_sources = (image, image_first, image_group, image_both, image_two, image_last)
+
+    keep, other = left(offsets, (keep, other), (high, low), image_sources, pair)
     if pair:
-        begin, result = 0, ()
-        for slot in range(1, slot_count):
-            keep_now, other_now = left(
-                offsets, (slot,), begin, (keep, other), (high, low), image_sources, pair)
-            result = (finish(offsets, step, local_tiles, keep_now, swap(other_now), factor, begin, result),)
-            begin = slot + 1
-        return result[0][None]
-    slots = tuple(range(1, slot_count))
-    keep, other = left(offsets, slots, 0, (keep, other), (high, low), image_sources, pair)
+        result = finish(offsets, step, local_tiles, keep0, swap(other0), factor, 0)
+        return finish(offsets, step, local_tiles, keep, swap(other), factor, 1, (result,))[None]
+    keep, other = (jnp.concatenate(both) for both in ((keep0, keep), (other0, other)))
     summed = lax.psum_scatter(jnp.concatenate([keep, other], axis=1), "samp", scatter_dimension=1, tiled=True)
     none = jnp.zeros_like(summed)
     return finish(offsets, step, local_tiles, summed, none, factor, 0)[None]

time: 129 us -> 133 us (1.031); the launches traced: 126 us -> 134 us
  waiting for transfers between devices: 46.1 us -> 64.3 us
  starting transfers between devices: 52.9 us -> 41.3 us
  other arithmetic: 0.37 us -> 3.5 us
  Pallas kernels: 20.9 us -> 18.8 us
    ppermute x16, waiting for transfers between devices: 46.1 us -> 62 us  [send(): return lax.ppermute(value, ('var', 'samp'), pairs)]
    ppermute x2, starting transfers between devices: 12.2 us -> 4.53 us  [swap(): return lax.ppermute(value, 'samp', [(0, 1), (1, 0)])]
    ppermute x16, starting transfers between devices: 40.7 us -> 36.8 us  [send(): return lax.ppermute(value, ('var', 'samp'), pairs)]
    add x2 -> x3, other arithmetic: 0.37 us -> 3.5 us  [the longest x1 1.36 us: shards(): bin_group = bin_group + got_both + jnp.where(onward, got_first, 0.0)]
    pallas_call x2 -> x1, Pallas kernels: 5.34 us -> 2.76 us  [left(): pl.pallas_call(functools.partial(left_kernel, slots, pair), grid=(slots,)...]
    ppermute x2, waiting for transfers between devices: 0.01 us -> 2.31 us  [swap(): return lax.ppermute(value, 'samp', [(0, 1), (1, 0)])]
    unnamed x14 -> x24, local copies, waits for them, and re-layouts: 5.16 us -> 4.9 us
  transfers between devices with their start and end apart: 18 -> 18, of which waited for: 9 -> 9; matrix products, arithmetic and copies ran while one was open for 0% -> 2% of each run, Pallas kernels for 13% -> 10%
where the time goes in v2:
time: 133 us; the launch traced here: 134 us
  waiting for transfers between devices  64.3 us (48%)
  starting transfers between devices  41.3 us (31%)
  Pallas kernels  18.8 us (14%)
  local copies, waits for them, and re-layouts  4.9 us (4%)
  other arithmetic  3.5 us (3%)
    ppermute x16, waiting for transfers between devices, send(): return lax.ppermute(value, ('var', 'samp'), pairs)  62 us
    ppermute x16, starting transfers between devices, send(): return lax.ppermute(value, ('var', 'samp'), pairs)  36.8 us
    unnamed x24, local copies, waits for them, and re-layouts  4.9 us
    ppermute x2, starting transfers between devices, swap(): return lax.ppermute(value, 'samp', [(0, 1), (1, 0)])  4.53 us
    pallas_call x1, Pallas kernels, right(): pl.pallas_call(functools.partial(right_kernel, slots, pair), in_specs=[sm...  4.06 us
    pallas_call x2, Pallas kernels, finish(): pl.pallas_call(functools.partial(finish_kernel, begin, factor), grid=(cou...  3.37 us
    pallas_call x1, Pallas kernels, backward(): pl.pallas_call(functools.partial(backward_kernel, slots), grid=(slots,),...  3.07 us
    pallas_call x1, Pallas kernels, left(): pl.pallas_call(functools.partial(left_kernel, slots, pair), grid=(slots,)...  2.76 us
  transfers between devices with their start and end apart: 18, of which 9 were waited for; matrix products, arithmetic and copies ran while one was open for 2% of the time, Pallas kernels for 10%

profile of v2, /device:TPU:7, one launch (start us, length us, event | category | flops | bytes accessed | tf_op | source)
XLA Modules:
  0.0 133.7 jit_solution(2329503252723768177)
XLA Ops:
  0.3 1.9 %copy-done = f32[1,3,512,512]{3,2,1,0:T(8,128)S(1)} copy-done((f32[1,3,512,512]{3,2,1,0:T(8,128)S(1)}, f32[1,3,512,512]{3,2,1,0:T(8,128)}, u32[]{:S(2)}) %copy-start) | copy-done | bytes 3145752
  3.2 1.9 %forward.1 = (f32[256,512]{1,0:T(8,128)S(1)}, f32[2,256,512]{2,1,0:T(8,128)S(1)}) custom-call(f32[256,512]{1,0:T(8,128)S(1)} %copy-done.2, f32[3,512,512]{2,1,0:T(8,128)S(1)} %bitcast.3), custom_call_target="tpu_custom_call" | custom-call | tf_op jit(solution)/shard_map/forward/pallas_call | solution.py:122
  5.1 3.5 %collective-permute-done.1.refs_1_.first = f32[256,512]{1,0:T(8,128)S(1)} collective-permute-done((f32[256,512]{1,0:T(8,128)}, f32[256,512]{1,0:T(8,128)S(1)}, u32[]{:S(2)}, u32[]{:S(2)}) %collective-permute-start.1) | collective-permute-done | bytes 524320 | tf_op jit(solution)/shard_map/ppermute | solution.py:103
  8.8 3.3 %collective-permute-start.3 = (f32[256,512]{1,0:T(8,128)S(1)}, f32[256,512]{1,0:T(8,128)S(1)}, u32[]{:S(2)}, u32[]{:S(2)}) collective-permute-start(f32[256,512]{1,0:T(8,128)S(1)} %copy-done.2), channel_id=1, source_target_pairs={{0,24},{1,25},{2,26},{3,27},{4,28},{5,29},{6,30},{7,31},{8,0},{9,1... | collective-permute-start | bytes 1572872 | tf_op jit(solution)/shard_map/ppermute | solution.py:103
  12.1 9.4 %collective-permute-done.3.refs_2_.group = f32[256,512]{1,0:T(8,128)S(1)} collective-permute-done((f32[256,512]{1,0:T(8,128)S(1)}, f32[256,512]{1,0:T(8,128)S(1)}, u32[]{:S(2)}, u32[]{:S(2)}) %collective-permute-start.3) | collective-permute-done | bytes 524320 | tf_op jit(solution)/shard_map/ppermute | solution.py:103
  21.6 4.0 %collective-permute-start.4 = (f32[256,512]{1,0:T(8,128)S(1)}, f32[256,512]{1,0:T(8,128)S(1)}, u32[]{:S(2)}, u32[]{:S(2)}) collective-permute-start(f32[256,512]{1,0:T(8,128)S(1)} %collective-permute-done.1.refs_1_.first), channel_id=1, source_target_pairs={{0,24},{1,25},{2,26},{3,27},{4,28},{5,29},{6,30},{7,31},{8,0},{9,1... | collective-permute-start | bytes 1572872 | tf_op jit(solution)/shard_map/ppermute | solution.py:103
  25.6 2.5 %bins.1 = (f32[256,512]{1,0:T(8,128)S(1)}, f32[256,512]{1,0:T(8,128)S(1)}, f32[256,512]{1,0:T(8,128)S(1)}, f32[256,512]{1,0:T(8,128)}, f32[256,512]{1,0:T(8,128)S(1)}) custom-call(s32[1,3]{1,0:T(1,128)S(1)} %copy-done.10, s32[1,3]{1,0:T(1,128)S(1)} %collective-permute-done.next_ref.offs_ref, f32[256,512]{1,0:T(8,128)S(1)} %get-tuple-element.24.own_in, ...), custom_call_target="tpu_custom_call" | custom-call | tf_op jit(solution)/shard_map/bins/pallas_call | solution.py:246
  28.8 5.3 %collective-permute-done.4.refs_3_.both = f32[256,512]{1,0:T(8,128)S(1)} collective-permute-done((f32[256,512]{1,0:T(8,128)S(1)}, f32[256,512]{1,0:T(8,128)S(1)}, u32[]{:S(2)}, u32[]{:S(2)}) %collective-permute-start.4) | collective-permute-done | bytes 524320 | tf_op jit(solution)/shard_map/ppermute | solution.py:103
  35.7 1.4 %collective-permute-start.8 = (f32[256,512]{1,0:T(8,128)}, f32[256,512]{1,0:T(8,128)}, u32[]{:S(2)}, u32[]{:S(2)}) collective-permute-start(f32[256,512]{1,0:T(8,128)} %add.19), channel_id=1, source_target_pairs={{0,2},{1,5},{2,0},{3,7},{4,6},{5,1},{6,4},{7,3},{8,10},{9,13},{10,... | collective-permute-start | bytes 1572872 | tf_op jit(solution)/shard_map/ppermute | solution.py:103
  37.8 14.3 %collective-permute-start.6 = (f32[2,256,512]{2,1,0:T(8,128)}, f32[2,256,512]{2,1,0:T(8,128)S(1)}, u32[]{:S(2)}, u32[]{:S(2)}) collective-permute-start(f32[2,256,512]{2,1,0:T(8,128)} %choose.2), channel_id=1, source_target_pairs={{0,4},{1,3},{2,6},{3,1},{4,0},{5,7},{6,2},{7,5},{8,12},{9,11},{10,... | collective-permute-start | bytes 3145736 | tf_op jit(solution)/shard_map/ppermute | solution.py:103
  54.5 12.6 %collective-permute-done.6.refs_0_ = f32[2,256,512]{2,1,0:T(8,128)S(1)} collective-permute-done((f32[2,256,512]{2,1,0:T(8,128)}, f32[2,256,512]{2,1,0:T(8,128)S(1)}, u32[]{:S(2)}, u32[]{:S(2)}) %collective-permute-start.6) | collective-permute-done | bytes 1048608 | tf_op jit(solution)/shard_map/ppermute | solution.py:103
  67.1 3.1 %backward.1 = f32[256,512]{1,0:T(8,128)S(1)} custom-call(s32[1,3]{1,0:T(1,128)S(1)} %copy-done.10, f32[3,512,512]{2,1,0:T(8,128)} %bitcast.2, f32[256,512]{1,0:T(8,128)S(1)} %copy-done.3, f32[256,512]{1,0:T(8,128)S(1)} %collective-permute-done.1.refs_1_.first, f32[256,512]{1,0:T(8,128)S(1)} %collective-permute-done.3.refs_2_.group, ...), custom_call_target="tpu_custom_call" | custom-call | tf_op jit(solution)/shard_map/backward/pallas_call | solution.py:209
  71.5 4.1 %collective-permute-start.12 = (f32[256,512]{1,0:T(8,128)S(1)}, f32[256,512]{1,0:T(8,128)S(1)}, u32[]{:S(2)}, u32[]{:S(2)}) collective-permute-start(f32[256,512]{1,0:T(8,128)S(1)} %add_add_fusion.refs_0_.image_ref.own), channel_id=1, source_target_pairs={{0,24},{1,25},{2,26},{3,27},{4,28},{5,29},{6,30},{7,31},{8,0},{9,1... | collective-permute-start | bytes 1572872 | tf_op jit(solution)/shard_map/ppermute | solution.py:103
  75.5 11.1 %collective-permute-done.12.refs_2_.group = f32[256,512]{1,0:T(8,128)S(1)} collective-permute-done((f32[256,512]{1,0:T(8,128)S(1)}, f32[256,512]{1,0:T(8,128)S(1)}, u32[]{:S(2)}, u32[]{:S(2)}) %collective-permute-start.12) | collective-permute-done | bytes 524320 | tf_op jit(solution)/shard_map/ppermute | solution.py:103
  86.6 8.3 %collective-permute-done.13.refs_3_.both = f32[256,512]{1,0:T(8,128)S(1)} collective-permute-done((f32[256,512]{1,0:T(8,128)S(1)}, f32[256,512]{1,0:T(8,128)S(1)}, u32[]{:S(2)}, u32[]{:S(2)}) %collective-permute-start.13) | collective-permute-done | bytes 524320 | tf_op jit(solution)/shard_map/ppermute | solution.py:103
  95.6 5.4 %collective-permute-start.15 = (f32[2,256,512]{2,1,0:T(8,128)S(1)}, f32[2,256,512]{2,1,0:T(8,128)S(1)}, u32[]{:S(2)}, u32[]{:S(2)}) collective-permute-start(f32[2,256,512]{2,1,0:T(8,128)S(1)} %choose.3.refs_1_), channel_id=1, source_target_pairs={{0,4},{1,3},{2,6},{3,1},{4,0},{5,7},{6,2},{7,5},{8,12},{9,11},{10,... | collective-permute-start | bytes 3145736 | tf_op jit(solution)/shard_map/ppermute | solution.py:103
  102.3 4.1 %right.1 = (f32[1,256,512]{2,1,0:T(8,128)S(1)}, f32[1,256,512]{2,1,0:T(8,128)S(1)}, f32[2,256,512]{2,1,0:T(8,128)S(1)}, f32[2,256,512]{2,1,0:T(8,128)}, bf16[512...) custom-call(s32[1,3]{1,0:T(1,128)S(1)} %copy-done.10, f32[256,512]{1,0:T(8,128)S(1)} %copy-done.3, ...), custom_call_target="tpu_custom_call" | custom-call | flops 26843545600 | tf_op jit(solution)/shard_map/right/pallas_call | solution.py:302
  107.3 4.8 %collective-permute-done.14.two = f32[256,512]{1,0:T(8,128)S(1)} collective-permute-done((f32[256,512]{1,0:T(8,128)S(1)}, f32[256,512]{1,0:T(8,128)S(1)}, u32[]{:S(2)}, u32[]{:S(2)}) %collective-permute-start.14) | collective-permute-done | bytes 524320 | tf_op jit(solution)/shard_map/ppermute | solution.py:103
  112.1 7.0 %collective-permute-done.15.lasts_ref = f32[2,256,512]{2,1,0:T(8,128)S(1)} collective-permute-done((f32[2,256,512]{2,1,0:T(8,128)S(1)}, f32[2,256,512]{2,1,0:T(8,128)S(1)}, u32[]{:S(2)}, u32[]{:S(2)}) %collective-permute-start.15) | collective-permute-done | bytes 1048608 | tf_op jit(solution)/shard_map/ppermute | solution.py:103
  120.1 2.8 %left.1 = (f32[2,256,512]{2,1,0:T(8,128)S(1)}, f32[2,256,512]{2,1,0:T(8,128)S(1)}) custom-call(s32[1,3]{1,0:T(1,128)S(1)} %copy-done.10, f32[2,256,512]{2,1,0:T(8,128)} %copy-done.4, f32[2,256,512]{2,1,0:T(8,128)} %get-tuple-element.35.send_in, bf16[512,256]{1,0:T(8,128)(2,1)S(1)} %get-tuple-element.36.high_ref, ...), custom_call_target="tpu_custom_call" | custom-call | tf_op jit(solution)/shard_map/left/pallas_call | solution.py:340
  122.8 4.5 %collective-permute-start.16 = (f32[2,256,512]{2,1,0:T(8,128)S(1)}, f32[2,256,512]{2,1,0:T(8,128)S(1)}, u32[]{:S(2)}, u32[]{:S(2)}) collective-permute-start(f32[2,256,512]{2,1,0:T(8,128)S(1)} %get-tuple-element.40), channel_id=1, source_target_pairs={{0,1},{1,0},{2,3},{3,2},{4,5},{5,4},{6,7},{7,6},{8,9},{9,8},{10,11... | collective-permute-start | bytes 3145736 | tf_op jit(solution)/shard_map/ppermute | solution.py:399
  128.0 2.3 %collective-permute-done.17.other_ref = f32[1,256,512]{2,1,0:T(8,128)S(1)} collective-permute-done((f32[1,256,512]{2,1,0:T(8,128)S(1)}, f32[1,256,512]{2,1,0:T(8,128)S(1)}, u32[]{:S(2)}, u32[]{:S(2)}) %collective-permute-start.17) | collective-permute-done | bytes 524320 | tf_op jit(solution)/shard_map/ppermute | solution.py:399
  130.3 1.6 %finish.2.refs_0_ = f32[3,256,512]{2,1,0:T(8,128)} custom-call(s32[1,3]{1,0:T(1,128)S(1)} %copy-done.10, f32[1]{0:T(128)S(6)} %copy.7.step_ref, f32[3,512,512]{2,1,0:T(8,128)S(1)} %bitcast.4, f32[1,256,512]{2,1,0:T(8,128)S(1)} %get-tuple-element.41.keep_ref, f32[1,256,512]{2,1,0:T(8,128)S(1)} %collective-permute-done.17.other_ref), custom_call_target="tpu_custom_call" | custom-call | tf_op jit(solution)/shard_map/finish/pallas_call | solution.py:381
  131.9 1.8 %finish.3 = f32[3,256,512]{2,1,0:T(8,128)} custom-call(s32[1,3]{1,0:T(1,128)S(1)} %copy-done.10, f32[1]{0:T(128)S(6)} %copy.7.step_ref, f32[3,512,512]{2,1,0:T(8,128)S(1)} %bitcast.5, f32[2,256,512]{2,1,0:T(8,128)S(1)} %get-tuple-element.39.keep_ref, f32[2,256,512]{2,1,0:T(8,128)S(1)} %collective-permute-done.16.other_ref, ...), custom_call_target="tpu_custom_call", output_to_operand_aliasing={{}: (5, {})} | custom-call | tf_op jit(solution)/shard_map/finish/pallas_call | solution.py:381
  (48 shorter events, 12.1 us)
Async XLA Ops:
  0.0 8.5 %collective-permute-start.1 = (f32[256,512]{1,0:T(8,128)}, f32[256,512]{1,0:T(8,128)S(1)}, u32[]{:S(2)}, u32[]{:S(2)}) collective-permute-start(f32[256,512]{1,0:T(8,128)} %own.3), channel_id=1, source_target_pairs={{0,2},{1,5},{2,0},{3,7},{4,6},{5,1},{6,4},{7,3},{8,10},{9,13},{10,... | collective-permute-start | bytes 1572872 | tf_op jit(solution)/shard_map/ppermute | solution.py:103
  0.2 4.8 %collective-permute-start = (s32[1,3]{1,0:T(1,128)}, s32[1,3]{1,0:T(1,128)S(1)}, u32[]{:S(2)}, u32[]{:S(2)}) collective-permute-start(s32[1,3]{1,0:T(1,128)} %offs_ref.11), channel_id=1, source_target_pairs={{0,4},{1,3},{2,6},{3,1},{4,0},{5,7},{6,2},{7,5},{8,12},{9,11},{10,... | collective-permute-start | bytes 44 | tf_op jit(solution)/shard_map/ppermute | solution.py:103
  3.2 22.4 %copy-start.10 = (s32[1,3]{1,0:T(1,128)S(1)}, s32[1,3]{1,0:T(1,128)}, u32[]{:S(2)}) copy-start(s32[1,3]{1,0:T(1,128)} %offs_ref.11) | copy-start | bytes 40
  8.5 17.0 %collective-permute-start.2 = (f32[2,256,512]{2,1,0:T(8,128)S(1)}, f32[2,256,512]{2,1,0:T(8,128)S(1)}, u32[]{:S(2)}, u32[]{:S(2)}) collective-permute-start(f32[2,256,512]{2,1,0:T(8,128)S(1)} %get-tuple-element.26.mine_ref), channel_id=1, source_target_pairs={{0,4},{1,3},{2,6},{3,1},{4,0},{5,7},{6,2},{7,5},{8,12},{9,11},{10,... | collective-permute-start | bytes 3145736 | tf_op jit(solution)/shard_map/ppermute | solution.py:103
  8.8 12.8 %collective-permute-start.3 = (f32[256,512]{1,0:T(8,128)S(1)}, f32[256,512]{1,0:T(8,128)S(1)}, u32[]{:S(2)}, u32[]{:S(2)}) collective-permute-start(f32[256,512]{1,0:T(8,128)S(1)} %copy-done.2), channel_id=1, source_target_pairs={{0,24},{1,25},{2,26},{3,27},{4,28},{5,29},{6,30},{7,31},{8,0},{9,1... | collective-permute-start | bytes 1572872 | tf_op jit(solution)/shard_map/ppermute | solution.py:103
  21.6 12.5 %collective-permute-start.4 = (f32[256,512]{1,0:T(8,128)S(1)}, f32[256,512]{1,0:T(8,128)S(1)}, u32[]{:S(2)}, u32[]{:S(2)}) collective-permute-start(f32[256,512]{1,0:T(8,128)S(1)} %collective-permute-done.1.refs_1_.first), channel_id=1, source_target_pairs={{0,24},{1,25},{2,26},{3,27},{4,28},{5,29},{6,30},{7,31},{8,0},{9,1... | collective-permute-start | bytes 1572872 | tf_op jit(solution)/shard_map/ppermute | solution.py:103
  25.6 11.6 %copy-start.3 = (f32[256,512]{1,0:T(8,128)S(1)}, f32[256,512]{1,0:T(8,128)}, u32[]{:S(2)}) copy-start(f32[256,512]{1,0:T(8,128)} %own.3) | copy-start | bytes 1572868
  28.1 9.7 %copy-start.7 = (f32[256,512]{1,0:T(8,128)}, f32[256,512]{1,0:T(8,128)S(1)}, u32[]{:S(2)}) copy-start(f32[256,512]{1,0:T(8,128)S(1)} %get-tuple-element.32) | copy-start | bytes 1572868
  28.1 9.7 %copy-start.8 = (f32[256,512]{1,0:T(8,128)}, f32[256,512]{1,0:T(8,128)S(1)}, u32[]{:S(2)}) copy-start(f32[256,512]{1,0:T(8,128)S(1)} %get-tuple-element.27) | copy-start | bytes 1572868
  28.1 6.8 %collective-permute-start.7 = (f32[256,512]{1,0:T(8,128)S(1)}, f32[256,512]{1,0:T(8,128)S(1)}, u32[]{:S(2)}, u32[]{:S(2)}) collective-permute-start(f32[256,512]{1,0:T(8,128)S(1)} %get-tuple-element.31), channel_id=1, source_target_pairs={{0,0},{1,1},{26,2},{3,3},{4,4},{29,5},{6,6},{7,7},{8,8},{9,9},{2,1... | collective-permute-start | bytes 1572872 | tf_op jit(solution)/shard_map/ppermute | solution.py:103
  34.1 3.1 %collective-permute-start.5 = (f32[256,512]{1,0:T(8,128)S(1)}, f32[256,512]{1,0:T(8,128)S(1)}, u32[]{:S(2)}, u32[]{:S(2)}) collective-permute-start(f32[256,512]{1,0:T(8,128)S(1)} %collective-permute-done.4.refs_3_.both), channel_id=1, source_target_pairs={{0,0},{1,1},{2,26},{3,3},{4,4},{5,29},{6,6},{7,7},{8,8},{9,9},{10,... | collective-permute-start | bytes 1572872 | tf_op jit(solution)/shard_map/ppermute | solution.py:103
  34.8 17.4 %collective-permute-start.9 = (f32[256,512]{1,0:T(8,128)}, f32[256,512]{1,0:T(8,128)}, u32[]{:S(2)}, u32[]{:S(2)}) collective-permute-start(f32[256,512]{1,0:T(8,128)} %get-tuple-element.33), channel_id=1, source_target_pairs={{0,2},{1,5},{2,0},{3,7},{4,6},{5,1},{6,4},{7,3},{8,10},{9,13},{10,... | collective-permute-start | bytes 1572872 | tf_op jit(solution)/shard_map/ppermute | solution.py:103
  35.7 16.4 %collective-permute-start.8 = (f32[256,512]{1,0:T(8,128)}, f32[256,512]{1,0:T(8,128)}, u32[]{:S(2)}, u32[]{:S(2)}) collective-permute-start(f32[256,512]{1,0:T(8,128)} %add.19), channel_id=1, source_target_pairs={{0,2},{1,5},{2,0},{3,7},{4,6},{5,1},{6,4},{7,3},{8,10},{9,13},{10,... | collective-permute-start | bytes 1572872 | tf_op jit(solution)/shard_map/ppermute | solution.py:103
  37.8 29.3 %collective-permute-start.6 = (f32[2,256,512]{2,1,0:T(8,128)}, f32[2,256,512]{2,1,0:T(8,128)S(1)}, u32[]{:S(2)}, u32[]{:S(2)}) collective-permute-start(f32[2,256,512]{2,1,0:T(8,128)} %choose.2), channel_id=1, source_target_pairs={{0,4},{1,3},{2,6},{3,1},{4,0},{5,7},{6,2},{7,5},{8,12},{9,11},{10,... | collective-permute-start | bytes 3145736 | tf_op jit(solution)/shard_map/ppermute | solution.py:103
  53.5 16.7 %copy-start.9 = (f32[256,512]{1,0:T(8,128)S(1)}, f32[256,512]{1,0:T(8,128)}, u32[]{:S(2)}) copy-start(f32[256,512]{1,0:T(8,128)} %copy-done.8) | copy-start | bytes 1572868
  53.5 16.7 %collective-permute-start.10 = (f32[256,512]{1,0:T(8,128)S(1)}, f32[256,512]{1,0:T(8,128)S(1)}, u32[]{:S(2)}, u32[]{:S(2)}) collective-permute-start(f32[256,512]{1,0:T(8,128)S(1)} %select_add_fusion), channel_id=1, source_target_pairs={{24,0},{25,1},{26,2},{27,3},{28,4},{29,5},{30,6},{31,7},{0,8},{1,9... | collective-permute-start | bytes 1572872 | tf_op jit(solution)/shard_map/ppermute | solution.py:103
  71.5 15.2 %collective-permute-start.12 = (f32[256,512]{1,0:T(8,128)S(1)}, f32[256,512]{1,0:T(8,128)S(1)}, u32[]{:S(2)}, u32[]{:S(2)}) collective-permute-start(f32[256,512]{1,0:T(8,128)S(1)} %add_add_fusion.refs_0_.image_ref.own), channel_id=1, source_target_pairs={{0,24},{1,25},{2,26},{3,27},{4,28},{5,29},{6,30},{7,31},{8,0},{9,1... | collective-permute-start | bytes 1572872 | tf_op jit(solution)/shard_map/ppermute | solution.py:103
  75.5 11.1 %collective-permute-start.11 = (f32[256,512]{1,0:T(8,128)S(1)}, f32[256,512]{1,0:T(8,128)S(1)}, u32[]{:S(2)}, u32[]{:S(2)}) collective-permute-start(f32[256,512]{1,0:T(8,128)S(1)} %add_add_fusion.refs_0_.image_ref.own), channel_id=1, source_target_pairs={{0,2},{1,5},{2,0},{3,7},{4,6},{5,1},{6,4},{7,3},{8,10},{9,13},{10,... | collective-permute-start | bytes 1572872 | tf_op jit(solution)/shard_map/ppermute | solution.py:103
  86.6 8.3 %collective-permute-start.13 = (f32[256,512]{1,0:T(8,128)S(1)}, f32[256,512]{1,0:T(8,128)S(1)}, u32[]{:S(2)}, u32[]{:S(2)}) collective-permute-start(f32[256,512]{1,0:T(8,128)S(1)} %collective-permute-done.12.refs_2_.group), channel_id=1, source_target_pairs={{0,2},{1,5},{2,0},{3,7},{4,6},{5,1},{6,4},{7,3},{8,10},{9,13},{10,... | collective-permute-start | bytes 1572872 | tf_op jit(solution)/shard_map/ppermute | solution.py:103
  95.6 23.5 %collective-permute-start.15 = (f32[2,256,512]{2,1,0:T(8,128)S(1)}, f32[2,256,512]{2,1,0:T(8,128)S(1)}, u32[]{:S(2)}, u32[]{:S(2)}) collective-permute-start(f32[2,256,512]{2,1,0:T(8,128)S(1)} %choose.3.refs_1_), channel_id=1, source_target_pairs={{0,4},{1,3},{2,6},{3,1},{4,0},{5,7},{6,2},{7,5},{8,12},{9,11},{10,... | collective-permute-start | bytes 3145736 | tf_op jit(solution)/shard_map/ppermute | solution.py:103
  101.0 11.2 %collective-permute-start.14 = (f32[256,512]{1,0:T(8,128)S(1)}, f32[256,512]{1,0:T(8,128)S(1)}, u32[]{:S(2)}, u32[]{:S(2)}) collective-permute-start(f32[256,512]{1,0:T(8,128)S(1)} %collective-permute-done.13.refs_3_.both), channel_id=1, source_target_pairs={{2,30},{5,31},{10,6},{13,7},{18,14},{21,15},{26,22},{29,23}} | collective-permute-start | bytes 1572872 | tf_op jit(solution)/shard_map/ppermute | solution.py:103
  120.1 10.3 %copy-start.1 = (f32[1,3,512,512]{3,2,1,0:T(8,128)S(1)}, f32[1,3,512,512]{3,2,1,0:T(8,128)}, u32[]{:S(2)}) copy-start(f32[1,3,512,512]{3,2,1,0:T(8,128)} %param.5) | copy-start | bytes 9437188
  122.8 9.1 %collective-permute-start.16 = (f32[2,256,512]{2,1,0:T(8,128)S(1)}, f32[2,256,512]{2,1,0:T(8,128)S(1)}, u32[]{:S(2)}, u32[]{:S(2)}) collective-permute-start(f32[2,256,512]{2,1,0:T(8,128)S(1)} %get-tuple-element.40), channel_id=1, source_target_pairs={{0,1},{1,0},{2,3},{3,2},{4,5},{5,4},{6,7},{7,6},{8,9},{9,8},{10,11... | collective-permute-start | bytes 3145736 | tf_op jit(solution)/shard_map/ppermute | solution.py:399
  127.3 3.0 %collective-permute-start.17 = (f32[1,256,512]{2,1,0:T(8,128)S(1)}, f32[1,256,512]{2,1,0:T(8,128)S(1)}, u32[]{:S(2)}, u32[]{:S(2)}) collective-permute-start(f32[1,256,512]{2,1,0:T(8,128)S(1)} %get-tuple-element.42), channel_id=1, source_target_pairs={{0,1},{1,0},{2,3},{3,2},{4,5},{5,4},{6,7},{7,6},{8,9},{9,8},{10,11... | collective-permute-start | bytes 1572872 | tf_op jit(solution)/shard_map/ppermute | solution.py:399
  (6 other events, 14.6 us)

commit v3 on v2

--- a/solution.py
+++ b/solution.py
@@ -210,7 +210,8 @@
         functools.partial(backward_kernel, slots),
         grid=(slots,),
         in_specs=[smem_spec(), pl.BlockSpec((None, block, block), lambda j: (j + 1, 0, 0))]
-        + [any_spec()] * len(sources),
+        + [any_spec()] * (len(sources) - 1)
+        + [vmem_spec()],
         out_specs=pl.BlockSpec((rows, block), lambda j: (0, 0)),
         out_shape=jax.ShapeDtypeStruct((rows, block), f32),
         scratch_shapes=[pltpu.VMEM((slots, rows, block), f32), pltpu.SemaphoreType.DMA((slots,))],
@@ -340,7 +341,7 @@
     return pl.pallas_call(
         functools.partial(left_kernel, slots, pair),
         grid=(slots,),
-        in_specs=[smem_spec(), spec, spec, whole, whole] + [any_spec()] * len(sources),
+        in_specs=[smem_spec(), spec, spec, whole, whole] + [any_spec()] * (len(sources) - 1) + [vmem_spec()],
         out_specs=[spec, spec],
         out_shape=[part, part],
         scratch_shapes=[pltpu.VMEM((slots, rows, block), f32), pltpu.SemaphoreType.DMA((slots,))],
@@ -410,19 +411,17 @@
     data_first = send(data, "first")
     data_group = send(data, "group")
     own, far = forward(data, local_tiles)
-    theirs = send(after(far, (offsets_next, data_first)), "last")
+    theirs = send(after(far, offsets_next), "last")
     data_both = send(after(data_first, data_group), "group")
     own, bin_first, bin_group, bin_both, bin_two = make_bins(offsets, offsets_next, own, far, theirs)
     got_two = send(bin_two, "column", reverse=True)
-    got_both = send(bin_both, "first")
-    got_first = send(bin_first + got_two, "first")
-    onward = (lax.axis_index("var") & 3) == 0
-    bin_group = bin_group + got_both + jnp.where(onward, got_first, 0.0)
-    data_two = send(after(data_both, own), "column")
+    got_both = send(bin_both + got_two, "group", reverse=True)
+    got_group = send(after(bin_group, got_both), "group", reverse=True)
+    data_two = send(data_both, "column")
     chosen = choose(offsets_next, data, data_first, data_group, data_both, data_two)
     data_sources = (data, data_first, data_group, data_both, send(chosen, "last"))
-    got_group = send(bin_group, "group", reverse=True)
-    image = own + backward(offsets, local_tiles, data_sources) + jnp.where(onward, 0.0, got_first) + got_group
+    got_first = send(bin_first + got_both, "first")
+    image = own + backward(offsets, local_tiles, data_sources) + got_first + got_group
 
     image_group = send(image, "group")
     image_first = send(image, "first")
@@ -433,9 +432,11 @@
     image_two = send(after(image_both, chosen), "direct")
     image_sources = (image, image_first, image_group, image_both, image_two, image_last)
 
+    if pair:
+        result = finish(offsets, step, local_tiles, keep0, swap(other0), factor, 0)
+        keep = after(keep, result)
     keep, other = left(offsets, (keep, other), (high, low), image_sources, pair)
     if pair:
-        result = finish(offsets, step, local_tiles, keep0, swap(other0), factor, 0)
         return finish(offsets, step, local_tiles, keep, swap(other), factor, 1, (result,))[None]
     keep, other = (jnp.concatenate(both) for both in ((keep0, keep), (other0, other)))
     summed = lax.psum_scatter(jnp.concatenate([keep, other], axis=1), "samp", scatter_dimension=1, tiled=True)

time: 133 us -> 143 us (1.075)
  starting transfers between devices: 41.3 us -> 55.6 us
  other arithmetic: 3.5 us -> 0.39 us
  waiting for transfers between devices: 64.3 us -> 62.5 us
    ppermute x2, starting transfers between devices: 4.53 us -> 17 us  [swap(): return lax.ppermute(value, 'samp', [(0, 1), (1, 0)])]
    add x3, other arithmetic: 3.5 us -> 0.39 us  [the longest x1 0.23 us: shards(): own + backward(offsets, local_tiles, data_sources) + got_first + got_group]
    ppermute x16, starting transfers between devices: 36.8 us -> 38.6 us  [send(): return lax.ppermute(value, ('var', 'samp'), pairs)]
    ppermute x16, waiting for transfers between devices: 62 us -> 60.2 us  [send(): return lax.ppermute(value, ('var', 'samp'), pairs)]
    unnamed x24 -> x18, local copies, waits for them, and re-layouts: 4.9 us -> 4.89 us
  transfers between devices with their start and end apart: 18 -> 18, of which waited for: 9 -> 9; matrix products, arithmetic and copies ran while one was open for 2% -> 0% of each run, Pallas kernels for 10% -> 9%
where the time goes in v3:
time: 143 us; the launch traced here: 142 us
  waiting for transfers between devices  62.5 us (44%)
  starting transfers between devices  55.6 us (39%)
  Pallas kernels  18.3 us (13%)
  local copies, waits for them, and re-layouts  4.89 us (3%)
    ppermute x16, waiting for transfers between devices, send(): return lax.ppermute(value, ('var', 'samp'), pairs)  60.2 us
    ppermute x16, starting transfers between devices, send(): return lax.ppermute(value, ('var', 'samp'), pairs)  38.6 us
    ppermute x2, starting transfers between devices, swap(): return lax.ppermute(value, 'samp', [(0, 1), (1, 0)])  17 us
    unnamed x18, local copies, waits for them, and re-layouts  4.89 us
    pallas_call x1, Pallas kernels, right(): pl.pallas_call(functools.partial(right_kernel, slots, pair), in_specs=[sm...  4.19 us
    pallas_call x2, Pallas kernels, finish(): pl.pallas_call(functools.partial(finish_kernel, begin, factor), grid=(cou...  3.37 us
    pallas_call x1, Pallas kernels, backward(): pl.pallas_call(functools.partial(backward_kernel, slots), grid=(slots,),...  3.06 us
    pallas_call x1, Pallas kernels, left(): pl.pallas_call(functools.partial(left_kernel, slots, pair), grid=(slots,)...  2.97 us
  transfers between devices with their start and end apart: 18, of which 9 were waited for; matrix products, arithmetic and copies ran while one was open for 0% of the time, Pallas kernels for 9%

profile of v3, /device:TPU:7, one launch (start us, length us, event | category | flops | bytes accessed | tf_op | source)
XLA Modules:
  0.0 142.5 jit_solution(4652655503985481271)
XLA Ops:
  0.3 1.9 %copy-done = f32[1,3,512,512]{3,2,1,0:T(8,128)S(1)} copy-done((f32[1,3,512,512]{3,2,1,0:T(8,128)S(1)}, f32[1,3,512,512]{3,2,1,0:T(8,128)}, u32[]{:S(2)}) %copy-start) | copy-done | bytes 3145752
  3.2 1.9 %forward.1 = (f32[256,512]{1,0:T(8,128)S(1)}, f32[2,256,512]{2,1,0:T(8,128)S(1)}) custom-call(f32[256,512]{1,0:T(8,128)S(1)} %copy-done.2, f32[3,512,512]{2,1,0:T(8,128)S(1)} %bitcast.3), custom_call_target="tpu_custom_call" | custom-call | tf_op jit(solution)/shard_map/forward/pallas_call | solution.py:122
  5.1 1.3 collective-permute-start.1
  6.4 3.3 %collective-permute-start.3 = (f32[256,512]{1,0:T(8,128)S(1)}, f32[256,512]{1,0:T(8,128)S(1)}, u32[]{:S(2)}, u32[]{:S(2)}) collective-permute-start(f32[256,512]{1,0:T(8,128)S(1)} %copy-done.2), channel_id=1, source_target_pairs={{0,24},{1,25},{2,26},{3,27},{4,28},{5,29},{6,30},{7,31},{8,0},{9,1... | collective-permute-start | bytes 1572872 | tf_op jit(solution)/shard_map/ppermute | solution.py:103
  9.9 9.8 %collective-permute-done.3.refs_2_.group = f32[256,512]{1,0:T(8,128)S(1)} collective-permute-done((f32[256,512]{1,0:T(8,128)S(1)}, f32[256,512]{1,0:T(8,128)S(1)}, u32[]{:S(2)}, u32[]{:S(2)}) %collective-permute-start.3) | collective-permute-done | bytes 524320 | tf_op jit(solution)/shard_map/ppermute | solution.py:103
  19.7 4.0 %collective-permute-done.2.refs_1_.first = f32[256,512]{1,0:T(8,128)S(1)} collective-permute-done((f32[256,512]{1,0:T(8,128)S(1)}, f32[256,512]{1,0:T(8,128)S(1)}, u32[]{:S(2)}, u32[]{:S(2)}) %collective-permute-start.2) | collective-permute-done | bytes 524320 | tf_op jit(solution)/shard_map/ppermute | solution.py:103
  23.8 1.6 %bins.1 = (f32[256,512]{1,0:T(8,128)S(1)}, f32[256,512]{1,0:T(8,128)S(1)}, f32[256,512]{1,0:T(8,128)S(1)}, f32[256,512]{1,0:T(8,128)S(1)}, f32[256,512]{1,0:T(8,128)S(1)}) custom-call(s32[1,3]{1,0:T(1,128)S(1)} %copy-done.7, s32[1,3]{1,0:T(1,128)S(1)} %collective-permute-done.next_ref.offs_ref, f32[256,512]{1,0:T(8,128)S(1)} %get-tuple-element.25.own_in, ...), custom_call_target="tpu_custom_call" | custom-call | tf_op jit(solution)/shard_map/bins/pallas_call | solution.py:247
  26.1 9.6 %collective-permute-done.4.refs_3_.both = f32[256,512]{1,0:T(8,128)S(1)} collective-permute-done((f32[256,512]{1,0:T(8,128)S(1)}, f32[256,512]{1,0:T(8,128)S(1)}, u32[]{:S(2)}, u32[]{:S(2)}) %collective-permute-start.4) | collective-permute-done | bytes 524320 | tf_op jit(solution)/shard_map/ppermute | solution.py:103
  37.2 23.9 %collective-permute-start.6 = (f32[2,256,512]{2,1,0:T(8,128)S(1)}, f32[2,256,512]{2,1,0:T(8,128)S(1)}, u32[]{:S(2)}, u32[]{:S(2)}) collective-permute-start(f32[2,256,512]{2,1,0:T(8,128)S(1)} %choose.2), channel_id=1, source_target_pairs={{0,4},{1,3},{2,6},{3,1},{4,0},{5,7},{6,2},{7,5},{8,12},{9,11},{10,... | collective-permute-start | bytes 3145736 | tf_op jit(solution)/shard_map/ppermute | solution.py:103
  61.3 13.3 %collective-permute-done.6.refs_0_ = f32[2,256,512]{2,1,0:T(8,128)S(1)} collective-permute-done((f32[2,256,512]{2,1,0:T(8,128)S(1)}, f32[2,256,512]{2,1,0:T(8,128)S(1)}, u32[]{:S(2)}, u32[]{:S(2)}) %collective-permute-start.6) | collective-permute-done | bytes 1048608 | tf_op jit(solution)/shard_map/ppermute | solution.py:103
  74.6 3.1 %backward.1 = f32[256,512]{1,0:T(8,128)S(1)} custom-call(s32[1,3]{1,0:T(1,128)S(1)} %copy-done.7, f32[3,512,512]{2,1,0:T(8,128)} %bitcast.2, f32[256,512]{1,0:T(8,128)S(1)} %copy-done.3, f32[256,512]{1,0:T(8,128)S(1)} %collective-permute-done.2.refs_1_.first, f32[256,512]{1,0:T(8,128)S(1)} %collective-permute-done.3.refs_2_.group, ...), custom_call_target="tpu_custom_call" | custom-call | tf_op jit(solution)/shard_map/backward/pallas_call | solution.py:209
  78.8 7.6 %collective-permute-done.12.refs_2_.group = f32[256,512]{1,0:T(8,128)S(1)} collective-permute-done((f32[256,512]{1,0:T(8,128)S(1)}, f32[256,512]{1,0:T(8,128)S(1)}, u32[]{:S(2)}, u32[]{:S(2)}) %collective-permute-start.12) | collective-permute-done | bytes 524320 | tf_op jit(solution)/shard_map/ppermute | solution.py:103
  86.4 1.5 %collective-permute-done.11.refs_1_.first = f32[256,512]{1,0:T(8,128)S(1)} collective-permute-done((f32[256,512]{1,0:T(8,128)S(1)}, f32[256,512]{1,0:T(8,128)S(1)}, u32[]{:S(2)}, u32[]{:S(2)}) %collective-permute-start.11) | collective-permute-done | bytes 524320 | tf_op jit(solution)/shard_map/ppermute | solution.py:103
  88.0 6.8 %collective-permute-done.13.refs_3_.both = f32[256,512]{1,0:T(8,128)S(1)} collective-permute-done((f32[256,512]{1,0:T(8,128)S(1)}, f32[256,512]{1,0:T(8,128)S(1)}, u32[]{:S(2)}, u32[]{:S(2)}) %collective-permute-start.13) | collective-permute-done | bytes 524320 | tf_op jit(solution)/shard_map/ppermute | solution.py:103
  95.4 5.7 %collective-permute-start.16 = (f32[2,256,512]{2,1,0:T(8,128)S(1)}, f32[2,256,512]{2,1,0:T(8,128)S(1)}, u32[]{:S(2)}, u32[]{:S(2)}) collective-permute-start(f32[2,256,512]{2,1,0:T(8,128)S(1)} %choose.3.refs_1_), channel_id=1, source_target_pairs={{0,4},{1,3},{2,6},{3,1},{4,0},{5,7},{6,2},{7,5},{8,12},{9,11},{10,... | collective-permute-start | bytes 3145736 | tf_op jit(solution)/shard_map/ppermute | solution.py:103
  101.2 4.2 %right.1 = (f32[1,256,512]{2,1,0:T(8,128)S(1)}, f32[1,256,512]{2,1,0:T(8,128)S(1)}, f32[2,256,512]{2,1,0:T(8,128)S(1)}, f32[2,256,512]{2,1,0:T(8,128)}, bf16[512...) custom-call(s32[1,3]{1,0:T(1,128)S(1)} %copy-done.7, f32[256,512]{1,0:T(8,128)S(1)} %copy-done.3, ...), custom_call_target="tpu_custom_call" | custom-call | flops 26843545600 | tf_op jit(solution)/shard_map/right/pallas_call | solution.py:303
  106.3 14.6 %collective-permute-start.14 = (f32[1,256,512]{2,1,0:T(8,128)S(1)}, f32[1,256,512]{2,1,0:T(8,128)S(1)}, u32[]{:S(2)}, u32[]{:S(2)}) collective-permute-start(f32[1,256,512]{2,1,0:T(8,128)S(1)} %get-tuple-element.37), channel_id=1, source_target_pairs={{0,1},{1,0},{2,3},{3,2},{4,5},{5,4},{6,7},{7,6},{8,9},{9,8},{10,11... | collective-permute-start | bytes 1572872 | tf_op jit(solution)/shard_map/ppermute | solution.py:400
  120.9 1.3 collective-permute-start.15
  122.9 1.6 %finish.2.refs_0_ = f32[3,256,512]{2,1,0:T(8,128)} custom-call(s32[1,3]{1,0:T(1,128)S(1)} %copy-done.7, f32[1]{0:T(128)S(6)} %copy.7.step_ref, f32[3,512,512]{2,1,0:T(8,128)S(1)} %bitcast.4, f32[1,256,512]{2,1,0:T(8,128)S(1)} %get-tuple-element.36.keep_ref, f32[1,256,512]{2,1,0:T(8,128)S(1)} %collective-permute-done.14.other_ref), custom_call_target="tpu_custom_call" | custom-call | tf_op jit(solution)/shard_map/finish/pallas_call | solution.py:382
  124.4 7.6 %collective-permute-done.15.two = f32[256,512]{1,0:T(8,128)S(1)} collective-permute-done((f32[256,512]{1,0:T(8,128)S(1)}, f32[256,512]{1,0:T(8,128)S(1)}, u32[]{:S(2)}, u32[]{:S(2)}) %collective-permute-start.15) | collective-permute-done | bytes 524320 | tf_op jit(solution)/shard_map/ppermute | solution.py:103
  133.0 3.0 %left.1 = (f32[2,256,512]{2,1,0:T(8,128)S(1)}, f32[2,256,512]{2,1,0:T(8,128)S(1)}) custom-call(s32[1,3]{1,0:T(1,128)S(1)} %copy-done.7, f32[2,256,512]{2,1,0:T(8,128)} %copy-done.4, f32[2,256,512]{2,1,0:T(8,128)} %get-tuple-element.39.send_in, bf16[512,256]{1,0:T(8,128)(2,1)S(1)} %get-tuple-element.40.high_ref, ...), custom_call_target="tpu_custom_call" | custom-call | tf_op jit(solution)/shard_map/left/pallas_call | solution.py:341
  136.0 2.4 %collective-permute-start.17 = (f32[2,256,512]{2,1,0:T(8,128)S(1)}, f32[2,256,512]{2,1,0:T(8,128)S(1)}, u32[]{:S(2)}, u32[]{:S(2)}) collective-permute-start(f32[2,256,512]{2,1,0:T(8,128)S(1)} %get-tuple-element.44), channel_id=1, source_target_pairs={{0,1},{1,0},{2,3},{3,2},{4,5},{5,4},{6,7},{7,6},{8,9},{9,8},{10,11... | collective-permute-start | bytes 3145736 | tf_op jit(solution)/shard_map/ppermute | solution.py:400
  138.4 2.3 %collective-permute-done.17.other_ref = f32[2,256,512]{2,1,0:T(8,128)S(1)} collective-permute-done((f32[2,256,512]{2,1,0:T(8,128)S(1)}, f32[2,256,512]{2,1,0:T(8,128)S(1)}, u32[]{:S(2)}, u32[]{:S(2)}) %collective-permute-start.17) | collective-permute-done | bytes 1048608 | tf_op jit(solution)/shard_map/ppermute | solution.py:400
  140.7 1.8 %finish.3 = f32[3,256,512]{2,1,0:T(8,128)} custom-call(s32[1,3]{1,0:T(1,128)S(1)} %copy-done.7, f32[1]{0:T(128)S(6)} %copy.7.step_ref, f32[3,512,512]{2,1,0:T(8,128)S(1)} %bitcast.5, f32[2,256,512]{2,1,0:T(8,128)S(1)} %get-tuple-element.43.keep_ref, f32[2,256,512]{2,1,0:T(8,128)S(1)} %collective-permute-done.17.other_ref, ...), custom_call_target="tpu_custom_call", output_to_operand_aliasing={{}: (5, {})} | custom-call | tf_op jit(solution)/shard_map/finish/pallas_call | solution.py:382
  (42 shorter events, 7.7 us)
Async XLA Ops:
  0.0 5.1 %collective-permute-start = (s32[1,3]{1,0:T(1,128)}, s32[1,3]{1,0:T(1,128)S(1)}, u32[]{:S(2)}, u32[]{:S(2)}) collective-permute-start(s32[1,3]{1,0:T(1,128)} %offs_ref.11), channel_id=1, source_target_pairs={{0,4},{1,3},{2,6},{3,1},{4,0},{5,7},{6,2},{7,5},{8,12},{9,11},{10,... | collective-permute-start | bytes 44 | tf_op jit(solution)/shard_map/ppermute | solution.py:103
  0.3 1.9 %copy-start = (f32[1,3,512,512]{3,2,1,0:T(8,128)S(1)}, f32[1,3,512,512]{3,2,1,0:T(8,128)}, u32[]{:S(2)}) copy-start(f32[1,3,512,512]{3,2,1,0:T(8,128)} %param.5) | copy-start | bytes 9437188
  3.2 20.6 %copy-start.7 = (s32[1,3]{1,0:T(1,128)S(1)}, s32[1,3]{1,0:T(1,128)}, u32[]{:S(2)}) copy-start(s32[1,3]{1,0:T(1,128)} %offs_ref.11) | copy-start | bytes 40
  5.1 18.7 %collective-permute-start.1 = (f32[2,256,512]{2,1,0:T(8,128)S(1)}, f32[2,256,512]{2,1,0:T(8,128)S(1)}, u32[]{:S(2)}, u32[]{:S(2)}) collective-permute-start(f32[2,256,512]{2,1,0:T(8,128)S(1)} %get-tuple-element.27.mine_ref), channel_id=1, source_target_pairs={{0,4},{1,3},{2,6},{3,1},{4,0},{5,7},{6,2},{7,5},{8,12},{9,11},{10,... | collective-permute-start | bytes 3145736 | tf_op jit(solution)/shard_map/ppermute | solution.py:103
  6.4 13.3 %collective-permute-start.3 = (f32[256,512]{1,0:T(8,128)S(1)}, f32[256,512]{1,0:T(8,128)S(1)}, u32[]{:S(2)}, u32[]{:S(2)}) collective-permute-start(f32[256,512]{1,0:T(8,128)S(1)} %copy-done.2), channel_id=1, source_target_pairs={{0,24},{1,25},{2,26},{3,27},{4,28},{5,29},{6,30},{7,31},{8,0},{9,1... | collective-permute-start | bytes 1572872 | tf_op jit(solution)/shard_map/ppermute | solution.py:103
  9.7 14.0 %collective-permute-start.2 = (f32[256,512]{1,0:T(8,128)S(1)}, f32[256,512]{1,0:T(8,128)S(1)}, u32[]{:S(2)}, u32[]{:S(2)}) collective-permute-start(f32[256,512]{1,0:T(8,128)S(1)} %copy-done.2), channel_id=1, source_target_pairs={{0,2},{1,5},{2,0},{3,7},{4,6},{5,1},{6,4},{7,3},{8,10},{9,13},{10,... | collective-permute-start | bytes 1572872 | tf_op jit(solution)/shard_map/ppermute | solution.py:103
  23.7 12.0 %collective-permute-start.4 = (f32[256,512]{1,0:T(8,128)S(1)}, f32[256,512]{1,0:T(8,128)S(1)}, u32[]{:S(2)}, u32[]{:S(2)}) collective-permute-start(f32[256,512]{1,0:T(8,128)S(1)} %collective-permute-done.2.refs_1_.first), channel_id=1, source_target_pairs={{0,24},{1,25},{2,26},{3,27},{4,28},{5,29},{6,30},{7,31},{8,0},{9,1... | collective-permute-start | bytes 1572872 | tf_op jit(solution)/shard_map/ppermute | solution.py:103
  23.8 12.8 %copy-start.3 = (f32[256,512]{1,0:T(8,128)S(1)}, f32[256,512]{1,0:T(8,128)}, u32[]{:S(2)}) copy-start(f32[256,512]{1,0:T(8,128)} %own.3) | copy-start | bytes 1572868
  25.4 11.0 %collective-permute-start.7 = (f32[256,512]{1,0:T(8,128)S(1)}, f32[256,512]{1,0:T(8,128)S(1)}, u32[]{:S(2)}, u32[]{:S(2)}) collective-permute-start(f32[256,512]{1,0:T(8,128)S(1)} %get-tuple-element.32), channel_id=1, source_target_pairs={{0,0},{1,1},{26,2},{3,3},{4,4},{29,5},{6,6},{7,7},{8,8},{9,9},{2,1... | collective-permute-start | bytes 1572872 | tf_op jit(solution)/shard_map/ppermute | solution.py:103
  35.7 0.9 collective-permute-start.5
  36.5 24.7 %collective-permute-start.8 = (f32[256,512]{1,0:T(8,128)S(1)}, f32[256,512]{1,0:T(8,128)S(1)}, u32[]{:S(2)}, u32[]{:S(2)}) collective-permute-start(f32[256,512]{1,0:T(8,128)S(1)} %add.16), channel_id=1, source_target_pairs={{24,0},{25,1},{26,2},{27,3},{28,4},{29,5},{30,6},{31,7},{0,8},{1,9... | collective-permute-start | bytes 1572872 | tf_op jit(solution)/shard_map/ppermute | solution.py:103
  37.2 37.3 %collective-permute-start.6 = (f32[2,256,512]{2,1,0:T(8,128)S(1)}, f32[2,256,512]{2,1,0:T(8,128)S(1)}, u32[]{:S(2)}, u32[]{:S(2)}) collective-permute-start(f32[2,256,512]{2,1,0:T(8,128)S(1)} %choose.2), channel_id=1, source_target_pairs={{0,4},{1,3},{2,6},{3,1},{4,0},{5,7},{6,2},{7,5},{8,12},{9,11},{10,... | collective-permute-start | bytes 3145736 | tf_op jit(solution)/shard_map/ppermute | solution.py:103
  61.1 16.5 %collective-permute-start.10 = (f32[256,512]{1,0:T(8,128)S(1)}, f32[256,512]{1,0:T(8,128)S(1)}, u32[]{:S(2)}, u32[]{:S(2)}) collective-permute-start(f32[256,512]{1,0:T(8,128)S(1)} %get-tuple-element.34), channel_id=1, source_target_pairs={{24,0},{25,1},{26,2},{27,3},{28,4},{29,5},{30,6},{31,7},{0,8},{1,9... | collective-permute-start | bytes 1572872 | tf_op jit(solution)/shard_map/ppermute | solution.py:103
  61.2 16.4 %collective-permute-start.9 = (f32[256,512]{1,0:T(8,128)S(1)}, f32[256,512]{1,0:T(8,128)S(1)}, u32[]{:S(2)}, u32[]{:S(2)}) collective-permute-start(f32[256,512]{1,0:T(8,128)S(1)} %add.17), channel_id=1, source_target_pairs={{0,2},{1,5},{2,0},{3,7},{4,6},{5,1},{6,4},{7,3},{8,10},{9,13},{10,... | collective-permute-start | bytes 1572872 | tf_op jit(solution)/shard_map/ppermute | solution.py:103
  74.6 3.1 %copy-start.6 = (f32[2,256,512]{2,1,0:T(8,128)}, f32[2,256,512]{2,1,0:T(8,128)S(1)}, u32[]{:S(2)}) copy-start(f32[2,256,512]{2,1,0:T(8,128)S(1)} %collective-permute-done.6.refs_0_) | copy-start | bytes 3145732
  77.9 8.5 %collective-permute-start.12 = (f32[256,512]{1,0:T(8,128)S(1)}, f32[256,512]{1,0:T(8,128)S(1)}, u32[]{:S(2)}, u32[]{:S(2)}) collective-permute-start(f32[256,512]{1,0:T(8,128)S(1)} %add_add_fusion.refs_0_.image_ref.own), channel_id=1, source_target_pairs={{0,24},{1,25},{2,26},{3,27},{4,28},{5,29},{6,30},{7,31},{8,0},{9,1... | collective-permute-start | bytes 1572872 | tf_op jit(solution)/shard_map/ppermute | solution.py:103
  78.8 9.1 %collective-permute-start.11 = (f32[256,512]{1,0:T(8,128)S(1)}, f32[256,512]{1,0:T(8,128)S(1)}, u32[]{:S(2)}, u32[]{:S(2)}) collective-permute-start(f32[256,512]{1,0:T(8,128)S(1)} %add_add_fusion.refs_0_.image_ref.own), channel_id=1, source_target_pairs={{0,2},{1,5},{2,0},{3,7},{4,6},{5,1},{6,4},{7,3},{8,10},{9,13},{10,... | collective-permute-start | bytes 1572872 | tf_op jit(solution)/shard_map/ppermute | solution.py:103
  86.4 8.3 %collective-permute-start.13 = (f32[256,512]{1,0:T(8,128)S(1)}, f32[256,512]{1,0:T(8,128)S(1)}, u32[]{:S(2)}, u32[]{:S(2)}) collective-permute-start(f32[256,512]{1,0:T(8,128)S(1)} %collective-permute-done.12.refs_2_.group), channel_id=1, source_target_pairs={{0,2},{1,5},{2,0},{3,7},{4,6},{5,1},{6,4},{7,3},{8,10},{9,13},{10,... | collective-permute-start | bytes 1572872 | tf_op jit(solution)/shard_map/ppermute | solution.py:103
  95.4 5.7 %copy-start.5 = (f32[2,256,512]{2,1,0:T(8,128)}, f32[2,256,512]{2,1,0:T(8,128)S(1)}, u32[]{:S(2)}) copy-start(f32[2,256,512]{2,1,0:T(8,128)S(1)} %choose.3.refs_1_) | copy-start | bytes 3145732
  95.4 36.6 %collective-permute-start.16 = (f32[2,256,512]{2,1,0:T(8,128)S(1)}, f32[2,256,512]{2,1,0:T(8,128)S(1)}, u32[]{:S(2)}, u32[]{:S(2)}) collective-permute-start(f32[2,256,512]{2,1,0:T(8,128)S(1)} %choose.3.refs_1_), channel_id=1, source_target_pairs={{0,4},{1,3},{2,6},{3,1},{4,0},{5,7},{6,2},{7,5},{8,12},{9,11},{10,... | collective-permute-start | bytes 3145736 | tf_op jit(solution)/shard_map/ppermute | solution.py:103
  101.2 21.7 %copy-start.1 = (f32[1,3,512,512]{3,2,1,0:T(8,128)S(1)}, f32[1,3,512,512]{3,2,1,0:T(8,128)}, u32[]{:S(2)}) copy-start(f32[1,3,512,512]{3,2,1,0:T(8,128)} %param.5) | copy-start | bytes 9437188
  106.3 16.5 %collective-permute-start.14 = (f32[1,256,512]{2,1,0:T(8,128)S(1)}, f32[1,256,512]{2,1,0:T(8,128)S(1)}, u32[]{:S(2)}, u32[]{:S(2)}) collective-permute-start(f32[1,256,512]{2,1,0:T(8,128)S(1)} %get-tuple-element.37), channel_id=1, source_target_pairs={{0,1},{1,0},{2,3},{3,2},{4,5},{5,4},{6,7},{7,6},{8,9},{9,8},{10,11... | collective-permute-start | bytes 1572872 | tf_op jit(solution)/shard_map/ppermute | solution.py:400
  120.9 11.1 %collective-permute-start.15 = (f32[256,512]{1,0:T(8,128)S(1)}, f32[256,512]{1,0:T(8,128)S(1)}, u32[]{:S(2)}, u32[]{:S(2)}) collective-permute-start(f32[256,512]{1,0:T(8,128)S(1)} %collective-permute-done.13.refs_3_.both), channel_id=1, source_target_pairs={{2,30},{5,31},{10,6},{13,7},{18,14},{21,15},{26,22},{29,23}} | collective-permute-start | bytes 1572872 | tf_op jit(solution)/shard_map/ppermute | solution.py:103
  136.0 4.7 %collective-permute-start.17 = (f32[2,256,512]{2,1,0:T(8,128)S(1)}, f32[2,256,512]{2,1,0:T(8,128)S(1)}, u32[]{:S(2)}, u32[]{:S(2)}) collective-permute-start(f32[2,256,512]{2,1,0:T(8,128)S(1)} %get-tuple-element.44), channel_id=1, source_target_pairs={{0,1},{1,0},{2,3},{3,2},{4,5},{5,4},{6,7},{7,6},{8,9},{9,8},{10,11... | collective-permute-start | bytes 3145736 | tf_op jit(solution)/shard_map/ppermute | solution.py:400
  (3 other events, 3.0 us)

commit v4 on v3

--- a/solution.py
+++ b/solution.py
@@ -84,14 +84,9 @@
                 target = var ^ last
             elif kind == "group":
                 target = back
-            elif kind == "column":
-                target = back
-                use = (var & 3) in wanted(first, last, 2)
             else:
                 target = back ^ last
                 use = (var & 3) in wanted(first, last, 2)
-            if kind == "column" and not use:
-                target, use = var, True
             pair = (var * samp_count + samp, target * samp_count + samp)
             if use:
                 pairs.append(pair[::-1] if reverse else pair)
@@ -103,41 +98,44 @@
     return lax.ppermute(value, ("var", "samp"), pairs)
 
 
-def forward_kernel(data_ref, tile_ref, own_ref, far_ref):
+def forward_kernel(offs_ref, data_ref, tile_ref, own_ref, far_ref, two_ref):
     slot = pl.program_id(0)
     value = dot3(split(data_ref[...]), split(tile_ref[...]), NN)
+    p, flip = place()
+    code = route(p, offs_ref[0, slot], flip)[1]
 
     @pl.when(slot == 0)
     def _():
         own_ref[...] = value
+        two_ref[...] = jnp.zeros_like(two_ref)
 
     @pl.when(slot > 0)
     def _():
         far_ref[...] = value
 
-
-def forward(data, tiles):
+    @pl.when(code == CODES[4])
+    def _():
+        two_ref[...] = value
+
+
+def forward(offsets, data, tiles):
     slots, block = tiles.shape[:2]
     rows = data.shape[0]
+    flat = pl.BlockSpec((rows, block), lambda j: (0, 0))
     return pl.pallas_call(
         forward_kernel,
         grid=(slots,),
-        in_specs=[
-            pl.BlockSpec((rows, block), lambda j: (0, 0)),
-            pl.BlockSpec((None, block, block), lambda j: (j, 0, 0)),
-        ],
-        out_specs=[
-            pl.BlockSpec((rows, block), lambda j: (0, 0)),
-            pl.BlockSpec((None, rows, block), lambda j: (jnp.maximum(j - 1, 0), 0, 0)),
-        ],
+        in_specs=[smem_spec(), flat, pl.BlockSpec((None, block, block), lambda j: (j, 0, 0))],
+        out_specs=[flat, pl.BlockSpec((None, rows, block), lambda j: (jnp.maximum(j - 1, 0), 0, 0)), flat],
         out_shape=[
             jax.ShapeDtypeStruct((rows, block), f32),
             jax.ShapeDtypeStruct((slots - 1, rows, block), f32),
+            jax.ShapeDtypeStruct((rows, block), f32),
         ],
         compiler_params=params(),
         cost_estimate=cost(6 * slots * rows * block * block, 4 * slots * block * (block + 2 * rows)),
         name="forward",
-    )(data, tiles)
+    )(offsets, data, tiles)
 
 
 CODES = (0, 1, 2, 3, 5)
@@ -153,7 +151,7 @@
         for value, source in zip(CODES, sources):
             copy = pltpu.make_async_copy(source, out.at[slot], sems.at[slot])
             pl.when((last == 1) & (code == value))(copy.start)
-        known = (last == 1) & (code <= CODES[count - 1])
+        known = (last == 1) & (code < CODES[4])
         copies.append((known, pltpu.make_async_copy(sources[0], out.at[slot], sems.at[slot])))
     for known, copy in copies:
         pl.when(known)(copy.wait)
@@ -177,16 +175,14 @@
 def start_pick(offset, sources, target, sem):
     p, flip = place()
     last, code = route(p, offset, flip)
-    for value, source in zip(CODES, sources[:4]):
+    for value, source in zip(CODES[:4], sources[:4]):
         pl.when((last == 0) & (code == value))(pltpu.make_async_copy(source, target, sem).start)
-    over_last = last == 1
-    if len(sources) > 5:
-        over_last = over_last & (code != CODES[4])
-        pl.when(code == CODES[4])(pltpu.make_async_copy(sources[5], target, sem).start)
-    pl.when(over_last)(pltpu.make_async_copy(sources[4], target, sem).start)
-
-
-def backward_kernel(slots, offs_ref, tile_ref, own, first, group, both, *refs):
+    two, lasts = sources[4:]
+    pl.when(code == CODES[4])(pltpu.make_async_copy(two, target, sem).start)
+    pl.when((last == 1) & (code != CODES[4]))(pltpu.make_async_copy(lasts, target, sem).start)
+
+
+def backward_kernel(slots, offs_ref, tile_ref, own, first, group, both, two, *refs):
     lasts_ref, out_ref, picked, sems = refs
     slot = pl.program_id(0)
 
@@ -194,7 +190,7 @@
     def _():
         out_ref[...] = jnp.zeros_like(out_ref)
         for each in range(slots):
-            sources = (own, first, group, both, lasts_ref.at[each])
+            sources = (own, first, group, both, two, lasts_ref.at[each])
             start_pick(offs_ref[0, each + 1], sources, picked.at[each], sems.at[each])
 
     pltpu.make_async_copy(own, picked.at[slot], sems.at[slot]).wait()
@@ -221,11 +217,11 @@
     )(offsets, tiles, *sources)
 
 
-def bins_kernel(slots, offs_ref, next_ref, own_in, mine_ref, theirs_ref, own_out, first, group, both, two):
+def bins_kernel(slots, offs_ref, next_ref, own_in, mine_ref, theirs_ref, own_out, first, group, both):
     p, flip = place()
     target = last_partner(p, flip)
-    totals = [own_in[...], None, None, None, None]
-    for which, value in enumerate((0, 1, 2, 3, 5)):
+    totals = [own_in[...], None, None, None]
+    for which, value in enumerate(CODES[:4]):
         total = totals[which]
         for slot in range(slots):
             for there, offs, source in ((0, offs_ref, mine_ref), (1, next_ref, theirs_ref)):
@@ -235,7 +231,7 @@
                 term = jnp.where(use, source[slot], 0.0)
                 total = term if total is None else total + term
         totals[which] = total
-    for ref, total in zip((own_out, first, group, both, two), totals):
+    for ref, total in zip((own_out, first, group, both), totals):
         ref[...] = total
 
 
@@ -248,8 +244,8 @@
         functools.partial(bins_kernel, slots),
         grid=(rows // step,),
         in_specs=[smem_spec(), smem_spec(), flat, deep, deep],
-        out_specs=[flat] * 5,
-        out_shape=[jax.ShapeDtypeStruct((rows, block), f32)] * 5,
+        out_specs=[flat] * 4,
+        out_shape=[jax.ShapeDtypeStruct((rows, block), f32)] * 4,
         compiler_params=params(),
         cost_estimate=cost(20 * rows * block, 40 * rows * block),
         name="bins",
@@ -260,11 +256,11 @@
     return lax.axis_index("samp") if pair else 0
 
 
-def right_kernel(slots, pair, offs_ref, data_ref, image_ref, own, first, group, both, *refs):
+def right_kernel(slots, pair, offs_ref, data_ref, image_ref, own, first, group, both, two, *refs):
     lasts_ref = refs[0]
     keep0_ref, send0_ref, keep_ref, send_ref, high_ref, low_ref, picked, sems = refs[-8:]
     for slot in range(slots):
-        sources = (own, first, group, both, lasts_ref.at[slot])
+        sources = (own, first, group, both, two, lasts_ref.at[slot])
         start_pick(offs_ref[0, slot + 1], sources, picked.at[slot], sems.at[slot])
     half = image_ref.shape[1] // 2
     samp = halves(pair)
@@ -319,7 +315,7 @@
     @pl.when(slot == 0)
     def _():
         for each in range(slots):
-            sources = (own, first, group, both, lasts_ref.at[each], two)
+            sources = (own, first, group, both, two, lasts_ref.at[each])
             start_pick(offs_ref[0, each + 1], sources, picked.at[each], sems.at[each])
 
     pltpu.make_async_copy(own, picked.at[slot], sems.at[slot]).wait()
@@ -410,17 +406,19 @@
     offsets_next = send(offsets, "last")
     data_first = send(data, "first")
     data_group = send(data, "group")
-    own, far = forward(data, local_tiles)
+    own, far, far_two = forward(offsets, data, local_tiles)
     theirs = send(after(far, offsets_next), "last")
+    got_two = send(after(far_two, data_first), "direct", reverse=True)
     data_both = send(after(data_first, data_group), "group")
-    own, bin_first, bin_group, bin_both, bin_two = make_bins(offsets, offsets_next, own, far, theirs)
-    got_two = send(bin_two, "column", reverse=True)
-    got_both = send(bin_both + got_two, "group", reverse=True)
-    got_group = send(after(bin_group, got_both), "group", reverse=True)
-    data_two = send(data_both, "column")
-    chosen = choose(offsets_next, data, data_first, data_group, data_both, data_two)
-    data_sources = (data, data_first, data_group, data_both, send(chosen, "last"))
-    got_first = send(bin_first + got_both, "first")
+    own, bin_first, bin_group, bin_both = make_bins(offsets, offsets_next, own, far, theirs)
+    got_both = send(bin_both + got_two, "first")
+    chosen = choose(offsets_next, data, data_first, data_group, data_both)
+    data_last = send(chosen, "last")
+    data_two = send(after(data_both, chosen), "direct")
+    data_sources = (data, data_first, data_group, data_both, data_two, data_last)
+
+    got_group = send(bin_group + got_both, "group", reverse=True)
+    got_first = send(after(bin_first, got_both), "first")
     image = own + backward(offsets, local_tiles, data_sources) + got_first + got_group
 
     image_group = send(image, "group")

time: 143 us -> 128 us (0.90)
  starting transfers between devices: 55.6 us -> 25.6 us
  waiting for transfers between devices: 62.5 us -> 76 us
    ppermute x16, starting transfers between devices: 38.6 us -> 17.8 us  [send(): return lax.ppermute(value, ('var', 'samp'), pairs)]
    ppermute x16, waiting for transfers between devices: 60.2 us -> 73.8 us  [send(): return lax.ppermute(value, ('var', 'samp'), pairs)]
    ppermute x2, starting transfers between devices: 17 us -> 7.76 us  [swap(): return lax.ppermute(value, 'samp', [(0, 1), (1, 0)])]
    unnamed x18 -> x20, local copies, waits for them, and re-layouts: 4.89 us -> 5.48 us
  transfers between devices with their start and end apart: 18 -> 18, of which waited for: 9 -> 9; matrix products, arithmetic and copies ran while one was open for 0% -> 0% of each run, Pallas kernels for 9% -> 11%
where the time goes in v4:
time: 128 us; the launch traced here: 127 us
  waiting for transfers between devices  76 us (59%)
  starting transfers between devices  25.6 us (20%)
  Pallas kernels  19 us (15%)
  local copies, waits for them, and re-layouts  5.48 us (4%)
    ppermute x16, waiting for transfers between devices, send(): return lax.ppermute(value, ('var', 'samp'), pairs)  73.8 us
    ppermute x16, starting transfers between devices, send(): return lax.ppermute(value, ('var', 'samp'), pairs)  17.8 us
    ppermute x2, starting transfers between devices, swap(): return lax.ppermute(value, 'samp', [(0, 1), (1, 0)])  7.76 us
    unnamed x20, local copies, waits for them, and re-layouts  5.48 us
    pallas_call x1, Pallas kernels, right(): pl.pallas_call(functools.partial(right_kernel, slots, pair), in_specs=[sm...  4.2 us
    pallas_call x2, Pallas kernels, finish(): pl.pallas_call(functools.partial(finish_kernel, begin, factor), grid=(cou...  3.37 us
    pallas_call x1, Pallas kernels, backward(): pl.pallas_call(functools.partial(backward_kernel, slots), grid=(slots,),...  3.08 us
    pallas_call x1, Pallas kernels, left(): pl.pallas_call(functools.partial(left_kernel, slots, pair), grid=(slots,)...  2.97 us
  transfers between devices with their start and end apart: 18, of which 9 were waited for; matrix products, arithmetic and copies ran while one was open for 0% of the time, Pallas kernels for 11%

profile of v4, /device:TPU:7, one launch (start us, length us, event | category | flops | bytes accessed | tf_op | source)
XLA Modules:
  0.0 127.3 jit_solution(5255938277068376891)
XLA Ops:
  0.3 1.9 %copy-done = f32[1,3,512,512]{3,2,1,0:T(8,128)S(1)} copy-done((f32[1,3,512,512]{3,2,1,0:T(8,128)S(1)}, f32[1,3,512,512]{3,2,1,0:T(8,128)}, u32[]{:S(2)}) %copy-start) | copy-done | bytes 3145752
  3.8 2.5 %forward.1 = (f32[256,512]{1,0:T(8,128)S(1)}, f32[2,256,512]{2,1,0:T(8,128)S(1)}, f32[256,512]{1,0:T(8,128)S(1)}) custom-call(s32[1,3]{1,0:T(1,128)S(1)} %copy-done.7, f32[256,512]{1,0:T(8,128)S(1)} %copy-done.2, f32[3,512,512]{2,1,0:T(8,128)S(1)} %bitcast.3), custom_call_target="tpu_custom_call" | custom-call | tf_op jit(solution)/shard_map/forward/pallas_call | solution.py:125
  6.4 1.5 %collective-permute-start.1 = (f32[2,256,512]{2,1,0:T(8,128)S(1)}, f32[2,256,512]{2,1,0:T(8,128)S(1)}, u32[]{:S(2)}, u32[]{:S(2)}) collective-permute-start(f32[2,256,512]{2,1,0:T(8,128)S(1)} %get-tuple-element.29.mine_ref), channel_id=1, source_target_pairs={{0,4},{1,3},{2,6},{3,1},{4,0},{5,7},{6,2},{7,5},{8,12},{9,11},{10,... | collective-permute-start | bytes 3145736 | tf_op jit(solution)/shard_map/ppermute | solution.py:98
  7.9 3.3 %collective-permute-start.3 = (f32[256,512]{1,0:T(8,128)S(1)}, f32[256,512]{1,0:T(8,128)S(1)}, u32[]{:S(2)}, u32[]{:S(2)}) collective-permute-start(f32[256,512]{1,0:T(8,128)S(1)} %copy-done.2), channel_id=1, source_target_pairs={{0,24},{1,25},{2,26},{3,27},{4,28},{5,29},{6,30},{7,31},{8,0},{9,1... | collective-permute-start | bytes 1572872 | tf_op jit(solution)/shard_map/ppermute | solution.py:98
  11.2 1.7 %collective-permute-start.7 = (f32[256,512]{1,0:T(8,128)S(1)}, f32[256,512]{1,0:T(8,128)S(1)}, u32[]{:S(2)}, u32[]{:S(2)}) collective-permute-start(f32[256,512]{1,0:T(8,128)S(1)} %get-tuple-element.36), channel_id=1, source_target_pairs={{30,2},{31,5},{6,10},{7,13},{14,18},{15,21},{22,26},{23,29}} | collective-permute-start | bytes 1572872 | tf_op jit(solution)/shard_map/ppermute | solution.py:98
  13.0 8.0 %collective-permute-done.3.refs_2_.group = f32[256,512]{1,0:T(8,128)S(1)} collective-permute-done((f32[256,512]{1,0:T(8,128)S(1)}, f32[256,512]{1,0:T(8,128)S(1)}, u32[]{:S(2)}, u32[]{:S(2)}) %collective-permute-start.3) | collective-permute-done | bytes 524320 | tf_op jit(solution)/shard_map/ppermute | solution.py:98
  20.9 4.0 %collective-permute-start.4 = (f32[256,512]{1,0:T(8,128)S(1)}, f32[256,512]{1,0:T(8,128)S(1)}, u32[]{:S(2)}, u32[]{:S(2)}) collective-permute-start(f32[256,512]{1,0:T(8,128)S(1)} %collective-permute-done.2.refs_1_.first), channel_id=1, source_target_pairs={{0,24},{1,25},{2,26},{3,27},{4,28},{5,29},{6,30},{7,31},{8,0},{9,1... | collective-permute-start | bytes 1572872 | tf_op jit(solution)/shard_map/ppermute | solution.py:98
  25.0 1.4 %bins.1 = (f32[256,512]{1,0:T(8,128)S(1)}, f32[256,512]{1,0:T(8,128)S(1)}, f32[256,512]{1,0:T(8,128)S(1)}, f32[256,512]{1,0:T(8,128)S(1)}) custom-call(s32[1,3]{1,0:T(1,128)S(1)} %copy-done.7, s32[1,3]{1,0:T(1,128)S(1)} %collective-permute-done.next_ref.offs_ref, f32[256,512]{1,0:T(8,128)S(1)} %get-tuple-element.27.own_in, ...), custom_call_target="tpu_custom_call" | custom-call | tf_op jit(solution)/shard_map/bins/pallas_call | solution.py:243
  26.4 5.8 %collective-permute-done.7 = f32[256,512]{1,0:T(8,128)S(1)} collective-permute-done((f32[256,512]{1,0:T(8,128)S(1)}, f32[256,512]{1,0:T(8,128)S(1)}, u32[]{:S(2)}, u32[]{:S(2)}) %collective-permute-start.7) | collective-permute-done | bytes 524320 | tf_op jit(solution)/shard_map/ppermute | solution.py:98
  32.3 11.5 %collective-permute-done.4.refs_3_.both = f32[256,512]{1,0:T(8,128)S(1)} collective-permute-done((f32[256,512]{1,0:T(8,128)S(1)}, f32[256,512]{1,0:T(8,128)S(1)}, u32[]{:S(2)}, u32[]{:S(2)}) %collective-permute-start.4) | collective-permute-done | bytes 524320 | tf_op jit(solution)/shard_map/ppermute | solution.py:98
  46.7 9.8 %collective-permute-done.5.two = f32[256,512]{1,0:T(8,128)S(1)} collective-permute-done((f32[256,512]{1,0:T(8,128)S(1)}, f32[256,512]{1,0:T(8,128)S(1)}, u32[]{:S(2)}, u32[]{:S(2)}) %collective-permute-start.5) | collective-permute-done | bytes 524320 | tf_op jit(solution)/shard_map/ppermute | solution.py:98
  56.5 13.3 %collective-permute-done.6.refs_0_ = f32[2,256,512]{2,1,0:T(8,128)S(1)} collective-permute-done((f32[2,256,512]{2,1,0:T(8,128)S(1)}, f32[2,256,512]{2,1,0:T(8,128)S(1)}, u32[]{:S(2)}, u32[]{:S(2)}) %collective-permute-start.6) | collective-permute-done | bytes 1048608 | tf_op jit(solution)/shard_map/ppermute | solution.py:98
  69.8 3.1 %backward.1 = f32[256,512]{1,0:T(8,128)S(1)} custom-call(s32[1,3]{1,0:T(1,128)S(1)} %copy-done.7, f32[3,512,512]{2,1,0:T(8,128)} %bitcast.2, f32[256,512]{1,0:T(8,128)S(1)} %copy-done.3, f32[256,512]{1,0:T(8,128)S(1)} %collective-permute-done.2.refs_1_.first, f32[256,512]{1,0:T(8,128)S(1)} %collective-permute-done.3.refs_2_.group, ...), custom_call_target="tpu_custom_call" | custom-call | tf_op jit(solution)/shard_map/backward/pallas_call | solution.py:205
  73.1 3.6 %collective-permute-start.12 = (f32[256,512]{1,0:T(8,128)S(1)}, f32[256,512]{1,0:T(8,128)S(1)}, u32[]{:S(2)}, u32[]{:S(2)}) collective-permute-start(f32[256,512]{1,0:T(8,128)S(1)} %add_add_fusion.refs_0_.image_ref.own), channel_id=1, source_target_pairs={{0,24},{1,25},{2,26},{3,27},{4,28},{5,29},{6,30},{7,31},{8,0},{9,1... | collective-permute-start | bytes 1572872 | tf_op jit(solution)/shard_map/ppermute | solution.py:98
  76.7 9.4 %collective-permute-done.12.refs_2_.group = f32[256,512]{1,0:T(8,128)S(1)} collective-permute-done((f32[256,512]{1,0:T(8,128)S(1)}, f32[256,512]{1,0:T(8,128)S(1)}, u32[]{:S(2)}, u32[]{:S(2)}) %collective-permute-start.12) | collective-permute-done | bytes 524320 | tf_op jit(solution)/shard_map/ppermute | solution.py:98
  86.2 8.3 %collective-permute-done.13.refs_3_.both = f32[256,512]{1,0:T(8,128)S(1)} collective-permute-done((f32[256,512]{1,0:T(8,128)S(1)}, f32[256,512]{1,0:T(8,128)S(1)}, u32[]{:S(2)}, u32[]{:S(2)}) %collective-permute-start.13) | collective-permute-done | bytes 524320 | tf_op jit(solution)/shard_map/ppermute | solution.py:98
  96.1 4.2 %right.1 = (f32[1,256,512]{2,1,0:T(8,128)S(1)}, f32[1,256,512]{2,1,0:T(8,128)S(1)}, f32[2,256,512]{2,1,0:T(8,128)S(1)}, f32[2,256,512]{2,1,0:T(8,128)}, bf16[512...) custom-call(s32[1,3]{1,0:T(1,128)S(1)} %copy-done.8, f32[256,512]{1,0:T(8,128)S(1)} %copy-done.3, ...), custom_call_target="tpu_custom_call" | custom-call | flops 26843545600 | tf_op jit(solution)/shard_map/right/pallas_call | solution.py:299
  100.4 3.4 %collective-permute-start.14 = (f32[1,256,512]{2,1,0:T(8,128)S(1)}, f32[1,256,512]{2,1,0:T(8,128)S(1)}, u32[]{:S(2)}, u32[]{:S(2)}) collective-permute-start(f32[1,256,512]{2,1,0:T(8,128)S(1)} %get-tuple-element.41), channel_id=1, source_target_pairs={{0,1},{1,0},{2,3},{3,2},{4,5},{5,4},{6,7},{7,6},{8,9},{9,8},{10,11... | collective-permute-start | bytes 1572872 | tf_op jit(solution)/shard_map/ppermute | solution.py:396
  105.7 1.6 %finish.2.refs_0_ = f32[3,256,512]{2,1,0:T(8,128)} custom-call(s32[1,3]{1,0:T(1,128)S(1)} %copy-done.8, f32[1]{0:T(128)S(6)} %copy.7.step_ref, f32[3,512,512]{2,1,0:T(8,128)S(1)} %bitcast.4, f32[1,256,512]{2,1,0:T(8,128)S(1)} %get-tuple-element.40.keep_ref, f32[1,256,512]{2,1,0:T(8,128)S(1)} %collective-permute-done.14.other_ref), custom_call_target="tpu_custom_call" | custom-call | tf_op jit(solution)/shard_map/finish/pallas_call | solution.py:378
  107.3 7.6 %collective-permute-done.15.two = f32[256,512]{1,0:T(8,128)S(1)} collective-permute-done((f32[256,512]{1,0:T(8,128)S(1)}, f32[256,512]{1,0:T(8,128)S(1)}, u32[]{:S(2)}, u32[]{:S(2)}) %collective-permute-start.15) | collective-permute-done | bytes 524320 | tf_op jit(solution)/shard_map/ppermute | solution.py:98
  115.8 3.0 %left.1 = (f32[2,256,512]{2,1,0:T(8,128)S(1)}, f32[2,256,512]{2,1,0:T(8,128)S(1)}) custom-call(s32[1,3]{1,0:T(1,128)S(1)} %copy-done.8, f32[2,256,512]{2,1,0:T(8,128)} %copy-done.4, f32[2,256,512]{2,1,0:T(8,128)} %get-tuple-element.43.send_in, bf16[512,256]{1,0:T(8,128)(2,1)S(1)} %get-tuple-element.44.high_ref, ...), custom_call_target="tpu_custom_call" | custom-call | tf_op jit(solution)/shard_map/left/pallas_call | solution.py:337
  118.8 4.4 %collective-permute-start.17 = (f32[2,256,512]{2,1,0:T(8,128)S(1)}, f32[2,256,512]{2,1,0:T(8,128)S(1)}, u32[]{:S(2)}, u32[]{:S(2)}) collective-permute-start(f32[2,256,512]{2,1,0:T(8,128)S(1)} %get-tuple-element.48), channel_id=1, source_target_pairs={{0,1},{1,0},{2,3},{3,2},{4,5},{5,4},{6,7},{7,6},{8,9},{9,8},{10,11... | collective-permute-start | bytes 3145736 | tf_op jit(solution)/shard_map/ppermute | solution.py:396
  123.2 2.3 %collective-permute-done.17.other_ref = f32[2,256,512]{2,1,0:T(8,128)S(1)} collective-permute-done((f32[2,256,512]{2,1,0:T(8,128)S(1)}, f32[2,256,512]{2,1,0:T(8,128)S(1)}, u32[]{:S(2)}, u32[]{:S(2)}) %collective-permute-start.17) | collective-permute-done | bytes 1048608 | tf_op jit(solution)/shard_map/ppermute | solution.py:396
  125.5 1.8 %finish.3 = f32[3,256,512]{2,1,0:T(8,128)} custom-call(s32[1,3]{1,0:T(1,128)S(1)} %copy-done.8, f32[1]{0:T(128)S(6)} %copy.7.step_ref, f32[3,512,512]{2,1,0:T(8,128)S(1)} %bitcast.5, f32[2,256,512]{2,1,0:T(8,128)S(1)} %get-tuple-element.47.keep_ref, f32[2,256,512]{2,1,0:T(8,128)S(1)} %collective-permute-done.17.other_ref, ...), custom_call_target="tpu_custom_call", output_to_operand_aliasing={{}: (5, {})} | custom-call | tf_op jit(solution)/shard_map/finish/pallas_call | solution.py:378
  (44 shorter events, 9.1 us)
Async XLA Ops:
  0.0 6.4 %collective-permute-start = (s32[1,3]{1,0:T(1,128)}, s32[1,3]{1,0:T(1,128)S(1)}, u32[]{:S(2)}, u32[]{:S(2)}) collective-permute-start(s32[1,3]{1,0:T(1,128)} %offs_ref.13), channel_id=1, source_target_pairs={{0,4},{1,3},{2,6},{3,1},{4,0},{5,7},{6,2},{7,5},{8,12},{9,11},{10,... | collective-permute-start | bytes 44 | tf_op jit(solution)/shard_map/ppermute | solution.py:98
  0.3 11.0 %collective-permute-start.2 = (f32[256,512]{1,0:T(8,128)}, f32[256,512]{1,0:T(8,128)S(1)}, u32[]{:S(2)}, u32[]{:S(2)}) collective-permute-start(f32[256,512]{1,0:T(8,128)} %own.3), channel_id=1, source_target_pairs={{0,2},{1,5},{2,0},{3,7},{4,6},{5,1},{6,4},{7,3},{8,10},{9,13},{10,... | collective-permute-start | bytes 1572872 | tf_op jit(solution)/shard_map/ppermute | solution.py:98
  0.3 1.9 %copy-start = (f32[1,3,512,512]{3,2,1,0:T(8,128)S(1)}, f32[1,3,512,512]{3,2,1,0:T(8,128)}, u32[]{:S(2)}) copy-start(f32[1,3,512,512]{3,2,1,0:T(8,128)} %param.5) | copy-start | bytes 9437188
  6.4 18.5 %collective-permute-start.1 = (f32[2,256,512]{2,1,0:T(8,128)S(1)}, f32[2,256,512]{2,1,0:T(8,128)S(1)}, u32[]{:S(2)}, u32[]{:S(2)}) collective-permute-start(f32[2,256,512]{2,1,0:T(8,128)S(1)} %get-tuple-element.29.mine_ref), channel_id=1, source_target_pairs={{0,4},{1,3},{2,6},{3,1},{4,0},{5,7},{6,2},{7,5},{8,12},{9,11},{10,... | collective-permute-start | bytes 3145736 | tf_op jit(solution)/shard_map/ppermute | solution.py:98
  7.9 13.0 %collective-permute-start.3 = (f32[256,512]{1,0:T(8,128)S(1)}, f32[256,512]{1,0:T(8,128)S(1)}, u32[]{:S(2)}, u32[]{:S(2)}) collective-permute-start(f32[256,512]{1,0:T(8,128)S(1)} %copy-done.2), channel_id=1, source_target_pairs={{0,24},{1,25},{2,26},{3,27},{4,28},{5,29},{6,30},{7,31},{8,0},{9,1... | collective-permute-start | bytes 1572872 | tf_op jit(solution)/shard_map/ppermute | solution.py:98
  11.2 20.9 %collective-permute-start.7 = (f32[256,512]{1,0:T(8,128)S(1)}, f32[256,512]{1,0:T(8,128)S(1)}, u32[]{:S(2)}, u32[]{:S(2)}) collective-permute-start(f32[256,512]{1,0:T(8,128)S(1)} %get-tuple-element.36), channel_id=1, source_target_pairs={{30,2},{31,5},{6,10},{7,13},{14,18},{15,21},{22,26},{23,29}} | collective-permute-start | bytes 1572872 | tf_op jit(solution)/shard_map/ppermute | solution.py:98
  20.9 22.9 %collective-permute-start.4 = (f32[256,512]{1,0:T(8,128)S(1)}, f32[256,512]{1,0:T(8,128)S(1)}, u32[]{:S(2)}, u32[]{:S(2)}) collective-permute-start(f32[256,512]{1,0:T(8,128)S(1)} %collective-permute-done.2.refs_1_.first), channel_id=1, source_target_pairs={{0,24},{1,25},{2,26},{3,27},{4,28},{5,29},{6,30},{7,31},{8,0},{9,1... | collective-permute-start | bytes 1572872 | tf_op jit(solution)/shard_map/ppermute | solution.py:98
  25.0 18.9 %copy-start.3 = (f32[256,512]{1,0:T(8,128)S(1)}, f32[256,512]{1,0:T(8,128)}, u32[]{:S(2)}) copy-start(f32[256,512]{1,0:T(8,128)} %own.3) | copy-start | bytes 1572868
  32.3 13.7 %collective-permute-start.8 = (f32[256,512]{1,0:T(8,128)S(1)}, f32[256,512]{1,0:T(8,128)S(1)}, u32[]{:S(2)}, u32[]{:S(2)}) collective-permute-start(f32[256,512]{1,0:T(8,128)S(1)} %add.16), channel_id=1, source_target_pairs={{0,2},{1,5},{2,0},{3,7},{4,6},{5,1},{6,4},{7,3},{8,10},{9,13},{10,... | collective-permute-start | bytes 1572872 | tf_op jit(solution)/shard_map/ppermute | solution.py:98
  44.5 25.2 %collective-permute-start.6 = (f32[2,256,512]{2,1,0:T(8,128)S(1)}, f32[2,256,512]{2,1,0:T(8,128)S(1)}, u32[]{:S(2)}, u32[]{:S(2)}) collective-permute-start(f32[2,256,512]{2,1,0:T(8,128)S(1)} %choose.2), channel_id=1, source_target_pairs={{0,4},{1,3},{2,6},{3,1},{4,0},{5,7},{6,2},{7,5},{8,12},{9,11},{10,... | collective-permute-start | bytes 3145736 | tf_op jit(solution)/shard_map/ppermute | solution.py:98
  44.6 11.8 %collective-permute-start.5 = (f32[256,512]{1,0:T(8,128)S(1)}, f32[256,512]{1,0:T(8,128)S(1)}, u32[]{:S(2)}, u32[]{:S(2)}) collective-permute-start(f32[256,512]{1,0:T(8,128)S(1)} %collective-permute-done.4.refs_3_.both), channel_id=1, source_target_pairs={{2,30},{5,31},{10,6},{13,7},{18,14},{21,15},{26,22},{29,23}} | collective-permute-start | bytes 1572872 | tf_op jit(solution)/shard_map/ppermute | solution.py:98
  45.9 27.0 %collective-permute-start.9 = (f32[256,512]{1,0:T(8,128)S(1)}, f32[256,512]{1,0:T(8,128)S(1)}, u32[]{:S(2)}, u32[]{:S(2)}) collective-permute-start(f32[256,512]{1,0:T(8,128)S(1)} %get-tuple-element.37), channel_id=1, source_target_pairs={{0,2},{1,5},{2,0},{3,7},{4,6},{5,1},{6,4},{7,3},{8,10},{9,13},{10,... | collective-permute-start | bytes 1572872 | tf_op jit(solution)/shard_map/ppermute | solution.py:98
  46.1 26.8 %collective-permute-start.10 = (f32[256,512]{1,0:T(8,128)S(1)}, f32[256,512]{1,0:T(8,128)S(1)}, u32[]{:S(2)}, u32[]{:S(2)}) collective-permute-start(f32[256,512]{1,0:T(8,128)S(1)} %add.18), channel_id=1, source_target_pairs={{24,0},{25,1},{26,2},{27,3},{28,4},{29,5},{30,6},{31,7},{0,8},{1,9... | collective-permute-start | bytes 1572872 | tf_op jit(solution)/shard_map/ppermute | solution.py:98
  69.8 3.1 %copy-start.6 = (f32[2,256,512]{2,1,0:T(8,128)}, f32[2,256,512]{2,1,0:T(8,128)S(1)}, u32[]{:S(2)}) copy-start(f32[2,256,512]{2,1,0:T(8,128)S(1)} %collective-permute-done.6.refs_0_) | copy-start | bytes 3145732
  73.1 23.0 %copy-start.8 = (s32[1,3]{1,0:T(1,128)S(1)}, s32[1,3]{1,0:T(1,128)}, u32[]{:S(2)}) copy-start(s32[1,3]{1,0:T(1,128)} %offs_ref.13) | copy-start | bytes 40
  73.1 13.0 %collective-permute-start.12 = (f32[256,512]{1,0:T(8,128)S(1)}, f32[256,512]{1,0:T(8,128)S(1)}, u32[]{:S(2)}, u32[]{:S(2)}) collective-permute-start(f32[256,512]{1,0:T(8,128)S(1)} %add_add_fusion.refs_0_.image_ref.own), channel_id=1, source_target_pairs={{0,24},{1,25},{2,26},{3,27},{4,28},{5,29},{6,30},{7,31},{8,0},{9,1... | collective-permute-start | bytes 1572872 | tf_op jit(solution)/shard_map/ppermute | solution.py:98
  76.7 9.4 %collective-permute-start.11 = (f32[256,512]{1,0:T(8,128)S(1)}, f32[256,512]{1,0:T(8,128)S(1)}, u32[]{:S(2)}, u32[]{:S(2)}) collective-permute-start(f32[256,512]{1,0:T(8,128)S(1)} %add_add_fusion.refs_0_.image_ref.own), channel_id=1, source_target_pairs={{0,2},{1,5},{2,0},{3,7},{4,6},{5,1},{6,4},{7,3},{8,10},{9,13},{10,... | collective-permute-start | bytes 1572872 | tf_op jit(solution)/shard_map/ppermute | solution.py:98
  86.1 8.3 %collective-permute-start.13 = (f32[256,512]{1,0:T(8,128)S(1)}, f32[256,512]{1,0:T(8,128)S(1)}, u32[]{:S(2)}, u32[]{:S(2)}) collective-permute-start(f32[256,512]{1,0:T(8,128)S(1)} %collective-permute-done.12.refs_2_.group), channel_id=1, source_target_pairs={{0,2},{1,5},{2,0},{3,7},{4,6},{5,1},{6,4},{7,3},{8,10},{9,13},{10,... | collective-permute-start | bytes 1572872 | tf_op jit(solution)/shard_map/ppermute | solution.py:98
  95.2 19.7 %collective-permute-start.16 = (f32[2,256,512]{2,1,0:T(8,128)S(1)}, f32[2,256,512]{2,1,0:T(8,128)S(1)}, u32[]{:S(2)}, u32[]{:S(2)}) collective-permute-start(f32[2,256,512]{2,1,0:T(8,128)S(1)} %choose.3.refs_1_), channel_id=1, source_target_pairs={{0,4},{1,3},{2,6},{3,1},{4,0},{5,7},{6,2},{7,5},{8,12},{9,11},{10,... | collective-permute-start | bytes 3145736 | tf_op jit(solution)/shard_map/ppermute | solution.py:98
  96.1 9.5 %copy-start.1 = (f32[1,3,512,512]{3,2,1,0:T(8,128)S(1)}, f32[1,3,512,512]{3,2,1,0:T(8,128)}, u32[]{:S(2)}) copy-start(f32[1,3,512,512]{3,2,1,0:T(8,128)} %param.5) | copy-start | bytes 9437188
  100.4 6.9 %copy-start.4 = (f32[2,256,512]{2,1,0:T(8,128)}, f32[2,256,512]{2,1,0:T(8,128)S(1)}, u32[]{:S(2)}) copy-start(f32[2,256,512]{2,1,0:T(8,128)S(1)} %get-tuple-element.42.keep_in) | copy-start | bytes 3145732
  100.4 5.3 %collective-permute-start.14 = (f32[1,256,512]{2,1,0:T(8,128)S(1)}, f32[1,256,512]{2,1,0:T(8,128)S(1)}, u32[]{:S(2)}, u32[]{:S(2)}) collective-permute-start(f32[1,256,512]{2,1,0:T(8,128)S(1)} %get-tuple-element.41), channel_id=1, source_target_pairs={{0,1},{1,0},{2,3},{3,2},{4,5},{5,4},{6,7},{7,6},{8,9},{9,8},{10,11... | collective-permute-start | bytes 1572872 | tf_op jit(solution)/shard_map/ppermute | solution.py:396
  103.7 11.1 %collective-permute-start.15 = (f32[256,512]{1,0:T(8,128)S(1)}, f32[256,512]{1,0:T(8,128)S(1)}, u32[]{:S(2)}, u32[]{:S(2)}) collective-permute-start(f32[256,512]{1,0:T(8,128)S(1)} %collective-permute-done.13.refs_3_.both), channel_id=1, source_target_pairs={{2,30},{5,31},{10,6},{13,7},{18,14},{21,15},{26,22},{29,23}} | collective-permute-start | bytes 1572872 | tf_op jit(solution)/shard_map/ppermute | solution.py:98
  118.8 6.7 %collective-permute-start.17 = (f32[2,256,512]{2,1,0:T(8,128)S(1)}, f32[2,256,512]{2,1,0:T(8,128)S(1)}, u32[]{:S(2)}, u32[]{:S(2)}) collective-permute-start(f32[2,256,512]{2,1,0:T(8,128)S(1)} %get-tuple-element.48), channel_id=1, source_target_pairs={{0,1},{1,0},{2,3},{3,2},{4,5},{5,4},{6,7},{7,6},{8,9},{9,8},{10,11... | collective-permute-start | bytes 3145736 | tf_op jit(solution)/shard_map/ppermute | solution.py:396
  (4 other events, 3.7 us)

commit v5 on v3

--- a/solution.py
+++ b/solution.py
@@ -84,14 +84,15 @@
                 target = var ^ last
             elif kind == "group":
                 target = back
+            elif kind == "two":
+                target = back ^ first
+                use = (var & 3) == 0
             elif kind == "column":
                 target = back
                 use = (var & 3) in wanted(first, last, 2)
             else:
                 target = back ^ last
                 use = (var & 3) in wanted(first, last, 2)
-            if kind == "column" and not use:
-                target, use = var, True
             pair = (var * samp_count + samp, target * samp_count + samp)
             if use:
                 pairs.append(pair[::-1] if reverse else pair)
@@ -177,7 +178,7 @@
 def start_pick(offset, sources, target, sem):
     p, flip = place()
     last, code = route(p, offset, flip)
-    for value, source in zip(CODES, sources[:4]):
+    for value, source in zip(CODES[:4], sources[:4]):
         pl.when((last == 0) & (code == value))(pltpu.make_async_copy(source, target, sem).start)
     over_last = last == 1
     if len(sources) > 5:
@@ -409,18 +410,21 @@
 
     offsets_next = send(offsets, "last")
     data_first = send(data, "first")
-    data_group = send(data, "group")
     own, far = forward(data, local_tiles)
     theirs = send(after(far, offsets_next), "last")
-    data_both = send(after(data_first, data_group), "group")
-    own, bin_first, bin_group, bin_both, bin_two = make_bins(offsets, offsets_next, own, far, theirs)
-    got_two = send(bin_two, "column", reverse=True)
-    got_both = send(bin_both + got_two, "group", reverse=True)
-    got_group = send(after(bin_group, got_both), "group", reverse=True)
+    data_both = send(data_first, "group")
     data_two = send(data_both, "column")
+    data_group = send(after(data, data_both), "group")
+    own, bin_first, bin_group, bin_both, bin_two = make_bins(offsets, offsets_next, own, far, after(theirs, data_both))
+    got_both = send(bin_both, "first")
+    got_two = send(bin_two, "two", reverse=True)
     chosen = choose(offsets_next, data, data_first, data_group, data_both, data_two)
-    data_sources = (data, data_first, data_group, data_both, send(chosen, "last"))
-    got_first = send(bin_first + got_both, "first")
+    data_last = send(chosen, "last")
+    data_sources = (data, data_first, data_group, data_both, data_last)
+
+    bin_group = bin_group + got_both + got_two
+    got_group = send(bin_group, "group", reverse=True)
+    got_first = send(after(bin_first, bin_group), "first")
     image = own + backward(offsets, local_tiles, data_sources) + got_first + got_group
 
     image_group = send(image, "group")

time: 143 us -> 121 us (0.85)
  starting transfers between devices: 55.6 us -> 34.4 us
  waiting for transfers between devices: 62.5 us -> 59.3 us
  Pallas kernels: 18.3 us -> 20.9 us
    ppermute x2, starting transfers between devices: 17 us -> 5.81 us  [swap(): return lax.ppermute(value, 'samp', [(0, 1), (1, 0)])]
    ppermute x16, starting transfers between devices: 38.6 us -> 28.6 us  [send(): return lax.ppermute(value, ('var', 'samp'), pairs)]
    ppermute x16, waiting for transfers between devices: 60.2 us -> 57 us  [send(): return lax.ppermute(value, ('var', 'samp'), pairs)]
    unnamed x18 -> x14, local copies, waits for them, and re-layouts: 4.89 us -> 3.85 us
  transfers between devices with their start and end apart: 18 -> 18, of which waited for: 9 -> 8; matrix products, arithmetic and copies ran while one was open for 0% -> 0% of each run, Pallas kernels for 9% -> 13%
where the time goes in v5:
time: 121 us; the launch traced here: 120 us
  waiting for transfers between devices  59.3 us (49%)
  starting transfers between devices  34.4 us (28%)
  Pallas kernels  20.9 us (17%)
  local copies, waits for them, and re-layouts  3.85 us (3%)
    ppermute x16, waiting for transfers between devices, send(): return lax.ppermute(value, ('var', 'samp'), pairs)  57 us
    ppermute x16, starting transfers between devices, send(): return lax.ppermute(value, ('var', 'samp'), pairs)  28.6 us
    ppermute x2, starting transfers between devices, swap(): return lax.ppermute(value, 'samp', [(0, 1), (1, 0)])  5.81 us
    pallas_call x1, Pallas kernels, right(): pl.pallas_call(functools.partial(right_kernel, slots, pair), in_specs=[sm...  4.7 us
    pallas_call x1, Pallas kernels, backward(): pl.pallas_call(functools.partial(backward_kernel, slots), grid=(slots,),...  4.04 us
    unnamed x14, local copies, waits for them, and re-layouts  3.85 us
    pallas_call x2, Pallas kernels, finish(): pl.pallas_call(functools.partial(finish_kernel, begin, factor), grid=(cou...  3.37 us
    pallas_call x1, Pallas kernels, left(): pl.pallas_call(functools.partial(left_kernel, slots, pair), grid=(slots,)...  2.96 us
  transfers between devices with their start and end apart: 18, of which 8 were waited for; matrix products, arithmetic and copies ran while one was open for 0% of the time, Pallas kernels for 13%

profile of v5, /device:TPU:7, one launch (start us, length us, event | category | flops | bytes accessed | tf_op | source)
XLA Modules:
  0.0 119.7 jit_solution(4253460832344630310)
XLA Ops:
  0.3 1.9 %copy-done = f32[1,3,512,512]{3,2,1,0:T(8,128)S(1)} copy-done((f32[1,3,512,512]{3,2,1,0:T(8,128)S(1)}, f32[1,3,512,512]{3,2,1,0:T(8,128)}, u32[]{:S(2)}) %copy-start) | copy-done | bytes 3145752
  2.2 2.9 %forward.1 = (f32[256,512]{1,0:T(8,128)S(1)}, f32[2,256,512]{2,1,0:T(8,128)S(1)}) custom-call(f32[256,512]{1,0:T(8,128)} %own.3, f32[3,512,512]{2,1,0:T(8,128)S(1)} %bitcast.3), custom_call_target="tpu_custom_call" | custom-call | tf_op jit(solution)/shard_map/forward/pallas_call | solution.py:123
  5.1 1.5 %collective-permute-start.1 = (f32[2,256,512]{2,1,0:T(8,128)S(1)}, f32[2,256,512]{2,1,0:T(8,128)S(1)}, u32[]{:S(2)}, u32[]{:S(2)}) collective-permute-start(f32[2,256,512]{2,1,0:T(8,128)S(1)} %get-tuple-element.28.mine_ref), channel_id=1, source_target_pairs={{0,4},{1,3},{2,6},{3,1},{4,0},{5,7},{6,2},{7,5},{8,12},{9,11},{10,... | collective-permute-start | bytes 3145736 | tf_op jit(solution)/shard_map/ppermute | solution.py:104
  6.6 1.9 %collective-permute-done.2.refs_1_.first = f32[256,512]{1,0:T(8,128)S(1)} collective-permute-done((f32[256,512]{1,0:T(8,128)}, f32[256,512]{1,0:T(8,128)S(1)}, u32[]{:S(2)}, u32[]{:S(2)}) %collective-permute-start.2) | collective-permute-done | bytes 524320 | tf_op jit(solution)/shard_map/ppermute | solution.py:104
  8.5 3.3 %collective-permute-start.3 = (f32[256,512]{1,0:T(8,128)S(1)}, f32[256,512]{1,0:T(8,128)S(1)}, u32[]{:S(2)}, u32[]{:S(2)}) collective-permute-start(f32[256,512]{1,0:T(8,128)S(1)} %collective-permute-done.2.refs_1_.first), channel_id=1, source_target_pairs={{0,24},{1,25},{2,26},{3,27},{4,28},{5,29},{6,30},{7,31},{8,0},{9,1... | collective-permute-start | bytes 1572872 | tf_op jit(solution)/shard_map/ppermute | solution.py:104
  11.9 8.2 %collective-permute-done.3.refs_3_.both = f32[256,512]{1,0:T(8,128)S(1)} collective-permute-done((f32[256,512]{1,0:T(8,128)S(1)}, f32[256,512]{1,0:T(8,128)S(1)}, u32[]{:S(2)}, u32[]{:S(2)}) %collective-permute-start.3) | collective-permute-done | bytes 524320 | tf_op jit(solution)/shard_map/ppermute | solution.py:104
  20.1 4.0 %collective-permute-start.4 = (f32[256,512]{1,0:T(8,128)}, f32[256,512]{1,0:T(8,128)S(1)}, u32[]{:S(2)}, u32[]{:S(2)}) collective-permute-start(f32[256,512]{1,0:T(8,128)} %own.3), channel_id=1, source_target_pairs={{0,24},{1,25},{2,26},{3,27},{4,28},{5,29},{6,30},{7,31},{8,0},{9,1... | collective-permute-start | bytes 1572872 | tf_op jit(solution)/shard_map/ppermute | solution.py:104
  24.8 1.6 %bins.1 = (f32[256,512]{1,0:T(8,128)S(1)}, f32[256,512]{1,0:T(8,128)S(1)}, f32[256,512]{1,0:T(8,128)S(1)}, f32[256,512]{1,0:T(8,128)S(1)}, f32[256,512]{1,0:T(8,128)S(1)}) custom-call(s32[1,3]{1,0:T(1,128)S(1)} %copy-done.5, s32[1,3]{1,0:T(1,128)S(1)} %collective-permute-done.next_ref.offs_ref, f32[256,512]{1,0:T(8,128)S(1)} %get-tuple-element.26.own_in, ...), custom_call_target="tpu_custom_call" | custom-call | tf_op jit(solution)/shard_map/bins/pallas_call | solution.py:248
  26.3 1.3 %collective-permute-start.7 = (f32[256,512]{1,0:T(8,128)S(1)}, f32[256,512]{1,0:T(8,128)S(1)}, u32[]{:S(2)}, u32[]{:S(2)}) collective-permute-start(f32[256,512]{1,0:T(8,128)S(1)} %get-tuple-element.34), channel_id=1, source_target_pairs={{0,2},{1,5},{2,0},{3,7},{4,6},{5,1},{6,4},{7,3},{8,10},{9,13},{10,... | collective-permute-start | bytes 1572872 | tf_op jit(solution)/shard_map/ppermute | solution.py:104
  28.3 3.3 %collective-permute-done.4.refs_2_.group = f32[256,512]{1,0:T(8,128)S(1)} collective-permute-done((f32[256,512]{1,0:T(8,128)}, f32[256,512]{1,0:T(8,128)S(1)}, u32[]{:S(2)}, u32[]{:S(2)}) %collective-permute-start.4) | collective-permute-done | bytes 524320 | tf_op jit(solution)/shard_map/ppermute | solution.py:104
  32.3 11.2 %collective-permute-start.6 = (f32[2,256,512]{2,1,0:T(8,128)S(1)}, f32[2,256,512]{2,1,0:T(8,128)S(1)}, u32[]{:S(2)}, u32[]{:S(2)}) collective-permute-start(f32[2,256,512]{2,1,0:T(8,128)S(1)} %choose.2), channel_id=1, source_target_pairs={{0,4},{1,3},{2,6},{3,1},{4,0},{5,7},{6,2},{7,5},{8,12},{9,11},{10,... | collective-permute-start | bytes 3145736 | tf_op jit(solution)/shard_map/ppermute | solution.py:104
  43.8 17.8 %collective-permute-done.6.refs_0_ = f32[2,256,512]{2,1,0:T(8,128)S(1)} collective-permute-done((f32[2,256,512]{2,1,0:T(8,128)S(1)}, f32[2,256,512]{2,1,0:T(8,128)S(1)}, u32[]{:S(2)}, u32[]{:S(2)}) %collective-permute-start.6) | collective-permute-done | bytes 1048608 | tf_op jit(solution)/shard_map/ppermute | solution.py:104
  61.6 4.0 %backward.1 = f32[256,512]{1,0:T(8,128)S(1)} custom-call(s32[1,3]{1,0:T(1,128)S(1)} %copy-done.5, f32[3,512,512]{2,1,0:T(8,128)} %bitcast.2, f32[256,512]{1,0:T(8,128)} %own.3, f32[256,512]{1,0:T(8,128)S(1)} %collective-permute-done.2.refs_1_.first, f32[256,512]{1,0:T(8,128)S(1)} %collective-permute-done.4.refs_2_.group, ...), custom_call_target="tpu_custom_call" | custom-call | tf_op jit(solution)/shard_map/backward/pallas_call | solution.py:210
  65.9 3.2 %collective-permute-start.12 = (f32[256,512]{1,0:T(8,128)S(1)}, f32[256,512]{1,0:T(8,128)S(1)}, u32[]{:S(2)}, u32[]{:S(2)}) collective-permute-start(f32[256,512]{1,0:T(8,128)S(1)} %add_add_fusion.refs_0_.image_ref.own), channel_id=1, source_target_pairs={{0,24},{1,25},{2,26},{3,27},{4,28},{5,29},{6,30},{7,31},{8,0},{9,1... | collective-permute-start | bytes 1572872 | tf_op jit(solution)/shard_map/ppermute | solution.py:104
  69.1 9.9 %collective-permute-done.12.refs_2_.group = f32[256,512]{1,0:T(8,128)S(1)} collective-permute-done((f32[256,512]{1,0:T(8,128)S(1)}, f32[256,512]{1,0:T(8,128)S(1)}, u32[]{:S(2)}, u32[]{:S(2)}) %collective-permute-start.12) | collective-permute-done | bytes 524320 | tf_op jit(solution)/shard_map/ppermute | solution.py:104
  79.0 8.3 %collective-permute-done.13.refs_3_.both = f32[256,512]{1,0:T(8,128)S(1)} collective-permute-done((f32[256,512]{1,0:T(8,128)S(1)}, f32[256,512]{1,0:T(8,128)S(1)}, u32[]{:S(2)}, u32[]{:S(2)}) %collective-permute-start.13) | collective-permute-done | bytes 524320 | tf_op jit(solution)/shard_map/ppermute | solution.py:104
  89.1 4.7 %right.1 = (f32[1,256,512]{2,1,0:T(8,128)S(1)}, f32[1,256,512]{2,1,0:T(8,128)S(1)}, f32[2,256,512]{2,1,0:T(8,128)S(1)}, f32[2,256,512]{2,1,0:T(8,128)}, bf16[512...) custom-call(s32[1,3]{1,0:T(1,128)S(1)} %copy-done.5, f32[256,512]{1,0:T(8,128)} %own.3, ...), custom_call_target="tpu_custom_call" | custom-call | flops 26843545600 | tf_op jit(solution)/shard_map/right/pallas_call | solution.py:304
  94.7 2.9 %collective-permute-start.14 = (f32[1,256,512]{2,1,0:T(8,128)S(1)}, f32[1,256,512]{2,1,0:T(8,128)S(1)}, u32[]{:S(2)}, u32[]{:S(2)}) collective-permute-start(f32[1,256,512]{2,1,0:T(8,128)S(1)} %get-tuple-element.39), channel_id=1, source_target_pairs={{0,1},{1,0},{2,3},{3,2},{4,5},{5,4},{6,7},{7,6},{8,9},{9,8},{10,11... | collective-permute-start | bytes 1572872 | tf_op jit(solution)/shard_map/ppermute | solution.py:401
  99.6 1.6 %finish.2.refs_0_ = f32[3,256,512]{2,1,0:T(8,128)} custom-call(s32[1,3]{1,0:T(1,128)S(1)} %copy-done.5, f32[1]{0:T(128)S(6)} %copy.7.step_ref, f32[3,512,512]{2,1,0:T(8,128)S(1)} %bitcast.4, f32[1,256,512]{2,1,0:T(8,128)S(1)} %get-tuple-element.38.keep_ref, f32[1,256,512]{2,1,0:T(8,128)S(1)} %collective-permute-done.14.other_ref), custom_call_target="tpu_custom_call" | custom-call | tf_op jit(solution)/shard_map/finish/pallas_call | solution.py:383
  101.2 7.6 %collective-permute-done.15.two = f32[256,512]{1,0:T(8,128)S(1)} collective-permute-done((f32[256,512]{1,0:T(8,128)S(1)}, f32[256,512]{1,0:T(8,128)S(1)}, u32[]{:S(2)}, u32[]{:S(2)}) %collective-permute-start.15) | collective-permute-done | bytes 524320 | tf_op jit(solution)/shard_map/ppermute | solution.py:104
  109.8 3.0 %left.1 = (f32[2,256,512]{2,1,0:T(8,128)S(1)}, f32[2,256,512]{2,1,0:T(8,128)S(1)}) custom-call(s32[1,3]{1,0:T(1,128)S(1)} %copy-done.5, f32[2,256,512]{2,1,0:T(8,128)} %copy-done.2, f32[2,256,512]{2,1,0:T(8,128)} %get-tuple-element.41.send_in, bf16[512,256]{1,0:T(8,128)(2,1)S(1)} %get-tuple-element.42.high_ref, ...), custom_call_target="tpu_custom_call" | custom-call | tf_op jit(solution)/shard_map/left/pallas_call | solution.py:342
  112.7 2.9 %collective-permute-start.17 = (f32[2,256,512]{2,1,0:T(8,128)S(1)}, f32[2,256,512]{2,1,0:T(8,128)S(1)}, u32[]{:S(2)}, u32[]{:S(2)}) collective-permute-start(f32[2,256,512]{2,1,0:T(8,128)S(1)} %get-tuple-element.46), channel_id=1, source_target_pairs={{0,1},{1,0},{2,3},{3,2},{4,5},{5,4},{6,7},{7,6},{8,9},{9,8},{10,11... | collective-permute-start | bytes 3145736 | tf_op jit(solution)/shard_map/ppermute | solution.py:401
  115.6 2.3 %collective-permute-done.17.other_ref = f32[2,256,512]{2,1,0:T(8,128)S(1)} collective-permute-done((f32[2,256,512]{2,1,0:T(8,128)S(1)}, f32[2,256,512]{2,1,0:T(8,128)S(1)}, u32[]{:S(2)}, u32[]{:S(2)}) %collective-permute-start.17) | collective-permute-done | bytes 1048608 | tf_op jit(solution)/shard_map/ppermute | solution.py:401
  117.9 1.8 %finish.3 = f32[3,256,512]{2,1,0:T(8,128)} custom-call(s32[1,3]{1,0:T(1,128)S(1)} %copy-done.5, f32[1]{0:T(128)S(6)} %copy.7.step_ref, f32[3,512,512]{2,1,0:T(8,128)S(1)} %bitcast.5, f32[2,256,512]{2,1,0:T(8,128)S(1)} %get-tuple-element.45.keep_ref, f32[2,256,512]{2,1,0:T(8,128)S(1)} %collective-permute-done.17.other_ref, ...), custom_call_target="tpu_custom_call", output_to_operand_aliasing={{}: (5, {})} | custom-call | tf_op jit(solution)/shard_map/finish/pallas_call | solution.py:383
  (37 shorter events, 7.8 us)
Async XLA Ops:
  0.0 8.5 %collective-permute-start.2 = (f32[256,512]{1,0:T(8,128)}, f32[256,512]{1,0:T(8,128)S(1)}, u32[]{:S(2)}, u32[]{:S(2)}) collective-permute-start(f32[256,512]{1,0:T(8,128)} %own.3), channel_id=1, source_target_pairs={{0,2},{1,5},{2,0},{3,7},{4,6},{5,1},{6,4},{7,3},{8,10},{9,13},{10,... | collective-permute-start | bytes 1572872 | tf_op jit(solution)/shard_map/ppermute | solution.py:104
  0.2 4.9 %collective-permute-start = (s32[1,3]{1,0:T(1,128)}, s32[1,3]{1,0:T(1,128)S(1)}, u32[]{:S(2)}, u32[]{:S(2)}) collective-permute-start(s32[1,3]{1,0:T(1,128)} %offs_ref.11), channel_id=1, source_target_pairs={{0,4},{1,3},{2,6},{3,1},{4,0},{5,7},{6,2},{7,5},{8,12},{9,11},{10,... | collective-permute-start | bytes 44 | tf_op jit(solution)/shard_map/ppermute | solution.py:104
  0.3 1.9 %copy-start = (f32[1,3,512,512]{3,2,1,0:T(8,128)S(1)}, f32[1,3,512,512]{3,2,1,0:T(8,128)}, u32[]{:S(2)}) copy-start(f32[1,3,512,512]{3,2,1,0:T(8,128)} %param.5) | copy-start | bytes 9437188
  2.1 22.6 %copy-start.5 = (s32[1,3]{1,0:T(1,128)S(1)}, s32[1,3]{1,0:T(1,128)}, u32[]{:S(2)}) copy-start(s32[1,3]{1,0:T(1,128)} %offs_ref.11) | copy-start | bytes 40
  5.1 19.6 %collective-permute-start.1 = (f32[2,256,512]{2,1,0:T(8,128)S(1)}, f32[2,256,512]{2,1,0:T(8,128)S(1)}, u32[]{:S(2)}, u32[]{:S(2)}) collective-permute-start(f32[2,256,512]{2,1,0:T(8,128)S(1)} %get-tuple-element.28.mine_ref), channel_id=1, source_target_pairs={{0,4},{1,3},{2,6},{3,1},{4,0},{5,7},{6,2},{7,5},{8,12},{9,11},{10,... | collective-permute-start | bytes 3145736 | tf_op jit(solution)/shard_map/ppermute | solution.py:104
  8.5 11.5 %collective-permute-start.3 = (f32[256,512]{1,0:T(8,128)S(1)}, f32[256,512]{1,0:T(8,128)S(1)}, u32[]{:S(2)}, u32[]{:S(2)}) collective-permute-start(f32[256,512]{1,0:T(8,128)S(1)} %collective-permute-done.2.refs_1_.first), channel_id=1, source_target_pairs={{0,24},{1,25},{2,26},{3,27},{4,28},{5,29},{6,30},{7,31},{8,0},{9,1... | collective-permute-start | bytes 1572872 | tf_op jit(solution)/shard_map/ppermute | solution.py:104
  20.1 11.6 %collective-permute-start.4 = (f32[256,512]{1,0:T(8,128)}, f32[256,512]{1,0:T(8,128)S(1)}, u32[]{:S(2)}, u32[]{:S(2)}) collective-permute-start(f32[256,512]{1,0:T(8,128)} %own.3), channel_id=1, source_target_pairs={{0,24},{1,25},{2,26},{3,27},{4,28},{5,29},{6,30},{7,31},{8,0},{9,1... | collective-permute-start | bytes 1572872 | tf_op jit(solution)/shard_map/ppermute | solution.py:104
  24.1 7.6 %collective-permute-start.5 = (f32[256,512]{1,0:T(8,128)S(1)}, f32[256,512]{1,0:T(8,128)S(1)}, u32[]{:S(2)}, u32[]{:S(2)}) collective-permute-start(f32[256,512]{1,0:T(8,128)S(1)} %collective-permute-done.3.refs_3_.both), channel_id=1, source_target_pairs={{2,26},{5,29},{10,2},{13,5},{18,10},{21,13},{26,18},{29,21}} | collective-permute-start | bytes 1572872 | tf_op jit(solution)/shard_map/ppermute | solution.py:104
  26.3 17.2 %collective-permute-start.7 = (f32[256,512]{1,0:T(8,128)S(1)}, f32[256,512]{1,0:T(8,128)S(1)}, u32[]{:S(2)}, u32[]{:S(2)}) collective-permute-start(f32[256,512]{1,0:T(8,128)S(1)} %get-tuple-element.34), channel_id=1, source_target_pairs={{0,2},{1,5},{2,0},{3,7},{4,6},{5,1},{6,4},{7,3},{8,10},{9,13},{10,... | collective-permute-start | bytes 1572872 | tf_op jit(solution)/shard_map/ppermute | solution.py:104
  27.6 15.9 %collective-permute-start.8 = (f32[256,512]{1,0:T(8,128)S(1)}, f32[256,512]{1,0:T(8,128)S(1)}, u32[]{:S(2)}, u32[]{:S(2)}) collective-permute-start(f32[256,512]{1,0:T(8,128)S(1)} %get-tuple-element.35), channel_id=1, source_target_pairs={{26,0},{29,1},{2,8},{5,9},{10,16},{13,17},{18,24},{21,25}} | collective-permute-start | bytes 1572872 | tf_op jit(solution)/shard_map/ppermute | solution.py:104
  32.3 29.3 %collective-permute-start.6 = (f32[2,256,512]{2,1,0:T(8,128)S(1)}, f32[2,256,512]{2,1,0:T(8,128)S(1)}, u32[]{:S(2)}, u32[]{:S(2)}) collective-permute-start(f32[2,256,512]{2,1,0:T(8,128)S(1)} %choose.2), channel_id=1, source_target_pairs={{0,4},{1,3},{2,6},{3,1},{4,0},{5,7},{6,2},{7,5},{8,12},{9,11},{10,... | collective-permute-start | bytes 3145736 | tf_op jit(solution)/shard_map/ppermute | solution.py:104
  43.7 22.0 %collective-permute-start.9 = (f32[256,512]{1,0:T(8,128)S(1)}, f32[256,512]{1,0:T(8,128)S(1)}, u32[]{:S(2)}, u32[]{:S(2)}) collective-permute-start(f32[256,512]{1,0:T(8,128)S(1)} %get-tuple-element.36), channel_id=1, source_target_pairs={{0,2},{1,5},{2,0},{3,7},{4,6},{5,1},{6,4},{7,3},{8,10},{9,13},{10,... | collective-permute-start | bytes 1572872 | tf_op jit(solution)/shard_map/ppermute | solution.py:104
  43.7 21.9 %collective-permute-start.10 = (f32[256,512]{1,0:T(8,128)S(1)}, f32[256,512]{1,0:T(8,128)S(1)}, u32[]{:S(2)}, u32[]{:S(2)}) collective-permute-start(f32[256,512]{1,0:T(8,128)S(1)} %add_add_fusion.1), channel_id=1, source_target_pairs={{24,0},{25,1},{26,2},{27,3},{28,4},{29,5},{30,6},{31,7},{0,8},{1,9... | collective-permute-start | bytes 1572872 | tf_op jit(solution)/shard_map/ppermute | solution.py:104
  61.6 4.1 %copy-start.4 = (f32[2,256,512]{2,1,0:T(8,128)}, f32[2,256,512]{2,1,0:T(8,128)S(1)}, u32[]{:S(2)}) copy-start(f32[2,256,512]{2,1,0:T(8,128)S(1)} %collective-permute-done.6.refs_0_) | copy-start | bytes 3145732
  65.9 13.1 %collective-permute-start.12 = (f32[256,512]{1,0:T(8,128)S(1)}, f32[256,512]{1,0:T(8,128)S(1)}, u32[]{:S(2)}, u32[]{:S(2)}) collective-permute-start(f32[256,512]{1,0:T(8,128)S(1)} %add_add_fusion.refs_0_.image_ref.own), channel_id=1, source_target_pairs={{0,24},{1,25},{2,26},{3,27},{4,28},{5,29},{6,30},{7,31},{8,0},{9,1... | collective-permute-start | bytes 1572872 | tf_op jit(solution)/shard_map/ppermute | solution.py:104
  69.1 9.9 %collective-permute-start.11 = (f32[256,512]{1,0:T(8,128)S(1)}, f32[256,512]{1,0:T(8,128)S(1)}, u32[]{:S(2)}, u32[]{:S(2)}) collective-permute-start(f32[256,512]{1,0:T(8,128)S(1)} %add_add_fusion.refs_0_.image_ref.own), channel_id=1, source_target_pairs={{0,2},{1,5},{2,0},{3,7},{4,6},{5,1},{6,4},{7,3},{8,10},{9,13},{10,... | collective-permute-start | bytes 1572872 | tf_op jit(solution)/shard_map/ppermute | solution.py:104
  79.0 8.3 %collective-permute-start.13 = (f32[256,512]{1,0:T(8,128)S(1)}, f32[256,512]{1,0:T(8,128)S(1)}, u32[]{:S(2)}, u32[]{:S(2)}) collective-permute-start(f32[256,512]{1,0:T(8,128)S(1)} %collective-permute-done.12.refs_2_.group), channel_id=1, source_target_pairs={{0,2},{1,5},{2,0},{3,7},{4,6},{5,1},{6,4},{7,3},{8,10},{9,13},{10,... | collective-permute-start | bytes 1572872 | tf_op jit(solution)/shard_map/ppermute | solution.py:104
  88.0 1.1 copy-start.3
  88.0 20.8 %collective-permute-start.16 = (f32[2,256,512]{2,1,0:T(8,128)S(1)}, f32[2,256,512]{2,1,0:T(8,128)S(1)}, u32[]{:S(2)}, u32[]{:S(2)}) collective-permute-start(f32[2,256,512]{2,1,0:T(8,128)S(1)} %choose.3.refs_1_), channel_id=1, source_target_pairs={{0,4},{1,3},{2,6},{3,1},{4,0},{5,7},{6,2},{7,5},{8,12},{9,11},{10,... | collective-permute-start | bytes 3145736 | tf_op jit(solution)/shard_map/ppermute | solution.py:104
  89.1 10.5 %copy-start.1 = (f32[1,3,512,512]{3,2,1,0:T(8,128)S(1)}, f32[1,3,512,512]{3,2,1,0:T(8,128)}, u32[]{:S(2)}) copy-start(f32[1,3,512,512]{3,2,1,0:T(8,128)} %param.5) | copy-start | bytes 9437188
  94.7 4.9 %collective-permute-start.14 = (f32[1,256,512]{2,1,0:T(8,128)S(1)}, f32[1,256,512]{2,1,0:T(8,128)S(1)}, u32[]{:S(2)}, u32[]{:S(2)}) collective-permute-start(f32[1,256,512]{2,1,0:T(8,128)S(1)} %get-tuple-element.39), channel_id=1, source_target_pairs={{0,1},{1,0},{2,3},{3,2},{4,5},{5,4},{6,7},{7,6},{8,9},{9,8},{10,11... | collective-permute-start | bytes 1572872 | tf_op jit(solution)/shard_map/ppermute | solution.py:401
  97.6 11.1 %collective-permute-start.15 = (f32[256,512]{1,0:T(8,128)S(1)}, f32[256,512]{1,0:T(8,128)S(1)}, u32[]{:S(2)}, u32[]{:S(2)}) collective-permute-start(f32[256,512]{1,0:T(8,128)S(1)} %collective-permute-done.13.refs_3_.both), channel_id=1, source_target_pairs={{2,30},{5,31},{10,6},{13,7},{18,14},{21,15},{26,22},{29,23}} | collective-permute-start | bytes 1572872 | tf_op jit(solution)/shard_map/ppermute | solution.py:104
  108.8 1.0 copy-start.6
  112.7 5.2 %collective-permute-start.17 = (f32[2,256,512]{2,1,0:T(8,128)S(1)}, f32[2,256,512]{2,1,0:T(8,128)S(1)}, u32[]{:S(2)}, u32[]{:S(2)}) collective-permute-start(f32[2,256,512]{2,1,0:T(8,128)S(1)} %get-tuple-element.46), channel_id=1, source_target_pairs={{0,1},{1,0},{2,3},{3,2},{4,5},{5,4},{6,7},{7,6},{8,9},{9,8},{10,11... | collective-permute-start | bytes 3145736 | tf_op jit(solution)/shard_map/ppermute | solution.py:401
  (1 other events, 1.0 us)

commit v6 on v5

--- a/solution.py
+++ b/solution.py
@@ -9,7 +9,7 @@
 
 penalty_weight = 0.05
 BAND = 6
-VMEM_LIMIT = 48 * 1024 * 1024
+VMEM_LIMIT = 20 * 1024 * 1024
 NN = (((1,), (0,)), ((), ()))
 NT = (((1,), (1,)), ((), ()))
 f32, bf16 = jnp.float32, jnp.bfloat16
@@ -211,8 +211,7 @@
         functools.partial(backward_kernel, slots),
         grid=(slots,),
         in_specs=[smem_spec(), pl.BlockSpec((None, block, block), lambda j: (j + 1, 0, 0))]
-        + [any_spec()] * (len(sources) - 1)
-        + [vmem_spec()],
+        + [any_spec()] * len(sources),
         out_specs=pl.BlockSpec((rows, block), lambda j: (0, 0)),
         out_shape=jax.ShapeDtypeStruct((rows, block), f32),
         scratch_shapes=[pltpu.VMEM((slots, rows, block), f32), pltpu.SemaphoreType.DMA((slots,))],
@@ -342,7 +341,7 @@
     return pl.pallas_call(
         functools.partial(left_kernel, slots, pair),
         grid=(slots,),
-        in_specs=[smem_spec(), spec, spec, whole, whole] + [any_spec()] * (len(sources) - 1) + [vmem_spec()],
+        in_specs=[smem_spec(), spec, spec, whole, whole] + [any_spec()] * len(sources),
         out_specs=[spec, spec],
         out_shape=[part, part],
         scratch_shapes=[pltpu.VMEM((slots, rows, block), f32), pltpu.SemaphoreType.DMA((slots,))],
@@ -411,10 +410,10 @@
     offsets_next = send(offsets, "last")
     data_first = send(data, "first")
     own, far = forward(data, local_tiles)
-    theirs = send(after(far, offsets_next), "last")
-    data_both = send(data_first, "group")
+    theirs = send(after(far, (offsets_next, data_first)), "last")
+    data_group = send(data, "group")
+    data_both = send(after(data_first, data_group), "group")
     data_two = send(data_both, "column")
-    data_group = send(after(data, data_both), "group")
     own, bin_first, bin_group, bin_both, bin_two = make_bins(offsets, offsets_next, own, far, after(theirs, data_both))
     got_both = send(bin_both, "first")
     got_two = send(bin_two, "two", reverse=True)
@@ -424,7 +423,7 @@
 
     bin_group = bin_group + got_both + got_two
     got_group = send(bin_group, "group", reverse=True)
-    got_first = send(after(bin_first, bin_group), "first")
+    got_first = send(bin_first, "first")
     image = own + backward(offsets, local_tiles, data_sources) + got_first + got_group
 
     image_group = send(image, "group")

time: 121 us -> 116 us (0.959)
  starting transfers between devices: 34.4 us -> 52.3 us
  waiting for transfers between devices: 59.3 us -> 44.2 us
  Pallas kernels: 20.9 us -> 15.2 us
    ppermute x16, waiting for transfers between devices: 57 us -> 41.9 us  [send(): return lax.ppermute(value, ('var', 'samp'), pairs)]
    ppermute x16, starting transfers between devices: 28.6 us -> 43.7 us  [send(): return lax.ppermute(value, ('var', 'samp'), pairs)]
    ppermute x2, starting transfers between devices: 5.81 us -> 8.63 us  [swap(): return lax.ppermute(value, 'samp', [(0, 1), (1, 0)])]
    pallas_call x1, Pallas kernels: 4.04 us -> 2.05 us  [backward(): pl.pallas_call(functools.partial(backward_kernel, slots), grid=(slots,),...]
    pallas_call x1, Pallas kernels: 4.7 us -> 3.1 us  [right(): pl.pallas_call(functools.partial(right_kernel, slots, pair), in_specs=[sm...]
    unnamed x14 -> x10, local copies, waits for them, and re-layouts: 3.85 us -> 2.95 us
  transfers between devices with their start and end apart: 18 -> 18, of which waited for: 8 -> 7; matrix products, arithmetic and copies ran while one was open for 0% -> 0% of each run, Pallas kernels for 13% -> 9%
where the time goes in v6:
time: 116 us
  starting transfers between devices  52.3 us (45%)
  waiting for transfers between devices  44.2 us (38%)
  Pallas kernels  15.2 us (13%)
  local copies, waits for them, and re-layouts  2.95 us (3%)
    ppermute x16, starting transfers between devices, send(): return lax.ppermute(value, ('var', 'samp'), pairs)  43.7 us
    ppermute x16, waiting for transfers between devices, send(): return lax.ppermute(value, ('var', 'samp'), pairs)  41.9 us
    ppermute x2, starting transfers between devices, swap(): return lax.ppermute(value, 'samp', [(0, 1), (1, 0)])  8.63 us
    pallas_call x2, Pallas kernels, finish(): pl.pallas_call(functools.partial(finish_kernel, begin, factor), grid=(cou...  3.37 us
    pallas_call x1, Pallas kernels, right(): pl.pallas_call(functools.partial(right_kernel, slots, pair), in_specs=[sm...  3.1 us
    unnamed x10, local copies, waits for them, and re-layouts  2.95 us
  transfers between devices with their start and end apart: 18, of which 7 were waited for; matrix products, arithmetic and copies ran while one was open for 0% of the time, Pallas kernels for 9%

profile of v6, /device:TPU:7, one launch (start us, length us, event | category | flops | bytes accessed | tf_op | source)
XLA Modules:
  0.0 115.9 jit_solution(15561947355313071603)
XLA Ops:
  0.2 3.3 %collective-permute-start.3 = (f32[256,512]{1,0:T(8,128)}, f32[256,512]{1,0:T(8,128)S(1)}, u32[]{:S(2)}, u32[]{:S(2)}) collective-permute-start(f32[256,512]{1,0:T(8,128)} %own.3), channel_id=1, source_target_pairs={{0,24},{1,25},{2,26},{3,27},{4,28},{5,29},{6,30},{7,31},{8,0},{9,1... | collective-permute-start | bytes 1572872 | tf_op jit(solution)/shard_map/ppermute | solution.py:104
  3.8 1.9 %copy-done = f32[1,3,512,512]{3,2,1,0:T(8,128)S(1)} copy-done((f32[1,3,512,512]{3,2,1,0:T(8,128)S(1)}, f32[1,3,512,512]{3,2,1,0:T(8,128)}, u32[]{:S(2)}) %copy-start) | copy-done | bytes 3145752
  6.7 1.9 %forward.1 = (f32[256,512]{1,0:T(8,128)S(1)}, f32[2,256,512]{2,1,0:T(8,128)S(1)}) custom-call(f32[256,512]{1,0:T(8,128)S(1)} %copy-done.2, f32[3,512,512]{2,1,0:T(8,128)S(1)} %bitcast.2), custom_call_target="tpu_custom_call" | custom-call | tf_op jit(solution)/shard_map/forward/pallas_call | solution.py:123
  9.9 4.2 %collective-permute-done.3.refs_2_.group = f32[256,512]{1,0:T(8,128)S(1)} collective-permute-done((f32[256,512]{1,0:T(8,128)}, f32[256,512]{1,0:T(8,128)S(1)}, u32[]{:S(2)}, u32[]{:S(2)}) %collective-permute-start.3) | collective-permute-done | bytes 524320 | tf_op jit(solution)/shard_map/ppermute | solution.py:104
  14.1 3.9 %collective-permute-start.4 = (f32[256,512]{1,0:T(8,128)S(1)}, f32[256,512]{1,0:T(8,128)S(1)}, u32[]{:S(2)}, u32[]{:S(2)}) collective-permute-start(f32[256,512]{1,0:T(8,128)S(1)} %collective-permute-done.1.refs_1_.first), channel_id=1, source_target_pairs={{0,24},{1,25},{2,26},{3,27},{4,28},{5,29},{6,30},{7,31},{8,0},{9,1... | collective-permute-start | bytes 1572872 | tf_op jit(solution)/shard_map/ppermute | solution.py:104
  18.0 9.3 %collective-permute-done.4.refs_3_.both = f32[256,512]{1,0:T(8,128)S(1)} collective-permute-done((f32[256,512]{1,0:T(8,128)S(1)}, f32[256,512]{1,0:T(8,128)S(1)}, u32[]{:S(2)}, u32[]{:S(2)}) %collective-permute-start.4) | collective-permute-done | bytes 524320 | tf_op jit(solution)/shard_map/ppermute | solution.py:104
  29.6 3.7 %collective-permute-start.8 = (f32[256,512]{1,0:T(8,128)S(1)}, f32[256,512]{1,0:T(8,128)S(1)}, u32[]{:S(2)}, u32[]{:S(2)}) collective-permute-start(f32[256,512]{1,0:T(8,128)S(1)} %get-tuple-element.33), channel_id=1, source_target_pairs={{0,2},{1,5},{2,0},{3,7},{4,6},{5,1},{6,4},{7,3},{8,10},{9,13},{10,... | collective-permute-start | bytes 1572872 | tf_op jit(solution)/shard_map/ppermute | solution.py:104
  34.6 3.8 %collective-permute-start.6 = (f32[2,256,512]{2,1,0:T(8,128)S(1)}, f32[2,256,512]{2,1,0:T(8,128)S(1)}, u32[]{:S(2)}, u32[]{:S(2)}) collective-permute-start(f32[2,256,512]{2,1,0:T(8,128)S(1)} %choose.2), channel_id=1, source_target_pairs={{0,4},{1,3},{2,6},{3,1},{4,0},{5,7},{6,2},{7,5},{8,12},{9,11},{10,... | collective-permute-start | bytes 3145736 | tf_op jit(solution)/shard_map/ppermute | solution.py:104
  38.4 1.7 %collective-permute-done.8 = f32[256,512]{1,0:T(8,128)S(1)} collective-permute-done((f32[256,512]{1,0:T(8,128)S(1)}, f32[256,512]{1,0:T(8,128)S(1)}, u32[]{:S(2)}, u32[]{:S(2)}) %collective-permute-start.8) | collective-permute-done | bytes 524320 | tf_op jit(solution)/shard_map/ppermute | solution.py:104
  40.3 12.3 %collective-permute-done.6.refs_0_ = f32[2,256,512]{2,1,0:T(8,128)S(1)} collective-permute-done((f32[2,256,512]{2,1,0:T(8,128)S(1)}, f32[2,256,512]{2,1,0:T(8,128)S(1)}, u32[]{:S(2)}, u32[]{:S(2)}) %collective-permute-start.6) | collective-permute-done | bytes 1048608 | tf_op jit(solution)/shard_map/ppermute | solution.py:104
  52.7 2.1 %backward.1 = f32[256,512]{1,0:T(8,128)S(1)} custom-call(s32[1,3]{1,0:T(1,128)S(1)} %copy-done.4, f32[3,512,512]{2,1,0:T(8,128)S(1)} %bitcast.3, f32[256,512]{1,0:T(8,128)S(1)} %copy-done.3, f32[256,512]{1,0:T(8,128)S(1)} %collective-permute-done.1.refs_1_.first, f32[256,512]{1,0:T(8,128)S(1)} %collective-permute-done.3.refs_2_.group, ...), custom_call_target="tpu_custom_call" | custom-call | tf_op jit(solution)/shard_map/backward/pallas_call | solution.py:210
  55.0 4.0 %collective-permute-start.12 = (f32[256,512]{1,0:T(8,128)S(1)}, f32[256,512]{1,0:T(8,128)S(1)}, u32[]{:S(2)}, u32[]{:S(2)}) collective-permute-start(f32[256,512]{1,0:T(8,128)S(1)} %add_add_fusion.1.refs_0_.image_ref.own), channel_id=1, source_target_pairs={{0,24},{1,25},{2,26},{3,27},{4,28},{5,29},{6,30},{7,31},{8,0},{9,1... | collective-permute-start | bytes 1572872 | tf_op jit(solution)/shard_map/ppermute | solution.py:104
  59.0 9.0 %collective-permute-start.11 = (f32[256,512]{1,0:T(8,128)S(1)}, f32[256,512]{1,0:T(8,128)S(1)}, u32[]{:S(2)}, u32[]{:S(2)}) collective-permute-start(f32[256,512]{1,0:T(8,128)S(1)} %add_add_fusion.1.refs_0_.image_ref.own), channel_id=1, source_target_pairs={{0,2},{1,5},{2,0},{3,7},{4,6},{5,1},{6,4},{7,3},{8,10},{9,13},{10,... | collective-permute-start | bytes 1572872 | tf_op jit(solution)/shard_map/ppermute | solution.py:104
  68.0 9.3 %collective-permute-start.13 = (f32[256,512]{1,0:T(8,128)S(1)}, f32[256,512]{1,0:T(8,128)S(1)}, u32[]{:S(2)}, u32[]{:S(2)}) collective-permute-start(f32[256,512]{1,0:T(8,128)S(1)} %collective-permute-done.12.refs_2_.group), channel_id=1, source_target_pairs={{0,2},{1,5},{2,0},{3,7},{4,6},{5,1},{6,4},{7,3},{8,10},{9,13},{10,... | collective-permute-start | bytes 1572872 | tf_op jit(solution)/shard_map/ppermute | solution.py:104
  77.3 6.8 %collective-permute-done.13.refs_3_.both = f32[256,512]{1,0:T(8,128)S(1)} collective-permute-done((f32[256,512]{1,0:T(8,128)S(1)}, f32[256,512]{1,0:T(8,128)S(1)}, u32[]{:S(2)}, u32[]{:S(2)}) %collective-permute-start.13) | collective-permute-done | bytes 524320 | tf_op jit(solution)/shard_map/ppermute | solution.py:104
  84.8 2.2 %collective-permute-start.16 = (f32[2,256,512]{2,1,0:T(8,128)S(1)}, f32[2,256,512]{2,1,0:T(8,128)S(1)}, u32[]{:S(2)}, u32[]{:S(2)}) collective-permute-start(f32[2,256,512]{2,1,0:T(8,128)S(1)} %choose.3.refs_1_), channel_id=1, source_target_pairs={{0,4},{1,3},{2,6},{3,1},{4,0},{5,7},{6,2},{7,5},{8,12},{9,11},{10,... | collective-permute-start | bytes 3145736 | tf_op jit(solution)/shard_map/ppermute | solution.py:104
  87.0 3.1 %right.1 = (f32[1,256,512]{2,1,0:T(8,128)S(1)}, f32[1,256,512]{2,1,0:T(8,128)S(1)}, f32[2,256,512]{2,1,0:T(8,128)S(1)}, f32[2,256,512]{2,1,0:T(8,128)S(1)}, bf16...) custom-call(s32[1,3]{1,0:T(1,128)S(1)} %copy-done.4, f32[256,512]{1,0:T(8,128)S(1)} %copy-done.3, ...), custom_call_target="tpu_custom_call" | custom-call | flops 26843545600 | tf_op jit(solution)/shard_map/right/pallas_call | solution.py:303
  90.1 4.4 %collective-permute-start.14 = (f32[1,256,512]{2,1,0:T(8,128)S(1)}, f32[1,256,512]{2,1,0:T(8,128)S(1)}, u32[]{:S(2)}, u32[]{:S(2)}) collective-permute-start(f32[1,256,512]{2,1,0:T(8,128)S(1)} %get-tuple-element.37), channel_id=1, source_target_pairs={{0,1},{1,0},{2,3},{3,2},{4,5},{5,4},{6,7},{7,6},{8,9},{9,8},{10,11... | collective-permute-start | bytes 1572872 | tf_op jit(solution)/shard_map/ppermute | solution.py:400
  96.5 1.6 %finish.2.refs_0_ = f32[3,256,512]{2,1,0:T(8,128)} custom-call(s32[1,3]{1,0:T(1,128)S(1)} %copy-done.4, f32[1]{0:T(128)S(6)} %copy.7.step_ref, f32[3,512,512]{2,1,0:T(8,128)S(1)} %bitcast.4, f32[1,256,512]{2,1,0:T(8,128)S(1)} %get-tuple-element.36.keep_ref, f32[1,256,512]{2,1,0:T(8,128)S(1)} %collective-permute-done.14.other_ref), custom_call_target="tpu_custom_call" | custom-call | tf_op jit(solution)/shard_map/finish/pallas_call | solution.py:382
  98.0 7.6 %collective-permute-done.15.two = f32[256,512]{1,0:T(8,128)S(1)} collective-permute-done((f32[256,512]{1,0:T(8,128)S(1)}, f32[256,512]{1,0:T(8,128)S(1)}, u32[]{:S(2)}, u32[]{:S(2)}) %collective-permute-start.15) | collective-permute-done | bytes 524320 | tf_op jit(solution)/shard_map/ppermute | solution.py:104
  105.6 1.9 %left.1 = (f32[2,256,512]{2,1,0:T(8,128)S(1)}, f32[2,256,512]{2,1,0:T(8,128)S(1)}) custom-call(s32[1,3]{1,0:T(1,128)S(1)} %copy-done.4, f32[2,256,512]{2,1,0:T(8,128)S(1)} %get-tuple-element.38.keep_in, f32[2,256,512]{2,1,0:T(8,128)S(1)} %get-tuple-element.39.send_in, bf16[512,256]{1,0:T(8,128)(2,1)S(1)} %get-tuple-element.40.high_ref, ...), custom_call_target="tpu_custom_call" | custom-call | tf_op jit(solution)/shard_map/left/pallas_call | solution.py:341
  107.6 4.2 %collective-permute-start.17 = (f32[2,256,512]{2,1,0:T(8,128)S(1)}, f32[2,256,512]{2,1,0:T(8,128)S(1)}, u32[]{:S(2)}, u32[]{:S(2)}) collective-permute-start(f32[2,256,512]{2,1,0:T(8,128)S(1)} %get-tuple-element.44), channel_id=1, source_target_pairs={{0,1},{1,0},{2,3},{3,2},{4,5},{5,4},{6,7},{7,6},{8,9},{9,8},{10,11... | collective-permute-start | bytes 3145736 | tf_op jit(solution)/shard_map/ppermute | solution.py:400
  111.8 2.3 %collective-permute-done.17.other_ref = f32[2,256,512]{2,1,0:T(8,128)S(1)} collective-permute-done((f32[2,256,512]{2,1,0:T(8,128)S(1)}, f32[2,256,512]{2,1,0:T(8,128)S(1)}, u32[]{:S(2)}, u32[]{:S(2)}) %collective-permute-start.17) | collective-permute-done | bytes 1048608 | tf_op jit(solution)/shard_map/ppermute | solution.py:400
  114.1 1.8 %finish.3 = f32[3,256,512]{2,1,0:T(8,128)} custom-call(s32[1,3]{1,0:T(1,128)S(1)} %copy-done.4, f32[1]{0:T(128)S(6)} %copy.7.step_ref, f32[3,512,512]{2,1,0:T(8,128)S(1)} %bitcast.5, f32[2,256,512]{2,1,0:T(8,128)S(1)} %get-tuple-element.43.keep_ref, f32[2,256,512]{2,1,0:T(8,128)S(1)} %collective-permute-done.17.other_ref, ...), custom_call_target="tpu_custom_call", output_to_operand_aliasing={{}: (5, {})} | custom-call | tf_op jit(solution)/shard_map/finish/pallas_call | solution.py:382
  (33 shorter events, 8.8 us)
Async XLA Ops:
  0.0 8.6 %collective-permute-start.1 = (f32[256,512]{1,0:T(8,128)}, f32[256,512]{1,0:T(8,128)S(1)}, u32[]{:S(2)}, u32[]{:S(2)}) collective-permute-start(f32[256,512]{1,0:T(8,128)} %own.3), channel_id=1, source_target_pairs={{0,2},{1,5},{2,0},{3,7},{4,6},{5,1},{6,4},{7,3},{8,10},{9,13},{10,... | collective-permute-start | bytes 1572872 | tf_op jit(solution)/shard_map/ppermute | solution.py:104
  0.2 13.9 %collective-permute-start.3 = (f32[256,512]{1,0:T(8,128)}, f32[256,512]{1,0:T(8,128)S(1)}, u32[]{:S(2)}, u32[]{:S(2)}) collective-permute-start(f32[256,512]{1,0:T(8,128)} %own.3), channel_id=1, source_target_pairs={{0,24},{1,25},{2,26},{3,27},{4,28},{5,29},{6,30},{7,31},{8,0},{9,1... | collective-permute-start | bytes 1572872 | tf_op jit(solution)/shard_map/ppermute | solution.py:104
  3.5 5.1 %collective-permute-start = (s32[1,3]{1,0:T(1,128)}, s32[1,3]{1,0:T(1,128)S(1)}, u32[]{:S(2)}, u32[]{:S(2)}) collective-permute-start(s32[1,3]{1,0:T(1,128)} %offs_ref.11), channel_id=1, source_target_pairs={{0,4},{1,3},{2,6},{3,1},{4,0},{5,7},{6,2},{7,5},{8,12},{9,11},{10,... | collective-permute-start | bytes 44 | tf_op jit(solution)/shard_map/ppermute | solution.py:104
  3.8 1.9 %copy-start = (f32[1,3,512,512]{3,2,1,0:T(8,128)S(1)}, f32[1,3,512,512]{3,2,1,0:T(8,128)}, u32[]{:S(2)}) copy-start(f32[1,3,512,512]{3,2,1,0:T(8,128)} %param.5) | copy-start | bytes 9437188
  5.7 1.0 copy-start.2
  6.7 21.3 %copy-start.4 = (s32[1,3]{1,0:T(1,128)S(1)}, s32[1,3]{1,0:T(1,128)}, u32[]{:S(2)}) copy-start(s32[1,3]{1,0:T(1,128)} %offs_ref.11) | copy-start | bytes 40
  8.6 25.3 %copy-start.3 = (f32[256,512]{1,0:T(8,128)S(1)}, f32[256,512]{1,0:T(8,128)}, u32[]{:S(2)}) copy-start(f32[256,512]{1,0:T(8,128)} %own.3) | copy-start | bytes 1572868
  8.7 19.3 %collective-permute-start.2 = (f32[2,256,512]{2,1,0:T(8,128)S(1)}, f32[2,256,512]{2,1,0:T(8,128)S(1)}, u32[]{:S(2)}, u32[]{:S(2)}) collective-permute-start(f32[2,256,512]{2,1,0:T(8,128)S(1)} %get-tuple-element.27.mine_ref), channel_id=1, source_target_pairs={{0,4},{1,3},{2,6},{3,1},{4,0},{5,7},{6,2},{7,5},{8,12},{9,11},{10,... | collective-permute-start | bytes 3145736 | tf_op jit(solution)/shard_map/ppermute | solution.py:104
  14.1 13.2 %collective-permute-start.4 = (f32[256,512]{1,0:T(8,128)S(1)}, f32[256,512]{1,0:T(8,128)S(1)}, u32[]{:S(2)}, u32[]{:S(2)}) collective-permute-start(f32[256,512]{1,0:T(8,128)S(1)} %collective-permute-done.1.refs_1_.first), channel_id=1, source_target_pairs={{0,24},{1,25},{2,26},{3,27},{4,28},{5,29},{6,30},{7,31},{8,0},{9,1... | collective-permute-start | bytes 1572872 | tf_op jit(solution)/shard_map/ppermute | solution.py:104
  27.3 6.6 %collective-permute-start.5 = (f32[256,512]{1,0:T(8,128)S(1)}, f32[256,512]{1,0:T(8,128)S(1)}, u32[]{:S(2)}, u32[]{:S(2)}) collective-permute-start(f32[256,512]{1,0:T(8,128)S(1)} %collective-permute-done.4.refs_3_.both), channel_id=1, source_target_pairs={{2,26},{5,29},{10,2},{13,5},{18,10},{21,13},{26,18},{29,21}} | collective-permute-start | bytes 1572872 | tf_op jit(solution)/shard_map/ppermute | solution.py:104
  29.6 10.5 %collective-permute-start.8 = (f32[256,512]{1,0:T(8,128)S(1)}, f32[256,512]{1,0:T(8,128)S(1)}, u32[]{:S(2)}, u32[]{:S(2)}) collective-permute-start(f32[256,512]{1,0:T(8,128)S(1)} %get-tuple-element.33), channel_id=1, source_target_pairs={{0,2},{1,5},{2,0},{3,7},{4,6},{5,1},{6,4},{7,3},{8,10},{9,13},{10,... | collective-permute-start | bytes 1572872 | tf_op jit(solution)/shard_map/ppermute | solution.py:104
  33.2 6.9 %collective-permute-start.9 = (f32[256,512]{1,0:T(8,128)S(1)}, f32[256,512]{1,0:T(8,128)S(1)}, u32[]{:S(2)}, u32[]{:S(2)}) collective-permute-start(f32[256,512]{1,0:T(8,128)S(1)} %get-tuple-element.34), channel_id=1, source_target_pairs={{26,0},{29,1},{2,8},{5,9},{10,16},{13,17},{18,24},{21,25}} | collective-permute-start | bytes 1572872 | tf_op jit(solution)/shard_map/ppermute | solution.py:104
  34.0 18.7 %copy-start.1 = (f32[1,3,512,512]{3,2,1,0:T(8,128)S(1)}, f32[1,3,512,512]{3,2,1,0:T(8,128)}, u32[]{:S(2)}) copy-start(f32[1,3,512,512]{3,2,1,0:T(8,128)} %param.5) | copy-start | bytes 9437188
  34.6 18.0 %collective-permute-start.6 = (f32[2,256,512]{2,1,0:T(8,128)S(1)}, f32[2,256,512]{2,1,0:T(8,128)S(1)}, u32[]{:S(2)}, u32[]{:S(2)}) collective-permute-start(f32[2,256,512]{2,1,0:T(8,128)S(1)} %choose.2), channel_id=1, source_target_pairs={{0,4},{1,3},{2,6},{3,1},{4,0},{5,7},{6,2},{7,5},{8,12},{9,11},{10,... | collective-permute-start | bytes 3145736 | tf_op jit(solution)/shard_map/ppermute | solution.py:104
  38.4 16.3 %collective-permute-start.7 = (f32[256,512]{1,0:T(8,128)S(1)}, f32[256,512]{1,0:T(8,128)S(1)}, u32[]{:S(2)}, u32[]{:S(2)}) collective-permute-start(f32[256,512]{1,0:T(8,128)S(1)} %get-tuple-element.31), channel_id=1, source_target_pairs={{0,2},{1,5},{2,0},{3,7},{4,6},{5,1},{6,4},{7,3},{8,10},{9,13},{10,... | collective-permute-start | bytes 1572872 | tf_op jit(solution)/shard_map/ppermute | solution.py:104
  40.3 14.5 %collective-permute-start.10 = (f32[256,512]{1,0:T(8,128)S(1)}, f32[256,512]{1,0:T(8,128)S(1)}, u32[]{:S(2)}, u32[]{:S(2)}) collective-permute-start(f32[256,512]{1,0:T(8,128)S(1)} %add_add_fusion), channel_id=1, source_target_pairs={{24,0},{25,1},{26,2},{27,3},{28,4},{29,5},{30,6},{31,7},{0,8},{1,9... | collective-permute-start | bytes 1572872 | tf_op jit(solution)/shard_map/ppermute | solution.py:104
  55.0 13.1 %collective-permute-start.12 = (f32[256,512]{1,0:T(8,128)S(1)}, f32[256,512]{1,0:T(8,128)S(1)}, u32[]{:S(2)}, u32[]{:S(2)}) collective-permute-start(f32[256,512]{1,0:T(8,128)S(1)} %add_add_fusion.1.refs_0_.image_ref.own), channel_id=1, source_target_pairs={{0,24},{1,25},{2,26},{3,27},{4,28},{5,29},{6,30},{7,31},{8,0},{9,1... | collective-permute-start | bytes 1572872 | tf_op jit(solution)/shard_map/ppermute | solution.py:104
  59.0 18.3 %collective-permute-start.11 = (f32[256,512]{1,0:T(8,128)S(1)}, f32[256,512]{1,0:T(8,128)S(1)}, u32[]{:S(2)}, u32[]{:S(2)}) collective-permute-start(f32[256,512]{1,0:T(8,128)S(1)} %add_add_fusion.1.refs_0_.image_ref.own), channel_id=1, source_target_pairs={{0,2},{1,5},{2,0},{3,7},{4,6},{5,1},{6,4},{7,3},{8,10},{9,13},{10,... | collective-permute-start | bytes 1572872 | tf_op jit(solution)/shard_map/ppermute | solution.py:104
  68.0 16.1 %collective-permute-start.13 = (f32[256,512]{1,0:T(8,128)S(1)}, f32[256,512]{1,0:T(8,128)S(1)}, u32[]{:S(2)}, u32[]{:S(2)}) collective-permute-start(f32[256,512]{1,0:T(8,128)S(1)} %collective-permute-done.12.refs_2_.group), channel_id=1, source_target_pairs={{0,2},{1,5},{2,0},{3,7},{4,6},{5,1},{6,4},{7,3},{8,10},{9,13},{10,... | collective-permute-start | bytes 1572872 | tf_op jit(solution)/shard_map/ppermute | solution.py:104
  84.8 20.8 %collective-permute-start.16 = (f32[2,256,512]{2,1,0:T(8,128)S(1)}, f32[2,256,512]{2,1,0:T(8,128)S(1)}, u32[]{:S(2)}, u32[]{:S(2)}) collective-permute-start(f32[2,256,512]{2,1,0:T(8,128)S(1)} %choose.3.refs_1_), channel_id=1, source_target_pairs={{0,4},{1,3},{2,6},{3,1},{4,0},{5,7},{6,2},{7,5},{8,12},{9,11},{10,... | collective-permute-start | bytes 3145736 | tf_op jit(solution)/shard_map/ppermute | solution.py:104
  90.1 6.3 %collective-permute-start.14 = (f32[1,256,512]{2,1,0:T(8,128)S(1)}, f32[1,256,512]{2,1,0:T(8,128)S(1)}, u32[]{:S(2)}, u32[]{:S(2)}) collective-permute-start(f32[1,256,512]{2,1,0:T(8,128)S(1)} %get-tuple-element.37), channel_id=1, source_target_pairs={{0,1},{1,0},{2,3},{3,2},{4,5},{5,4},{6,7},{7,6},{8,9},{9,8},{10,11... | collective-permute-start | bytes 1572872 | tf_op jit(solution)/shard_map/ppermute | solution.py:400
  94.5 11.1 %collective-permute-start.15 = (f32[256,512]{1,0:T(8,128)S(1)}, f32[256,512]{1,0:T(8,128)S(1)}, u32[]{:S(2)}, u32[]{:S(2)}) collective-permute-start(f32[256,512]{1,0:T(8,128)S(1)} %collective-permute-done.13.refs_3_.both), channel_id=1, source_target_pairs={{2,30},{5,31},{10,6},{13,7},{18,14},{21,15},{26,22},{29,23}} | collective-permute-start | bytes 1572872 | tf_op jit(solution)/shard_map/ppermute | solution.py:104
  107.6 6.5 %collective-permute-start.17 = (f32[2,256,512]{2,1,0:T(8,128)S(1)}, f32[2,256,512]{2,1,0:T(8,128)S(1)}, u32[]{:S(2)}, u32[]{:S(2)}) collective-permute-start(f32[2,256,512]{2,1,0:T(8,128)S(1)} %get-tuple-element.44), channel_id=1, source_target_pairs={{0,1},{1,0},{2,3},{3,2},{4,5},{5,4},{6,7},{7,6},{8,9},{9,8},{10,11... | collective-permute-start | bytes 3145736 | tf_op jit(solution)/shard_map/ppermute | solution.py:400

commit v7 on v6

--- a/solution.py
+++ b/solution.py
@@ -88,7 +88,7 @@
                 target = back ^ first
                 use = (var & 3) == 0
             elif kind == "column":
-                target = back
+                target = (var - 8) % var_count
                 use = (var & 3) in wanted(first, last, 2)
             else:
                 target = back ^ last
@@ -411,10 +411,10 @@
     data_first = send(data, "first")
     own, far = forward(data, local_tiles)
     theirs = send(after(far, (offsets_next, data_first)), "last")
+    data_both = send(data_first, "group")
+    data_two = send(data_first, "column")
     data_group = send(data, "group")
-    data_both = send(after(data_first, data_group), "group")
-    data_two = send(data_both, "column")
-    own, bin_first, bin_group, bin_both, bin_two = make_bins(offsets, offsets_next, own, far, after(theirs, data_both))
+    own, bin_first, bin_group, bin_both, bin_two = make_bins(offsets, offsets_next, own, far, theirs)
     got_both = send(bin_both, "first")
     got_two = send(bin_two, "two", reverse=True)
     chosen = choose(offsets_next, data, data_first, data_group, data_both, data_two)

time: 116 us -> 125 us (1.078)
  waiting for transfers between devices: 44.2 us -> 63.7 us
  starting transfers between devices: 52.3 us -> 39.7 us
  Pallas kernels: 15.2 us -> 17.5 us
    ppermute x16, waiting for transfers between devices: 41.9 us -> 61.4 us  [send(): return lax.ppermute(value, ('var', 'samp'), pairs)]
    ppermute x16, starting transfers between devices: 43.7 us -> 35.3 us  [send(): return lax.ppermute(value, ('var', 'samp'), pairs)]
    ppermute x2, starting transfers between devices: 8.63 us -> 4.33 us  [swap(): return lax.ppermute(value, 'samp', [(0, 1), (1, 0)])]
    unnamed x10 -> x6, local copies, waits for them, and re-layouts: 2.95 us -> 1.9 us
  transfers between devices with their start and end apart: 18 -> 18, of which waited for: 7 -> 10; matrix products, arithmetic and copies ran while one was open for 0% -> 0% of each run, Pallas kernels for 9% -> 11%
where the time goes in v7:
time: 125 us; the launch traced here: 124 us
  waiting for transfers between devices  63.7 us (51%)
  starting transfers between devices  39.7 us (32%)
  Pallas kernels  17.5 us (14%)
  local copies, waits for them, and re-layouts  1.9 us (2%)
    ppermute x16, waiting for transfers between devices, send(): return lax.ppermute(value, ('var', 'samp'), pairs)  61.4 us
    ppermute x16, starting transfers between devices, send(): return lax.ppermute(value, ('var', 'samp'), pairs)  35.3 us
    ppermute x2, starting transfers between devices, swap(): return lax.ppermute(value, 'samp', [(0, 1), (1, 0)])  4.33 us
    pallas_call x1, Pallas kernels, right(): pl.pallas_call(functools.partial(right_kernel, slots, pair), in_specs=[sm...  3.54 us
    pallas_call x2, Pallas kernels, finish(): pl.pallas_call(functools.partial(finish_kernel, begin, factor), grid=(cou...  3.37 us
    pallas_call x1, Pallas kernels, backward(): pl.pallas_call(functools.partial(backward_kernel, slots), grid=(slots,),...  2.95 us
    pallas_call x1, Pallas kernels, forward(): pl.pallas_call(forward_kernel, grid=(slots,), in_specs=[pl.BlockSpec((row...  2.93 us
  transfers between devices with their start and end apart: 18, of which 10 were waited for; matrix products, arithmetic and copies ran while one was open for 0% of the time, Pallas kernels for 11%

profile of v7, /device:TPU:7, one launch (start us, length us, event | category | flops | bytes accessed | tf_op | source)
XLA Modules:
  0.0 123.9 jit_solution(12368331070292294278)
XLA Ops:
  0.3 1.9 %copy-done = f32[1,3,512,512]{3,2,1,0:T(8,128)S(1)} copy-done((f32[1,3,512,512]{3,2,1,0:T(8,128)S(1)}, f32[1,3,512,512]{3,2,1,0:T(8,128)}, u32[]{:S(2)}) %copy-start) | copy-done | bytes 3145752
  2.2 2.9 %forward.1 = (f32[256,512]{1,0:T(8,128)S(1)}, f32[2,256,512]{2,1,0:T(8,128)S(1)}) custom-call(f32[256,512]{1,0:T(8,128)} %own.3, f32[3,512,512]{2,1,0:T(8,128)S(1)} %bitcast.2), custom_call_target="tpu_custom_call" | custom-call | tf_op jit(solution)/shard_map/forward/pallas_call | solution.py:123
  5.1 3.4 %collective-permute-done.1.refs_1_.first = f32[256,512]{1,0:T(8,128)S(1)} collective-permute-done((f32[256,512]{1,0:T(8,128)}, f32[256,512]{1,0:T(8,128)S(1)}, u32[]{:S(2)}, u32[]{:S(2)}) %collective-permute-start.1) | collective-permute-done | bytes 524320 | tf_op jit(solution)/shard_map/ppermute | solution.py:104
  8.8 3.3 %collective-permute-start.3 = (f32[256,512]{1,0:T(8,128)}, f32[256,512]{1,0:T(8,128)S(1)}, u32[]{:S(2)}, u32[]{:S(2)}) collective-permute-start(f32[256,512]{1,0:T(8,128)} %own.3), channel_id=1, source_target_pairs={{0,24},{1,25},{2,26},{3,27},{4,28},{5,29},{6,30},{7,31},{8,0},{9,1... | collective-permute-start | bytes 1572872 | tf_op jit(solution)/shard_map/ppermute | solution.py:104
  13.0 9.5 %collective-permute-done.2.theirs_ref = f32[2,256,512]{2,1,0:T(8,128)S(1)} collective-permute-done((f32[2,256,512]{2,1,0:T(8,128)S(1)}, f32[2,256,512]{2,1,0:T(8,128)S(1)}, u32[]{:S(2)}, u32[]{:S(2)}) %collective-permute-start.2) | collective-permute-done | bytes 1048608 | tf_op jit(solution)/shard_map/ppermute | solution.py:104
  22.5 1.5 %bins.1 = (f32[256,512]{1,0:T(8,128)S(1)}, f32[256,512]{1,0:T(8,128)S(1)}, f32[256,512]{1,0:T(8,128)S(1)}, f32[256,512]{1,0:T(8,128)S(1)}, f32[256,512]{1,0:T(8,128)S(1)}) custom-call(s32[1,3]{1,0:T(1,128)S(1)} %copy-done.2, s32[1,3]{1,0:T(1,128)S(1)} %collective-permute-done.next_ref.offs_ref, f32[256,512]{1,0:T(8,128)S(1)} %get-tuple-element.23.own_in, ...), custom_call_target="tpu_custom_call" | custom-call | tf_op jit(solution)/shard_map/bins/pallas_call | solution.py:247
  25.0 8.0 %collective-permute-done.4.refs_3_.both = f32[256,512]{1,0:T(8,128)S(1)} collective-permute-done((f32[256,512]{1,0:T(8,128)S(1)}, f32[256,512]{1,0:T(8,128)S(1)}, u32[]{:S(2)}, u32[]{:S(2)}) %collective-permute-start.4) | collective-permute-done | bytes 524320 | tf_op jit(solution)/shard_map/ppermute | solution.py:104
  33.6 9.3 %collective-permute-start.6 = (f32[2,256,512]{2,1,0:T(8,128)S(1)}, f32[2,256,512]{2,1,0:T(8,128)S(1)}, u32[]{:S(2)}, u32[]{:S(2)}) collective-permute-start(f32[2,256,512]{2,1,0:T(8,128)S(1)} %choose.2), channel_id=1, source_target_pairs={{0,4},{1,3},{2,6},{3,1},{4,0},{5,7},{6,2},{7,5},{8,12},{9,11},{10,... | collective-permute-start | bytes 3145736 | tf_op jit(solution)/shard_map/ppermute | solution.py:104
  43.1 11.1 %collective-permute-start.10 = (f32[256,512]{1,0:T(8,128)S(1)}, f32[256,512]{1,0:T(8,128)S(1)}, u32[]{:S(2)}, u32[]{:S(2)}) collective-permute-start(f32[256,512]{1,0:T(8,128)S(1)} %add_add_fusion), channel_id=1, source_target_pairs={{24,0},{25,1},{26,2},{27,3},{28,4},{29,5},{30,6},{31,7},{0,8},{1,9... | collective-permute-start | bytes 1572872 | tf_op jit(solution)/shard_map/ppermute | solution.py:104
  54.2 6.8 %collective-permute-done.6.refs_0_ = f32[2,256,512]{2,1,0:T(8,128)S(1)} collective-permute-done((f32[2,256,512]{2,1,0:T(8,128)S(1)}, f32[2,256,512]{2,1,0:T(8,128)S(1)}, u32[]{:S(2)}, u32[]{:S(2)}) %collective-permute-start.6) | collective-permute-done | bytes 1048608 | tf_op jit(solution)/shard_map/ppermute | solution.py:104
  61.0 2.9 %backward.1 = f32[256,512]{1,0:T(8,128)S(1)} custom-call(s32[1,3]{1,0:T(1,128)S(1)} %copy-done.2, f32[3,512,512]{2,1,0:T(8,128)S(1)} %bitcast.3, f32[256,512]{1,0:T(8,128)} %own.3, f32[256,512]{1,0:T(8,128)S(1)} %collective-permute-done.1.refs_1_.first, f32[256,512]{1,0:T(8,128)S(1)} %collective-permute-done.3.refs_2_.group, ...), custom_call_target="tpu_custom_call" | custom-call | tf_op jit(solution)/shard_map/backward/pallas_call | solution.py:210
  64.0 1.5 %collective-permute-done.10 = f32[256,512]{1,0:T(8,128)S(1)} collective-permute-done((f32[256,512]{1,0:T(8,128)S(1)}, f32[256,512]{1,0:T(8,128)S(1)}, u32[]{:S(2)}, u32[]{:S(2)}) %collective-permute-start.10) | collective-permute-done | bytes 524320 | tf_op jit(solution)/shard_map/ppermute | solution.py:104
  65.8 7.8 %collective-permute-start.12 = (f32[256,512]{1,0:T(8,128)S(1)}, f32[256,512]{1,0:T(8,128)S(1)}, u32[]{:S(2)}, u32[]{:S(2)}) collective-permute-start(f32[256,512]{1,0:T(8,128)S(1)} %add_add_fusion.1.refs_0_.image_ref.own), channel_id=1, source_target_pairs={{0,24},{1,25},{2,26},{3,27},{4,28},{5,29},{6,30},{7,31},{8,0},{9,1... | collective-permute-start | bytes 1572872 | tf_op jit(solution)/shard_map/ppermute | solution.py:104
  73.5 13.1 %collective-permute-done.12.refs_2_.group = f32[256,512]{1,0:T(8,128)S(1)} collective-permute-done((f32[256,512]{1,0:T(8,128)S(1)}, f32[256,512]{1,0:T(8,128)S(1)}, u32[]{:S(2)}, u32[]{:S(2)}) %collective-permute-start.12) | collective-permute-done | bytes 524320 | tf_op jit(solution)/shard_map/ppermute | solution.py:104
  86.6 8.3 %collective-permute-done.13.refs_3_.both = f32[256,512]{1,0:T(8,128)S(1)} collective-permute-done((f32[256,512]{1,0:T(8,128)S(1)}, f32[256,512]{1,0:T(8,128)S(1)}, u32[]{:S(2)}, u32[]{:S(2)}) %collective-permute-start.13) | collective-permute-done | bytes 524320 | tf_op jit(solution)/shard_map/ppermute | solution.py:104
  95.8 3.5 %right.1 = (f32[1,256,512]{2,1,0:T(8,128)S(1)}, f32[1,256,512]{2,1,0:T(8,128)S(1)}, f32[2,256,512]{2,1,0:T(8,128)S(1)}, f32[2,256,512]{2,1,0:T(8,128)S(1)}, bf16...) custom-call(s32[1,3]{1,0:T(1,128)S(1)} %copy-done.2, f32[256,512]{1,0:T(8,128)} %own.3, ...), custom_call_target="tpu_custom_call" | custom-call | flops 26843545600 | tf_op jit(solution)/shard_map/right/pallas_call | solution.py:303
  99.3 1.6 %collective-permute-start.14 = (f32[1,256,512]{2,1,0:T(8,128)S(1)}, f32[1,256,512]{2,1,0:T(8,128)S(1)}, u32[]{:S(2)}, u32[]{:S(2)}) collective-permute-start(f32[1,256,512]{2,1,0:T(8,128)S(1)} %get-tuple-element.33), channel_id=1, source_target_pairs={{0,1},{1,0},{2,3},{3,2},{4,5},{5,4},{6,7},{7,6},{8,9},{9,8},{10,11... | collective-permute-start | bytes 1572872 | tf_op jit(solution)/shard_map/ppermute | solution.py:400
  102.9 1.6 %finish.2.refs_0_ = f32[3,256,512]{2,1,0:T(8,128)} custom-call(s32[1,3]{1,0:T(1,128)S(1)} %copy-done.2, f32[1]{0:T(128)S(6)} %copy.7.step_ref, f32[3,512,512]{2,1,0:T(8,128)S(1)} %bitcast.4, f32[1,256,512]{2,1,0:T(8,128)S(1)} %get-tuple-element.32.keep_ref, f32[1,256,512]{2,1,0:T(8,128)S(1)} %collective-permute-done.14.other_ref), custom_call_target="tpu_custom_call" | custom-call | tf_op jit(solution)/shard_map/finish/pallas_call | solution.py:382
  104.5 7.6 %collective-permute-done.15.two = f32[256,512]{1,0:T(8,128)S(1)} collective-permute-done((f32[256,512]{1,0:T(8,128)S(1)}, f32[256,512]{1,0:T(8,128)S(1)}, u32[]{:S(2)}, u32[]{:S(2)}) %collective-permute-start.15) | collective-permute-done | bytes 524320 | tf_op jit(solution)/shard_map/ppermute | solution.py:104
  112.1 3.1 %collective-permute-done.16.lasts_ref = f32[2,256,512]{2,1,0:T(8,128)S(1)} collective-permute-done((f32[2,256,512]{2,1,0:T(8,128)S(1)}, f32[2,256,512]{2,1,0:T(8,128)S(1)}, u32[]{:S(2)}, u32[]{:S(2)}) %collective-permute-start.16) | collective-permute-done | bytes 1048608 | tf_op jit(solution)/shard_map/ppermute | solution.py:104
  115.2 1.9 %left.1 = (f32[2,256,512]{2,1,0:T(8,128)S(1)}, f32[2,256,512]{2,1,0:T(8,128)S(1)}) custom-call(s32[1,3]{1,0:T(1,128)S(1)} %copy-done.2, f32[2,256,512]{2,1,0:T(8,128)S(1)} %get-tuple-element.34.keep_in, f32[2,256,512]{2,1,0:T(8,128)S(1)} %get-tuple-element.35.send_in, bf16[512,256]{1,0:T(8,128)(2,1)S(1)} %get-tuple-element.36.high_ref, ...), custom_call_target="tpu_custom_call" | custom-call | tf_op jit(solution)/shard_map/left/pallas_call | solution.py:341
  117.1 2.7 %collective-permute-start.17 = (f32[2,256,512]{2,1,0:T(8,128)S(1)}, f32[2,256,512]{2,1,0:T(8,128)S(1)}, u32[]{:S(2)}, u32[]{:S(2)}) collective-permute-start(f32[2,256,512]{2,1,0:T(8,128)S(1)} %get-tuple-element.40), channel_id=1, source_target_pairs={{0,1},{1,0},{2,3},{3,2},{4,5},{5,4},{6,7},{7,6},{8,9},{9,8},{10,11... | collective-permute-start | bytes 3145736 | tf_op jit(solution)/shard_map/ppermute | solution.py:400
  119.8 2.3 %collective-permute-done.17.other_ref = f32[2,256,512]{2,1,0:T(8,128)S(1)} collective-permute-done((f32[2,256,512]{2,1,0:T(8,128)S(1)}, f32[2,256,512]{2,1,0:T(8,128)S(1)}, u32[]{:S(2)}, u32[]{:S(2)}) %collective-permute-start.17) | collective-permute-done | bytes 1048608 | tf_op jit(solution)/shard_map/ppermute | solution.py:400
  122.1 1.8 %finish.3 = f32[3,256,512]{2,1,0:T(8,128)} custom-call(s32[1,3]{1,0:T(1,128)S(1)} %copy-done.2, f32[1]{0:T(128)S(6)} %copy.7.step_ref, f32[3,512,512]{2,1,0:T(8,128)S(1)} %bitcast.5, f32[2,256,512]{2,1,0:T(8,128)S(1)} %get-tuple-element.39.keep_ref, f32[2,256,512]{2,1,0:T(8,128)S(1)} %collective-permute-done.17.other_ref, ...), custom_call_target="tpu_custom_call", output_to_operand_aliasing={{}: (5, {})} | custom-call | tf_op jit(solution)/shard_map/finish/pallas_call | solution.py:382
  (29 shorter events, 5.6 us)
Async XLA Ops:
  0.0 8.5 %collective-permute-start.1 = (f32[256,512]{1,0:T(8,128)}, f32[256,512]{1,0:T(8,128)S(1)}, u32[]{:S(2)}, u32[]{:S(2)}) collective-permute-start(f32[256,512]{1,0:T(8,128)} %own.3), channel_id=1, source_target_pairs={{0,2},{1,5},{2,0},{3,7},{4,6},{5,1},{6,4},{7,3},{8,10},{9,13},{10,... | collective-permute-start | bytes 1572872 | tf_op jit(solution)/shard_map/ppermute | solution.py:104
  0.2 4.9 %collective-permute-start = (s32[1,3]{1,0:T(1,128)}, s32[1,3]{1,0:T(1,128)S(1)}, u32[]{:S(2)}, u32[]{:S(2)}) collective-permute-start(s32[1,3]{1,0:T(1,128)} %offs_ref.11), channel_id=1, source_target_pairs={{0,4},{1,3},{2,6},{3,1},{4,0},{5,7},{6,2},{7,5},{8,12},{9,11},{10,... | collective-permute-start | bytes 44 | tf_op jit(solution)/shard_map/ppermute | solution.py:104
  0.3 1.9 %copy-start = (f32[1,3,512,512]{3,2,1,0:T(8,128)S(1)}, f32[1,3,512,512]{3,2,1,0:T(8,128)}, u32[]{:S(2)}) copy-start(f32[1,3,512,512]{3,2,1,0:T(8,128)} %param.5) | copy-start | bytes 9437188
  2.1 20.3 %copy-start.2 = (s32[1,3]{1,0:T(1,128)S(1)}, s32[1,3]{1,0:T(1,128)}, u32[]{:S(2)}) copy-start(s32[1,3]{1,0:T(1,128)} %offs_ref.11) | copy-start | bytes 40
  8.5 13.9 %collective-permute-start.2 = (f32[2,256,512]{2,1,0:T(8,128)S(1)}, f32[2,256,512]{2,1,0:T(8,128)S(1)}, u32[]{:S(2)}, u32[]{:S(2)}) collective-permute-start(f32[2,256,512]{2,1,0:T(8,128)S(1)} %get-tuple-element.25.mine_ref), channel_id=1, source_target_pairs={{0,4},{1,3},{2,6},{3,1},{4,0},{5,7},{6,2},{7,5},{8,12},{9,11},{10,... | collective-permute-start | bytes 3145736 | tf_op jit(solution)/shard_map/ppermute | solution.py:104
  8.8 16.2 %collective-permute-start.3 = (f32[256,512]{1,0:T(8,128)}, f32[256,512]{1,0:T(8,128)S(1)}, u32[]{:S(2)}, u32[]{:S(2)}) collective-permute-start(f32[256,512]{1,0:T(8,128)} %own.3), channel_id=1, source_target_pairs={{0,24},{1,25},{2,26},{3,27},{4,28},{5,29},{6,30},{7,31},{8,0},{9,1... | collective-permute-start | bytes 1572872 | tf_op jit(solution)/shard_map/ppermute | solution.py:104
  12.1 12.9 %collective-permute-start.5 = (f32[256,512]{1,0:T(8,128)S(1)}, f32[256,512]{1,0:T(8,128)S(1)}, u32[]{:S(2)}, u32[]{:S(2)}) collective-permute-start(f32[256,512]{1,0:T(8,128)S(1)} %collective-permute-done.1.refs_1_.first), channel_id=1, source_target_pairs={{2,18},{5,21},{10,26},{13,29},{18,2},{21,5},{26,10},{29,13}} | collective-permute-start | bytes 1572872 | tf_op jit(solution)/shard_map/ppermute | solution.py:104
  12.8 20.2 %collective-permute-start.4 = (f32[256,512]{1,0:T(8,128)S(1)}, f32[256,512]{1,0:T(8,128)S(1)}, u32[]{:S(2)}, u32[]{:S(2)}) collective-permute-start(f32[256,512]{1,0:T(8,128)S(1)} %collective-permute-done.1.refs_1_.first), channel_id=1, source_target_pairs={{0,24},{1,25},{2,26},{3,27},{4,28},{5,29},{6,30},{7,31},{8,0},{9,1... | collective-permute-start | bytes 1572872 | tf_op jit(solution)/shard_map/ppermute | solution.py:104
  24.0 18.9 %collective-permute-start.8 = (f32[256,512]{1,0:T(8,128)S(1)}, f32[256,512]{1,0:T(8,128)S(1)}, u32[]{:S(2)}, u32[]{:S(2)}) collective-permute-start(f32[256,512]{1,0:T(8,128)S(1)} %get-tuple-element.29), channel_id=1, source_target_pairs={{0,2},{1,5},{2,0},{3,7},{4,6},{5,1},{6,4},{7,3},{8,10},{9,13},{10,... | collective-permute-start | bytes 1572872 | tf_op jit(solution)/shard_map/ppermute | solution.py:104
  24.3 18.6 %collective-permute-start.9 = (f32[256,512]{1,0:T(8,128)S(1)}, f32[256,512]{1,0:T(8,128)S(1)}, u32[]{:S(2)}, u32[]{:S(2)}) collective-permute-start(f32[256,512]{1,0:T(8,128)S(1)} %get-tuple-element.30), channel_id=1, source_target_pairs={{26,0},{29,1},{2,8},{5,9},{10,16},{13,17},{18,24},{21,25}} | collective-permute-start | bytes 1572872 | tf_op jit(solution)/shard_map/ppermute | solution.py:104
  33.0 28.0 %copy-start.1 = (f32[1,3,512,512]{3,2,1,0:T(8,128)S(1)}, f32[1,3,512,512]{3,2,1,0:T(8,128)}, u32[]{:S(2)}) copy-start(f32[1,3,512,512]{3,2,1,0:T(8,128)} %param.5) | copy-start | bytes 9437188
  33.6 27.4 %collective-permute-start.6 = (f32[2,256,512]{2,1,0:T(8,128)S(1)}, f32[2,256,512]{2,1,0:T(8,128)S(1)}, u32[]{:S(2)}, u32[]{:S(2)}) collective-permute-start(f32[2,256,512]{2,1,0:T(8,128)S(1)} %choose.2), channel_id=1, source_target_pairs={{0,4},{1,3},{2,6},{3,1},{4,0},{5,7},{6,2},{7,5},{8,12},{9,11},{10,... | collective-permute-start | bytes 3145736 | tf_op jit(solution)/shard_map/ppermute | solution.py:104
  42.9 21.1 %collective-permute-start.7 = (f32[256,512]{1,0:T(8,128)S(1)}, f32[256,512]{1,0:T(8,128)S(1)}, u32[]{:S(2)}, u32[]{:S(2)}) collective-permute-start(f32[256,512]{1,0:T(8,128)S(1)} %get-tuple-element.27), channel_id=1, source_target_pairs={{0,2},{1,5},{2,0},{3,7},{4,6},{5,1},{6,4},{7,3},{8,10},{9,13},{10,... | collective-permute-start | bytes 1572872 | tf_op jit(solution)/shard_map/ppermute | solution.py:104
  43.1 22.4 %collective-permute-start.10 = (f32[256,512]{1,0:T(8,128)S(1)}, f32[256,512]{1,0:T(8,128)S(1)}, u32[]{:S(2)}, u32[]{:S(2)}) collective-permute-start(f32[256,512]{1,0:T(8,128)S(1)} %add_add_fusion), channel_id=1, source_target_pairs={{24,0},{25,1},{26,2},{27,3},{28,4},{29,5},{30,6},{31,7},{0,8},{1,9... | collective-permute-start | bytes 1572872 | tf_op jit(solution)/shard_map/ppermute | solution.py:104
  65.8 20.9 %collective-permute-start.12 = (f32[256,512]{1,0:T(8,128)S(1)}, f32[256,512]{1,0:T(8,128)S(1)}, u32[]{:S(2)}, u32[]{:S(2)}) collective-permute-start(f32[256,512]{1,0:T(8,128)S(1)} %add_add_fusion.1.refs_0_.image_ref.own), channel_id=1, source_target_pairs={{0,24},{1,25},{2,26},{3,27},{4,28},{5,29},{6,30},{7,31},{8,0},{9,1... | collective-permute-start | bytes 1572872 | tf_op jit(solution)/shard_map/ppermute | solution.py:104
  73.5 13.1 %collective-permute-start.11 = (f32[256,512]{1,0:T(8,128)S(1)}, f32[256,512]{1,0:T(8,128)S(1)}, u32[]{:S(2)}, u32[]{:S(2)}) collective-permute-start(f32[256,512]{1,0:T(8,128)S(1)} %add_add_fusion.1.refs_0_.image_ref.own), channel_id=1, source_target_pairs={{0,2},{1,5},{2,0},{3,7},{4,6},{5,1},{6,4},{7,3},{8,10},{9,13},{10,... | collective-permute-start | bytes 1572872 | tf_op jit(solution)/shard_map/ppermute | solution.py:104
  86.6 8.3 %collective-permute-start.13 = (f32[256,512]{1,0:T(8,128)S(1)}, f32[256,512]{1,0:T(8,128)S(1)}, u32[]{:S(2)}, u32[]{:S(2)}) collective-permute-start(f32[256,512]{1,0:T(8,128)S(1)} %collective-permute-done.12.refs_2_.group), channel_id=1, source_target_pairs={{0,2},{1,5},{2,0},{3,7},{4,6},{5,1},{6,4},{7,3},{8,10},{9,13},{10,... | collective-permute-start | bytes 1572872 | tf_op jit(solution)/shard_map/ppermute | solution.py:104
  95.6 19.6 %collective-permute-start.16 = (f32[2,256,512]{2,1,0:T(8,128)S(1)}, f32[2,256,512]{2,1,0:T(8,128)S(1)}, u32[]{:S(2)}, u32[]{:S(2)}) collective-permute-start(f32[2,256,512]{2,1,0:T(8,128)S(1)} %choose.3.refs_1_), channel_id=1, source_target_pairs={{0,4},{1,3},{2,6},{3,1},{4,0},{5,7},{6,2},{7,5},{8,12},{9,11},{10,... | collective-permute-start | bytes 3145736 | tf_op jit(solution)/shard_map/ppermute | solution.py:104
  99.3 3.6 %collective-permute-start.14 = (f32[1,256,512]{2,1,0:T(8,128)S(1)}, f32[1,256,512]{2,1,0:T(8,128)S(1)}, u32[]{:S(2)}, u32[]{:S(2)}) collective-permute-start(f32[1,256,512]{2,1,0:T(8,128)S(1)} %get-tuple-element.33), channel_id=1, source_target_pairs={{0,1},{1,0},{2,3},{3,2},{4,5},{5,4},{6,7},{7,6},{8,9},{9,8},{10,11... | collective-permute-start | bytes 1572872 | tf_op jit(solution)/shard_map/ppermute | solution.py:400
  101.0 11.2 %collective-permute-start.15 = (f32[256,512]{1,0:T(8,128)S(1)}, f32[256,512]{1,0:T(8,128)S(1)}, u32[]{:S(2)}, u32[]{:S(2)}) collective-permute-start(f32[256,512]{1,0:T(8,128)S(1)} %collective-permute-done.13.refs_3_.both), channel_id=1, source_target_pairs={{2,30},{5,31},{10,6},{13,7},{18,14},{21,15},{26,22},{29,23}} | collective-permute-start | bytes 1572872 | tf_op jit(solution)/shard_map/ppermute | solution.py:104
  117.1 5.0 %collective-permute-start.17 = (f32[2,256,512]{2,1,0:T(8,128)S(1)}, f32[2,256,512]{2,1,0:T(8,128)S(1)}, u32[]{:S(2)}, u32[]{:S(2)}) collective-permute-start(f32[2,256,512]{2,1,0:T(8,128)S(1)} %get-tuple-element.40), channel_id=1, source_target_pairs={{0,1},{1,0},{2,3},{3,2},{4,5},{5,4},{6,7},{7,6},{8,9},{9,8},{10,11... | collective-permute-start | bytes 3145736 | tf_op jit(solution)/shard_map/ppermute | solution.py:400

commit v8 on v7

--- a/solution.py
+++ b/solution.py
@@ -104,37 +104,26 @@
     return lax.ppermute(value, ("var", "samp"), pairs)
 
 
-def forward_kernel(data_ref, tile_ref, own_ref, far_ref):
+def forward_kernel(data_ref, tile_ref, *out_refs):
     slot = pl.program_id(0)
     value = dot3(split(data_ref[...]), split(tile_ref[...]), NN)
-
-    @pl.when(slot == 0)
-    def _():
-        own_ref[...] = value
-
-    @pl.when(slot > 0)
-    def _():
-        far_ref[...] = value
+    for which, ref in enumerate(out_refs):
+
+        @pl.when(slot == which)
+        def _():
+            ref[...] = value
 
 
 def forward(data, tiles):
     slots, block = tiles.shape[:2]
     rows = data.shape[0]
+    flat = pl.BlockSpec((rows, block), lambda j: (0, 0))
     return pl.pallas_call(
         forward_kernel,
         grid=(slots,),
-        in_specs=[
-            pl.BlockSpec((rows, block), lambda j: (0, 0)),
-            pl.BlockSpec((None, block, block), lambda j: (j, 0, 0)),
-        ],
-        out_specs=[
-            pl.BlockSpec((rows, block), lambda j: (0, 0)),
-            pl.BlockSpec((None, rows, block), lambda j: (jnp.maximum(j - 1, 0), 0, 0)),
-        ],
-        out_shape=[
-            jax.ShapeDtypeStruct((rows, block), f32),
-            jax.ShapeDtypeStruct((slots - 1, rows, block), f32),
-        ],
+        in_specs=[flat, pl.BlockSpec((None, block, block), lambda j: (j, 0, 0))],
+        out_specs=[flat] * slots,
+        out_shape=[jax.ShapeDtypeStruct((rows, block), f32)] * slots,
         compiler_params=params(),
         cost_estimate=cost(6 * slots * rows * block * block, 4 * slots * block * (block + 2 * rows)),
         name="forward",
@@ -221,39 +210,40 @@
     )(offsets, tiles, *sources)
 
 
-def bins_kernel(slots, offs_ref, next_ref, own_in, mine_ref, theirs_ref, own_out, first, group, both, two):
+def bins_kernel(slots, offs_ref, next_ref, own_in, *refs):
     p, flip = place()
     target = last_partner(p, flip)
+    mine, theirs, outs = refs[:slots], refs[slots : 2 * slots], refs[2 * slots :]
     totals = [own_in[...], None, None, None, None]
     for which, value in enumerate((0, 1, 2, 3, 5)):
         total = totals[which]
         for slot in range(slots):
-            for there, offs, source in ((0, offs_ref, mine_ref), (1, next_ref, theirs_ref)):
+            for there, offs, source in ((0, offs_ref, mine), (1, next_ref, theirs)):
                 offset = offs[0, slot + 1]
                 last, code = route(jnp.where(there == 1, target, p), offset, flip)
                 use = (last == there) & (code == value) & (offset > 0)
-                term = jnp.where(use, source[slot], 0.0)
+                term = jnp.where(use, source[slot][...], 0.0)
                 total = term if total is None else total + term
         totals[which] = total
-    for ref, total in zip((own_out, first, group, both, two), totals):
+    for ref, total in zip(outs, totals):
         ref[...] = total
 
 
 def make_bins(offsets, offsets_next, own, mine, theirs):
-    slots, rows, block = mine.shape
+    slots = len(mine)
+    rows, block = own.shape
     step = rows // 4
     flat = pl.BlockSpec((step, block), lambda i: (i, 0))
-    deep = pl.BlockSpec((slots, step, block), lambda i: (0, i, 0))
     return pl.pallas_call(
         functools.partial(bins_kernel, slots),
         grid=(rows // step,),
-        in_specs=[smem_spec(), smem_spec(), flat, deep, deep],
+        in_specs=[smem_spec(), smem_spec()] + [flat] * (1 + 2 * slots),
         out_specs=[flat] * 5,
         out_shape=[jax.ShapeDtypeStruct((rows, block), f32)] * 5,
         compiler_params=params(),
         cost_estimate=cost(20 * rows * block, 40 * rows * block),
         name="bins",
-    )(offsets, offsets_next, own, mine, theirs)
+    )(offsets, offsets_next, own, *mine, *theirs)
 
 
 def halves(pair):
@@ -409,11 +399,11 @@
 
     offsets_next = send(offsets, "last")
     data_first = send(data, "first")
-    own, far = forward(data, local_tiles)
-    theirs = send(after(far, (offsets_next, data_first)), "last")
-    data_both = send(data_first, "group")
+    own, *far = forward(data, local_tiles)
+    theirs = [send(after(each, (offsets_next, data_first)), "last") for each in far]
+    data_group = send(data, "group")
+    data_both = send(data_group, "first")
     data_two = send(data_first, "column")
-    data_group = send(data, "group")
     own, bin_first, bin_group, bin_both, bin_two = make_bins(offsets, offsets_next, own, far, theirs)
     got_both = send(bin_both, "first")
     got_two = send(bin_two, "two", reverse=True)

time: 125 us -> 112 us (0.90)
  starting transfers between devices: 39.7 us -> 29.8 us
  Pallas kernels: 17.5 us -> 15.2 us
    ppermute x16 -> x17, starting transfers between devices: 35.3 us -> 22.5 us  [send(): return lax.ppermute(value, ('var', 'samp'), pairs)]
    ppermute x2, starting transfers between devices: 4.33 us -> 7.32 us  [swap(): return lax.ppermute(value, 'samp', [(0, 1), (1, 0)])]
    unnamed x6 -> x10, local copies, waits for them, and re-layouts: 1.9 us -> 2.95 us
    ppermute x16 -> x17, waiting for transfers between devices: 61.4 us -> 60.4 us  [send(): return lax.ppermute(value, ('var', 'samp'), pairs)]
  transfers between devices with their start and end apart: 18 -> 19, of which waited for: 10 -> 9; matrix products, arithmetic and copies ran while one was open for 0% -> 0% of each run, Pallas kernels for 11% -> 10%
where the time goes in v8:
time: 112 us
  waiting for transfers between devices  62.7 us (56%)
  starting transfers between devices  29.8 us (27%)
  Pallas kernels  15.2 us (14%)
  local copies, waits for them, and re-layouts  2.95 us (3%)
    ppermute x17, waiting for transfers between devices, send(): return lax.ppermute(value, ('var', 'samp'), pairs)  60.4 us
    ppermute x17, starting transfers between devices, send(): return lax.ppermute(value, ('var', 'samp'), pairs)  22.5 us
    ppermute x2, starting transfers between devices, swap(): return lax.ppermute(value, 'samp', [(0, 1), (1, 0)])  7.32 us
    pallas_call x2, Pallas kernels, finish(): pl.pallas_call(functools.partial(finish_kernel, begin, factor), grid=(cou...  3.37 us
    pallas_call x1, Pallas kernels, right(): pl.pallas_call(functools.partial(right_kernel, slots, pair), in_specs=[sm...  3.1 us
    unnamed x10, local copies, waits for them, and re-layouts  2.95 us
    ppermute x2, waiting for transfers between devices, swap(): return lax.ppermute(value, 'samp', [(0, 1), (1, 0)])  2.29 us
  transfers between devices with their start and end apart: 19, of which 9 were waited for; matrix products, arithmetic and copies ran while one was open for 0% of the time, Pallas kernels for 10%

profile of v8, /device:TPU:7, one launch (start us, length us, event | category | flops | bytes accessed | tf_op | source)
XLA Modules:
  0.0 111.9 jit_solution(5436553489347829244)
XLA Ops:
  0.2 3.3 %collective-permute-start.4 = (f32[256,512]{1,0:T(8,128)}, f32[256,512]{1,0:T(8,128)S(1)}, u32[]{:S(2)}, u32[]{:S(2)}) collective-permute-start(f32[256,512]{1,0:T(8,128)} %own.3), channel_id=1, source_target_pairs={{0,24},{1,25},{2,26},{3,27},{4,28},{5,29},{6,30},{7,31},{8,0},{9,1... | collective-permute-start | bytes 1572872 | tf_op jit(solution)/shard_map/ppermute | solution.py:104
  3.8 1.9 %copy-done = f32[1,3,512,512]{3,2,1,0:T(8,128)S(1)} copy-done((f32[1,3,512,512]{3,2,1,0:T(8,128)S(1)}, f32[1,3,512,512]{3,2,1,0:T(8,128)}, u32[]{:S(2)}) %copy-start) | copy-done | bytes 3145752
  6.7 1.9 %forward.1 = (f32[256,512]{1,0:T(8,128)S(1)}, f32[256,512]{1,0:T(8,128)S(1)}, f32[256,512]{1,0:T(8,128)S(1)}) custom-call(f32[256,512]{1,0:T(8,128)S(1)} %copy-done.2, f32[3,512,512]{2,1,0:T(8,128)S(1)} %bitcast.2), custom_call_target="tpu_custom_call" | custom-call | tf_op jit(solution)/shard_map/forward/pallas_call | solution.py:121
  10.2 3.9 %collective-permute-done.4.refs_2_.group = f32[256,512]{1,0:T(8,128)S(1)} collective-permute-done((f32[256,512]{1,0:T(8,128)}, f32[256,512]{1,0:T(8,128)S(1)}, u32[]{:S(2)}, u32[]{:S(2)}) %collective-permute-start.4) | collective-permute-done | bytes 524320 | tf_op jit(solution)/shard_map/ppermute | solution.py:104
  14.1 2.4 %collective-permute-start.5 = (f32[256,512]{1,0:T(8,128)S(1)}, f32[256,512]{1,0:T(8,128)S(1)}, u32[]{:S(2)}, u32[]{:S(2)}) collective-permute-start(f32[256,512]{1,0:T(8,128)S(1)} %collective-permute-done.4.refs_2_.group), channel_id=1, source_target_pairs={{0,2},{1,5},{2,0},{3,7},{4,6},{5,1},{6,4},{7,3},{8,10},{9,13},{10,... | collective-permute-start | bytes 1572872 | tf_op jit(solution)/shard_map/ppermute | solution.py:104
  17.2 8.9 %collective-permute-done.2.refs_2_ = f32[256,512]{1,0:T(8,128)S(1)} collective-permute-done((f32[256,512]{1,0:T(8,128)S(1)}, f32[256,512]{1,0:T(8,128)S(1)}, u32[]{:S(2)}, u32[]{:S(2)}) %collective-permute-start.2) | collective-permute-done | bytes 524320 | tf_op jit(solution)/shard_map/ppermute | solution.py:104
  26.1 1.5 %bins.1 = (f32[256,512]{1,0:T(8,128)S(1)}, f32[256,512]{1,0:T(8,128)S(1)}, f32[256,512]{1,0:T(8,128)S(1)}, f32[256,512]{1,0:T(8,128)S(1)}, f32[256,512]{1,0:T(8,128)S(1)}) custom-call(s32[1,3]{1,0:T(1,128)S(1)} %copy-done.4, s32[1,3]{1,0:T(1,128)S(1)} %collective-permute-done.next_ref.offs_ref, f32[256,512]{1,0:T(8,128)S(1)} %get-tuple-element.25.own_in, ...), custom_call_target="tpu_custom_call" | custom-call | tf_op jit(solution)/shard_map/bins/pallas_call | solution.py:237
  27.6 1.3 %collective-permute-start.9 = (f32[256,512]{1,0:T(8,128)S(1)}, f32[256,512]{1,0:T(8,128)S(1)}, u32[]{:S(2)}, u32[]{:S(2)}) collective-permute-start(f32[256,512]{1,0:T(8,128)S(1)} %get-tuple-element.33), channel_id=1, source_target_pairs={{0,2},{1,5},{2,0},{3,7},{4,6},{5,1},{6,4},{7,3},{8,10},{9,13},{10,... | collective-permute-start | bytes 1572872 | tf_op jit(solution)/shard_map/ppermute | solution.py:104
  30.3 3.6 %collective-permute-start.7 = (f32[2,256,512]{2,1,0:T(8,128)S(1)}, f32[2,256,512]{2,1,0:T(8,128)S(1)}, u32[]{:S(2)}, u32[]{:S(2)}) collective-permute-start(f32[2,256,512]{2,1,0:T(8,128)S(1)} %choose.2), channel_id=1, source_target_pairs={{0,4},{1,3},{2,6},{3,1},{4,0},{5,7},{6,2},{7,5},{8,12},{9,11},{10,... | collective-permute-start | bytes 3145736 | tf_op jit(solution)/shard_map/ppermute | solution.py:104
  33.9 2.0 %collective-permute-done.9 = f32[256,512]{1,0:T(8,128)S(1)} collective-permute-done((f32[256,512]{1,0:T(8,128)S(1)}, f32[256,512]{1,0:T(8,128)S(1)}, u32[]{:S(2)}, u32[]{:S(2)}) %collective-permute-start.9) | collective-permute-done | bytes 524320 | tf_op jit(solution)/shard_map/ppermute | solution.py:104
  36.1 2.2 %collective-permute-start.11 = (f32[256,512]{1,0:T(8,128)S(1)}, f32[256,512]{1,0:T(8,128)S(1)}, u32[]{:S(2)}, u32[]{:S(2)}) collective-permute-start(f32[256,512]{1,0:T(8,128)S(1)} %add_add_fusion), channel_id=1, source_target_pairs={{24,0},{25,1},{26,2},{27,3},{28,4},{29,5},{30,6},{31,7},{0,8},{1,9... | collective-permute-start | bytes 1572872 | tf_op jit(solution)/shard_map/ppermute | solution.py:104
  38.3 19.1 %collective-permute-done.7.refs_0_ = f32[2,256,512]{2,1,0:T(8,128)S(1)} collective-permute-done((f32[2,256,512]{2,1,0:T(8,128)S(1)}, f32[2,256,512]{2,1,0:T(8,128)S(1)}, u32[]{:S(2)}, u32[]{:S(2)}) %collective-permute-start.7) | collective-permute-done | bytes 1048608 | tf_op jit(solution)/shard_map/ppermute | solution.py:104
  57.4 2.1 %backward.1 = f32[256,512]{1,0:T(8,128)S(1)} custom-call(s32[1,3]{1,0:T(1,128)S(1)} %copy-done.4, f32[3,512,512]{2,1,0:T(8,128)S(1)} %bitcast.3, f32[256,512]{1,0:T(8,128)S(1)} %copy-done.3, f32[256,512]{1,0:T(8,128)S(1)} %collective-permute-done.1.refs_1_.first, f32[256,512]{1,0:T(8,128)S(1)} %collective-permute-done.4.refs_2_.group, ...), custom_call_target="tpu_custom_call" | custom-call | tf_op jit(solution)/shard_map/backward/pallas_call | solution.py:199
  59.8 2.5 %collective-permute-start.13 = (f32[256,512]{1,0:T(8,128)S(1)}, f32[256,512]{1,0:T(8,128)S(1)}, u32[]{:S(2)}, u32[]{:S(2)}) collective-permute-start(f32[256,512]{1,0:T(8,128)S(1)} %add_add_fusion.1.refs_0_.image_ref.own), channel_id=1, source_target_pairs={{0,24},{1,25},{2,26},{3,27},{4,28},{5,29},{6,30},{7,31},{8,0},{9,1... | collective-permute-start | bytes 1572872 | tf_op jit(solution)/shard_map/ppermute | solution.py:104
  63.1 10.5 %collective-permute-done.13.refs_2_.group = f32[256,512]{1,0:T(8,128)S(1)} collective-permute-done((f32[256,512]{1,0:T(8,128)S(1)}, f32[256,512]{1,0:T(8,128)S(1)}, u32[]{:S(2)}, u32[]{:S(2)}) %collective-permute-start.13) | collective-permute-done | bytes 524320 | tf_op jit(solution)/shard_map/ppermute | solution.py:104
  74.1 7.8 %collective-permute-done.14.refs_3_.both = f32[256,512]{1,0:T(8,128)S(1)} collective-permute-done((f32[256,512]{1,0:T(8,128)S(1)}, f32[256,512]{1,0:T(8,128)S(1)}, u32[]{:S(2)}, u32[]{:S(2)}) %collective-permute-start.14) | collective-permute-done | bytes 524320 | tf_op jit(solution)/shard_map/ppermute | solution.py:104
  83.8 3.1 %right.1 = (f32[1,256,512]{2,1,0:T(8,128)S(1)}, f32[1,256,512]{2,1,0:T(8,128)S(1)}, f32[2,256,512]{2,1,0:T(8,128)S(1)}, f32[2,256,512]{2,1,0:T(8,128)S(1)}, bf16...) custom-call(s32[1,3]{1,0:T(1,128)S(1)} %copy-done.4, f32[256,512]{1,0:T(8,128)S(1)} %copy-done.3, ...), custom_call_target="tpu_custom_call" | custom-call | flops 26843545600 | tf_op jit(solution)/shard_map/right/pallas_call | solution.py:293
  86.9 3.6 %collective-permute-start.15 = (f32[1,256,512]{2,1,0:T(8,128)S(1)}, f32[1,256,512]{2,1,0:T(8,128)S(1)}, u32[]{:S(2)}, u32[]{:S(2)}) collective-permute-start(f32[1,256,512]{2,1,0:T(8,128)S(1)} %get-tuple-element.37), channel_id=1, source_target_pairs={{0,1},{1,0},{2,3},{3,2},{4,5},{5,4},{6,7},{7,6},{8,9},{9,8},{10,11... | collective-permute-start | bytes 1572872 | tf_op jit(solution)/shard_map/ppermute | solution.py:390
  92.5 1.6 %finish.2.refs_0_ = f32[3,256,512]{2,1,0:T(8,128)} custom-call(s32[1,3]{1,0:T(1,128)S(1)} %copy-done.4, f32[1]{0:T(128)S(6)} %copy.7.step_ref, f32[3,512,512]{2,1,0:T(8,128)S(1)} %bitcast.4, f32[1,256,512]{2,1,0:T(8,128)S(1)} %get-tuple-element.36.keep_ref, f32[1,256,512]{2,1,0:T(8,128)S(1)} %collective-permute-done.15.other_ref), custom_call_target="tpu_custom_call" | custom-call | tf_op jit(solution)/shard_map/finish/pallas_call | solution.py:372
  94.0 7.6 %collective-permute-done.16.two = f32[256,512]{1,0:T(8,128)S(1)} collective-permute-done((f32[256,512]{1,0:T(8,128)S(1)}, f32[256,512]{1,0:T(8,128)S(1)}, u32[]{:S(2)}, u32[]{:S(2)}) %collective-permute-start.16) | collective-permute-done | bytes 524320 | tf_op jit(solution)/shard_map/ppermute | solution.py:104
  102.2 1.9 %left.1 = (f32[2,256,512]{2,1,0:T(8,128)S(1)}, f32[2,256,512]{2,1,0:T(8,128)S(1)}) custom-call(s32[1,3]{1,0:T(1,128)S(1)} %copy-done.4, f32[2,256,512]{2,1,0:T(8,128)S(1)} %get-tuple-element.38.keep_in, f32[2,256,512]{2,1,0:T(8,128)S(1)} %get-tuple-element.39.send_in, bf16[512,256]{1,0:T(8,128)(2,1)S(1)} %get-tuple-element.40.high_ref, ...), custom_call_target="tpu_custom_call" | custom-call | tf_op jit(solution)/shard_map/left/pallas_call | solution.py:331
  104.1 3.7 %collective-permute-start.18 = (f32[2,256,512]{2,1,0:T(8,128)S(1)}, f32[2,256,512]{2,1,0:T(8,128)S(1)}, u32[]{:S(2)}, u32[]{:S(2)}) collective-permute-start(f32[2,256,512]{2,1,0:T(8,128)S(1)} %get-tuple-element.44), channel_id=1, source_target_pairs={{0,1},{1,0},{2,3},{3,2},{4,5},{5,4},{6,7},{7,6},{8,9},{9,8},{10,11... | collective-permute-start | bytes 3145736 | tf_op jit(solution)/shard_map/ppermute | solution.py:390
  107.8 2.3 %collective-permute-done.18.other_ref = f32[2,256,512]{2,1,0:T(8,128)S(1)} collective-permute-done((f32[2,256,512]{2,1,0:T(8,128)S(1)}, f32[2,256,512]{2,1,0:T(8,128)S(1)}, u32[]{:S(2)}, u32[]{:S(2)}) %collective-permute-start.18) | collective-permute-done | bytes 1048608 | tf_op jit(solution)/shard_map/ppermute | solution.py:390
  110.1 1.8 %finish.3 = f32[3,256,512]{2,1,0:T(8,128)} custom-call(s32[1,3]{1,0:T(1,128)S(1)} %copy-done.4, f32[1]{0:T(128)S(6)} %copy.7.step_ref, f32[3,512,512]{2,1,0:T(8,128)S(1)} %bitcast.5, f32[2,256,512]{2,1,0:T(8,128)S(1)} %get-tuple-element.43.keep_ref, f32[2,256,512]{2,1,0:T(8,128)S(1)} %collective-permute-done.18.other_ref, ...), custom_call_target="tpu_custom_call", output_to_operand_aliasing={{}: (5, {})} | custom-call | tf_op jit(solution)/shard_map/finish/pallas_call | solution.py:372
  (35 shorter events, 10.6 us)
Async XLA Ops:
  0.0 8.7 %collective-permute-start.1 = (f32[256,512]{1,0:T(8,128)}, f32[256,512]{1,0:T(8,128)S(1)}, u32[]{:S(2)}, u32[]{:S(2)}) collective-permute-start(f32[256,512]{1,0:T(8,128)} %own.3), channel_id=1, source_target_pairs={{0,2},{1,5},{2,0},{3,7},{4,6},{5,1},{6,4},{7,3},{8,10},{9,13},{10,... | collective-permute-start | bytes 1572872 | tf_op jit(solution)/shard_map/ppermute | solution.py:104
  0.2 13.9 %collective-permute-start.4 = (f32[256,512]{1,0:T(8,128)}, f32[256,512]{1,0:T(8,128)S(1)}, u32[]{:S(2)}, u32[]{:S(2)}) collective-permute-start(f32[256,512]{1,0:T(8,128)} %own.3), channel_id=1, source_target_pairs={{0,24},{1,25},{2,26},{3,27},{4,28},{5,29},{6,30},{7,31},{8,0},{9,1... | collective-permute-start | bytes 1572872 | tf_op jit(solution)/shard_map/ppermute | solution.py:104
  3.5 5.1 %collective-permute-start = (s32[1,3]{1,0:T(1,128)}, s32[1,3]{1,0:T(1,128)S(1)}, u32[]{:S(2)}, u32[]{:S(2)}) collective-permute-start(s32[1,3]{1,0:T(1,128)} %offs_ref.11), channel_id=1, source_target_pairs={{0,4},{1,3},{2,6},{3,1},{4,0},{5,7},{6,2},{7,5},{8,12},{9,11},{10,... | collective-permute-start | bytes 44 | tf_op jit(solution)/shard_map/ppermute | solution.py:104
  3.8 1.9 %copy-start = (f32[1,3,512,512]{3,2,1,0:T(8,128)S(1)}, f32[1,3,512,512]{3,2,1,0:T(8,128)}, u32[]{:S(2)}) copy-start(f32[1,3,512,512]{3,2,1,0:T(8,128)} %param.5) | copy-start | bytes 9437188
  5.7 1.0 copy-start.2
  6.7 19.4 %copy-start.4 = (s32[1,3]{1,0:T(1,128)S(1)}, s32[1,3]{1,0:T(1,128)}, u32[]{:S(2)}) copy-start(s32[1,3]{1,0:T(1,128)} %offs_ref.11) | copy-start | bytes 40
  8.6 21.0 %copy-start.3 = (f32[256,512]{1,0:T(8,128)S(1)}, f32[256,512]{1,0:T(8,128)}, u32[]{:S(2)}) copy-start(f32[256,512]{1,0:T(8,128)} %own.3) | copy-start | bytes 1572868
  8.7 8.5 %collective-permute-start.3 = (f32[256,512]{1,0:T(8,128)S(1)}, f32[256,512]{1,0:T(8,128)S(1)}, u32[]{:S(2)}, u32[]{:S(2)}) collective-permute-start(f32[256,512]{1,0:T(8,128)S(1)} %get-tuple-element.29.refs_1_), channel_id=1, source_target_pairs={{0,4},{1,3},{2,6},{3,1},{4,0},{5,7},{6,2},{7,5},{8,12},{9,11},{10,... | collective-permute-start | bytes 1572872 | tf_op jit(solution)/shard_map/ppermute | solution.py:104
  9.9 16.2 %collective-permute-start.2 = (f32[256,512]{1,0:T(8,128)S(1)}, f32[256,512]{1,0:T(8,128)S(1)}, u32[]{:S(2)}, u32[]{:S(2)}) collective-permute-start(f32[256,512]{1,0:T(8,128)S(1)} %get-tuple-element.28.refs_0_), channel_id=1, source_target_pairs={{0,4},{1,3},{2,6},{3,1},{4,0},{5,7},{6,2},{7,5},{8,12},{9,11},{10,... | collective-permute-start | bytes 1572872 | tf_op jit(solution)/shard_map/ppermute | solution.py:104
  14.1 15.5 %collective-permute-start.5 = (f32[256,512]{1,0:T(8,128)S(1)}, f32[256,512]{1,0:T(8,128)S(1)}, u32[]{:S(2)}, u32[]{:S(2)}) collective-permute-start(f32[256,512]{1,0:T(8,128)S(1)} %collective-permute-done.4.refs_2_.group), channel_id=1, source_target_pairs={{0,2},{1,5},{2,0},{3,7},{4,6},{5,1},{6,4},{7,3},{8,10},{9,13},{10,... | collective-permute-start | bytes 1572872 | tf_op jit(solution)/shard_map/ppermute | solution.py:104
  16.5 13.1 %collective-permute-start.6 = (f32[256,512]{1,0:T(8,128)S(1)}, f32[256,512]{1,0:T(8,128)S(1)}, u32[]{:S(2)}, u32[]{:S(2)}) collective-permute-start(f32[256,512]{1,0:T(8,128)S(1)} %collective-permute-done.1.refs_1_.first), channel_id=1, source_target_pairs={{2,18},{5,21},{10,26},{13,29},{18,2},{21,5},{26,10},{29,13}} | collective-permute-start | bytes 1572872 | tf_op jit(solution)/shard_map/ppermute | solution.py:104
  27.6 8.4 %collective-permute-start.9 = (f32[256,512]{1,0:T(8,128)S(1)}, f32[256,512]{1,0:T(8,128)S(1)}, u32[]{:S(2)}, u32[]{:S(2)}) collective-permute-start(f32[256,512]{1,0:T(8,128)S(1)} %get-tuple-element.33), channel_id=1, source_target_pairs={{0,2},{1,5},{2,0},{3,7},{4,6},{5,1},{6,4},{7,3},{8,10},{9,13},{10,... | collective-permute-start | bytes 1572872 | tf_op jit(solution)/shard_map/ppermute | solution.py:104
  28.9 7.1 %collective-permute-start.10 = (f32[256,512]{1,0:T(8,128)S(1)}, f32[256,512]{1,0:T(8,128)S(1)}, u32[]{:S(2)}, u32[]{:S(2)}) collective-permute-start(f32[256,512]{1,0:T(8,128)S(1)} %get-tuple-element.34), channel_id=1, source_target_pairs={{26,0},{29,1},{2,8},{5,9},{10,16},{13,17},{18,24},{21,25}} | collective-permute-start | bytes 1572872 | tf_op jit(solution)/shard_map/ppermute | solution.py:104
  29.6 27.8 %copy-start.1 = (f32[1,3,512,512]{3,2,1,0:T(8,128)S(1)}, f32[1,3,512,512]{3,2,1,0:T(8,128)}, u32[]{:S(2)}) copy-start(f32[1,3,512,512]{3,2,1,0:T(8,128)} %param.5) | copy-start | bytes 9437188
  30.3 27.1 %collective-permute-start.7 = (f32[2,256,512]{2,1,0:T(8,128)S(1)}, f32[2,256,512]{2,1,0:T(8,128)S(1)}, u32[]{:S(2)}, u32[]{:S(2)}) collective-permute-start(f32[2,256,512]{2,1,0:T(8,128)S(1)} %choose.2), channel_id=1, source_target_pairs={{0,4},{1,3},{2,6},{3,1},{4,0},{5,7},{6,2},{7,5},{8,12},{9,11},{10,... | collective-permute-start | bytes 3145736 | tf_op jit(solution)/shard_map/ppermute | solution.py:104
  33.9 25.6 %collective-permute-start.8 = (f32[256,512]{1,0:T(8,128)S(1)}, f32[256,512]{1,0:T(8,128)S(1)}, u32[]{:S(2)}, u32[]{:S(2)}) collective-permute-start(f32[256,512]{1,0:T(8,128)S(1)} %get-tuple-element.31), channel_id=1, source_target_pairs={{0,2},{1,5},{2,0},{3,7},{4,6},{5,1},{6,4},{7,3},{8,10},{9,13},{10,... | collective-permute-start | bytes 1572872 | tf_op jit(solution)/shard_map/ppermute | solution.py:104
  36.1 23.4 %collective-permute-start.11 = (f32[256,512]{1,0:T(8,128)S(1)}, f32[256,512]{1,0:T(8,128)S(1)}, u32[]{:S(2)}, u32[]{:S(2)}) collective-permute-start(f32[256,512]{1,0:T(8,128)S(1)} %add_add_fusion), channel_id=1, source_target_pairs={{24,0},{25,1},{26,2},{27,3},{28,4},{29,5},{30,6},{31,7},{0,8},{1,9... | collective-permute-start | bytes 1572872 | tf_op jit(solution)/shard_map/ppermute | solution.py:104
  59.8 13.8 %collective-permute-start.13 = (f32[256,512]{1,0:T(8,128)S(1)}, f32[256,512]{1,0:T(8,128)S(1)}, u32[]{:S(2)}, u32[]{:S(2)}) collective-permute-start(f32[256,512]{1,0:T(8,128)S(1)} %add_add_fusion.1.refs_0_.image_ref.own), channel_id=1, source_target_pairs={{0,24},{1,25},{2,26},{3,27},{4,28},{5,29},{6,30},{7,31},{8,0},{9,1... | collective-permute-start | bytes 1572872 | tf_op jit(solution)/shard_map/ppermute | solution.py:104
  62.3 11.8 %collective-permute-start.12 = (f32[256,512]{1,0:T(8,128)S(1)}, f32[256,512]{1,0:T(8,128)S(1)}, u32[]{:S(2)}, u32[]{:S(2)}) collective-permute-start(f32[256,512]{1,0:T(8,128)S(1)} %add_add_fusion.1.refs_0_.image_ref.own), channel_id=1, source_target_pairs={{0,2},{1,5},{2,0},{3,7},{4,6},{5,1},{6,4},{7,3},{8,10},{9,13},{10,... | collective-permute-start | bytes 1572872 | tf_op jit(solution)/shard_map/ppermute | solution.py:104
  73.6 8.3 %collective-permute-start.14 = (f32[256,512]{1,0:T(8,128)S(1)}, f32[256,512]{1,0:T(8,128)S(1)}, u32[]{:S(2)}, u32[]{:S(2)}) collective-permute-start(f32[256,512]{1,0:T(8,128)S(1)} %collective-permute-done.13.refs_2_.group), channel_id=1, source_target_pairs={{0,2},{1,5},{2,0},{3,7},{4,6},{5,1},{6,4},{7,3},{8,10},{9,13},{10,... | collective-permute-start | bytes 1572872 | tf_op jit(solution)/shard_map/ppermute | solution.py:104
  82.6 19.6 %collective-permute-start.17 = (f32[2,256,512]{2,1,0:T(8,128)S(1)}, f32[2,256,512]{2,1,0:T(8,128)S(1)}, u32[]{:S(2)}, u32[]{:S(2)}) collective-permute-start(f32[2,256,512]{2,1,0:T(8,128)S(1)} %choose.3.refs_1_), channel_id=1, source_target_pairs={{0,4},{1,3},{2,6},{3,1},{4,0},{5,7},{6,2},{7,5},{8,12},{9,11},{10,... | collective-permute-start | bytes 3145736 | tf_op jit(solution)/shard_map/ppermute | solution.py:104
  86.9 5.6 %collective-permute-start.15 = (f32[1,256,512]{2,1,0:T(8,128)S(1)}, f32[1,256,512]{2,1,0:T(8,128)S(1)}, u32[]{:S(2)}, u32[]{:S(2)}) collective-permute-start(f32[1,256,512]{2,1,0:T(8,128)S(1)} %get-tuple-element.37), channel_id=1, source_target_pairs={{0,1},{1,0},{2,3},{3,2},{4,5},{5,4},{6,7},{7,6},{8,9},{9,8},{10,11... | collective-permute-start | bytes 1572872 | tf_op jit(solution)/shard_map/ppermute | solution.py:390
  90.5 11.2 %collective-permute-start.16 = (f32[256,512]{1,0:T(8,128)S(1)}, f32[256,512]{1,0:T(8,128)S(1)}, u32[]{:S(2)}, u32[]{:S(2)}) collective-permute-start(f32[256,512]{1,0:T(8,128)S(1)} %collective-permute-done.14.refs_3_.both), channel_id=1, source_target_pairs={{2,30},{5,31},{10,6},{13,7},{18,14},{21,15},{26,22},{29,23}} | collective-permute-start | bytes 1572872 | tf_op jit(solution)/shard_map/ppermute | solution.py:104
  104.1 6.0 %collective-permute-start.18 = (f32[2,256,512]{2,1,0:T(8,128)S(1)}, f32[2,256,512]{2,1,0:T(8,128)S(1)}, u32[]{:S(2)}, u32[]{:S(2)}) collective-permute-start(f32[2,256,512]{2,1,0:T(8,128)S(1)} %get-tuple-element.44), channel_id=1, source_target_pairs={{0,1},{1,0},{2,3},{3,2},{4,5},{5,4},{6,7},{7,6},{8,9},{9,8},{10,11... | collective-permute-start | bytes 3145736 | tf_op jit(solution)/shard_map/ppermute | solution.py:390

commit v9 on v8

--- a/solution.py
+++ b/solution.py
@@ -9,6 +9,7 @@
 
 penalty_weight = 0.05
 BAND = 6
+PARTS = 2
 VMEM_LIMIT = 20 * 1024 * 1024
 NN = (((1,), (0,)), ((), ()))
 NT = (((1,), (1,)), ((), ()))
@@ -133,8 +134,10 @@
 CODES = (0, 1, 2, 3, 5)
 
 
-def choose_kernel(slots, count, offs_ref, *refs):
+def choose_kernel(slots, count, part, offs_ref, *refs):
     sources, (out, sems) = refs[:count], refs[count:]
+    size = out.shape[1]
+    sources = [ref if ref.shape[0] == size else ref.at[pl.ds(part * size, size)] for ref in sources]
     p, flip = place()
     target = last_partner(p, flip)
     copies = []
@@ -149,17 +152,17 @@
         pl.when(known)(copy.wait)
 
 
-def choose(offsets_next, *sources):
+def choose(offsets_next, *sources, part=0):
     slots = offsets_next.shape[1] - 1
-    own = sources[0]
-    return pl.pallas_call(
-        functools.partial(choose_kernel, slots, len(sources)),
+    shape = sources[3].shape
+    return pl.pallas_call(
+        functools.partial(choose_kernel, slots, len(sources), part),
         in_specs=[smem_spec()] + [any_spec()] * len(sources),
         out_specs=any_spec(),
-        out_shape=jax.ShapeDtypeStruct((slots,) + own.shape, f32),
+        out_shape=jax.ShapeDtypeStruct((slots,) + shape, f32),
         scratch_shapes=[pltpu.SemaphoreType.DMA((slots,))],
         compiler_params=params(),
-        cost_estimate=cost(0, 8 * slots * own.size),
+        cost_estimate=cost(0, 8 * slots * shape[0] * shape[1]),
         name="choose",
     )(offsets_next, *sources)
 
@@ -302,15 +305,20 @@
     )(offsets, data, image, *sources, *gate)
 
 
-def left_kernel(slots, pair, offs_ref, keep_in, send_in, high_ref, low_ref, own, first, group, both, two, lasts_ref,
-                keep_ref, send_ref, picked, sems):
+def left_kernel(slots, pair, offs_ref, keep_in, send_in, high_ref, low_ref, own, first, *refs):
     slot = pl.program_id(0)
+    keep_ref, send_ref, picked, sems = refs[-4:]
+    parts = (len(refs) - 4) // 4
+    groups, boths, twos, lasts = (refs[i * parts : (i + 1) * parts] for i in range(4))
+    size = groups[0].shape[0]
 
     @pl.when(slot == 0)
     def _():
         for each in range(slots):
-            sources = (own, first, group, both, lasts_ref.at[each], two)
-            start_pick(offs_ref[0, each + 1], sources, picked.at[each], sems.at[each])
+            for part in range(parts):
+                rows = pl.ds(part * size, size)
+                sources = (own.at[rows], first.at[rows], groups[part], boths[part], lasts[part].at[each], twos[part])
+                start_pick(offs_ref[0, each + 1], sources, picked.at[each, rows], sems.at[each])
 
     pltpu.make_async_copy(own, picked.at[slot], sems.at[slot]).wait()
     half = send_ref.shape[0]
@@ -416,18 +424,21 @@
     got_first = send(bin_first, "first")
     image = own + backward(offsets, local_tiles, data_sources) + got_first + got_group
 
-    image_group = send(image, "group")
+    size = image.shape[0] // PARTS
+    image_groups = [send(image[part * size : (part + 1) * size], "group") for part in range(PARTS)]
     image_first = send(image, "first")
-    image_both = send(image_group, "first")
-    chosen = choose(offsets_next, image, image_first, image_group, image_both)
-    image_last = send(chosen, "last")
+    image_boths = [send(each, "first") for each in image_groups]
+    image_lasts, ready = [], after(offsets_next, image_groups[-1])
+    for part in range(PARTS):
+        chosen = choose(ready, image, image_first, image_groups[part], image_boths[part], part=part)
+        image_lasts.append(send(chosen, "last"))
+        ready = after(offsets_next, image_lasts[-1])
     keep0, other0, keep, other, high, low = right(offsets, data, image, (chosen,), data_sources, pair)
-    image_two = send(after(image_both, chosen), "direct")
-    image_sources = (image, image_first, image_group, image_both, image_two, image_last)
+    image_twos = [send(after(each, chosen), "direct") for each in image_boths]
+    image_sources = (image, image_first, *image_groups, *image_boths, *image_twos, *image_lasts)
 
     if pair:
         result = finish(offsets, step, local_tiles, keep0, swap(other0), factor, 0)
-        keep = after(keep, result)
     keep, other = left(offsets, (keep, other), (high, low), image_sources, pair)
     if pair:
         return finish(offsets, step, local_tiles, keep, swap(other), factor, 1, (result,))[None]

time: 112 us -> 118 us (1.054); the launches traced: 112 us -> 116 us
  starting transfers between devices: 29.8 us -> 43.1 us
  waiting for transfers between devices: 62.7 us -> 52.9 us
    ppermute x17 -> x21, starting transfers between devices: 22.5 us -> 40.5 us  [send(): return lax.ppermute(value, ('var', 'samp'), pairs)]
    ppermute x17 -> x21, waiting for transfers between devices: 60.4 us -> 50.6 us  [send(): return lax.ppermute(value, ('var', 'samp'), pairs)]
    ppermute x2, starting transfers between devices: 7.32 us -> 2.67 us  [swap(): return lax.ppermute(value, 'samp', [(0, 1), (1, 0)])]
  transfers between devices with their start and end apart: 19 -> 23, of which waited for: 9 -> 10; matrix products, arithmetic and copies ran while one was open for 0% -> 0% of each run, Pallas kernels for 10% -> 9%
where the time goes in v9:
time: 118 us; the launch traced here: 116 us
  waiting for transfers between devices  52.9 us (45%)
  starting transfers between devices  43.1 us (37%)
  Pallas kernels  15.7 us (13%)
  local copies, waits for them, and re-layouts  2.98 us (3%)
    ppermute x21, waiting for transfers between devices, send(): return lax.ppermute(value, ('var', 'samp'), pairs)  50.6 us
    ppermute x21, starting transfers between devices, send(): return lax.ppermute(value, ('var', 'samp'), pairs)  40.5 us
    pallas_call x2, Pallas kernels, finish(): pl.pallas_call(functools.partial(finish_kernel, begin, factor), grid=(cou...  3.37 us
    pallas_call x1, Pallas kernels, right(): pl.pallas_call(functools.partial(right_kernel, slots, pair), in_specs=[sm...  3.1 us
    unnamed x10, local copies, waits for them, and re-layouts  2.95 us
    ppermute x2, starting transfers between devices, swap(): return lax.ppermute(value, 'samp', [(0, 1), (1, 0)])  2.67 us
  transfers between devices with their start and end apart: 23, of which 10 were waited for; matrix products, arithmetic and copies ran while one was open for 0% of the time, Pallas kernels for 9%

profile of v9, /device:TPU:7, one launch (start us, length us, event | category | flops | bytes accessed | tf_op | source)
XLA Modules:
  0.0 116.0 jit_solution(13852384672530885107)
XLA Ops:
  0.2 3.3 %collective-permute-start.4 = (f32[256,512]{1,0:T(8,128)}, f32[256,512]{1,0:T(8,128)S(1)}, u32[]{:S(2)}, u32[]{:S(2)}) collective-permute-start(f32[256,512]{1,0:T(8,128)} %own.3), channel_id=1, source_target_pairs={{0,24},{1,25},{2,26},{3,27},{4,28},{5,29},{6,30},{7,31},{8,0},{9,1... | collective-permute-start | bytes 1572872 | tf_op jit(solution)/shard_map/ppermute | solution.py:105
  3.8 1.9 %copy-done = f32[1,3,512,512]{3,2,1,0:T(8,128)S(1)} copy-done((f32[1,3,512,512]{3,2,1,0:T(8,128)S(1)}, f32[1,3,512,512]{3,2,1,0:T(8,128)}, u32[]{:S(2)}) %copy-start) | copy-done | bytes 3145752
  6.7 1.9 %forward.1 = (f32[256,512]{1,0:T(8,128)S(1)}, f32[256,512]{1,0:T(8,128)S(1)}, f32[256,512]{1,0:T(8,128)S(1)}) custom-call(f32[256,512]{1,0:T(8,128)S(1)} %copy-done.2, f32[3,512,512]{2,1,0:T(8,128)S(1)} %bitcast.2), custom_call_target="tpu_custom_call" | custom-call | tf_op jit(solution)/shard_map/forward/pallas_call | solution.py:122
  10.2 3.9 %collective-permute-done.4.refs_2_.group = f32[256,512]{1,0:T(8,128)S(1)} collective-permute-done((f32[256,512]{1,0:T(8,128)}, f32[256,512]{1,0:T(8,128)S(1)}, u32[]{:S(2)}, u32[]{:S(2)}) %collective-permute-start.4) | collective-permute-done | bytes 524320 | tf_op jit(solution)/shard_map/ppermute | solution.py:105
  14.1 2.4 %collective-permute-start.5 = (f32[256,512]{1,0:T(8,128)S(1)}, f32[256,512]{1,0:T(8,128)S(1)}, u32[]{:S(2)}, u32[]{:S(2)}) collective-permute-start(f32[256,512]{1,0:T(8,128)S(1)} %collective-permute-done.4.refs_2_.group), channel_id=1, source_target_pairs={{0,2},{1,5},{2,0},{3,7},{4,6},{5,1},{6,4},{7,3},{8,10},{9,13},{10,... | collective-permute-start | bytes 1572872 | tf_op jit(solution)/shard_map/ppermute | solution.py:105
  17.2 8.9 %collective-permute-done.3.refs_3_ = f32[256,512]{1,0:T(8,128)S(1)} collective-permute-done((f32[256,512]{1,0:T(8,128)S(1)}, f32[256,512]{1,0:T(8,128)S(1)}, u32[]{:S(2)}, u32[]{:S(2)}) %collective-permute-start.3) | collective-permute-done | bytes 524320 | tf_op jit(solution)/shard_map/ppermute | solution.py:105
  30.2 2.8 %collective-permute-start.7 = (f32[2,256,512]{2,1,0:T(8,128)S(1)}, f32[2,256,512]{2,1,0:T(8,128)S(1)}, u32[]{:S(2)}, u32[]{:S(2)}) collective-permute-start(f32[2,256,512]{2,1,0:T(8,128)S(1)} %choose.3), channel_id=1, source_target_pairs={{0,4},{1,3},{2,6},{3,1},{4,0},{5,7},{6,2},{7,5},{8,12},{9,11},{10,... | collective-permute-start | bytes 3145736 | tf_op jit(solution)/shard_map/ppermute | solution.py:105
  33.3 3.3 %collective-permute-done.9 = f32[256,512]{1,0:T(8,128)S(1)} collective-permute-done((f32[256,512]{1,0:T(8,128)S(1)}, f32[256,512]{1,0:T(8,128)S(1)}, u32[]{:S(2)}, u32[]{:S(2)}) %collective-permute-start.9) | collective-permute-done | bytes 524320 | tf_op jit(solution)/shard_map/ppermute | solution.py:105
  36.8 2.2 %collective-permute-start.11 = (f32[256,512]{1,0:T(8,128)S(1)}, f32[256,512]{1,0:T(8,128)S(1)}, u32[]{:S(2)}, u32[]{:S(2)}) collective-permute-start(f32[256,512]{1,0:T(8,128)S(1)} %add_add_fusion), channel_id=1, source_target_pairs={{24,0},{25,1},{26,2},{27,3},{28,4},{29,5},{30,6},{31,7},{0,8},{1,9... | collective-permute-start | bytes 1572872 | tf_op jit(solution)/shard_map/ppermute | solution.py:105
  39.0 16.0 %collective-permute-done.7.refs_0_ = f32[2,256,512]{2,1,0:T(8,128)S(1)} collective-permute-done((f32[2,256,512]{2,1,0:T(8,128)S(1)}, f32[2,256,512]{2,1,0:T(8,128)S(1)}, u32[]{:S(2)}, u32[]{:S(2)}) %collective-permute-start.7) | collective-permute-done | bytes 1048608 | tf_op jit(solution)/shard_map/ppermute | solution.py:105
  55.0 2.1 %backward.1 = f32[256,512]{1,0:T(8,128)S(1)} custom-call(s32[1,3]{1,0:T(1,128)S(1)} %copy-done.4, f32[3,512,512]{2,1,0:T(8,128)S(1)} %bitcast.3, f32[256,512]{1,0:T(8,128)S(1)} %copy-done.3, f32[256,512]{1,0:T(8,128)S(1)} %collective-permute-done.1.refs_1_.first, f32[256,512]{1,0:T(8,128)S(1)} %collective-permute-done.4.refs_2_.group, ...), custom_call_target="tpu_custom_call" | custom-call | tf_op jit(solution)/shard_map/backward/pallas_call | solution.py:202
  57.3 4.7 %collective-permute-start.14 = (f32[128,512]{1,0:T(8,128)S(1)}, f32[128,512]{1,0:T(8,128)S(1)}, u32[]{:S(2)}, u32[]{:S(2)}) collective-permute-start(f32[128,512]{1,0:T(8,128)S(1)} %get-tuple-element.49), channel_id=1, source_target_pairs={{0,24},{1,25},{2,26},{3,27},{4,28},{5,29},{6,30},{7,31},{8,0},{9,1... | collective-permute-start | bytes 786440 | tf_op jit(solution)/shard_map/ppermute | solution.py:105
  62.1 6.1 %collective-permute-start.13 = (f32[256,512]{1,0:T(8,128)S(1)}, f32[256,512]{1,0:T(8,128)S(1)}, u32[]{:S(2)}, u32[]{:S(2)}) collective-permute-start(f32[256,512]{1,0:T(8,128)S(1)} %add_add_fusion.1.refs_0_.image_ref.own), channel_id=1, source_target_pairs={{0,2},{1,5},{2,0},{3,7},{4,6},{5,1},{6,4},{7,3},{8,10},{9,13},{10,... | collective-permute-start | bytes 1572872 | tf_op jit(solution)/shard_map/ppermute | solution.py:105
  68.2 6.0 %collective-permute-start.15 = (f32[128,512]{1,0:T(8,128)S(1)}, f32[128,512]{1,0:T(8,128)S(1)}, u32[]{:S(2)}, u32[]{:S(2)}) collective-permute-start(f32[128,512]{1,0:T(8,128)S(1)} %collective-permute-done.14.refs_2_.refs_0_), channel_id=1, source_target_pairs={{0,2},{1,5},{2,0},{3,7},{4,6},{5,1},{6,4},{7,3},{8,10},{9,13},{10,... | collective-permute-start | bytes 786440 | tf_op jit(solution)/shard_map/ppermute | solution.py:105
  74.2 3.8 %collective-permute-done.15.refs_3_.refs_2_ = f32[128,512]{1,0:T(8,128)S(1)} collective-permute-done((f32[128,512]{1,0:T(8,128)S(1)}, f32[128,512]{1,0:T(8,128)S(1)}, u32[]{:S(2)}, u32[]{:S(2)}) %collective-permute-start.15) | collective-permute-done | bytes 262176 | tf_op jit(solution)/shard_map/ppermute | solution.py:105
  78.6 2.3 %collective-permute-start.16 = (f32[2,128,512]{2,1,0:T(8,128)S(1)}, f32[2,128,512]{2,1,0:T(8,128)S(1)}, u32[]{:S(2)}, u32[]{:S(2)}) collective-permute-start(f32[2,128,512]{2,1,0:T(8,128)S(1)} %choose.4), channel_id=1, source_target_pairs={{0,4},{1,3},{2,6},{3,1},{4,0},{5,7},{6,2},{7,5},{8,12},{9,11},{10,... | collective-permute-start | bytes 1572872 | tf_op jit(solution)/shard_map/ppermute | solution.py:105
  82.7 7.6 %collective-permute-done.16.refs_6_ = f32[2,128,512]{2,1,0:T(8,128)S(1)} collective-permute-done((f32[2,128,512]{2,1,0:T(8,128)S(1)}, f32[2,128,512]{2,1,0:T(8,128)S(1)}, u32[]{:S(2)}, u32[]{:S(2)}) %collective-permute-start.16) | collective-permute-done | bytes 524320 | tf_op jit(solution)/shard_map/ppermute | solution.py:105
  94.8 3.1 %right.1 = (f32[1,256,512]{2,1,0:T(8,128)S(1)}, f32[1,256,512]{2,1,0:T(8,128)S(1)}, f32[2,256,512]{2,1,0:T(8,128)S(1)}, f32[2,256,512]{2,1,0:T(8,128)S(1)}, bf16...) custom-call(s32[1,3]{1,0:T(1,128)S(1)} %copy-done.4, f32[256,512]{1,0:T(8,128)S(1)} %copy-done.3, ...), custom_call_target="tpu_custom_call" | custom-call | flops 26843545600 | tf_op jit(solution)/shard_map/right/pallas_call | solution.py:296
  97.9 2.4 %collective-permute-done.18.refs_4_ = f32[128,512]{1,0:T(8,128)S(1)} collective-permute-done((f32[128,512]{1,0:T(8,128)S(1)}, f32[128,512]{1,0:T(8,128)S(1)}, u32[]{:S(2)}, u32[]{:S(2)}) %collective-permute-start.18) | collective-permute-done | bytes 262176 | tf_op jit(solution)/shard_map/ppermute | solution.py:105
  100.3 3.0 %collective-permute-done.19.refs_5_ = f32[128,512]{1,0:T(8,128)S(1)} collective-permute-done((f32[128,512]{1,0:T(8,128)S(1)}, f32[128,512]{1,0:T(8,128)S(1)}, u32[]{:S(2)}, u32[]{:S(2)}) %collective-permute-start.19) | collective-permute-done | bytes 262176 | tf_op jit(solution)/shard_map/ppermute | solution.py:105
  105.0 2.0 %left.1 = (f32[2,256,512]{2,1,0:T(8,128)S(1)}, f32[2,256,512]{2,1,0:T(8,128)S(1)}) custom-call(s32[1,3]{1,0:T(1,128)S(1)} %copy-done.4, f32[2,256,512]{2,1,0:T(8,128)S(1)} %get-tuple-element.39.keep_in, f32[2,256,512]{2,1,0:T(8,128)S(1)} %get-tuple-element.40.send_in, bf16[512,256]{1,0:T(8,128)(2,1)S(1)} %get-tuple-element.41.high_ref, ...), custom_call_target="tpu_custom_call" | custom-call | tf_op jit(solution)/shard_map/left/pallas_call | solution.py:339
  107.0 2.6 %collective-permute-start.21 = (f32[2,256,512]{2,1,0:T(8,128)S(1)}, f32[2,256,512]{2,1,0:T(8,128)S(1)}, u32[]{:S(2)}, u32[]{:S(2)}) collective-permute-start(f32[2,256,512]{2,1,0:T(8,128)S(1)} %get-tuple-element.46), channel_id=1, source_target_pairs={{0,1},{1,0},{2,3},{3,2},{4,5},{5,4},{6,7},{7,6},{8,9},{9,8},{10,11... | collective-permute-start | bytes 3145736 | tf_op jit(solution)/shard_map/ppermute | solution.py:398
  110.3 2.3 %collective-permute-done.22.other_ref = f32[1,256,512]{2,1,0:T(8,128)S(1)} collective-permute-done((f32[1,256,512]{2,1,0:T(8,128)S(1)}, f32[1,256,512]{2,1,0:T(8,128)S(1)}, u32[]{:S(2)}, u32[]{:S(2)}) %collective-permute-start.22) | collective-permute-done | bytes 524320 | tf_op jit(solution)/shard_map/ppermute | solution.py:398
  114.2 1.8 %finish.3 = f32[3,256,512]{2,1,0:T(8,128)} custom-call(s32[1,3]{1,0:T(1,128)S(1)} %copy-done.4, f32[1]{0:T(128)S(6)} %copy.7.step_ref, f32[3,512,512]{2,1,0:T(8,128)S(1)} %bitcast.5, f32[2,256,512]{2,1,0:T(8,128)S(1)} %get-tuple-element.45.keep_ref, f32[2,256,512]{2,1,0:T(8,128)S(1)} %collective-permute-done.21.other_ref, ...), custom_call_target="tpu_custom_call", output_to_operand_aliasing={{}: (5, {})} | custom-call | tf_op jit(solution)/shard_map/finish/pallas_call | solution.py:380
  (45 shorter events, 18.7 us)
Async XLA Ops:
  0.0 8.7 %collective-permute-start.1 = (f32[256,512]{1,0:T(8,128)}, f32[256,512]{1,0:T(8,128)S(1)}, u32[]{:S(2)}, u32[]{:S(2)}) collective-permute-start(f32[256,512]{1,0:T(8,128)} %own.3), channel_id=1, source_target_pairs={{0,2},{1,5},{2,0},{3,7},{4,6},{5,1},{6,4},{7,3},{8,10},{9,13},{10,... | collective-permute-start | bytes 1572872 | tf_op jit(solution)/shard_map/ppermute | solution.py:105
  0.2 13.9 %collective-permute-start.4 = (f32[256,512]{1,0:T(8,128)}, f32[256,512]{1,0:T(8,128)S(1)}, u32[]{:S(2)}, u32[]{:S(2)}) collective-permute-start(f32[256,512]{1,0:T(8,128)} %own.3), channel_id=1, source_target_pairs={{0,24},{1,25},{2,26},{3,27},{4,28},{5,29},{6,30},{7,31},{8,0},{9,1... | collective-permute-start | bytes 1572872 | tf_op jit(solution)/shard_map/ppermute | solution.py:105
  3.5 5.1 %collective-permute-start = (s32[1,3]{1,0:T(1,128)}, s32[1,3]{1,0:T(1,128)S(1)}, u32[]{:S(2)}, u32[]{:S(2)}) collective-permute-start(s32[1,3]{1,0:T(1,128)} %offs_ref.11), channel_id=1, source_target_pairs={{0,4},{1,3},{2,6},{3,1},{4,0},{5,7},{6,2},{7,5},{8,12},{9,11},{10,... | collective-permute-start | bytes 44 | tf_op jit(solution)/shard_map/ppermute | solution.py:105
  8.7 8.5 %collective-permute-start.2 = (f32[256,512]{1,0:T(8,128)S(1)}, f32[256,512]{1,0:T(8,128)S(1)}, u32[]{:S(2)}, u32[]{:S(2)}) collective-permute-start(f32[256,512]{1,0:T(8,128)S(1)} %get-tuple-element.30.refs_0_), channel_id=1, source_target_pairs={{0,4},{1,3},{2,6},{3,1},{4,0},{5,7},{6,2},{7,5},{8,12},{9,11},{10,... | collective-permute-start | bytes 1572872 | tf_op jit(solution)/shard_map/ppermute | solution.py:105
  9.9 16.2 %collective-permute-start.3 = (f32[256,512]{1,0:T(8,128)S(1)}, f32[256,512]{1,0:T(8,128)S(1)}, u32[]{:S(2)}, u32[]{:S(2)}) collective-permute-start(f32[256,512]{1,0:T(8,128)S(1)} %get-tuple-element.31.refs_1_), channel_id=1, source_target_pairs={{0,4},{1,3},{2,6},{3,1},{4,0},{5,7},{6,2},{7,5},{8,12},{9,11},{10,... | collective-permute-start | bytes 1572872 | tf_op jit(solution)/shard_map/ppermute | solution.py:105
  14.1 15.4 %collective-permute-start.5 = (f32[256,512]{1,0:T(8,128)S(1)}, f32[256,512]{1,0:T(8,128)S(1)}, u32[]{:S(2)}, u32[]{:S(2)}) collective-permute-start(f32[256,512]{1,0:T(8,128)S(1)} %collective-permute-done.4.refs_2_.group), channel_id=1, source_target_pairs={{0,2},{1,5},{2,0},{3,7},{4,6},{5,1},{6,4},{7,3},{8,10},{9,13},{10,... | collective-permute-start | bytes 1572872 | tf_op jit(solution)/shard_map/ppermute | solution.py:105
  16.5 13.0 %collective-permute-start.6 = (f32[256,512]{1,0:T(8,128)S(1)}, f32[256,512]{1,0:T(8,128)S(1)}, u32[]{:S(2)}, u32[]{:S(2)}) collective-permute-start(f32[256,512]{1,0:T(8,128)S(1)} %collective-permute-done.1.refs_1_.first), channel_id=1, source_target_pairs={{2,18},{5,21},{10,26},{13,29},{18,2},{21,5},{26,10},{29,13}} | collective-permute-start | bytes 1572872 | tf_op jit(solution)/shard_map/ppermute | solution.py:105
  27.5 5.8 %collective-permute-start.10 = (f32[256,512]{1,0:T(8,128)S(1)}, f32[256,512]{1,0:T(8,128)S(1)}, u32[]{:S(2)}, u32[]{:S(2)}) collective-permute-start(f32[256,512]{1,0:T(8,128)S(1)} %get-tuple-element.36), channel_id=1, source_target_pairs={{26,0},{29,1},{2,8},{5,9},{10,16},{13,17},{18,24},{21,25}} | collective-permute-start | bytes 1572872 | tf_op jit(solution)/shard_map/ppermute | solution.py:105
  28.2 8.4 %collective-permute-start.9 = (f32[256,512]{1,0:T(8,128)S(1)}, f32[256,512]{1,0:T(8,128)S(1)}, u32[]{:S(2)}, u32[]{:S(2)}) collective-permute-start(f32[256,512]{1,0:T(8,128)S(1)} %get-tuple-element.35), channel_id=1, source_target_pairs={{0,2},{1,5},{2,0},{3,7},{4,6},{5,1},{6,4},{7,3},{8,10},{9,13},{10,... | collective-permute-start | bytes 1572872 | tf_op jit(solution)/shard_map/ppermute | solution.py:105
  29.5 25.4 %copy-start.1 = (f32[1,3,512,512]{3,2,1,0:T(8,128)S(1)}, f32[1,3,512,512]{3,2,1,0:T(8,128)}, u32[]{:S(2)}) copy-start(f32[1,3,512,512]{3,2,1,0:T(8,128)} %param.5) | copy-start | bytes 9437188
  30.2 24.8 %collective-permute-start.7 = (f32[2,256,512]{2,1,0:T(8,128)S(1)}, f32[2,256,512]{2,1,0:T(8,128)S(1)}, u32[]{:S(2)}, u32[]{:S(2)}) collective-permute-start(f32[2,256,512]{2,1,0:T(8,128)S(1)} %choose.3), channel_id=1, source_target_pairs={{0,4},{1,3},{2,6},{3,1},{4,0},{5,7},{6,2},{7,5},{8,12},{9,11},{10,... | collective-permute-start | bytes 3145736 | tf_op jit(solution)/shard_map/ppermute | solution.py:105
  33.0 24.0 %collective-permute-start.8 = (f32[256,512]{1,0:T(8,128)S(1)}, f32[256,512]{1,0:T(8,128)S(1)}, u32[]{:S(2)}, u32[]{:S(2)}) collective-permute-start(f32[256,512]{1,0:T(8,128)S(1)} %get-tuple-element.33), channel_id=1, source_target_pairs={{0,2},{1,5},{2,0},{3,7},{4,6},{5,1},{6,4},{7,3},{8,10},{9,13},{10,... | collective-permute-start | bytes 1572872 | tf_op jit(solution)/shard_map/ppermute | solution.py:105
  36.8 20.2 %collective-permute-start.11 = (f32[256,512]{1,0:T(8,128)S(1)}, f32[256,512]{1,0:T(8,128)S(1)}, u32[]{:S(2)}, u32[]{:S(2)}) collective-permute-start(f32[256,512]{1,0:T(8,128)S(1)} %add_add_fusion), channel_id=1, source_target_pairs={{24,0},{25,1},{26,2},{27,3},{28,4},{29,5},{30,6},{31,7},{0,8},{1,9... | collective-permute-start | bytes 1572872 | tf_op jit(solution)/shard_map/ppermute | solution.py:105
  57.3 10.9 %collective-permute-start.14 = (f32[128,512]{1,0:T(8,128)S(1)}, f32[128,512]{1,0:T(8,128)S(1)}, u32[]{:S(2)}, u32[]{:S(2)}) collective-permute-start(f32[128,512]{1,0:T(8,128)S(1)} %get-tuple-element.49), channel_id=1, source_target_pairs={{0,24},{1,25},{2,26},{3,27},{4,28},{5,29},{6,30},{7,31},{8,0},{9,1... | collective-permute-start | bytes 786440 | tf_op jit(solution)/shard_map/ppermute | solution.py:105
  62.1 15.9 %collective-permute-start.13 = (f32[256,512]{1,0:T(8,128)S(1)}, f32[256,512]{1,0:T(8,128)S(1)}, u32[]{:S(2)}, u32[]{:S(2)}) collective-permute-start(f32[256,512]{1,0:T(8,128)S(1)} %add_add_fusion.1.refs_0_.image_ref.own), channel_id=1, source_target_pairs={{0,2},{1,5},{2,0},{3,7},{4,6},{5,1},{6,4},{7,3},{8,10},{9,13},{10,... | collective-permute-start | bytes 1572872 | tf_op jit(solution)/shard_map/ppermute | solution.py:105
  68.1 6.1 %collective-permute-start.12 = (f32[128,512]{1,0:T(8,128)S(1)}, f32[128,512]{1,0:T(8,128)S(1)}, u32[]{:S(2)}, u32[]{:S(2)}) collective-permute-start(f32[128,512]{1,0:T(8,128)S(1)} %get-tuple-element.50), channel_id=1, source_target_pairs={{0,24},{1,25},{2,26},{3,27},{4,28},{5,29},{6,30},{7,31},{8,0},{9,1... | collective-permute-start | bytes 786440 | tf_op jit(solution)/shard_map/ppermute | solution.py:105
  68.2 9.8 %collective-permute-start.15 = (f32[128,512]{1,0:T(8,128)S(1)}, f32[128,512]{1,0:T(8,128)S(1)}, u32[]{:S(2)}, u32[]{:S(2)}) collective-permute-start(f32[128,512]{1,0:T(8,128)S(1)} %collective-permute-done.14.refs_2_.refs_0_), channel_id=1, source_target_pairs={{0,2},{1,5},{2,0},{3,7},{4,6},{5,1},{6,4},{7,3},{8,10},{9,13},{10,... | collective-permute-start | bytes 786440 | tf_op jit(solution)/shard_map/ppermute | solution.py:105
  78.6 11.7 %collective-permute-start.16 = (f32[2,128,512]{2,1,0:T(8,128)S(1)}, f32[2,128,512]{2,1,0:T(8,128)S(1)}, u32[]{:S(2)}, u32[]{:S(2)}) collective-permute-start(f32[2,128,512]{2,1,0:T(8,128)S(1)} %choose.4), channel_id=1, source_target_pairs={{0,4},{1,3},{2,6},{3,1},{4,0},{5,7},{6,2},{7,5},{8,12},{9,11},{10,... | collective-permute-start | bytes 1572872 | tf_op jit(solution)/shard_map/ppermute | solution.py:105
  80.9 9.4 %collective-permute-start.17 = (f32[128,512]{1,0:T(8,128)S(1)}, f32[128,512]{1,0:T(8,128)S(1)}, u32[]{:S(2)}, u32[]{:S(2)}) collective-permute-start(f32[128,512]{1,0:T(8,128)S(1)} %collective-permute-done.12.refs_2_.refs_1_), channel_id=1, source_target_pairs={{0,2},{1,5},{2,0},{3,7},{4,6},{5,1},{6,4},{7,3},{8,10},{9,13},{10,... | collective-permute-start | bytes 786440 | tf_op jit(solution)/shard_map/ppermute | solution.py:105
  90.9 14.0 %collective-permute-start.20 = (f32[2,128,512]{2,1,0:T(8,128)S(1)}, f32[2,128,512]{2,1,0:T(8,128)S(1)}, u32[]{:S(2)}, u32[]{:S(2)}) collective-permute-start(f32[2,128,512]{2,1,0:T(8,128)S(1)} %choose.5.refs_1_), channel_id=1, source_target_pairs={{0,4},{1,3},{2,6},{3,1},{4,0},{5,7},{6,2},{7,5},{8,12},{9,11},{10,... | collective-permute-start | bytes 1572872 | tf_op jit(solution)/shard_map/ppermute | solution.py:105
  92.2 8.1 %collective-permute-start.18 = (f32[128,512]{1,0:T(8,128)S(1)}, f32[128,512]{1,0:T(8,128)S(1)}, u32[]{:S(2)}, u32[]{:S(2)}) collective-permute-start(f32[128,512]{1,0:T(8,128)S(1)} %collective-permute-done.15.refs_3_.refs_2_), channel_id=1, source_target_pairs={{2,30},{5,31},{10,6},{13,7},{18,14},{21,15},{26,22},{29,23}} | collective-permute-start | bytes 786440 | tf_op jit(solution)/shard_map/ppermute | solution.py:105
  93.5 9.9 %collective-permute-start.19 = (f32[128,512]{1,0:T(8,128)S(1)}, f32[128,512]{1,0:T(8,128)S(1)}, u32[]{:S(2)}, u32[]{:S(2)}) collective-permute-start(f32[128,512]{1,0:T(8,128)S(1)} %collective-permute-done.17.refs_3_), channel_id=1, source_target_pairs={{2,30},{5,31},{10,6},{13,7},{18,14},{21,15},{26,22},{29,23}} | collective-permute-start | bytes 786440 | tf_op jit(solution)/shard_map/ppermute | solution.py:105
  107.0 7.2 %collective-permute-start.21 = (f32[2,256,512]{2,1,0:T(8,128)S(1)}, f32[2,256,512]{2,1,0:T(8,128)S(1)}, u32[]{:S(2)}, u32[]{:S(2)}) collective-permute-start(f32[2,256,512]{2,1,0:T(8,128)S(1)} %get-tuple-element.46), channel_id=1, source_target_pairs={{0,1},{1,0},{2,3},{3,2},{4,5},{5,4},{6,7},{7,6},{8,9},{9,8},{10,11... | collective-permute-start | bytes 3145736 | tf_op jit(solution)/shard_map/ppermute | solution.py:398
  109.6 3.0 %collective-permute-start.22 = (f32[1,256,512]{2,1,0:T(8,128)S(1)}, f32[1,256,512]{2,1,0:T(8,128)S(1)}, u32[]{:S(2)}, u32[]{:S(2)}) collective-permute-start(f32[1,256,512]{2,1,0:T(8,128)S(1)} %get-tuple-element.48), channel_id=1, source_target_pairs={{0,1},{1,0},{2,3},{3,2},{4,5},{5,4},{6,7},{7,6},{8,9},{9,8},{10,11... | collective-permute-start | bytes 1572872 | tf_op jit(solution)/shard_map/ppermute | solution.py:398
  (4 other events, 43.2 us)

commit v10 on v8

--- a/solution.py
+++ b/solution.py
@@ -80,6 +80,9 @@
             use = True
             if kind == "first":
                 target = var ^ first
+            elif kind == "near":
+                target = var ^ first
+                use = (target & 3) in wanted(first, last, 0)
             elif kind == "last":
                 target = var ^ last
             elif kind == "group":
@@ -413,7 +416,7 @@
 
     bin_group = bin_group + got_both + got_two
     got_group = send(bin_group, "group", reverse=True)
-    got_first = send(bin_first, "first")
+    got_first = send(bin_first, "near", reverse=True)
     image = own + backward(offsets, local_tiles, data_sources) + got_first + got_group
 
     image_group = send(image, "group")

time: 112 us -> 111 us (level)
  starting transfers between devices: 29.8 us -> 26.9 us
  waiting for transfers between devices: 62.7 us -> 64.2 us
    ppermute x2, starting transfers between devices: 7.32 us -> 4.75 us  [swap(): return lax.ppermute(value, 'samp', [(0, 1), (1, 0)])]
    ppermute x17, waiting for transfers between devices: 60.4 us -> 61.9 us  [send(): return lax.ppermute(value, ('var', 'samp'), pairs)]
where the time goes in v10:
time: 111 us; the launch traced here: 110 us
  waiting for transfers between devices  64.2 us (58%)
  starting transfers between devices  26.9 us (24%)
  Pallas kernels  15.2 us (14%)
  local copies, waits for them, and re-layouts  2.95 us (3%)
    ppermute x17, waiting for transfers between devices, send(): return lax.ppermute(value, ('var', 'samp'), pairs)  61.9 us
    ppermute x17, starting transfers between devices, send(): return lax.ppermute(value, ('var', 'samp'), pairs)  22.2 us
    ppermute x2, starting transfers between devices, swap(): return lax.ppermute(value, 'samp', [(0, 1), (1, 0)])  4.75 us
    pallas_call x2, Pallas kernels, finish(): pl.pallas_call(functools.partial(finish_kernel, begin, factor), grid=(cou...  3.37 us
    pallas_call x1, Pallas kernels, right(): pl.pallas_call(functools.partial(right_kernel, slots, pair), in_specs=[sm...  3.09 us
    unnamed x10, local copies, waits for them, and re-layouts  2.95 us
    ppermute x2, waiting for transfers between devices, swap(): return lax.ppermute(value, 'samp', [(0, 1), (1, 0)])  2.29 us
  transfers between devices with their start and end apart: 19, of which 9 were waited for; matrix products, arithmetic and copies ran while one was open for 0% of the time, Pallas kernels for 10%

profile of v10, /device:TPU:7, one launch (start us, length us, event | category | flops | bytes accessed | tf_op | source)
XLA Modules:
  0.0 110.5 jit_solution(1868770272223202958)
XLA Ops:
  0.2 3.3 %collective-permute-start.4 = (f32[256,512]{1,0:T(8,128)}, f32[256,512]{1,0:T(8,128)S(1)}, u32[]{:S(2)}, u32[]{:S(2)}) collective-permute-start(f32[256,512]{1,0:T(8,128)} %own.3), channel_id=1, source_target_pairs={{0,24},{1,25},{2,26},{3,27},{4,28},{5,29},{6,30},{7,31},{8,0},{9,1... | collective-permute-start | bytes 1572872 | tf_op jit(solution)/shard_map/ppermute | solution.py:107
  3.8 1.9 %copy-done = f32[1,3,512,512]{3,2,1,0:T(8,128)S(1)} copy-done((f32[1,3,512,512]{3,2,1,0:T(8,128)S(1)}, f32[1,3,512,512]{3,2,1,0:T(8,128)}, u32[]{:S(2)}) %copy-start) | copy-done | bytes 3145752
  6.7 1.9 %forward.1 = (f32[256,512]{1,0:T(8,128)S(1)}, f32[256,512]{1,0:T(8,128)S(1)}, f32[256,512]{1,0:T(8,128)S(1)}) custom-call(f32[256,512]{1,0:T(8,128)S(1)} %copy-done.2, f32[3,512,512]{2,1,0:T(8,128)S(1)} %bitcast.2), custom_call_target="tpu_custom_call" | custom-call | tf_op jit(solution)/shard_map/forward/pallas_call | solution.py:124
  10.2 3.9 %collective-permute-done.4.refs_2_.group = f32[256,512]{1,0:T(8,128)S(1)} collective-permute-done((f32[256,512]{1,0:T(8,128)}, f32[256,512]{1,0:T(8,128)S(1)}, u32[]{:S(2)}, u32[]{:S(2)}) %collective-permute-start.4) | collective-permute-done | bytes 524320 | tf_op jit(solution)/shard_map/ppermute | solution.py:107
  14.1 2.4 %collective-permute-start.5 = (f32[256,512]{1,0:T(8,128)S(1)}, f32[256,512]{1,0:T(8,128)S(1)}, u32[]{:S(2)}, u32[]{:S(2)}) collective-permute-start(f32[256,512]{1,0:T(8,128)S(1)} %collective-permute-done.4.refs_2_.group), channel_id=1, source_target_pairs={{0,2},{1,5},{2,0},{3,7},{4,6},{5,1},{6,4},{7,3},{8,10},{9,13},{10,... | collective-permute-start | bytes 1572872 | tf_op jit(solution)/shard_map/ppermute | solution.py:107
  17.2 8.9 %collective-permute-done.2.refs_2_ = f32[256,512]{1,0:T(8,128)S(1)} collective-permute-done((f32[256,512]{1,0:T(8,128)S(1)}, f32[256,512]{1,0:T(8,128)S(1)}, u32[]{:S(2)}, u32[]{:S(2)}) %collective-permute-start.2) | collective-permute-done | bytes 524320 | tf_op jit(solution)/shard_map/ppermute | solution.py:107
  26.1 1.5 %bins.1 = (f32[256,512]{1,0:T(8,128)S(1)}, f32[256,512]{1,0:T(8,128)S(1)}, f32[256,512]{1,0:T(8,128)S(1)}, f32[256,512]{1,0:T(8,128)S(1)}, f32[256,512]{1,0:T(8,128)S(1)}) custom-call(s32[1,3]{1,0:T(1,128)S(1)} %copy-done.4, s32[1,3]{1,0:T(1,128)S(1)} %collective-permute-done.next_ref.offs_ref, f32[256,512]{1,0:T(8,128)S(1)} %get-tuple-element.25.own_in, ...), custom_call_target="tpu_custom_call" | custom-call | tf_op jit(solution)/shard_map/bins/pallas_call | solution.py:240
  27.6 1.3 %collective-permute-start.9 = (f32[256,512]{1,0:T(8,128)S(1)}, f32[256,512]{1,0:T(8,128)S(1)}, u32[]{:S(2)}, u32[]{:S(2)}) collective-permute-start(f32[256,512]{1,0:T(8,128)S(1)} %get-tuple-element.33), channel_id=1, source_target_pairs={{0,2},{1,5},{2,0},{3,7},{4,6},{5,1},{6,4},{7,3},{8,10},{9,13},{10,... | collective-permute-start | bytes 1572872 | tf_op jit(solution)/shard_map/ppermute | solution.py:107
  30.3 3.6 %collective-permute-start.7 = (f32[2,256,512]{2,1,0:T(8,128)S(1)}, f32[2,256,512]{2,1,0:T(8,128)S(1)}, u32[]{:S(2)}, u32[]{:S(2)}) collective-permute-start(f32[2,256,512]{2,1,0:T(8,128)S(1)} %choose.2), channel_id=1, source_target_pairs={{0,4},{1,3},{2,6},{3,1},{4,0},{5,7},{6,2},{7,5},{8,12},{9,11},{10,... | collective-permute-start | bytes 3145736 | tf_op jit(solution)/shard_map/ppermute | solution.py:107
  36.1 2.2 %collective-permute-start.11 = (f32[256,512]{1,0:T(8,128)S(1)}, f32[256,512]{1,0:T(8,128)S(1)}, u32[]{:S(2)}, u32[]{:S(2)}) collective-permute-start(f32[256,512]{1,0:T(8,128)S(1)} %add_add_fusion), channel_id=1, source_target_pairs={{24,0},{25,1},{26,2},{27,3},{28,4},{29,5},{30,6},{31,7},{0,8},{1,9... | collective-permute-start | bytes 1572872 | tf_op jit(solution)/shard_map/ppermute | solution.py:107
  38.3 19.2 %collective-permute-done.7.refs_0_ = f32[2,256,512]{2,1,0:T(8,128)S(1)} collective-permute-done((f32[2,256,512]{2,1,0:T(8,128)S(1)}, f32[2,256,512]{2,1,0:T(8,128)S(1)}, u32[]{:S(2)}, u32[]{:S(2)}) %collective-permute-start.7) | collective-permute-done | bytes 1048608 | tf_op jit(solution)/shard_map/ppermute | solution.py:107
  57.5 2.1 %backward.1 = f32[256,512]{1,0:T(8,128)S(1)} custom-call(s32[1,3]{1,0:T(1,128)S(1)} %copy-done.4, f32[3,512,512]{2,1,0:T(8,128)S(1)} %bitcast.3, f32[256,512]{1,0:T(8,128)S(1)} %copy-done.3, f32[256,512]{1,0:T(8,128)S(1)} %collective-permute-done.1.refs_1_.first, f32[256,512]{1,0:T(8,128)S(1)} %collective-permute-done.4.refs_2_.group, ...), custom_call_target="tpu_custom_call" | custom-call | tf_op jit(solution)/shard_map/backward/pallas_call | solution.py:202
  59.8 2.5 %collective-permute-start.13 = (f32[256,512]{1,0:T(8,128)S(1)}, f32[256,512]{1,0:T(8,128)S(1)}, u32[]{:S(2)}, u32[]{:S(2)}) collective-permute-start(f32[256,512]{1,0:T(8,128)S(1)} %add_add_fusion.1.refs_0_.image_ref.own), channel_id=1, source_target_pairs={{0,24},{1,25},{2,26},{3,27},{4,28},{5,29},{6,30},{7,31},{8,0},{9,1... | collective-permute-start | bytes 1572872 | tf_op jit(solution)/shard_map/ppermute | solution.py:107
  62.4 11.2 %collective-permute-done.13.refs_2_.group = f32[256,512]{1,0:T(8,128)S(1)} collective-permute-done((f32[256,512]{1,0:T(8,128)S(1)}, f32[256,512]{1,0:T(8,128)S(1)}, u32[]{:S(2)}, u32[]{:S(2)}) %collective-permute-start.13) | collective-permute-done | bytes 524320 | tf_op jit(solution)/shard_map/ppermute | solution.py:107
  73.6 8.3 %collective-permute-done.14.refs_3_.both = f32[256,512]{1,0:T(8,128)S(1)} collective-permute-done((f32[256,512]{1,0:T(8,128)S(1)}, f32[256,512]{1,0:T(8,128)S(1)}, u32[]{:S(2)}, u32[]{:S(2)}) %collective-permute-start.14) | collective-permute-done | bytes 524320 | tf_op jit(solution)/shard_map/ppermute | solution.py:107
  83.5 3.1 %right.1 = (f32[1,256,512]{2,1,0:T(8,128)S(1)}, f32[1,256,512]{2,1,0:T(8,128)S(1)}, f32[2,256,512]{2,1,0:T(8,128)S(1)}, f32[2,256,512]{2,1,0:T(8,128)S(1)}, bf16...) custom-call(s32[1,3]{1,0:T(1,128)S(1)} %copy-done.4, f32[256,512]{1,0:T(8,128)S(1)} %copy-done.3, ...), custom_call_target="tpu_custom_call" | custom-call | flops 26843545600 | tf_op jit(solution)/shard_map/right/pallas_call | solution.py:296
  86.6 2.5 %collective-permute-start.15 = (f32[1,256,512]{2,1,0:T(8,128)S(1)}, f32[1,256,512]{2,1,0:T(8,128)S(1)}, u32[]{:S(2)}, u32[]{:S(2)}) collective-permute-start(f32[1,256,512]{2,1,0:T(8,128)S(1)} %get-tuple-element.37), channel_id=1, source_target_pairs={{0,1},{1,0},{2,3},{3,2},{4,5},{5,4},{6,7},{7,6},{8,9},{9,8},{10,11... | collective-permute-start | bytes 1572872 | tf_op jit(solution)/shard_map/ppermute | solution.py:393
  91.0 1.6 %finish.2.refs_0_ = f32[3,256,512]{2,1,0:T(8,128)} custom-call(s32[1,3]{1,0:T(1,128)S(1)} %copy-done.4, f32[1]{0:T(128)S(6)} %copy.7.step_ref, f32[3,512,512]{2,1,0:T(8,128)S(1)} %bitcast.4, f32[1,256,512]{2,1,0:T(8,128)S(1)} %get-tuple-element.36.keep_ref, f32[1,256,512]{2,1,0:T(8,128)S(1)} %collective-permute-done.15.other_ref), custom_call_target="tpu_custom_call" | custom-call | tf_op jit(solution)/shard_map/finish/pallas_call | solution.py:375
  92.6 7.6 %collective-permute-done.16.two = f32[256,512]{1,0:T(8,128)S(1)} collective-permute-done((f32[256,512]{1,0:T(8,128)S(1)}, f32[256,512]{1,0:T(8,128)S(1)}, u32[]{:S(2)}, u32[]{:S(2)}) %collective-permute-start.16) | collective-permute-done | bytes 524320 | tf_op jit(solution)/shard_map/ppermute | solution.py:107
  100.3 2.0 %collective-permute-done.17.lasts_ref = f32[2,256,512]{2,1,0:T(8,128)S(1)} collective-permute-done((f32[2,256,512]{2,1,0:T(8,128)S(1)}, f32[2,256,512]{2,1,0:T(8,128)S(1)}, u32[]{:S(2)}, u32[]{:S(2)}) %collective-permute-start.17) | collective-permute-done | bytes 1048608 | tf_op jit(solution)/shard_map/ppermute | solution.py:107
  102.2 1.9 %left.1 = (f32[2,256,512]{2,1,0:T(8,128)S(1)}, f32[2,256,512]{2,1,0:T(8,128)S(1)}) custom-call(s32[1,3]{1,0:T(1,128)S(1)} %copy-done.4, f32[2,256,512]{2,1,0:T(8,128)S(1)} %get-tuple-element.38.keep_in, f32[2,256,512]{2,1,0:T(8,128)S(1)} %get-tuple-element.39.send_in, bf16[512,256]{1,0:T(8,128)(2,1)S(1)} %get-tuple-element.40.high_ref, ...), custom_call_target="tpu_custom_call" | custom-call | tf_op jit(solution)/shard_map/left/pallas_call | solution.py:334
  104.2 2.2 %collective-permute-start.18 = (f32[2,256,512]{2,1,0:T(8,128)S(1)}, f32[2,256,512]{2,1,0:T(8,128)S(1)}, u32[]{:S(2)}, u32[]{:S(2)}) collective-permute-start(f32[2,256,512]{2,1,0:T(8,128)S(1)} %get-tuple-element.44), channel_id=1, source_target_pairs={{0,1},{1,0},{2,3},{3,2},{4,5},{5,4},{6,7},{7,6},{8,9},{9,8},{10,11... | collective-permute-start | bytes 3145736 | tf_op jit(solution)/shard_map/ppermute | solution.py:393
  106.4 2.3 %collective-permute-done.18.other_ref = f32[2,256,512]{2,1,0:T(8,128)S(1)} collective-permute-done((f32[2,256,512]{2,1,0:T(8,128)S(1)}, f32[2,256,512]{2,1,0:T(8,128)S(1)}, u32[]{:S(2)}, u32[]{:S(2)}) %collective-permute-start.18) | collective-permute-done | bytes 1048608 | tf_op jit(solution)/shard_map/ppermute | solution.py:393
  108.7 1.8 %finish.3 = f32[3,256,512]{2,1,0:T(8,128)} custom-call(s32[1,3]{1,0:T(1,128)S(1)} %copy-done.4, f32[1]{0:T(128)S(6)} %copy.7.step_ref, f32[3,512,512]{2,1,0:T(8,128)S(1)} %bitcast.5, f32[2,256,512]{2,1,0:T(8,128)S(1)} %get-tuple-element.43.keep_ref, f32[2,256,512]{2,1,0:T(8,128)S(1)} %collective-permute-done.18.other_ref, ...), custom_call_target="tpu_custom_call", output_to_operand_aliasing={{}: (5, {})} | custom-call | tf_op jit(solution)/shard_map/finish/pallas_call | solution.py:375
  (35 shorter events, 10.4 us)
Async XLA Ops:
  0.0 8.7 %collective-permute-start.1 = (f32[256,512]{1,0:T(8,128)}, f32[256,512]{1,0:T(8,128)S(1)}, u32[]{:S(2)}, u32[]{:S(2)}) collective-permute-start(f32[256,512]{1,0:T(8,128)} %own.3), channel_id=1, source_target_pairs={{0,2},{1,5},{2,0},{3,7},{4,6},{5,1},{6,4},{7,3},{8,10},{9,13},{10,... | collective-permute-start | bytes 1572872 | tf_op jit(solution)/shard_map/ppermute | solution.py:107
  0.2 13.9 %collective-permute-start.4 = (f32[256,512]{1,0:T(8,128)}, f32[256,512]{1,0:T(8,128)S(1)}, u32[]{:S(2)}, u32[]{:S(2)}) collective-permute-start(f32[256,512]{1,0:T(8,128)} %own.3), channel_id=1, source_target_pairs={{0,24},{1,25},{2,26},{3,27},{4,28},{5,29},{6,30},{7,31},{8,0},{9,1... | collective-permute-start | bytes 1572872 | tf_op jit(solution)/shard_map/ppermute | solution.py:107
  3.5 5.1 %collective-permute-start = (s32[1,3]{1,0:T(1,128)}, s32[1,3]{1,0:T(1,128)S(1)}, u32[]{:S(2)}, u32[]{:S(2)}) collective-permute-start(s32[1,3]{1,0:T(1,128)} %offs_ref.11), channel_id=1, source_target_pairs={{0,4},{1,3},{2,6},{3,1},{4,0},{5,7},{6,2},{7,5},{8,12},{9,11},{10,... | collective-permute-start | bytes 44 | tf_op jit(solution)/shard_map/ppermute | solution.py:107
  3.8 1.9 %copy-start = (f32[1,3,512,512]{3,2,1,0:T(8,128)S(1)}, f32[1,3,512,512]{3,2,1,0:T(8,128)}, u32[]{:S(2)}) copy-start(f32[1,3,512,512]{3,2,1,0:T(8,128)} %param.5) | copy-start | bytes 9437188
  5.7 1.0 copy-start.2
  6.7 19.4 %copy-start.4 = (s32[1,3]{1,0:T(1,128)S(1)}, s32[1,3]{1,0:T(1,128)}, u32[]{:S(2)}) copy-start(s32[1,3]{1,0:T(1,128)} %offs_ref.11) | copy-start | bytes 40
  8.6 21.0 %copy-start.3 = (f32[256,512]{1,0:T(8,128)S(1)}, f32[256,512]{1,0:T(8,128)}, u32[]{:S(2)}) copy-start(f32[256,512]{1,0:T(8,128)} %own.3) | copy-start | bytes 1572868
  8.7 8.5 %collective-permute-start.3 = (f32[256,512]{1,0:T(8,128)S(1)}, f32[256,512]{1,0:T(8,128)S(1)}, u32[]{:S(2)}, u32[]{:S(2)}) collective-permute-start(f32[256,512]{1,0:T(8,128)S(1)} %get-tuple-element.29.refs_1_), channel_id=1, source_target_pairs={{0,4},{1,3},{2,6},{3,1},{4,0},{5,7},{6,2},{7,5},{8,12},{9,11},{10,... | collective-permute-start | bytes 1572872 | tf_op jit(solution)/shard_map/ppermute | solution.py:107
  9.9 16.2 %collective-permute-start.2 = (f32[256,512]{1,0:T(8,128)S(1)}, f32[256,512]{1,0:T(8,128)S(1)}, u32[]{:S(2)}, u32[]{:S(2)}) collective-permute-start(f32[256,512]{1,0:T(8,128)S(1)} %get-tuple-element.28.refs_0_), channel_id=1, source_target_pairs={{0,4},{1,3},{2,6},{3,1},{4,0},{5,7},{6,2},{7,5},{8,12},{9,11},{10,... | collective-permute-start | bytes 1572872 | tf_op jit(solution)/shard_map/ppermute | solution.py:107
  14.1 15.5 %collective-permute-start.5 = (f32[256,512]{1,0:T(8,128)S(1)}, f32[256,512]{1,0:T(8,128)S(1)}, u32[]{:S(2)}, u32[]{:S(2)}) collective-permute-start(f32[256,512]{1,0:T(8,128)S(1)} %collective-permute-done.4.refs_2_.group), channel_id=1, source_target_pairs={{0,2},{1,5},{2,0},{3,7},{4,6},{5,1},{6,4},{7,3},{8,10},{9,13},{10,... | collective-permute-start | bytes 1572872 | tf_op jit(solution)/shard_map/ppermute | solution.py:107
  16.5 13.1 %collective-permute-start.6 = (f32[256,512]{1,0:T(8,128)S(1)}, f32[256,512]{1,0:T(8,128)S(1)}, u32[]{:S(2)}, u32[]{:S(2)}) collective-permute-start(f32[256,512]{1,0:T(8,128)S(1)} %collective-permute-done.1.refs_1_.first), channel_id=1, source_target_pairs={{2,18},{5,21},{10,26},{13,29},{18,2},{21,5},{26,10},{29,13}} | collective-permute-start | bytes 1572872 | tf_op jit(solution)/shard_map/ppermute | solution.py:107
  27.6 8.4 %collective-permute-start.9 = (f32[256,512]{1,0:T(8,128)S(1)}, f32[256,512]{1,0:T(8,128)S(1)}, u32[]{:S(2)}, u32[]{:S(2)}) collective-permute-start(f32[256,512]{1,0:T(8,128)S(1)} %get-tuple-element.33), channel_id=1, source_target_pairs={{0,2},{1,5},{2,0},{3,7},{4,6},{5,1},{6,4},{7,3},{8,10},{9,13},{10,... | collective-permute-start | bytes 1572872 | tf_op jit(solution)/shard_map/ppermute | solution.py:107
  28.9 7.1 %collective-permute-start.10 = (f32[256,512]{1,0:T(8,128)S(1)}, f32[256,512]{1,0:T(8,128)S(1)}, u32[]{:S(2)}, u32[]{:S(2)}) collective-permute-start(f32[256,512]{1,0:T(8,128)S(1)} %get-tuple-element.34), channel_id=1, source_target_pairs={{26,0},{29,1},{2,8},{5,9},{10,16},{13,17},{18,24},{21,25}} | collective-permute-start | bytes 1572872 | tf_op jit(solution)/shard_map/ppermute | solution.py:107
  29.6 27.9 %copy-start.1 = (f32[1,3,512,512]{3,2,1,0:T(8,128)S(1)}, f32[1,3,512,512]{3,2,1,0:T(8,128)}, u32[]{:S(2)}) copy-start(f32[1,3,512,512]{3,2,1,0:T(8,128)} %param.5) | copy-start | bytes 9437188
  30.3 27.2 %collective-permute-start.7 = (f32[2,256,512]{2,1,0:T(8,128)S(1)}, f32[2,256,512]{2,1,0:T(8,128)S(1)}, u32[]{:S(2)}, u32[]{:S(2)}) collective-permute-start(f32[2,256,512]{2,1,0:T(8,128)S(1)} %choose.2), channel_id=1, source_target_pairs={{0,4},{1,3},{2,6},{3,1},{4,0},{5,7},{6,2},{7,5},{8,12},{9,11},{10,... | collective-permute-start | bytes 3145736 | tf_op jit(solution)/shard_map/ppermute | solution.py:107
  34.0 25.6 %collective-permute-start.8 = (f32[256,512]{1,0:T(8,128)S(1)}, f32[256,512]{1,0:T(8,128)S(1)}, u32[]{:S(2)}, u32[]{:S(2)}) collective-permute-start(f32[256,512]{1,0:T(8,128)S(1)} %get-tuple-element.31), channel_id=1, source_target_pairs={{0,2},{6,4},{1,5},{4,6},{3,7},{8,10},{14,12},{9,13},{12,14},{11,15... | collective-permute-start | bytes 1572872 | tf_op jit(solution)/shard_map/ppermute | solution.py:107
  36.1 23.4 %collective-permute-start.11 = (f32[256,512]{1,0:T(8,128)S(1)}, f32[256,512]{1,0:T(8,128)S(1)}, u32[]{:S(2)}, u32[]{:S(2)}) collective-permute-start(f32[256,512]{1,0:T(8,128)S(1)} %add_add_fusion), channel_id=1, source_target_pairs={{24,0},{25,1},{26,2},{27,3},{28,4},{29,5},{30,6},{31,7},{0,8},{1,9... | collective-permute-start | bytes 1572872 | tf_op jit(solution)/shard_map/ppermute | solution.py:107
  59.8 13.8 %collective-permute-start.13 = (f32[256,512]{1,0:T(8,128)S(1)}, f32[256,512]{1,0:T(8,128)S(1)}, u32[]{:S(2)}, u32[]{:S(2)}) collective-permute-start(f32[256,512]{1,0:T(8,128)S(1)} %add_add_fusion.1.refs_0_.image_ref.own), channel_id=1, source_target_pairs={{0,24},{1,25},{2,26},{3,27},{4,28},{5,29},{6,30},{7,31},{8,0},{9,1... | collective-permute-start | bytes 1572872 | tf_op jit(solution)/shard_map/ppermute | solution.py:107
  62.4 11.2 %collective-permute-start.12 = (f32[256,512]{1,0:T(8,128)S(1)}, f32[256,512]{1,0:T(8,128)S(1)}, u32[]{:S(2)}, u32[]{:S(2)}) collective-permute-start(f32[256,512]{1,0:T(8,128)S(1)} %add_add_fusion.1.refs_0_.image_ref.own), channel_id=1, source_target_pairs={{0,2},{1,5},{2,0},{3,7},{4,6},{5,1},{6,4},{7,3},{8,10},{9,13},{10,... | collective-permute-start | bytes 1572872 | tf_op jit(solution)/shard_map/ppermute | solution.py:107
  73.6 8.3 %collective-permute-start.14 = (f32[256,512]{1,0:T(8,128)S(1)}, f32[256,512]{1,0:T(8,128)S(1)}, u32[]{:S(2)}, u32[]{:S(2)}) collective-permute-start(f32[256,512]{1,0:T(8,128)S(1)} %collective-permute-done.13.refs_2_.group), channel_id=1, source_target_pairs={{0,2},{1,5},{2,0},{3,7},{4,6},{5,1},{6,4},{7,3},{8,10},{9,13},{10,... | collective-permute-start | bytes 1572872 | tf_op jit(solution)/shard_map/ppermute | solution.py:107
  82.6 19.6 %collective-permute-start.17 = (f32[2,256,512]{2,1,0:T(8,128)S(1)}, f32[2,256,512]{2,1,0:T(8,128)S(1)}, u32[]{:S(2)}, u32[]{:S(2)}) collective-permute-start(f32[2,256,512]{2,1,0:T(8,128)S(1)} %choose.3.refs_1_), channel_id=1, source_target_pairs={{0,4},{1,3},{2,6},{3,1},{4,0},{5,7},{6,2},{7,5},{8,12},{9,11},{10,... | collective-permute-start | bytes 3145736 | tf_op jit(solution)/shard_map/ppermute | solution.py:107
  86.6 4.5 %collective-permute-start.15 = (f32[1,256,512]{2,1,0:T(8,128)S(1)}, f32[1,256,512]{2,1,0:T(8,128)S(1)}, u32[]{:S(2)}, u32[]{:S(2)}) collective-permute-start(f32[1,256,512]{2,1,0:T(8,128)S(1)} %get-tuple-element.37), channel_id=1, source_target_pairs={{0,1},{1,0},{2,3},{3,2},{4,5},{5,4},{6,7},{7,6},{8,9},{9,8},{10,11... | collective-permute-start | bytes 1572872 | tf_op jit(solution)/shard_map/ppermute | solution.py:393
  89.1 11.2 %collective-permute-start.16 = (f32[256,512]{1,0:T(8,128)S(1)}, f32[256,512]{1,0:T(8,128)S(1)}, u32[]{:S(2)}, u32[]{:S(2)}) collective-permute-start(f32[256,512]{1,0:T(8,128)S(1)} %collective-permute-done.14.refs_3_.both), channel_id=1, source_target_pairs={{2,30},{5,31},{10,6},{13,7},{18,14},{21,15},{26,22},{29,23}} | collective-permute-start | bytes 1572872 | tf_op jit(solution)/shard_map/ppermute | solution.py:107
  104.2 4.5 %collective-permute-start.18 = (f32[2,256,512]{2,1,0:T(8,128)S(1)}, f32[2,256,512]{2,1,0:T(8,128)S(1)}, u32[]{:S(2)}, u32[]{:S(2)}) collective-permute-start(f32[2,256,512]{2,1,0:T(8,128)S(1)} %get-tuple-element.44), channel_id=1, source_target_pairs={{0,1},{1,0},{2,3},{3,2},{4,5},{5,4},{6,7},{7,6},{8,9},{9,8},{10,11... | collective-permute-start | bytes 3145736 | tf_op jit(solution)/shard_map/ppermute | solution.py:393

commit v11 on v10

--- a/solution.py
+++ b/solution.py
@@ -410,7 +410,7 @@
     own, bin_first, bin_group, bin_both, bin_two = make_bins(offsets, offsets_next, own, far, theirs)
     got_both = send(bin_both, "first")
     got_two = send(bin_two, "two", reverse=True)
-    chosen = choose(offsets_next, data, data_first, data_group, data_both, data_two)
+    chosen = choose(after(offsets_next, got_both), data, data_first, data_group, data_both, data_two)
     data_last = send(chosen, "last")
     data_sources = (data, data_first, data_group, data_both, data_last)
 

time: 111 us -> 119 us (1.072)
  starting transfers between devices: 26.9 us -> 31.8 us
  waiting for transfers between devices: 64.2 us -> 66.9 us
  Pallas kernels: 15.2 us -> 16.6 us
    ppermute x17, starting transfers between devices: 22.2 us -> 29.2 us  [send(): return lax.ppermute(value, ('var', 'samp'), pairs)]
    ppermute x17, waiting for transfers between devices: 61.9 us -> 64.6 us  [send(): return lax.ppermute(value, ('var', 'samp'), pairs)]
    ppermute x2, starting transfers between devices: 4.75 us -> 2.55 us  [swap(): return lax.ppermute(value, 'samp', [(0, 1), (1, 0)])]
    unnamed x10 -> x6, local copies, waits for them, and re-layouts: 2.95 us -> 1.9 us
  transfers between devices with their start and end apart: 19 -> 19, of which waited for: 9 -> 12; matrix products, arithmetic and copies ran while one was open for 0% -> 0% of each run, Pallas kernels for 10% -> 10%
where the time goes in v11:
time: 119 us; the launch traced here: 118 us
  waiting for transfers between devices  66.9 us (56%)
  starting transfers between devices  31.8 us (27%)
  Pallas kernels  16.6 us (14%)
  local copies, waits for them, and re-layouts  1.9 us (2%)
    ppermute x17, waiting for transfers between devices, send(): return lax.ppermute(value, ('var', 'samp'), pairs)  64.6 us
    ppermute x17, starting transfers between devices, send(): return lax.ppermute(value, ('var', 'samp'), pairs)  29.2 us
    pallas_call x1, Pallas kernels, right(): pl.pallas_call(functools.partial(right_kernel, slots, pair), in_specs=[sm...  3.61 us
    pallas_call x2, Pallas kernels, finish(): pl.pallas_call(functools.partial(finish_kernel, begin, factor), grid=(cou...  3.37 us
    pallas_call x1, Pallas kernels, forward(): pl.pallas_call(forward_kernel, grid=(slots,), in_specs=[flat, pl.BlockSpe...  2.94 us
    ppermute x2, starting transfers between devices, swap(): return lax.ppermute(value, 'samp', [(0, 1), (1, 0)])  2.55 us
  transfers between devices with their start and end apart: 19, of which 12 were waited for; matrix products, arithmetic and copies ran while one was open for 0% of the time, Pallas kernels for 10%

profile of v11, /device:TPU:7, one launch (start us, length us, event | category | flops | bytes accessed | tf_op | source)
XLA Modules:
  0.0 118.3 jit_solution(2984071151961159455)
XLA Ops:
  0.3 1.9 %copy-done = f32[1,3,512,512]{3,2,1,0:T(8,128)S(1)} copy-done((f32[1,3,512,512]{3,2,1,0:T(8,128)S(1)}, f32[1,3,512,512]{3,2,1,0:T(8,128)}, u32[]{:S(2)}) %copy-start) | copy-done | bytes 3145752
  2.2 2.9 %forward.1 = (f32[256,512]{1,0:T(8,128)S(1)}, f32[256,512]{1,0:T(8,128)S(1)}, f32[256,512]{1,0:T(8,128)S(1)}) custom-call(f32[256,512]{1,0:T(8,128)} %own.3, f32[3,512,512]{2,1,0:T(8,128)S(1)} %bitcast.2), custom_call_target="tpu_custom_call" | custom-call | tf_op jit(solution)/shard_map/forward/pallas_call | solution.py:124
  5.1 3.4 %collective-permute-done.1.refs_1_.first = f32[256,512]{1,0:T(8,128)S(1)} collective-permute-done((f32[256,512]{1,0:T(8,128)}, f32[256,512]{1,0:T(8,128)S(1)}, u32[]{:S(2)}, u32[]{:S(2)}) %collective-permute-start.1) | collective-permute-done | bytes 524320 | tf_op jit(solution)/shard_map/ppermute | solution.py:107
  10.0 3.3 %collective-permute-start.4 = (f32[256,512]{1,0:T(8,128)}, f32[256,512]{1,0:T(8,128)S(1)}, u32[]{:S(2)}, u32[]{:S(2)}) collective-permute-start(f32[256,512]{1,0:T(8,128)} %own.3), channel_id=1, source_target_pairs={{0,24},{1,25},{2,26},{3,27},{4,28},{5,29},{6,30},{7,31},{8,0},{9,1... | collective-permute-start | bytes 1572872 | tf_op jit(solution)/shard_map/ppermute | solution.py:107
  13.3 3.5 %collective-permute-done.3.refs_3_ = f32[256,512]{1,0:T(8,128)S(1)} collective-permute-done((f32[256,512]{1,0:T(8,128)S(1)}, f32[256,512]{1,0:T(8,128)S(1)}, u32[]{:S(2)}, u32[]{:S(2)}) %collective-permute-start.3) | collective-permute-done | bytes 524320 | tf_op jit(solution)/shard_map/ppermute | solution.py:107
  16.9 5.6 %collective-permute-done.2.refs_2_ = f32[256,512]{1,0:T(8,128)S(1)} collective-permute-done((f32[256,512]{1,0:T(8,128)S(1)}, f32[256,512]{1,0:T(8,128)S(1)}, u32[]{:S(2)}, u32[]{:S(2)}) %collective-permute-start.2) | collective-permute-done | bytes 524320 | tf_op jit(solution)/shard_map/ppermute | solution.py:107
  22.5 1.4 %bins.1 = (f32[256,512]{1,0:T(8,128)S(1)}, f32[256,512]{1,0:T(8,128)S(1)}, f32[256,512]{1,0:T(8,128)S(1)}, f32[256,512]{1,0:T(8,128)S(1)}, f32[256,512]{1,0:T(8,128)S(1)}) custom-call(s32[1,3]{1,0:T(1,128)S(1)} %copy-done.2, s32[1,3]{1,0:T(1,128)S(1)} %collective-permute-done.next_ref.offs_ref, f32[256,512]{1,0:T(8,128)S(1)} %get-tuple-element.26.own_in, ...), custom_call_target="tpu_custom_call" | custom-call | tf_op jit(solution)/shard_map/bins/pallas_call | solution.py:240
  26.8 5.5 %collective-permute-done.6 = f32[256,512]{1,0:T(8,128)S(1)} collective-permute-done((f32[256,512]{1,0:T(8,128)S(1)}, f32[256,512]{1,0:T(8,128)S(1)}, u32[]{:S(2)}, u32[]{:S(2)}) %collective-permute-start.6) | collective-permute-done | bytes 524320 | tf_op jit(solution)/shard_map/ppermute | solution.py:107
  32.3 5.6 %collective-permute-done.5.refs_3_.both = f32[256,512]{1,0:T(8,128)S(1)} collective-permute-done((f32[256,512]{1,0:T(8,128)S(1)}, f32[256,512]{1,0:T(8,128)S(1)}, u32[]{:S(2)}, u32[]{:S(2)}) %collective-permute-start.5) | collective-permute-done | bytes 524320 | tf_op jit(solution)/shard_map/ppermute | solution.py:107
  38.6 10.0 %collective-permute-start.8 = (f32[2,256,512]{2,1,0:T(8,128)S(1)}, f32[2,256,512]{2,1,0:T(8,128)S(1)}, u32[]{:S(2)}, u32[]{:S(2)}) collective-permute-start(f32[2,256,512]{2,1,0:T(8,128)S(1)} %choose.2), channel_id=1, source_target_pairs={{0,4},{1,3},{2,6},{3,1},{4,0},{5,7},{6,2},{7,5},{8,12},{9,11},{10,... | collective-permute-start | bytes 3145736 | tf_op jit(solution)/shard_map/ppermute | solution.py:107
  48.5 1.3 %collective-permute-start.9 = (f32[256,512]{1,0:T(8,128)S(1)}, f32[256,512]{1,0:T(8,128)S(1)}, u32[]{:S(2)}, u32[]{:S(2)}) collective-permute-start(f32[256,512]{1,0:T(8,128)S(1)} %get-tuple-element.34), channel_id=1, source_target_pairs={{0,2},{6,4},{1,5},{4,6},{3,7},{8,10},{14,12},{9,13},{12,14},{11,15... | collective-permute-start | bytes 1572872 | tf_op jit(solution)/shard_map/ppermute | solution.py:107
  50.0 14.9 %collective-permute-done.8.refs_0_ = f32[2,256,512]{2,1,0:T(8,128)S(1)} collective-permute-done((f32[2,256,512]{2,1,0:T(8,128)S(1)}, f32[2,256,512]{2,1,0:T(8,128)S(1)}, u32[]{:S(2)}, u32[]{:S(2)}) %collective-permute-start.8) | collective-permute-done | bytes 1048608 | tf_op jit(solution)/shard_map/ppermute | solution.py:107
  65.0 2.0 %backward.1 = f32[256,512]{1,0:T(8,128)S(1)} custom-call(s32[1,3]{1,0:T(1,128)S(1)} %copy-done.2, f32[3,512,512]{2,1,0:T(8,128)S(1)} %bitcast.3, f32[256,512]{1,0:T(8,128)} %own.3, f32[256,512]{1,0:T(8,128)S(1)} %collective-permute-done.1.refs_1_.first, f32[256,512]{1,0:T(8,128)S(1)} %collective-permute-done.4.refs_2_.group, ...), custom_call_target="tpu_custom_call" | custom-call | tf_op jit(solution)/shard_map/backward/pallas_call | solution.py:202
  68.1 7.3 %collective-permute-done.13.refs_2_.group = f32[256,512]{1,0:T(8,128)S(1)} collective-permute-done((f32[256,512]{1,0:T(8,128)S(1)}, f32[256,512]{1,0:T(8,128)S(1)}, u32[]{:S(2)}, u32[]{:S(2)}) %collective-permute-start.13) | collective-permute-done | bytes 524320 | tf_op jit(solution)/shard_map/ppermute | solution.py:107
  75.4 8.0 %collective-permute-done.14.refs_3_.both = f32[256,512]{1,0:T(8,128)S(1)} collective-permute-done((f32[256,512]{1,0:T(8,128)S(1)}, f32[256,512]{1,0:T(8,128)S(1)}, u32[]{:S(2)}, u32[]{:S(2)}) %collective-permute-start.14) | collective-permute-done | bytes 524320 | tf_op jit(solution)/shard_map/ppermute | solution.py:107
  84.0 7.9 %collective-permute-start.17 = (f32[2,256,512]{2,1,0:T(8,128)S(1)}, f32[2,256,512]{2,1,0:T(8,128)S(1)}, u32[]{:S(2)}, u32[]{:S(2)}) collective-permute-start(f32[2,256,512]{2,1,0:T(8,128)S(1)} %choose.3.refs_1_), channel_id=1, source_target_pairs={{0,4},{1,3},{2,6},{3,1},{4,0},{5,7},{6,2},{7,5},{8,12},{9,11},{10,... | collective-permute-start | bytes 3145736 | tf_op jit(solution)/shard_map/ppermute | solution.py:107
  91.9 3.6 %right.1 = (f32[1,256,512]{2,1,0:T(8,128)S(1)}, f32[1,256,512]{2,1,0:T(8,128)S(1)}, f32[2,256,512]{2,1,0:T(8,128)S(1)}, f32[2,256,512]{2,1,0:T(8,128)S(1)}, bf16...) custom-call(s32[1,3]{1,0:T(1,128)S(1)} %copy-done.2, f32[256,512]{1,0:T(8,128)} %own.3, ...), custom_call_target="tpu_custom_call" | custom-call | flops 26843545600 | tf_op jit(solution)/shard_map/right/pallas_call | solution.py:296
  97.8 1.6 %finish.2.refs_0_ = f32[3,256,512]{2,1,0:T(8,128)} custom-call(s32[1,3]{1,0:T(1,128)S(1)} %copy-done.2, f32[1]{0:T(128)S(6)} %copy.7.step_ref, f32[3,512,512]{2,1,0:T(8,128)S(1)} %bitcast.4, f32[1,256,512]{2,1,0:T(8,128)S(1)} %get-tuple-element.38.keep_ref, f32[1,256,512]{2,1,0:T(8,128)S(1)} %collective-permute-done.15.other_ref), custom_call_target="tpu_custom_call" | custom-call | tf_op jit(solution)/shard_map/finish/pallas_call | solution.py:375
  99.4 7.6 %collective-permute-done.16.two = f32[256,512]{1,0:T(8,128)S(1)} collective-permute-done((f32[256,512]{1,0:T(8,128)S(1)}, f32[256,512]{1,0:T(8,128)S(1)}, u32[]{:S(2)}, u32[]{:S(2)}) %collective-permute-start.16) | collective-permute-done | bytes 524320 | tf_op jit(solution)/shard_map/ppermute | solution.py:107
  107.0 3.0 %collective-permute-done.17.lasts_ref = f32[2,256,512]{2,1,0:T(8,128)S(1)} collective-permute-done((f32[2,256,512]{2,1,0:T(8,128)S(1)}, f32[2,256,512]{2,1,0:T(8,128)S(1)}, u32[]{:S(2)}, u32[]{:S(2)}) %collective-permute-start.17) | collective-permute-done | bytes 1048608 | tf_op jit(solution)/shard_map/ppermute | solution.py:107
  110.0 1.9 %left.1 = (f32[2,256,512]{2,1,0:T(8,128)S(1)}, f32[2,256,512]{2,1,0:T(8,128)S(1)}) custom-call(s32[1,3]{1,0:T(1,128)S(1)} %copy-done.2, f32[2,256,512]{2,1,0:T(8,128)S(1)} %get-tuple-element.40.keep_in, f32[2,256,512]{2,1,0:T(8,128)S(1)} %get-tuple-element.41.send_in, bf16[512,256]{1,0:T(8,128)(2,1)S(1)} %get-tuple-element.42.high_ref, ...), custom_call_target="tpu_custom_call" | custom-call | tf_op jit(solution)/shard_map/left/pallas_call | solution.py:334
  112.0 2.2 %collective-permute-start.18 = (f32[2,256,512]{2,1,0:T(8,128)S(1)}, f32[2,256,512]{2,1,0:T(8,128)S(1)}, u32[]{:S(2)}, u32[]{:S(2)}) collective-permute-start(f32[2,256,512]{2,1,0:T(8,128)S(1)} %get-tuple-element.46), channel_id=1, source_target_pairs={{0,1},{1,0},{2,3},{3,2},{4,5},{5,4},{6,7},{7,6},{8,9},{9,8},{10,11... | collective-permute-start | bytes 3145736 | tf_op jit(solution)/shard_map/ppermute | solution.py:393
  114.2 2.3 %collective-permute-done.18.other_ref = f32[2,256,512]{2,1,0:T(8,128)S(1)} collective-permute-done((f32[2,256,512]{2,1,0:T(8,128)S(1)}, f32[2,256,512]{2,1,0:T(8,128)S(1)}, u32[]{:S(2)}, u32[]{:S(2)}) %collective-permute-start.18) | collective-permute-done | bytes 1048608 | tf_op jit(solution)/shard_map/ppermute | solution.py:393
  116.5 1.8 %finish.3 = f32[3,256,512]{2,1,0:T(8,128)} custom-call(s32[1,3]{1,0:T(1,128)S(1)} %copy-done.2, f32[1]{0:T(128)S(6)} %copy.7.step_ref, f32[3,512,512]{2,1,0:T(8,128)S(1)} %bitcast.5, f32[2,256,512]{2,1,0:T(8,128)S(1)} %get-tuple-element.45.keep_ref, f32[2,256,512]{2,1,0:T(8,128)S(1)} %collective-permute-done.18.other_ref, ...), custom_call_target="tpu_custom_call", output_to_operand_aliasing={{}: (5, {})} | custom-call | tf_op jit(solution)/shard_map/finish/pallas_call | solution.py:375
  (31 shorter events, 8.8 us)
Async XLA Ops:
  0.0 8.5 %collective-permute-start.1 = (f32[256,512]{1,0:T(8,128)}, f32[256,512]{1,0:T(8,128)S(1)}, u32[]{:S(2)}, u32[]{:S(2)}) collective-permute-start(f32[256,512]{1,0:T(8,128)} %own.3), channel_id=1, source_target_pairs={{0,2},{1,5},{2,0},{3,7},{4,6},{5,1},{6,4},{7,3},{8,10},{9,13},{10,... | collective-permute-start | bytes 1572872 | tf_op jit(solution)/shard_map/ppermute | solution.py:107
  0.2 4.9 %collective-permute-start = (s32[1,3]{1,0:T(1,128)}, s32[1,3]{1,0:T(1,128)S(1)}, u32[]{:S(2)}, u32[]{:S(2)}) collective-permute-start(s32[1,3]{1,0:T(1,128)} %offs_ref.11), channel_id=1, source_target_pairs={{0,4},{1,3},{2,6},{3,1},{4,0},{5,7},{6,2},{7,5},{8,12},{9,11},{10,... | collective-permute-start | bytes 44 | tf_op jit(solution)/shard_map/ppermute | solution.py:107
  0.3 1.9 %copy-start = (f32[1,3,512,512]{3,2,1,0:T(8,128)S(1)}, f32[1,3,512,512]{3,2,1,0:T(8,128)}, u32[]{:S(2)}) copy-start(f32[1,3,512,512]{3,2,1,0:T(8,128)} %param.5) | copy-start | bytes 9437188
  2.1 20.3 %copy-start.2 = (s32[1,3]{1,0:T(1,128)S(1)}, s32[1,3]{1,0:T(1,128)}, u32[]{:S(2)}) copy-start(s32[1,3]{1,0:T(1,128)} %offs_ref.11) | copy-start | bytes 40
  8.5 8.3 %collective-permute-start.3 = (f32[256,512]{1,0:T(8,128)S(1)}, f32[256,512]{1,0:T(8,128)S(1)}, u32[]{:S(2)}, u32[]{:S(2)}) collective-permute-start(f32[256,512]{1,0:T(8,128)S(1)} %get-tuple-element.30.refs_1_), channel_id=1, source_target_pairs={{0,4},{1,3},{2,6},{3,1},{4,0},{5,7},{6,2},{7,5},{8,12},{9,11},{10,... | collective-permute-start | bytes 1572872 | tf_op jit(solution)/shard_map/ppermute | solution.py:107
  8.8 13.7 %collective-permute-start.2 = (f32[256,512]{1,0:T(8,128)S(1)}, f32[256,512]{1,0:T(8,128)S(1)}, u32[]{:S(2)}, u32[]{:S(2)}) collective-permute-start(f32[256,512]{1,0:T(8,128)S(1)} %get-tuple-element.29.refs_0_), channel_id=1, source_target_pairs={{0,4},{1,3},{2,6},{3,1},{4,0},{5,7},{6,2},{7,5},{8,12},{9,11},{10,... | collective-permute-start | bytes 1572872 | tf_op jit(solution)/shard_map/ppermute | solution.py:107
  10.0 14.2 %collective-permute-start.4 = (f32[256,512]{1,0:T(8,128)}, f32[256,512]{1,0:T(8,128)S(1)}, u32[]{:S(2)}, u32[]{:S(2)}) collective-permute-start(f32[256,512]{1,0:T(8,128)} %own.3), channel_id=1, source_target_pairs={{0,24},{1,25},{2,26},{3,27},{4,28},{5,29},{6,30},{7,31},{8,0},{9,1... | collective-permute-start | bytes 1572872 | tf_op jit(solution)/shard_map/ppermute | solution.py:107
  23.9 8.4 %collective-permute-start.6 = (f32[256,512]{1,0:T(8,128)S(1)}, f32[256,512]{1,0:T(8,128)S(1)}, u32[]{:S(2)}, u32[]{:S(2)}) collective-permute-start(f32[256,512]{1,0:T(8,128)S(1)} %get-tuple-element.32), channel_id=1, source_target_pairs={{0,2},{1,5},{2,0},{3,7},{4,6},{5,1},{6,4},{7,3},{8,10},{9,13},{10,... | collective-permute-start | bytes 1572872 | tf_op jit(solution)/shard_map/ppermute | solution.py:107
  24.2 13.7 %collective-permute-start.5 = (f32[256,512]{1,0:T(8,128)S(1)}, f32[256,512]{1,0:T(8,128)S(1)}, u32[]{:S(2)}, u32[]{:S(2)}) collective-permute-start(f32[256,512]{1,0:T(8,128)S(1)} %collective-permute-done.4.refs_2_.group), channel_id=1, source_target_pairs={{0,2},{1,5},{2,0},{3,7},{4,6},{5,1},{6,4},{7,3},{8,10},{9,13},{10,... | collective-permute-start | bytes 1572872 | tf_op jit(solution)/shard_map/ppermute | solution.py:107
  25.4 12.5 %collective-permute-start.7 = (f32[256,512]{1,0:T(8,128)S(1)}, f32[256,512]{1,0:T(8,128)S(1)}, u32[]{:S(2)}, u32[]{:S(2)}) collective-permute-start(f32[256,512]{1,0:T(8,128)S(1)} %collective-permute-done.1.refs_1_.first), channel_id=1, source_target_pairs={{2,18},{5,21},{10,26},{13,29},{18,2},{21,5},{26,10},{29,13}} | collective-permute-start | bytes 1572872 | tf_op jit(solution)/shard_map/ppermute | solution.py:107
  26.1 23.7 %collective-permute-start.10 = (f32[256,512]{1,0:T(8,128)S(1)}, f32[256,512]{1,0:T(8,128)S(1)}, u32[]{:S(2)}, u32[]{:S(2)}) collective-permute-start(f32[256,512]{1,0:T(8,128)S(1)} %get-tuple-element.36), channel_id=1, source_target_pairs={{26,0},{29,1},{2,8},{5,9},{10,16},{13,17},{18,24},{21,25}} | collective-permute-start | bytes 1572872 | tf_op jit(solution)/shard_map/ppermute | solution.py:107
  37.9 27.0 %copy-start.1 = (f32[1,3,512,512]{3,2,1,0:T(8,128)S(1)}, f32[1,3,512,512]{3,2,1,0:T(8,128)}, u32[]{:S(2)}) copy-start(f32[1,3,512,512]{3,2,1,0:T(8,128)} %param.5) | copy-start | bytes 9437188
  38.6 26.4 %collective-permute-start.8 = (f32[2,256,512]{2,1,0:T(8,128)S(1)}, f32[2,256,512]{2,1,0:T(8,128)S(1)}, u32[]{:S(2)}, u32[]{:S(2)}) collective-permute-start(f32[2,256,512]{2,1,0:T(8,128)S(1)} %choose.2), channel_id=1, source_target_pairs={{0,4},{1,3},{2,6},{3,1},{4,0},{5,7},{6,2},{7,5},{8,12},{9,11},{10,... | collective-permute-start | bytes 3145736 | tf_op jit(solution)/shard_map/ppermute | solution.py:107
  48.5 18.5 %collective-permute-start.9 = (f32[256,512]{1,0:T(8,128)S(1)}, f32[256,512]{1,0:T(8,128)S(1)}, u32[]{:S(2)}, u32[]{:S(2)}) collective-permute-start(f32[256,512]{1,0:T(8,128)S(1)} %get-tuple-element.34), channel_id=1, source_target_pairs={{0,2},{6,4},{1,5},{4,6},{3,7},{8,10},{14,12},{9,13},{12,14},{11,15... | collective-permute-start | bytes 1572872 | tf_op jit(solution)/shard_map/ppermute | solution.py:107
  50.0 17.1 %collective-permute-start.11 = (f32[256,512]{1,0:T(8,128)S(1)}, f32[256,512]{1,0:T(8,128)S(1)}, u32[]{:S(2)}, u32[]{:S(2)}) collective-permute-start(f32[256,512]{1,0:T(8,128)S(1)} %add_add_fusion), channel_id=1, source_target_pairs={{24,0},{25,1},{26,2},{27,3},{28,4},{29,5},{30,6},{31,7},{0,8},{1,9... | collective-permute-start | bytes 1572872 | tf_op jit(solution)/shard_map/ppermute | solution.py:107
  67.3 8.1 %collective-permute-start.13 = (f32[256,512]{1,0:T(8,128)S(1)}, f32[256,512]{1,0:T(8,128)S(1)}, u32[]{:S(2)}, u32[]{:S(2)}) collective-permute-start(f32[256,512]{1,0:T(8,128)S(1)} %add_add_fusion.1.refs_0_.image_ref.own), channel_id=1, source_target_pairs={{0,24},{1,25},{2,26},{3,27},{4,28},{5,29},{6,30},{7,31},{8,0},{9,1... | collective-permute-start | bytes 1572872 | tf_op jit(solution)/shard_map/ppermute | solution.py:107
  67.3 8.1 %collective-permute-start.12 = (f32[256,512]{1,0:T(8,128)S(1)}, f32[256,512]{1,0:T(8,128)S(1)}, u32[]{:S(2)}, u32[]{:S(2)}) collective-permute-start(f32[256,512]{1,0:T(8,128)S(1)} %add_add_fusion.1.refs_0_.image_ref.own), channel_id=1, source_target_pairs={{0,2},{1,5},{2,0},{3,7},{4,6},{5,1},{6,4},{7,3},{8,10},{9,13},{10,... | collective-permute-start | bytes 1572872 | tf_op jit(solution)/shard_map/ppermute | solution.py:107
  75.4 8.0 %collective-permute-start.14 = (f32[256,512]{1,0:T(8,128)S(1)}, f32[256,512]{1,0:T(8,128)S(1)}, u32[]{:S(2)}, u32[]{:S(2)}) collective-permute-start(f32[256,512]{1,0:T(8,128)S(1)} %collective-permute-done.13.refs_2_.group), channel_id=1, source_target_pairs={{0,2},{1,5},{2,0},{3,7},{4,6},{5,1},{6,4},{7,3},{8,10},{9,13},{10,... | collective-permute-start | bytes 1572872 | tf_op jit(solution)/shard_map/ppermute | solution.py:107
  84.0 26.0 %collective-permute-start.17 = (f32[2,256,512]{2,1,0:T(8,128)S(1)}, f32[2,256,512]{2,1,0:T(8,128)S(1)}, u32[]{:S(2)}, u32[]{:S(2)}) collective-permute-start(f32[2,256,512]{2,1,0:T(8,128)S(1)} %choose.3.refs_1_), channel_id=1, source_target_pairs={{0,4},{1,3},{2,6},{3,1},{4,0},{5,7},{6,2},{7,5},{8,12},{9,11},{10,... | collective-permute-start | bytes 3145736 | tf_op jit(solution)/shard_map/ppermute | solution.py:107
  95.6 2.3 %collective-permute-start.15 = (f32[1,256,512]{2,1,0:T(8,128)S(1)}, f32[1,256,512]{2,1,0:T(8,128)S(1)}, u32[]{:S(2)}, u32[]{:S(2)}) collective-permute-start(f32[1,256,512]{2,1,0:T(8,128)S(1)} %get-tuple-element.39), channel_id=1, source_target_pairs={{0,1},{1,0},{2,3},{3,2},{4,5},{5,4},{6,7},{7,6},{8,9},{9,8},{10,11... | collective-permute-start | bytes 1572872 | tf_op jit(solution)/shard_map/ppermute | solution.py:393
  95.9 11.2 %collective-permute-start.16 = (f32[256,512]{1,0:T(8,128)S(1)}, f32[256,512]{1,0:T(8,128)S(1)}, u32[]{:S(2)}, u32[]{:S(2)}) collective-permute-start(f32[256,512]{1,0:T(8,128)S(1)} %collective-permute-done.14.refs_3_.both), channel_id=1, source_target_pairs={{2,30},{5,31},{10,6},{13,7},{18,14},{21,15},{26,22},{29,23}} | collective-permute-start | bytes 1572872 | tf_op jit(solution)/shard_map/ppermute | solution.py:107
  112.0 4.5 %collective-permute-start.18 = (f32[2,256,512]{2,1,0:T(8,128)S(1)}, f32[2,256,512]{2,1,0:T(8,128)S(1)}, u32[]{:S(2)}, u32[]{:S(2)}) collective-permute-start(f32[2,256,512]{2,1,0:T(8,128)S(1)} %get-tuple-element.46), channel_id=1, source_target_pairs={{0,1},{1,0},{2,3},{3,2},{4,5},{5,4},{6,7},{7,6},{8,9},{9,8},{10,11... | collective-permute-start | bytes 3145736 | tf_op jit(solution)/shard_map/ppermute | solution.py:393

commit v12 on v10

--- a/solution.py
+++ b/solution.py
@@ -107,30 +107,39 @@
     return lax.ppermute(value, ("var", "samp"), pairs)
 
 
-def forward_kernel(data_ref, tile_ref, *out_refs):
-    slot = pl.program_id(0)
-    value = dot3(split(data_ref[...]), split(tile_ref[...]), NN)
-    for which, ref in enumerate(out_refs):
-
-        @pl.when(slot == which)
-        def _():
-            ref[...] = value
+def forward_kernel(data_hbm, tiles_hbm, *refs):
+    slots = tiles_hbm.shape[0]
+    out_refs, (data_ref, tiles_ref, sems) = refs[:slots], refs[slots:]
+    data_copy = pltpu.make_async_copy(data_hbm, data_ref, sems.at[slots])
+    copies = [pltpu.make_async_copy(tiles_hbm.at[slot], tiles_ref.at[slot], sems.at[slot]) for slot in range(slots)]
+    order = list(range(1, slots)) + [0]
+    data_copy.start()
+    for slot in order:
+        copies[slot].start()
+    data_copy.wait()
+    data = split(data_ref[...])
+    for slot in order:
+        copies[slot].wait()
+        out_refs[slot][...] = dot3(data, split(tiles_ref[slot]), NN)
 
 
 def forward(data, tiles):
     slots, block = tiles.shape[:2]
     rows = data.shape[0]
-    flat = pl.BlockSpec((rows, block), lambda j: (0, 0))
     return pl.pallas_call(
         forward_kernel,
-        grid=(slots,),
-        in_specs=[flat, pl.BlockSpec((None, block, block), lambda j: (j, 0, 0))],
-        out_specs=[flat] * slots,
+        in_specs=[pl.BlockSpec(memory_space=pltpu.HBM)] * 2,
+        out_specs=[vmem_spec()] * slots,
         out_shape=[jax.ShapeDtypeStruct((rows, block), f32)] * slots,
+        scratch_shapes=[
+            pltpu.VMEM((rows, block), f32),
+            pltpu.VMEM((slots, block, block), f32),
+            pltpu.SemaphoreType.DMA((slots + 1,)),
+        ],
         compiler_params=params(),
         cost_estimate=cost(6 * slots * rows * block * block, 4 * slots * block * (block + 2 * rows)),
         name="forward",
-    )(data, tiles)
+    )(*(pltpu.with_memory_space_constraint(each, pltpu.HBM) for each in (data, tiles)))
 
 
 CODES = (0, 1, 2, 3, 5)

time: 111 us -> 110 us (level)
  waiting for transfers between devices: 64.2 us -> 67.2 us
  local copies, waits for them, and re-layouts: 2.95 us -> 0.01 us
  starting transfers between devices: 26.9 us -> 24.6 us
    ppermute x17, waiting for transfers between devices: 61.9 us -> 64.9 us  [send(): return lax.ppermute(value, ('var', 'samp'), pairs)]
    unnamed x10 -> x6, local copies, waits for them, and re-layouts: 2.95 us -> 0.01 us
    ppermute x17, starting transfers between devices: 22.2 us -> 19.8 us  [send(): return lax.ppermute(value, ('var', 'samp'), pairs)]
    pallas_call x1, Pallas kernels: 1.89 us -> 3.2 us  [forward(): pl.pallas_call(forward_kernel, in_specs=[pl.BlockSpec(memory_space=pltpu....]
  transfers between devices with their start and end apart: 19 -> 19, of which waited for: 9 -> 11; matrix products, arithmetic and copies ran while one was open for 0% -> 0% of each run, Pallas kernels for 10% -> 11%
where the time goes in v12:
time: 110 us; the launch traced here: 109 us
  waiting for transfers between devices  67.2 us (61%)
  starting transfers between devices  24.6 us (22%)
  Pallas kernels  16.3 us (15%)
    ppermute x17, waiting for transfers between devices, send(): return lax.ppermute(value, ('var', 'samp'), pairs)  64.9 us
    ppermute x17, starting transfers between devices, send(): return lax.ppermute(value, ('var', 'samp'), pairs)  19.8 us
    ppermute x2, starting transfers between devices, swap(): return lax.ppermute(value, 'samp', [(0, 1), (1, 0)])  4.77 us
    pallas_call x2, Pallas kernels, finish(): pl.pallas_call(functools.partial(finish_kernel, begin, factor), grid=(cou...  3.37 us
    pallas_call x1, Pallas kernels, forward(): pl.pallas_call(forward_kernel, in_specs=[pl.BlockSpec(memory_space=pltpu....  3.2 us
    pallas_call x1, Pallas kernels, right(): pl.pallas_call(functools.partial(right_kernel, slots, pair), in_specs=[sm...  3.1 us
    ppermute x2, waiting for transfers between devices, swap(): return lax.ppermute(value, 'samp', [(0, 1), (1, 0)])  2.29 us
  transfers between devices with their start and end apart: 19, of which 11 were waited for; matrix products, arithmetic and copies ran while one was open for 0% of the time, Pallas kernels for 11%

profile of v12, /device:TPU:7, one launch (start us, length us, event | category | flops | bytes accessed | tf_op | source)
XLA Modules:
  0.0 109.3 jit_solution(18246353843455089465)
XLA Ops:
  0.2 3.3 %collective-permute-start.4 = (f32[256,512]{1,0:T(8,128)}, f32[256,512]{1,0:T(8,128)S(1)}, u32[]{:S(2)}, u32[]{:S(2)}) collective-permute-start(f32[256,512]{1,0:T(8,128)} %own.3), channel_id=1, source_target_pairs={{0,24},{1,25},{2,26},{3,27},{4,28},{5,29},{6,30},{7,31},{8,0},{9,1... | collective-permute-start | bytes 1572872 | tf_op jit(solution)/shard_map/ppermute | solution.py:107
  3.8 3.2 %forward.1 = (f32[256,512]{1,0:T(8,128)S(1)}, f32[256,512]{1,0:T(8,128)S(1)}, f32[256,512]{1,0:T(8,128)S(1)}) custom-call(f32[256,512]{1,0:T(8,128)} %own.3, f32[3,512,512]{2,1,0:T(8,128)} %bitcast.2), custom_call_target="tpu_custom_call" | custom-call | tf_op jit(solution)/shard_map/forward/pallas_call | solution.py:129
  7.0 1.5 %collective-permute-done.1.refs_1_.first = f32[256,512]{1,0:T(8,128)S(1)} collective-permute-done((f32[256,512]{1,0:T(8,128)}, f32[256,512]{1,0:T(8,128)S(1)}, u32[]{:S(2)}, u32[]{:S(2)}) %collective-permute-start.1) | collective-permute-done | bytes 524320 | tf_op jit(solution)/shard_map/ppermute | solution.py:107
  10.0 4.1 %collective-permute-done.4.refs_2_.group = f32[256,512]{1,0:T(8,128)S(1)} collective-permute-done((f32[256,512]{1,0:T(8,128)}, f32[256,512]{1,0:T(8,128)S(1)}, u32[]{:S(2)}, u32[]{:S(2)}) %collective-permute-start.4) | collective-permute-done | bytes 524320 | tf_op jit(solution)/shard_map/ppermute | solution.py:107
  14.1 2.4 %collective-permute-start.5 = (f32[256,512]{1,0:T(8,128)S(1)}, f32[256,512]{1,0:T(8,128)S(1)}, u32[]{:S(2)}, u32[]{:S(2)}) collective-permute-start(f32[256,512]{1,0:T(8,128)S(1)} %collective-permute-done.4.refs_2_.group), channel_id=1, source_target_pairs={{0,2},{1,5},{2,0},{3,7},{4,6},{5,1},{6,4},{7,3},{8,10},{9,13},{10,... | collective-permute-start | bytes 1572872 | tf_op jit(solution)/shard_map/ppermute | solution.py:107
  17.2 8.5 %collective-permute-done.2.refs_2_ = f32[256,512]{1,0:T(8,128)S(1)} collective-permute-done((f32[256,512]{1,0:T(8,128)S(1)}, f32[256,512]{1,0:T(8,128)S(1)}, u32[]{:S(2)}, u32[]{:S(2)}) %collective-permute-start.2) | collective-permute-done | bytes 524320 | tf_op jit(solution)/shard_map/ppermute | solution.py:107
  25.7 1.4 %bins.1 = (f32[256,512]{1,0:T(8,128)S(1)}, f32[256,512]{1,0:T(8,128)S(1)}, f32[256,512]{1,0:T(8,128)S(1)}, f32[256,512]{1,0:T(8,128)S(1)}, f32[256,512]{1,0:T(8,128)S(1)}) custom-call(s32[1,3]{1,0:T(1,128)S(1)} %copy-done.2, s32[1,3]{1,0:T(1,128)S(1)} %collective-permute-done.next_ref.offs_ref, f32[256,512]{1,0:T(8,128)S(1)} %get-tuple-element.25.own_in, ...), custom_call_target="tpu_custom_call" | custom-call | tf_op jit(solution)/shard_map/bins/pallas_call | solution.py:249
  29.7 4.2 %collective-permute-start.7 = (f32[2,256,512]{2,1,0:T(8,128)S(1)}, f32[2,256,512]{2,1,0:T(8,128)S(1)}, u32[]{:S(2)}, u32[]{:S(2)}) collective-permute-start(f32[2,256,512]{2,1,0:T(8,128)S(1)} %choose.2), channel_id=1, source_target_pairs={{0,4},{1,3},{2,6},{3,1},{4,0},{5,7},{6,2},{7,5},{8,12},{9,11},{10,... | collective-permute-start | bytes 3145736 | tf_op jit(solution)/shard_map/ppermute | solution.py:107
  33.9 1.3 %collective-permute-start.8 = (f32[256,512]{1,0:T(8,128)S(1)}, f32[256,512]{1,0:T(8,128)S(1)}, u32[]{:S(2)}, u32[]{:S(2)}) collective-permute-start(f32[256,512]{1,0:T(8,128)S(1)} %get-tuple-element.31), channel_id=1, source_target_pairs={{0,2},{6,4},{1,5},{4,6},{3,7},{8,10},{14,12},{9,13},{12,14},{11,15... | collective-permute-start | bytes 1572872 | tf_op jit(solution)/shard_map/ppermute | solution.py:107
  35.9 2.4 %collective-permute-start.11 = (f32[256,512]{1,0:T(8,128)S(1)}, f32[256,512]{1,0:T(8,128)S(1)}, u32[]{:S(2)}, u32[]{:S(2)}) collective-permute-start(f32[256,512]{1,0:T(8,128)S(1)} %add_add_fusion), channel_id=1, source_target_pairs={{24,0},{25,1},{26,2},{27,3},{28,4},{29,5},{30,6},{31,7},{0,8},{1,9... | collective-permute-start | bytes 1572872 | tf_op jit(solution)/shard_map/ppermute | solution.py:107
  38.3 19.2 %collective-permute-done.7.refs_0_ = f32[2,256,512]{2,1,0:T(8,128)S(1)} collective-permute-done((f32[2,256,512]{2,1,0:T(8,128)S(1)}, f32[2,256,512]{2,1,0:T(8,128)S(1)}, u32[]{:S(2)}, u32[]{:S(2)}) %collective-permute-start.7) | collective-permute-done | bytes 1048608 | tf_op jit(solution)/shard_map/ppermute | solution.py:107
  57.5 2.1 %backward.1 = f32[256,512]{1,0:T(8,128)S(1)} custom-call(s32[1,3]{1,0:T(1,128)S(1)} %copy-done.2, f32[3,512,512]{2,1,0:T(8,128)S(1)} %bitcast.3, f32[256,512]{1,0:T(8,128)S(1)} %copy-done.1, f32[256,512]{1,0:T(8,128)S(1)} %collective-permute-done.1.refs_1_.first, f32[256,512]{1,0:T(8,128)S(1)} %collective-permute-done.4.refs_2_.group, ...), custom_call_target="tpu_custom_call" | custom-call | tf_op jit(solution)/shard_map/backward/pallas_call | solution.py:211
  60.8 11.8 %collective-permute-done.13.refs_2_.group = f32[256,512]{1,0:T(8,128)S(1)} collective-permute-done((f32[256,512]{1,0:T(8,128)S(1)}, f32[256,512]{1,0:T(8,128)S(1)}, u32[]{:S(2)}, u32[]{:S(2)}) %collective-permute-start.13) | collective-permute-done | bytes 524320 | tf_op jit(solution)/shard_map/ppermute | solution.py:107
  72.7 8.3 %collective-permute-done.14.refs_3_.both = f32[256,512]{1,0:T(8,128)S(1)} collective-permute-done((f32[256,512]{1,0:T(8,128)S(1)}, f32[256,512]{1,0:T(8,128)S(1)}, u32[]{:S(2)}, u32[]{:S(2)}) %collective-permute-start.14) | collective-permute-done | bytes 524320 | tf_op jit(solution)/shard_map/ppermute | solution.py:107
  82.1 3.1 %right.1 = (f32[1,256,512]{2,1,0:T(8,128)S(1)}, f32[1,256,512]{2,1,0:T(8,128)S(1)}, f32[2,256,512]{2,1,0:T(8,128)S(1)}, f32[2,256,512]{2,1,0:T(8,128)S(1)}, bf16...) custom-call(s32[1,3]{1,0:T(1,128)S(1)} %copy-done.2, f32[256,512]{1,0:T(8,128)S(1)} %copy-done.1, ...), custom_call_target="tpu_custom_call" | custom-call | flops 26843545600 | tf_op jit(solution)/shard_map/right/pallas_call | solution.py:305
  85.2 2.7 %collective-permute-start.15 = (f32[1,256,512]{2,1,0:T(8,128)S(1)}, f32[1,256,512]{2,1,0:T(8,128)S(1)}, u32[]{:S(2)}, u32[]{:S(2)}) collective-permute-start(f32[1,256,512]{2,1,0:T(8,128)S(1)} %get-tuple-element.37), channel_id=1, source_target_pairs={{0,1},{1,0},{2,3},{3,2},{4,5},{5,4},{6,7},{7,6},{8,9},{9,8},{10,11... | collective-permute-start | bytes 1572872 | tf_op jit(solution)/shard_map/ppermute | solution.py:402
  88.0 1.3 %collective-permute-start.16 = (f32[256,512]{1,0:T(8,128)S(1)}, f32[256,512]{1,0:T(8,128)S(1)}, u32[]{:S(2)}, u32[]{:S(2)}) collective-permute-start(f32[256,512]{1,0:T(8,128)S(1)} %collective-permute-done.14.refs_3_.both), channel_id=1, source_target_pairs={{2,30},{5,31},{10,6},{13,7},{18,14},{21,15},{26,22},{29,23}} | collective-permute-start | bytes 1572872 | tf_op jit(solution)/shard_map/ppermute | solution.py:107
  89.9 1.6 %finish.2.refs_0_ = f32[3,256,512]{2,1,0:T(8,128)} custom-call(s32[1,3]{1,0:T(1,128)S(1)} %copy-done.2, f32[1]{0:T(128)S(6)} %copy.7.step_ref, f32[3,512,512]{2,1,0:T(8,128)S(1)} %bitcast.4, f32[1,256,512]{2,1,0:T(8,128)S(1)} %get-tuple-element.36.keep_ref, f32[1,256,512]{2,1,0:T(8,128)S(1)} %collective-permute-done.15.other_ref), custom_call_target="tpu_custom_call" | custom-call | tf_op jit(solution)/shard_map/finish/pallas_call | solution.py:384
  91.5 7.6 %collective-permute-done.16.two = f32[256,512]{1,0:T(8,128)S(1)} collective-permute-done((f32[256,512]{1,0:T(8,128)S(1)}, f32[256,512]{1,0:T(8,128)S(1)}, u32[]{:S(2)}, u32[]{:S(2)}) %collective-permute-start.16) | collective-permute-done | bytes 524320 | tf_op jit(solution)/shard_map/ppermute | solution.py:107
  99.1 2.1 %collective-permute-done.17.lasts_ref = f32[2,256,512]{2,1,0:T(8,128)S(1)} collective-permute-done((f32[2,256,512]{2,1,0:T(8,128)S(1)}, f32[2,256,512]{2,1,0:T(8,128)S(1)}, u32[]{:S(2)}, u32[]{:S(2)}) %collective-permute-start.17) | collective-permute-done | bytes 1048608 | tf_op jit(solution)/shard_map/ppermute | solution.py:107
  101.3 1.9 %left.1 = (f32[2,256,512]{2,1,0:T(8,128)S(1)}, f32[2,256,512]{2,1,0:T(8,128)S(1)}) custom-call(s32[1,3]{1,0:T(1,128)S(1)} %copy-done.2, f32[2,256,512]{2,1,0:T(8,128)S(1)} %get-tuple-element.38.keep_in, f32[2,256,512]{2,1,0:T(8,128)S(1)} %get-tuple-element.39.send_in, bf16[512,256]{1,0:T(8,128)(2,1)S(1)} %get-tuple-element.40.high_ref, ...), custom_call_target="tpu_custom_call" | custom-call | tf_op jit(solution)/shard_map/left/pallas_call | solution.py:343
  103.2 2.1 %collective-permute-start.18 = (f32[2,256,512]{2,1,0:T(8,128)S(1)}, f32[2,256,512]{2,1,0:T(8,128)S(1)}, u32[]{:S(2)}, u32[]{:S(2)}) collective-permute-start(f32[2,256,512]{2,1,0:T(8,128)S(1)} %get-tuple-element.44), channel_id=1, source_target_pairs={{0,1},{1,0},{2,3},{3,2},{4,5},{5,4},{6,7},{7,6},{8,9},{9,8},{10,11... | collective-permute-start | bytes 3145736 | tf_op jit(solution)/shard_map/ppermute | solution.py:402
  105.3 2.3 %collective-permute-done.18.other_ref = f32[2,256,512]{2,1,0:T(8,128)S(1)} collective-permute-done((f32[2,256,512]{2,1,0:T(8,128)S(1)}, f32[2,256,512]{2,1,0:T(8,128)S(1)}, u32[]{:S(2)}, u32[]{:S(2)}) %collective-permute-start.18) | collective-permute-done | bytes 1048608 | tf_op jit(solution)/shard_map/ppermute | solution.py:402
  107.5 1.8 %finish.3 = f32[3,256,512]{2,1,0:T(8,128)} custom-call(s32[1,3]{1,0:T(1,128)S(1)} %copy-done.2, f32[1]{0:T(128)S(6)} %copy.7.step_ref, f32[3,512,512]{2,1,0:T(8,128)S(1)} %bitcast.5, f32[2,256,512]{2,1,0:T(8,128)S(1)} %get-tuple-element.43.keep_ref, f32[2,256,512]{2,1,0:T(8,128)S(1)} %collective-permute-done.18.other_ref, ...), custom_call_target="tpu_custom_call", output_to_operand_aliasing={{}: (5, {})} | custom-call | tf_op jit(solution)/shard_map/finish/pallas_call | solution.py:384
  (31 shorter events, 8.2 us)
Async XLA Ops:
  0.0 8.5 %collective-permute-start.1 = (f32[256,512]{1,0:T(8,128)}, f32[256,512]{1,0:T(8,128)S(1)}, u32[]{:S(2)}, u32[]{:S(2)}) collective-permute-start(f32[256,512]{1,0:T(8,128)} %own.3), channel_id=1, source_target_pairs={{0,2},{1,5},{2,0},{3,7},{4,6},{5,1},{6,4},{7,3},{8,10},{9,13},{10,... | collective-permute-start | bytes 1572872 | tf_op jit(solution)/shard_map/ppermute | solution.py:107
  0.2 13.9 %collective-permute-start.4 = (f32[256,512]{1,0:T(8,128)}, f32[256,512]{1,0:T(8,128)S(1)}, u32[]{:S(2)}, u32[]{:S(2)}) collective-permute-start(f32[256,512]{1,0:T(8,128)} %own.3), channel_id=1, source_target_pairs={{0,24},{1,25},{2,26},{3,27},{4,28},{5,29},{6,30},{7,31},{8,0},{9,1... | collective-permute-start | bytes 1572872 | tf_op jit(solution)/shard_map/ppermute | solution.py:107
  3.5 3.5 %collective-permute-start = (s32[1,3]{1,0:T(1,128)}, s32[1,3]{1,0:T(1,128)S(1)}, u32[]{:S(2)}, u32[]{:S(2)}) collective-permute-start(s32[1,3]{1,0:T(1,128)} %offs_ref.11), channel_id=1, source_target_pairs={{0,4},{1,3},{2,6},{3,1},{4,0},{5,7},{6,2},{7,5},{8,12},{9,11},{10,... | collective-permute-start | bytes 44 | tf_op jit(solution)/shard_map/ppermute | solution.py:107
  3.8 21.9 %copy-start.2 = (s32[1,3]{1,0:T(1,128)S(1)}, s32[1,3]{1,0:T(1,128)}, u32[]{:S(2)}) copy-start(s32[1,3]{1,0:T(1,128)} %offs_ref.11) | copy-start | bytes 40
  7.0 22.0 %copy-start.1 = (f32[256,512]{1,0:T(8,128)S(1)}, f32[256,512]{1,0:T(8,128)}, u32[]{:S(2)}) copy-start(f32[256,512]{1,0:T(8,128)} %own.3) | copy-start | bytes 1572868
  8.5 8.6 %collective-permute-start.3 = (f32[256,512]{1,0:T(8,128)S(1)}, f32[256,512]{1,0:T(8,128)S(1)}, u32[]{:S(2)}, u32[]{:S(2)}) collective-permute-start(f32[256,512]{1,0:T(8,128)S(1)} %get-tuple-element.29.refs_1_), channel_id=1, source_target_pairs={{0,4},{1,3},{2,6},{3,1},{4,0},{5,7},{6,2},{7,5},{8,12},{9,11},{10,... | collective-permute-start | bytes 1572872 | tf_op jit(solution)/shard_map/ppermute | solution.py:107
  8.8 16.9 %collective-permute-start.2 = (f32[256,512]{1,0:T(8,128)S(1)}, f32[256,512]{1,0:T(8,128)S(1)}, u32[]{:S(2)}, u32[]{:S(2)}) collective-permute-start(f32[256,512]{1,0:T(8,128)S(1)} %get-tuple-element.28.refs_0_), channel_id=1, source_target_pairs={{0,4},{1,3},{2,6},{3,1},{4,0},{5,7},{6,2},{7,5},{8,12},{9,11},{10,... | collective-permute-start | bytes 1572872 | tf_op jit(solution)/shard_map/ppermute | solution.py:107
  14.1 14.9 %collective-permute-start.5 = (f32[256,512]{1,0:T(8,128)S(1)}, f32[256,512]{1,0:T(8,128)S(1)}, u32[]{:S(2)}, u32[]{:S(2)}) collective-permute-start(f32[256,512]{1,0:T(8,128)S(1)} %collective-permute-done.4.refs_2_.group), channel_id=1, source_target_pairs={{0,2},{1,5},{2,0},{3,7},{4,6},{5,1},{6,4},{7,3},{8,10},{9,13},{10,... | collective-permute-start | bytes 1572872 | tf_op jit(solution)/shard_map/ppermute | solution.py:107
  16.5 12.5 %collective-permute-start.6 = (f32[256,512]{1,0:T(8,128)S(1)}, f32[256,512]{1,0:T(8,128)S(1)}, u32[]{:S(2)}, u32[]{:S(2)}) collective-permute-start(f32[256,512]{1,0:T(8,128)S(1)} %collective-permute-done.1.refs_1_.first), channel_id=1, source_target_pairs={{2,18},{5,21},{10,26},{13,29},{18,2},{21,5},{26,10},{29,13}} | collective-permute-start | bytes 1572872 | tf_op jit(solution)/shard_map/ppermute | solution.py:107
  27.2 8.5 %collective-permute-start.9 = (f32[256,512]{1,0:T(8,128)S(1)}, f32[256,512]{1,0:T(8,128)S(1)}, u32[]{:S(2)}, u32[]{:S(2)}) collective-permute-start(f32[256,512]{1,0:T(8,128)S(1)} %get-tuple-element.33), channel_id=1, source_target_pairs={{0,2},{1,5},{2,0},{3,7},{4,6},{5,1},{6,4},{7,3},{8,10},{9,13},{10,... | collective-permute-start | bytes 1572872 | tf_op jit(solution)/shard_map/ppermute | solution.py:107
  27.3 8.5 %collective-permute-start.10 = (f32[256,512]{1,0:T(8,128)S(1)}, f32[256,512]{1,0:T(8,128)S(1)}, u32[]{:S(2)}, u32[]{:S(2)}) collective-permute-start(f32[256,512]{1,0:T(8,128)S(1)} %get-tuple-element.34), channel_id=1, source_target_pairs={{26,0},{29,1},{2,8},{5,9},{10,16},{13,17},{18,24},{21,25}} | collective-permute-start | bytes 1572872 | tf_op jit(solution)/shard_map/ppermute | solution.py:107
  29.0 28.5 %copy-start = (f32[1,3,512,512]{3,2,1,0:T(8,128)S(1)}, f32[1,3,512,512]{3,2,1,0:T(8,128)}, u32[]{:S(2)}) copy-start(f32[1,3,512,512]{3,2,1,0:T(8,128)} %param.5) | copy-start | bytes 9437188
  29.7 27.8 %collective-permute-start.7 = (f32[2,256,512]{2,1,0:T(8,128)S(1)}, f32[2,256,512]{2,1,0:T(8,128)S(1)}, u32[]{:S(2)}, u32[]{:S(2)}) collective-permute-start(f32[2,256,512]{2,1,0:T(8,128)S(1)} %choose.2), channel_id=1, source_target_pairs={{0,4},{1,3},{2,6},{3,1},{4,0},{5,7},{6,2},{7,5},{8,12},{9,11},{10,... | collective-permute-start | bytes 3145736 | tf_op jit(solution)/shard_map/ppermute | solution.py:107
  33.9 25.7 %collective-permute-start.8 = (f32[256,512]{1,0:T(8,128)S(1)}, f32[256,512]{1,0:T(8,128)S(1)}, u32[]{:S(2)}, u32[]{:S(2)}) collective-permute-start(f32[256,512]{1,0:T(8,128)S(1)} %get-tuple-element.31), channel_id=1, source_target_pairs={{0,2},{6,4},{1,5},{4,6},{3,7},{8,10},{14,12},{9,13},{12,14},{11,15... | collective-permute-start | bytes 1572872 | tf_op jit(solution)/shard_map/ppermute | solution.py:107
  35.9 23.7 %collective-permute-start.11 = (f32[256,512]{1,0:T(8,128)S(1)}, f32[256,512]{1,0:T(8,128)S(1)}, u32[]{:S(2)}, u32[]{:S(2)}) collective-permute-start(f32[256,512]{1,0:T(8,128)S(1)} %add_add_fusion), channel_id=1, source_target_pairs={{24,0},{25,1},{26,2},{27,3},{28,4},{29,5},{30,6},{31,7},{0,8},{1,9... | collective-permute-start | bytes 1572872 | tf_op jit(solution)/shard_map/ppermute | solution.py:107
  59.8 12.9 %collective-permute-start.13 = (f32[256,512]{1,0:T(8,128)S(1)}, f32[256,512]{1,0:T(8,128)S(1)}, u32[]{:S(2)}, u32[]{:S(2)}) collective-permute-start(f32[256,512]{1,0:T(8,128)S(1)} %add_add_fusion.1.refs_0_.image_ref.own), channel_id=1, source_target_pairs={{0,24},{1,25},{2,26},{3,27},{4,28},{5,29},{6,30},{7,31},{8,0},{9,1... | collective-permute-start | bytes 1572872 | tf_op jit(solution)/shard_map/ppermute | solution.py:107
  59.9 12.8 %collective-permute-start.12 = (f32[256,512]{1,0:T(8,128)S(1)}, f32[256,512]{1,0:T(8,128)S(1)}, u32[]{:S(2)}, u32[]{:S(2)}) collective-permute-start(f32[256,512]{1,0:T(8,128)S(1)} %add_add_fusion.1.refs_0_.image_ref.own), channel_id=1, source_target_pairs={{0,2},{1,5},{2,0},{3,7},{4,6},{5,1},{6,4},{7,3},{8,10},{9,13},{10,... | collective-permute-start | bytes 1572872 | tf_op jit(solution)/shard_map/ppermute | solution.py:107
  72.7 8.3 %collective-permute-start.14 = (f32[256,512]{1,0:T(8,128)S(1)}, f32[256,512]{1,0:T(8,128)S(1)}, u32[]{:S(2)}, u32[]{:S(2)}) collective-permute-start(f32[256,512]{1,0:T(8,128)S(1)} %collective-permute-done.13.refs_2_.group), channel_id=1, source_target_pairs={{0,2},{1,5},{2,0},{3,7},{4,6},{5,1},{6,4},{7,3},{8,10},{9,13},{10,... | collective-permute-start | bytes 1572872 | tf_op jit(solution)/shard_map/ppermute | solution.py:107
  81.6 19.6 %collective-permute-start.17 = (f32[2,256,512]{2,1,0:T(8,128)S(1)}, f32[2,256,512]{2,1,0:T(8,128)S(1)}, u32[]{:S(2)}, u32[]{:S(2)}) collective-permute-start(f32[2,256,512]{2,1,0:T(8,128)S(1)} %choose.3.refs_1_), channel_id=1, source_target_pairs={{0,4},{1,3},{2,6},{3,1},{4,0},{5,7},{6,2},{7,5},{8,12},{9,11},{10,... | collective-permute-start | bytes 3145736 | tf_op jit(solution)/shard_map/ppermute | solution.py:107
  85.2 4.7 %collective-permute-start.15 = (f32[1,256,512]{2,1,0:T(8,128)S(1)}, f32[1,256,512]{2,1,0:T(8,128)S(1)}, u32[]{:S(2)}, u32[]{:S(2)}) collective-permute-start(f32[1,256,512]{2,1,0:T(8,128)S(1)} %get-tuple-element.37), channel_id=1, source_target_pairs={{0,1},{1,0},{2,3},{3,2},{4,5},{5,4},{6,7},{7,6},{8,9},{9,8},{10,11... | collective-permute-start | bytes 1572872 | tf_op jit(solution)/shard_map/ppermute | solution.py:402
  88.0 11.2 %collective-permute-start.16 = (f32[256,512]{1,0:T(8,128)S(1)}, f32[256,512]{1,0:T(8,128)S(1)}, u32[]{:S(2)}, u32[]{:S(2)}) collective-permute-start(f32[256,512]{1,0:T(8,128)S(1)} %collective-permute-done.14.refs_3_.both), channel_id=1, source_target_pairs={{2,30},{5,31},{10,6},{13,7},{18,14},{21,15},{26,22},{29,23}} | collective-permute-start | bytes 1572872 | tf_op jit(solution)/shard_map/ppermute | solution.py:107
  103.2 4.3 %collective-permute-start.18 = (f32[2,256,512]{2,1,0:T(8,128)S(1)}, f32[2,256,512]{2,1,0:T(8,128)S(1)}, u32[]{:S(2)}, u32[]{:S(2)}) collective-permute-start(f32[2,256,512]{2,1,0:T(8,128)S(1)} %get-tuple-element.44), channel_id=1, source_target_pairs={{0,1},{1,0},{2,3},{3,2},{4,5},{5,4},{6,7},{7,6},{8,9},{9,8},{10,11... | collective-permute-start | bytes 3145736 | tf_op jit(solution)/shard_map/ppermute | solution.py:402
